TPU v7x, 32 devices: a whole 2x2x4 slice. The times are simulated.
32 devices in a mesh: seq: 8 (over y, x, core), tp: 4 (over z).
Axes of the slice: x: 2, y: 2, z: 4, core: 2. Of those that a mesh axis runs over, the one named last changes fastest.
Arguments:
- byte_ids: int32 [1024, 8], P('seq'), may hold values from 0 to 255
- global_out: bfloat16 [1024, 8192], P('seq', 'tp'), may hold values from -6 to 6
- global_in_grad: bfloat16 [1024, 8192], P('seq', 'tp'), may hold values from -6 to 6
- out_grad: bfloat16 [8192, 1024], P(('seq', 'tp')), may hold values from -6 to 6
- proj_weight: bfloat16 [1024, 1024], replicated, may hold values from -0.1875 to 0.1875
- emb_local: bfloat16 [256, 1024], replicated, may hold values from -6 to 6
- norm_gain: float32 [1024], replicated, may hold values from 0.1 to 1.9
- up_weight: bfloat16 [1024, 2048], replicated, may hold values from -0.1875 to 0.1875
- down_weight: bfloat16 [2048, 1024], replicated, may hold values from -0.125 to 0.125
Outputs:
- glob_out_grad: bfloat16 [1024, 8192], P('seq', 'tp')
- emb_global_grad: float32 [256, 1024], replicated
- emb_local_grad: float32 [256, 1024], replicated
- gain_grad: float32 [1024], replicated
- proj_grad: float32 [1024, 1024], P(None, ('seq', 'tp'))
- up_grad: float32 [1024, 2048], P(None, ('seq', 'tp'))
- down_grad: float32 [2048, 1024], P(('seq', 'tp'))
All inputs are finite; a program needn't handle non-finite values.
Results may differ from a plain program's by a relative error of at most 0.015.
Values may be sent and summed in bfloat16 or wider, within the bound.
No kernel may reach another device: no remote copies, remote signals or barrier semaphores. Data moves between devices by JAX's collectives and lax.ppermute only.
A program may use at most 128 MiB of HBM per device.

v0:
```python
import functools

import jax
import jax.numpy as jnp
from jax import lax
from jax.experimental import pallas as pl
from jax.experimental.pallas import tpu as pltpu
from jax.sharding import PartitionSpec as P

BF = jnp.bfloat16
F32 = jnp.float32
ROOM = 8 * 1024 * 1024
STEP = 6 * 1000 * 1000 * 1000
VMEM = pltpu.VMEM


def inner(left, right):
    return lax.dot_general(
        left, right, (((0,), (0,)), ((), ())), preferred_element_type=F32
    )


def outer(left, right):
    return lax.dot_general(
        left, right, (((1,), (1,)), ((), ())), preferred_element_type=F32
    )


def times(left, right):
    return jnp.dot(left, right, preferred_element_type=F32)


def swap(value, axis, masks):
    count = lax.axis_size(axis)
    pairs = [(i, i ^ masks[i % len(masks)]) for i in range(count)]
    return lax.ppermute(value, axis, pairs)


def like(rows, columns, kind):
    return jax.ShapeDtypeStruct((rows, columns), kind)


def whole(array):
    return pl.BlockSpec(array.shape, lambda n, s: (0,) * len(array.shape))


def run(
    body, outs, ins, after, numbers, in_specs=None, out_specs=None, scratch=(), room=ROOM,
    alias=None, flops=0, grid=1,
):
    count, late = 1 + len(ins), len(after)

    def kernel(*refs):
        body(*refs[:count], *refs[count + late :])

    in_specs = in_specs or [None] * len(ins)
    out_specs = out_specs or [None] * len(outs)
    return pl.pallas_call(
        kernel,
        out_shape=tuple(outs),
        grid_spec=pltpu.PrefetchScalarGridSpec(
            num_scalar_prefetch=1,
            grid=(grid,),
            in_specs=[s or whole(a) for s, a in zip(in_specs, ins)]
            + [pl.BlockSpec(memory_space=pl.ANY)] * late,
            out_specs=tuple(s or whole(a) for s, a in zip(out_specs, outs)),
            scratch_shapes=list(scratch),
        ),
        input_output_aliases=alias or {},
        compiler_params=pltpu.CompilerParams(vmem_limit_bytes=room),
        cost_estimate=pl.CostEstimate(flops=flops, bytes_accessed=0, transcendentals=0),
    )(numbers, *ins, *after)


def sort_body(patch, part, own, numbers, grad, *blocks):
    size = own * part
    row = lax.broadcasted_iota(jnp.int32, (size, grad.shape[0]), 0)
    source = lax.broadcasted_iota(jnp.int32, (size, grad.shape[0]), 1)
    for m, block in enumerate(blocks):
        wanted = (row % part) * patch + numbers[m] * own + row // part
        block[...] = times((source == wanted).astype(BF), grad[...]).astype(BF)


def join_body(part, own, count, numbers, *refs):
    blocks, joined = refs[:-1], refs[-1]
    for m, block in enumerate(blocks):
        for j in range(own):
            start = pl.multiple_of((j * count + numbers[m]) * part, part)
            joined[pl.ds(start, part), :] = block[j * part : (j + 1) * part, :]


def sent_order(count):
    return sorted(range(count), key=lambda m: bin(m + count)[:2:-1])


def id_of(ids, place):
    lane = lax.broadcasted_iota(jnp.int32, ids.shape, 1)
    return jnp.sum(jnp.where(lane == place, ids + 1, 0), axis=1, keepdims=True) - 1


def vocab_line(numbers, first, count, height):
    lane = lax.broadcasted_iota(jnp.int32, (1, count * height), 1)
    line = lane % height
    for n in range(count):
        line = line + jnp.where(lane // height == n, numbers[first + n] * height, 0)
    return line


def hot(ids, line):
    return jnp.where(ids == line, 1.0, 0.0).astype(BF)


def place_body(own, core_at, numbers, mine, other, both):
    patches, width = mine.shape[0], mine.shape[1] // own
    rows = own * patches
    for side, value in ((numbers[core_at], mine), (1 - numbers[core_at], other)):
        for j in range(own):
            start = pl.multiple_of(side * rows + j * patches, patches)
            both[pl.ds(start, patches), :] = value[:, j * width : (j + 1) * width]


def hots_body(own, tp_count, share_count, height, core_at, numbers, ids_own, ids_other, prev, here, mine):
    patches = ids_own.shape[1]
    plain = lax.broadcasted_iota(jnp.int32, (1, prev.shape[1]), 1)
    line = vocab_line(numbers, tp_count, share_count, height)
    both = vocab_line(numbers, tp_count, 2 * share_count, height)
    core = numbers[core_at]
    for side, which in ((core, ids_own), (1 - core, ids_other)):
        ids = which[...].T
        for j in range(own):
            start = pl.multiple_of(side * own * patches + j * patches, patches)
            at = pl.ds(start, patches)
            before = id_of(ids, numbers[0] * own + j - 1)
            prev[at, :] = hot(before, plain)
            here[at, :] = hot(before, line)
            if which is ids_own:
                wanted = id_of(ids, numbers[0] * own + j)
                mine[j * patches : (j + 1) * patches, :] = hot(wanted, both)


def turn_matrix(tp_count, chunk, numbers):
    unit = chunk // tp_count
    row = lax.broadcasted_iota(jnp.int32, (chunk, chunk), 0)
    column = lax.broadcasted_iota(jnp.int32, (chunk, chunk), 1)
    source = column % unit
    for i, m in enumerate(sent_order(tp_count)):
        source = source + jnp.where(column // unit == i, numbers[m] * unit, 0)
    return (row == source).astype(BF)


def pick_up_body(tp_count, share_count, numbers, up, up_here, ups, ready):
    chunk = ups.shape[2]
    half = chunk // 2
    copies = []
    for n in range(share_count):
        at = pl.ds(pl.multiple_of(numbers[tp_count + n] * chunk, chunk), chunk)
        copies.append(pltpu.make_async_copy(up.at[:, at], ups.at[n], ready.at[n]))
        copies[-1].start()
    turn = turn_matrix(tp_count, chunk, numbers)
    for n in range(share_count):
        copies[n].wait()
        value = times(ups[n], turn).astype(BF)
        for z in range(2):
            first = (z * share_count + n) * half
            up_here[:, first : first + half] = value[:, z * half : (z + 1) * half]


def pick_down_body(tp_count, share_count, numbers, down, down_here, downs, ready):
    chunk = downs.shape[1]
    unit = chunk // tp_count
    half = chunk // 2
    copies = []
    for n in range(share_count):
        at = pl.ds(pl.multiple_of(numbers[tp_count + n] * chunk, chunk), chunk)
        copies.append(pltpu.make_async_copy(down.at[at, :], downs.at[n], ready.at[n]))
        copies[-1].start()
    for n in range(share_count):
        copies[n].wait()
        for i, m in enumerate(sent_order(tp_count)):
            z, place = i // (tp_count // 2), i % (tp_count // 2)
            first = (z * share_count + n) * half + place * unit
            start = pl.multiple_of(numbers[m] * unit, unit)
            down_here[first : first + unit, :] = downs[n, pl.ds(start, unit), :]


def split_body(tp_count, share, numbers, value, kept, sent):
    unit = share // tp_count
    half = kept.shape[0]
    for n in range(value.shape[0] // share):
        for i, m in enumerate(sent_order(tp_count)):
            at = pl.ds(n * share + pl.multiple_of(numbers[m] * unit, unit), unit)
            place = n * share + i * unit
            target = kept if place < half else sent
            row = place % half
            target[row : row + unit, :] = value[at, :].astype(target.dtype)


def tables_in_body(
    share_count, first_share, height, numbers, glob, glob_more, local, gains, kept, sent
):
    width = glob.shape[1]
    strip = width // (2 * share_count)
    lines = width // 128
    lane = lax.broadcasted_iota(jnp.int32, (1, width), 1)
    both = glob[...].astype(F32) + glob_more[...].astype(F32)
    size = 2 * height
    kept[:, width:] = jnp.zeros((kept.shape[0], 128), BF)
    sent[:, width:] = jnp.zeros((sent.shape[0], 128), BF)
    for n in range(share_count):
        target = kept if n < share_count // 2 else sent
        first = (n % (share_count // 2)) * size
        at = slice(n * height, (n + 1) * height)
        target[first : first + height, :width] = both[at, :].astype(BF)
        target[first + height : first + size, :width] = local[at, :].astype(BF)
        mine = jnp.where(lane // strip == numbers[first_share + n], gains[...], 0.0)
        rows = [mine[:, i * 128 : (i + 1) * 128] for i in range(lines)]
        rows.append(jnp.zeros((16 - lines, 128), F32))
        target[first : first + 16, width:] = jnp.concatenate(rows, axis=0).astype(BF)


def gate_body(numbers, value, same):
    pass


def add_body(numbers, kept, arrived, keep, send):
    half = keep.shape[0]
    keep[...] = (kept[:half, :].astype(F32) + arrived[:half, :].astype(F32)).astype(keep.dtype)
    send[...] = (kept[half:, :].astype(F32) + arrived[half:, :].astype(F32)).astype(send.dtype)


def sum_body(numbers, kept, arrived, summed):
    summed[...] = (kept[...].astype(F32) + arrived[...].astype(F32)).astype(summed.dtype)


def stack_body(numbers, first, second, both):
    rows = first.shape[0]
    both[:rows, :] = first[...]
    both[rows:, :] = second[...]


def sort_out_body(numbers, place, sort):
    vocab = (sort.shape[0] - 16) // 2
    row = lax.broadcasted_iota(jnp.int32, (vocab, sort.shape[1]), 0)
    sort[:vocab, :] = hot(row, place[:1, :])
    sort[vocab : 2 * vocab, :] = hot(row, place[1:2, :])
    sort[2 * vocab :, :] = place[2:, :].astype(F32).astype(BF)


def tables_body(numbers, first, second, first_gain, second_gain, sort, glob, local, gain):
    half = first.shape[0]
    vocab = glob.shape[0]
    tall = sort[: 2 * vocab]
    value = times(tall[:, :half], first[...]) + times(tall[:, half:], second[...])
    glob[...] = value[:vocab]
    local[...] = value[vocab:]

    @pl.when(pl.program_id(0) == 0)
    def _():
        flat = sort[2 * vocab :]
        value = times(flat[:, :half], first_gain[...])
        value = value + times(flat[:, half:], second_gain[...])
        gain[...] = value[: gain.shape[0]]


def on_device(
    byte_ids,
    global_out,
    global_in_grad,
    out_grad,
    proj_weight,
    emb_local,
    norm_gain,
    up_weight,
    down_weight,
):
    seq_count = lax.axis_size("seq")
    tp_count = lax.axis_size("tp")
    seq_place = lax.axis_index("seq")
    tp_place = lax.axis_index("tp")
    core = seq_place & 1
    chip = seq_place >> 1
    stages = seq_count.bit_length() - 2
    levels = tp_count.bit_length() - 1
    share_count = 1 << stages
    walks = (list(range(1, stages + 1)), list(range(stages, 0, -1)))
    patches, patch = byte_ids.shape
    slot, width = proj_weight.shape
    hidden = up_weight.shape[1]
    vocab = emb_local.shape[0]
    own = patch // tp_count
    part = patches // tp_count
    rows = own * patches
    height = vocab // seq_count
    chunk = hidden // seq_count

    def share_mask(number, walk):
        mask = 0
        for k in range(stages):
            if (number >> (stages - 1 - k)) & 1:
                mask |= 1 << (walk[k] - 1)
        return mask

    def shares_of(which):
        return [
            2 * (chip ^ jnp.where(which == 0, share_mask(n, walks[0]), share_mask(n, walks[1])))
            + which
            for n in range(share_count)
        ]

    shares = shares_of(core)
    others = shares_of(1 - core)
    near = [tp_place ^ m for m in range(tp_count)]
    numbers = jnp.stack(near + shares + others + [core]).astype(jnp.int32)
    core_at = tp_count + 2 * share_count
    call = functools.partial(run, numbers=numbers)

    def core_swap(value):
        return swap(value, "seq", (1,))

    def go(value, step):
        kind, k = step
        if kind == "seq":
            return swap(value, "seq", (1 << walks[0][k], 1 << walks[1][k]))
        return swap(value, "tp", (1 << k,))

    def gate(value, after):
        there = pl.BlockSpec(memory_space=pl.ANY)
        (value,) = call(
            gate_body,
            [like(*value.shape, value.dtype)],
            [value],
            after,
            in_specs=[there],
            out_specs=[there],
            alias={1: 0},
        )
        return value

    ids_own = byte_ids.T
    ids_other = core_swap(ids_own)
    out_other = core_swap(global_out)
    blocks = call(
        functools.partial(sort_body, patch, part, own),
        [like(own * part, width, BF)] * tp_count,
        [out_grad],
        [],
    )
    blocks = [swap(b, "tp", (m,)) if m else b for m, b in enumerate(blocks)]
    prev_hot, prev_here, own_hot = call(
        functools.partial(hots_body, own, tp_count, share_count, height, core_at),
        [like(2 * rows, vocab, BF), like(2 * rows, vocab // 2, BF), like(rows, vocab, BF)],
        [ids_own, ids_other],
        [blocks[0]],
    )

    def by_slot(value):
        return [value[:, j * slot : (j + 1) * slot] for j in range(own)]

    (slot_in,) = call(
        functools.partial(place_body, own, core_at),
        [like(2 * rows, slot, BF)],
        [global_out, out_other],
        [prev_hot],
    )
    u_rows = times(slot_in, proj_weight) + times(prev_hot, emb_local)
    scale = lax.rsqrt(jnp.mean(u_rows * u_rows, axis=1, keepdims=True) + 1e-05)
    normed = u_rows * scale
    r_rows = (normed * norm_gain).astype(BF)
    far = pl.BlockSpec(memory_space=pltpu.HBM)
    (up_here,) = call(
        functools.partial(pick_up_body, tp_count, share_count),
        [like(width, hidden // 2, BF)],
        [up_weight],
        [r_rows],
        in_specs=[far],
        scratch=[VMEM((share_count, width, chunk), BF), pltpu.SemaphoreType.DMA((share_count,))],
    )
    a_rows = times(r_rows, up_here)
    sig = jax.nn.sigmoid(a_rows)
    h_rows = (a_rows * sig).astype(BF)
    slope = (sig * (1.0 + a_rows * (1.0 - sig))).astype(BF)
    h_rows, slope = lax.optimization_barrier((h_rows, slope))
    (down_here,) = call(
        functools.partial(pick_down_body, tp_count, share_count),
        [like(hidden // 2, width, BF)],
        [down_weight],
        [h_rows],
        in_specs=[far],
        scratch=[VMEM((share_count, chunk, width), BF), pltpu.SemaphoreType.DMA((share_count,))],
    )
    strip = chunk // 2
    h_rows = jnp.concatenate(
        [
            h_rows[:, (z * share_count + n) * strip : (z * share_count + n + 1) * strip]
            for n in range(share_count)
            for z in range(2)
        ],
        axis=1,
    )

    (grad_own,) = call(
        functools.partial(join_body, part, own, tp_count),
        [like(rows, width, BF)],
        blocks,
        [h_rows, down_here],
    )
    grad_other = core_swap(grad_own)
    own_hot = gate(own_hot, [grad_own])
    glob = [
        inner(own_hot[j * patches : (j + 1) * patches], value)
        for j, value in enumerate(by_slot(global_in_grad))
    ]
    glob = sum(glob[1:], glob[0])
    glob_sent = glob[vocab // 2 :].astype(BF)
    glob_kept = glob[: vocab // 2].astype(BF)
    glob_more = core_swap(glob_sent)

    (out_rows,) = call(
        functools.partial(place_body, 1, core_at),
        [like(2 * rows, width, BF)],
        [grad_own, grad_other],
        [glob_kept],
    )

    seq_steps = [("seq", k) for k in range(stages)]
    tp_steps = [("tp", k) for k in range(levels)]

    step = functools.partial(call, flops=STEP)

    class Chain:
        def __init__(self, kept, sent, steps):
            self.kept, self.steps, self.at = kept, steps, 0
            self.arrived = go(sent, self.steps[0])
            self.left = len(self.steps)

        def next(self, after):
            self.at += 1
            self.left -= 1
            rows, columns = self.kept.shape
            ins = [self.kept, self.arrived]
            if self.left:
                outs = [like(rows // 2, columns, self.kept.dtype)] * 2
                self.kept, sent = step(add_body, outs, ins, after)
                self.arrived = go(sent, self.steps[self.at])
            else:
                (self.kept,) = step(sum_body, [like(rows, columns, F32)], ins, after)
            return self.kept

    class Table:
        def __init__(self, kept, sent):
            self.kept, self.at = kept, 0
            self.plan = (
                [("half", s) for s in seq_steps]
                + [("sum", s) for s in tp_steps]
                + [("join", s) for s in reversed(seq_steps)]
                + [("join", None)]
            )
            self.left = len(self.plan) - 1
            self.arrived = go(sent, self.plan[0][1])

        def next(self, after):
            last, (kind, hop) = self.plan[self.at][0], self.plan[self.at + 1]
            rows, columns = self.kept.shape
            ins = [self.kept, self.arrived]
            if last == "half" and kind == "half":
                self.kept, sent = step(add_body, [like(rows // 2, columns, BF)] * 2, ins, after)
            elif last == "join":
                (self.kept,) = step(stack_body, [like(2 * rows, columns, BF)], ins, after)
                sent = self.kept
            else:
                (self.kept,) = step(sum_body, [like(rows, columns, BF)], ins, after)
                sent = self.kept
            self.at += 1
            self.left -= 1
            self.arrived = core_swap(sent) if hop is None else go(sent, hop)
            return self.kept

    dh_rows = outer(out_rows, down_here)
    da_rows = (dh_rows * slope.astype(F32)).astype(BF)
    dr_part = outer(da_rows, up_here)
    dr_sent = dr_part.astype(BF)
    kind = BF if chunk // tp_count % 16 == 0 else F32
    half = h_rows.shape[1] // 2
    down_kept = inner(h_rows[:, :half], out_rows).astype(kind)
    down_sent = inner(h_rows[:, half:], out_rows).astype(kind)
    up_kept = inner(da_rows[:, :half], r_rows).astype(kind)
    up_sent = inner(da_rows[:, half:], r_rows).astype(kind)
    down = Chain(down_kept, down_sent, seq_steps + tp_steps)
    up = Chain(up_kept, up_sent, tp_steps[:1] + seq_steps + tp_steps[1:])
    dr_more = gate(core_swap(dr_sent), [down_sent, up_sent])
    dr_rows = dr_part + dr_more.astype(F32)

    gain_part = jnp.sum(dr_rows * normed, axis=0, keepdims=True)
    dn_rows = dr_rows * norm_gain
    du_rows = (
        out_rows.astype(F32)
        + scale * (dn_rows - normed * jnp.mean(dn_rows * normed, axis=1, keepdims=True))
    ).astype(BF)
    size = 2 * height
    kept, sent = call(
        functools.partial(tables_in_body, share_count, tp_count, height),
        [like(share_count // 2 * size, width + 128, BF)] * 2,
        [glob_kept, glob_more, inner(prev_here, du_rows), gain_part],
        [up.kept],
    )
    table = Table(kept, sent)
    share = width // seq_count
    kind = BF if share // tp_count % 16 == 0 else F32
    du_here = jnp.concatenate(
        [lax.dynamic_slice_in_dim(du_rows, s * share, share, 1) for s in shares], axis=1
    )
    value = inner(du_here, slot_in)
    kept, sent = call(
        functools.partial(split_body, tp_count, share),
        [like(value.shape[0] // 2, slot, kind)] * 2,
        [value],
        [table.kept],
    )
    proj = Chain(kept, sent, seq_steps + tp_steps)
    du_own = lax.dynamic_slice_in_dim(du_rows, core * rows, rows, 0)
    back = outer(du_own, proj_weight).astype(BF)
    glob_out_grad = jnp.concatenate(
        [back[j * patches : (j + 1) * patches] for j in range(own)], axis=1
    )

    all_numbers = jnp.stack(shares + others)
    inside = jnp.arange(size)[None, :]
    own_row = all_numbers[:, None] * height + inside
    place = jnp.stack(
        [
            jnp.where(inside < height, own_row, -1).reshape(-1),
            jnp.where(inside >= height, own_row - height, -1).reshape(-1),
        ]
        + [
            jnp.broadcast_to(inside == line, own_row.shape).reshape(-1).astype(jnp.int32)
            for line in range(16)
        ]
    ).astype(jnp.int32)
    count = seq_count * size
    (sort,) = call(
        sort_out_body, [like(2 * vocab + 16, count, BF)], [place], [table.kept]
    )
    last = [up.kept, proj.kept, table.kept, down.kept, glob_out_grad, sort]
    names = {"T": table, "D": down, "U": up, "P": proj}
    queue = [names[c] for c in "TDTUTPDUPTUTPDTPUTD"]
    for chain in queue + [table, proj, down, up] * 16:
        if chain.left:
            last = [chain.next(last)]

    parts = 4
    wide = width // parts

    def columns(height):
        return pl.BlockSpec((height, wide), lambda n, s: (0, n))

    lines = width // 128
    beside = pl.BlockSpec((count // 2, 128), lambda n, s: (0, lines))
    emb_global_grad, emb_local_grad, gain_grad = call(
        tables_body,
        [like(vocab, width, F32), like(vocab, width, F32), like(lines, 128, F32)],
        [table.kept, table.arrived, table.kept, table.arrived, sort],
        last,
        grid=parts,
        in_specs=[columns(count // 2), columns(count // 2), beside, beside, None],
        out_specs=[columns(vocab), columns(vocab), None],
    )
    return (
        glob_out_grad,
        emb_global_grad,
        emb_local_grad,
        gain_grad.reshape(width),
        proj.kept.T,
        up.kept.T,
        down.kept,
    )


def solution(mesh):
    placed = (
        P("seq", None),
        P("seq", "tp"),
        P("seq", "tp"),
        P(("seq", "tp"), None),
        P(),
        P(),
        P(),
        P(),
        P(),
    )
    return jax.shard_map(
        on_device,
        mesh=mesh,
        in_specs=placed,
        out_specs=(
            P("seq", "tp"),
            P(),
            P(),
            P(),
            P(None, ("seq", "tp")),
            P(None, ("seq", "tp")),
            P(("seq", "tp"), None),
        ),
        check_vma=False,
    )
```

profile of v0, /device:TPU:0, one launch (start us, length us, event | category | flops | bytes accessed | tf_op | source)
XLA Modules:
  0.0 107.6 jit_solution(286297634003251329)
XLA Ops:
  0.8 1.2 %copy-done.4 = bf16[256,1024]{1,0:T(8,128)(2,1)S(1)} copy-done((bf16[256,1024]{1,0:T(8,128)(2,1)S(1)}, bf16[256,1024]{1,0:T(8,128)(2,1)}, u32[]{:S(2)}) %copy-start.4) | copy-done | bytes 524312
  2.0 1.7 %shard_map.144 = (bf16[64,1024]{1,0:T(8,128)(2,1)S(1)}, bf16[64,1024]{1,0:T(8,128)(2,1)}, bf16[64,1024]{1,0:T(8,128)(2,1)}, bf16[64,1024]{1,0:T(8,128)(2,1)}) custom-call(s32[13]{0:T(128)S(1)} %stack.85.refs_0_, bf16[256,1024]{1,0:T(8,128)(2,1)S(1)} %copy-done.4), custom_call_target="tpu_custom_call" | custom-call | tf_op jit(solution)/shard_map/pallas_call | solution.py:58
  3.7 3.0 %collective-permute-start = (bf16[64,1024]{1,0:T(8,128)(2,1)}, bf16[64,1024]{1,0:T(8,128)(2,1)S(1)}, u32[]{:S(2)}, u32[]{:S(2)}) collective-permute-start(bf16[64,1024]{1,0:T(8,128)(2,1)} %get-tuple-element.44), channel_id=1, source_target_pairs={{0,1},{1,0},{2,3},{3,2},{4,5},{5,4},{6,7},{7,6},{8,9},{9,8},{10,11... | collective-permute-start | bytes 393224 | tf_op jit(solution)/shard_map/ppermute | solution.py:36
  6.7 2.6 %collective-permute-start.1 = (bf16[64,1024]{1,0:T(8,128)(2,1)}, bf16[64,1024]{1,0:T(8,128)(2,1)}, u32[]{:S(2)}, u32[]{:S(2)}) collective-permute-start(bf16[64,1024]{1,0:T(8,128)(2,1)} %get-tuple-element.45), channel_id=1, source_target_pairs={{0,2},{1,3},{2,0},{3,1},{4,6},{5,7},{6,4},{7,5},{8,10},{9,11},{10,... | collective-permute-start | bytes 393224 | tf_op jit(solution)/shard_map/ppermute | solution.py:36
  13.3 1.5 %fusion.40 = f32[512,1024]{1,0:T(8,128)S(1)} fusion(bf16[512,256]{1,0:T(8,128)(2,1)S(1)} %get-tuple-element.47.refs_3_, bf16[256,1024]{1,0:T(8,128)(2,1)} %param.14), kind=kOutput, calls=%fused_computation.93 | convolution fusion | flops 268435456 | bytes 2883584 | tf_op jit(solution)/shard_map/dot_general | solution.py:30
  15.5 1.4 %multiply_reduce_fusion.2 = (f32[512]{0:T(512)S(1)}, f32[512,1024]{1,0:T(8,128)S(1)}) fusion(f32[512,1024]{1,0:T(8,128)S(1)} %fusion.40, bf16[512,1024]{1,0:T(8,128)(2,1)S(1)} %shard_map.146, bf16[1024,1024]{1,0:T(8,128)(2,1)S(1)} %copy-done), kind=kOutput, calls=%fused_computation.9 | convolution fusion | flops 1075314176 | bytes 7342080 | tf_op jit(solution)/shard_map/dot_general | solution.py:30
  17.7 2.6 %shard_map.147 = bf16[1024,1024]{1,0:T(8,128)(2,1)S(1)} custom-call(s32[13]{0:T(128)S(1)} %stack.85.refs_0_, bf16[1024,2048]{1,0:T(8,128)(2,1)S(1)} %copy-done.1, bf16[512,1024]{1,0:T(8,128)(2,1)S(1)} %multiply_convert_fusion.3.refs_2_), custom_call_target="tpu_custom_call" | custom-call | tf_op jit(solution)/shard_map/pallas_call | solution.py:58
  20.3 1.8 %multiply_convert_fusion.1 = (bf16[512,1024]{1,0:T(8,128)(2,1)S(1)}, bf16[512,1024]{1,0:T(8,128)(2,1)S(1)}) fusion(bf16[512,1024]{1,0:T(8,128)(2,1)S(1)} %multiply_convert_fusion.3.refs_2_, bf16[1024,1024]{1,0:T(8,128)(2,1)S(1)} %shard_map.147), kind=kOutput, calls=%fused_computation.5 | convolution fusion | flops 1078984704 | bytes 5242880 | tf_op jit(solution)/shard_map/dot_general | solution.py:30
  23.9 1.5 %shard_map.149.refs_2_.refs_1_ = bf16[256,1024]{1,0:T(8,128)(2,1)S(1)} custom-call(s32[13]{0:T(128)S(1)} %stack.85.refs_0_, bf16[64,1024]{1,0:T(8,128)(2,1)S(1)} %get-tuple-element.43.refs_3_.refs_1_, bf16[64,1024]{1,0:T(8,128)(2,1)S(1)} %collective-permute-done.refs_2_, bf16[64,1024]{1,0:T(8,128)(2,1)} %collective-permute-done.1.refs_3_, ...), custom_call_target="tpu_custom_call" | custom-call | tf_op jit(solution)/shard_map/pallas_call | solution.py:58
  28.0 1.3 %multiply_convert_fusion = bf16[512,1024]{1,0:T(8,128)(2,1)S(1)} fusion(bf16[512,1024]{1,0:T(8,128)(2,1)S(1)} %get-tuple-element.50, bf16[512,1024]{1,0:T(8,128)(2,1)S(1)} %shard_map.151, bf16[1024,1024]{1,0:T(8,128)(2,1)S(1)} %shard_map.148.refs_6_), kind=kOutput, calls=%fused_computation.4 | convolution fusion | flops 1075314688 | bytes 5242880 | tf_op jit(solution)/shard_map/dot_general | solution.py:24
  29.3 1.3 %fusion.39 = (bf16[512,1024]{1,0:T(8,128)(2,1)S(1)}, f32[512,1024]{1,0:T(8,128)S(1)}) fusion(bf16[512,1024]{1,0:T(8,128)(2,1)S(1)} %multiply_convert_fusion, bf16[1024,1024]{1,0:T(8,128)(2,1)S(1)} %shard_map.147), kind=kOutput, calls=%fused_computation.92 | convolution fusion | flops 1074266112 | bytes 6291456 | tf_op jit(solution)/shard_map/dot_general | solution.py:24
  31.6 1.8 %collective-permute-start.10 = (bf16[512,1024]{1,0:T(8,128)(2,1)S(1)}, bf16[512,1024]{1,0:T(8,128)(2,1)S(1)}, u32[]{:S(2)}, u32[]{:S(2)}) collective-permute-start(bf16[512,1024]{1,0:T(8,128)(2,1)S(1)} %convolution_convert_fusion.3.refs_2_), channel_id=1, source_target_pairs={{0,8},{4,20},{8,0},{12,28},{16,24},{20,4},{24,16},{28,12},{1,9},{5... | collective-permute-start | bytes 3145736 | tf_op jit(solution)/shard_map/ppermute | solution.py:36
  43.0 1.6 %collective-permute-start.14 = (bf16[256,1024]{1,0:T(8,128)(2,1)S(1)}, bf16[256,1024]{1,0:T(8,128)(2,1)S(1)}, u32[]{:S(2)}, u32[]{:S(2)}) collective-permute-start(bf16[256,1024]{1,0:T(8,128)(2,1)S(1)} %get-tuple-element.59), channel_id=1, source_target_pairs={{0,8},{4,20},{8,0},{12,28},{16,24},{20,4},{24,16},{28,12},{1,9},{5... | collective-permute-start | bytes 1572872 | tf_op jit(solution)/shard_map/ppermute | solution.py:36
  44.6 5.0 %collective-permute-done.8.refs_2_ = bf16[128,1152]{1,0:T(8,128)(2,1)S(1)} collective-permute-done((bf16[128,1152]{1,0:T(8,128)(2,1)S(1)}, bf16[128,1152]{1,0:T(8,128)(2,1)S(1)}, u32[]{:S(2)}, u32[]{:S(2)}) %collective-permute-start.8) | collective-permute-done | bytes 294944 | tf_op jit(solution)/shard_map/ppermute | solution.py:36
  50.2 1.8 %collective-permute-start.9 = (bf16[64,1152]{1,0:T(8,128)(2,1)S(1)}, bf16[64,1152]{1,0:T(8,128)(2,1)S(1)}, u32[]{:S(2)}, u32[]{:S(2)}) collective-permute-start(bf16[64,1152]{1,0:T(8,128)(2,1)S(1)} %get-tuple-element.56), channel_id=1, source_target_pairs={{0,16},{4,12},{8,24},{12,4},{16,0},{20,28},{24,8},{28,20},{1,17},{... | collective-permute-start | bytes 442376 | tf_op jit(solution)/shard_map/ppermute | solution.py:36
  53.2 3.0 %collective-permute-done.9.refs_2_ = bf16[64,1152]{1,0:T(8,128)(2,1)S(1)} collective-permute-done((bf16[64,1152]{1,0:T(8,128)(2,1)S(1)}, bf16[64,1152]{1,0:T(8,128)(2,1)S(1)}, u32[]{:S(2)}, u32[]{:S(2)}) %collective-permute-start.9) | collective-permute-done | bytes 147488 | tf_op jit(solution)/shard_map/ppermute | solution.py:36
  57.7 1.9 %collective-permute-done.12.refs_2_ = bf16[512,1024]{1,0:T(8,128)(2,1)S(1)} collective-permute-done((bf16[512,1024]{1,0:T(8,128)(2,1)S(1)}, bf16[512,1024]{1,0:T(8,128)(2,1)S(1)}, u32[]{:S(2)}, u32[]{:S(2)}) %collective-permute-start.12) | collective-permute-done | bytes 1048608 | tf_op jit(solution)/shard_map/ppermute | solution.py:36
  61.0 1.5 %collective-permute-done.11.refs_2_ = bf16[64,1152]{1,0:T(8,128)(2,1)S(1)} collective-permute-done((bf16[64,1152]{1,0:T(8,128)(2,1)S(1)}, bf16[64,1152]{1,0:T(8,128)(2,1)S(1)}, u32[]{:S(2)}, u32[]{:S(2)}) %collective-permute-start.11) | collective-permute-done | bytes 147488 | tf_op jit(solution)/shard_map/ppermute | solution.py:36
  63.1 2.5 %collective-permute-start.13 = (bf16[64,1152]{1,0:T(8,128)(2,1)S(1)}, bf16[64,1152]{1,0:T(8,128)(2,1)S(1)}, u32[]{:S(2)}, u32[]{:S(2)}) collective-permute-start(bf16[64,1152]{1,0:T(8,128)(2,1)S(1)} %shard_map.160.refs_3_.refs_1_), channel_id=1, source_target_pairs={{0,2},{1,3},{2,0},{3,1},{4,6},{5,7},{6,4},{7,5},{8,10},{9,11},{10,... | collective-permute-start | bytes 442376 | tf_op jit(solution)/shard_map/ppermute | solution.py:36
  66.2 1.5 %collective-permute-start.15 = (bf16[128,1024]{1,0:T(8,128)(2,1)S(1)}, bf16[128,1024]{1,0:T(8,128)(2,1)S(1)}, u32[]{:S(2)}, u32[]{:S(2)}) collective-permute-start(bf16[128,1024]{1,0:T(8,128)(2,1)S(1)} %get-tuple-element.61), channel_id=1, source_target_pairs={{0,16},{4,12},{8,24},{12,4},{16,0},{20,28},{24,8},{28,20},{1,17},{... | collective-permute-start | bytes 786440 | tf_op jit(solution)/shard_map/ppermute | solution.py:36
  68.4 1.8 %collective-permute-start.21 = (bf16[128,1024]{1,0:T(8,128)(2,1)S(1)}, bf16[128,1024]{1,0:T(8,128)(2,1)S(1)}, u32[]{:S(2)}, u32[]{:S(2)}) collective-permute-start(bf16[128,1024]{1,0:T(8,128)(2,1)S(1)} %get-tuple-element.69), channel_id=1, source_target_pairs={{0,1},{1,0},{2,3},{3,2},{4,5},{5,4},{6,7},{7,6},{8,9},{9,8},{10,11... | collective-permute-start | bytes 786440 | tf_op jit(solution)/shard_map/ppermute | solution.py:36
  70.2 1.4 %collective-permute-done.16.refs_2_ = bf16[256,1024]{1,0:T(8,128)(2,1)S(1)} collective-permute-done((bf16[256,1024]{1,0:T(8,128)(2,1)S(1)}, bf16[256,1024]{1,0:T(8,128)(2,1)S(1)}, u32[]{:S(2)}, u32[]{:S(2)}) %collective-permute-start.16) | collective-permute-done | bytes 524320 | tf_op jit(solution)/shard_map/ppermute | solution.py:36
  73.9 1.7 %collective-permute-start.18 = (bf16[64,1152]{1,0:T(8,128)(2,1)S(1)}, bf16[64,1152]{1,0:T(8,128)(2,1)S(1)}, u32[]{:S(2)}, u32[]{:S(2)}) collective-permute-start(bf16[64,1152]{1,0:T(8,128)(2,1)S(1)} %shard_map.165.refs_3_.refs_1_), channel_id=1, source_target_pairs={{0,16},{4,12},{8,24},{12,4},{16,0},{20,28},{24,8},{28,20},{1,17},{... | collective-permute-start | bytes 442376 | tf_op jit(solution)/shard_map/ppermute | solution.py:36
  75.6 1.5 %collective-permute-start.22 = (bf16[64,1024]{1,0:T(8,128)(2,1)S(1)}, bf16[64,1024]{1,0:T(8,128)(2,1)S(1)}, u32[]{:S(2)}, u32[]{:S(2)}) collective-permute-start(bf16[64,1024]{1,0:T(8,128)(2,1)S(1)} %get-tuple-element.70), channel_id=1, source_target_pairs={{0,1},{1,0},{2,3},{3,2},{4,5},{5,4},{6,7},{7,6},{8,9},{9,8},{10,11... | collective-permute-start | bytes 393224 | tf_op jit(solution)/shard_map/ppermute | solution.py:36
  77.1 1.6 %collective-permute-done.19.refs_2_ = bf16[128,1024]{1,0:T(8,128)(2,1)S(1)} collective-permute-done((bf16[128,1024]{1,0:T(8,128)(2,1)S(1)}, bf16[128,1024]{1,0:T(8,128)(2,1)S(1)}, u32[]{:S(2)}, u32[]{:S(2)}) %collective-permute-start.19) | collective-permute-done | bytes 262176 | tf_op jit(solution)/shard_map/ppermute | solution.py:36
  82.3 5.7 %collective-permute-start.24 = (bf16[64,1024]{1,0:T(8,128)(2,1)S(1)}, bf16[64,1024]{1,0:T(8,128)(2,1)S(1)}, u32[]{:S(2)}, u32[]{:S(2)}) collective-permute-start(bf16[64,1024]{1,0:T(8,128)(2,1)S(1)} %get-tuple-element.73), channel_id=1, source_target_pairs={{0,2},{1,3},{2,0},{3,1},{4,6},{5,7},{6,4},{7,5},{8,10},{9,11},{10,... | collective-permute-start | bytes 393224 | tf_op jit(solution)/shard_map/ppermute | solution.py:36
  88.0 2.8 %collective-permute-start.26 = (bf16[32,1024]{1,0:T(8,128)(2,1)S(1)}, bf16[32,1024]{1,0:T(8,128)(2,1)S(1)}, u32[]{:S(2)}, u32[]{:S(2)}) collective-permute-start(bf16[32,1024]{1,0:T(8,128)(2,1)S(1)} %get-tuple-element.75), channel_id=1, source_target_pairs={{0,2},{1,3},{2,0},{3,1},{4,6},{5,7},{6,4},{7,5},{8,10},{9,11},{10,... | collective-permute-start | bytes 196616 | tf_op jit(solution)/shard_map/ppermute | solution.py:36
  91.5 6.1 %collective-permute-done.26.refs_2_ = bf16[32,1024]{1,0:T(8,128)(2,1)S(1)} collective-permute-done((bf16[32,1024]{1,0:T(8,128)(2,1)S(1)}, bf16[32,1024]{1,0:T(8,128)(2,1)S(1)}, u32[]{:S(2)}, u32[]{:S(2)}) %collective-permute-start.26) | collective-permute-done | bytes 65568 | tf_op jit(solution)/shard_map/ppermute | solution.py:36
  97.6 1.2 %shard_map.171.refs_3_ = f32[32,1024]{1,0:T(8,128)} custom-call(s32[13]{0:T(128)S(1)} %stack.85.refs_0_, bf16[32,1024]{1,0:T(8,128)(2,1)S(1)} %get-tuple-element.71.refs_3_.refs_1_, bf16[32,1024]{1,0:T(8,128)(2,1)S(1)} %collective-permute-done.26.refs_2_, bf16[256,1152]{1,0:T(8,128)(2,1)S(1)} %shard_map.170.refs_3_.refs_1_), custom_call_target="tpu_custom_call" | custom-call | flops 6000000000 | tf_op jit(solution)/shard_map/pallas_call | solution.py:58
  99.7 1.3 %shard_map.172.refs_3_ = f32[64,1024]{1,0:T(8,128)} custom-call(s32[13]{0:T(128)S(1)} %stack.85.refs_0_, bf16[64,1024]{1,0:T(8,128)(2,1)S(1)} %get-tuple-element.68.refs_3_.refs_1_, bf16[64,1024]{1,0:T(8,128)(2,1)S(1)} %collective-permute-done.25.refs_2_, f32[32,1024]{1,0:T(8,128)S(1)} %copy-done.9), custom_call_target="tpu_custom_call" | custom-call | flops 6000000000 | tf_op jit(solution)/shard_map/pallas_call | solution.py:58
  101.9 1.3 %shard_map.173.refs_6_ = f32[64,1024]{1,0:T(8,128)} custom-call(s32[13]{0:T(128)S(1)} %stack.85.refs_0_, bf16[64,1024]{1,0:T(8,128)(2,1)S(1)} %get-tuple-element.72.refs_3_.refs_1_, bf16[64,1024]{1,0:T(8,128)(2,1)S(1)} %collective-permute-done.24.refs_2_, f32[64,1024]{1,0:T(8,128)S(1)} %copy-done.8), custom_call_target="tpu_custom_call" | custom-call | flops 6000000000 | tf_op jit(solution)/shard_map/pallas_call | solution.py:58
  104.2 3.4 %shard_map.174 = (f32[256,1024]{1,0:T(8,128)}, f32[256,1024]{1,0:T(8,128)}, f32[8,128]{1,0:T(8,128)}) custom-call(s32[13]{0:T(128)S(1)} %stack.85.refs_0_, bf16[256,1152]{1,0:T(8,128)(2,1)S(1)} %shard_map.170.refs_3_.refs_1_, bf16[256,1152]{1,0:T(8,128)(2,1)S(1)} %collective-permute-done.23.refs_2_.refs_4_, ...), custom_call_target="tpu_custom_call" | custom-call | tf_op jit(solution)/shard_map/pallas_call | solution.py:58
  (164 shorter events, 36.2 us)
Async XLA Ops:
  0.6 14.8 %copy-start = (bf16[1024,1024]{1,0:T(8,128)(2,1)S(1)}, bf16[1024,1024]{1,0:T(8,128)(2,1)}, u32[]{:S(2)}) copy-start(bf16[1024,1024]{1,0:T(8,128)(2,1)} %param.13) | copy-start | bytes 6291460
  0.6 14.2 %copy-start.3 = (bf16[128,2048]{1,0:T(8,128)(2,1)S(1)}, bf16[128,2048]{1,0:T(8,128)(2,1)}, u32[]{:S(2)}) copy-start(bf16[128,2048]{1,0:T(8,128)(2,1)} %refs_1_.5) | copy-start | bytes 1572868
  3.7 20.2 %collective-permute-start = (bf16[64,1024]{1,0:T(8,128)(2,1)}, bf16[64,1024]{1,0:T(8,128)(2,1)S(1)}, u32[]{:S(2)}, u32[]{:S(2)}) collective-permute-start(bf16[64,1024]{1,0:T(8,128)(2,1)} %get-tuple-element.44), channel_id=1, source_target_pairs={{0,1},{1,0},{2,3},{3,2},{4,5},{5,4},{6,7},{7,6},{8,9},{9,8},{10,11... | collective-permute-start | bytes 393224 | tf_op jit(solution)/shard_map/ppermute | solution.py:36
  6.7 17.2 %collective-permute-start.1 = (bf16[64,1024]{1,0:T(8,128)(2,1)}, bf16[64,1024]{1,0:T(8,128)(2,1)}, u32[]{:S(2)}, u32[]{:S(2)}) collective-permute-start(bf16[64,1024]{1,0:T(8,128)(2,1)} %get-tuple-element.45), channel_id=1, source_target_pairs={{0,2},{1,3},{2,0},{3,1},{4,6},{5,7},{6,4},{7,5},{8,10},{9,11},{10,... | collective-permute-start | bytes 393224 | tf_op jit(solution)/shard_map/ppermute | solution.py:36
  9.3 14.6 %collective-permute-start.2 = (bf16[64,1024]{1,0:T(8,128)(2,1)}, bf16[64,1024]{1,0:T(8,128)(2,1)}, u32[]{:S(2)}, u32[]{:S(2)}) collective-permute-start(bf16[64,1024]{1,0:T(8,128)(2,1)} %get-tuple-element.46), channel_id=1, source_target_pairs={{0,3},{1,2},{2,1},{3,0},{4,7},{5,6},{6,5},{7,4},{8,11},{9,10},{10,... | collective-permute-start | bytes 393224 | tf_op jit(solution)/shard_map/ppermute | solution.py:36
  9.3 2.4 %collective-permute-start.4 = (s32[8,128]{1,0:T(8,128)}, s32[8,128]{1,0:T(8,128)S(1)}, u32[]{:S(2)}, u32[]{:S(2)}) collective-permute-start(s32[8,128]{1,0:T(8,128)} %bitcast.37), channel_id=1, source_target_pairs={{0,4},{4,0},{8,12},{12,8},{16,20},{20,16},{24,28},{28,24},{1,5},{5... | collective-permute-start | bytes 12296 | tf_op jit(solution)/shard_map/ppermute | solution.py:36
  9.3 5.5 %collective-permute-start.3 = (bf16[128,2048]{1,0:T(8,128)(2,1)}, bf16[128,2048]{1,0:T(8,128)(2,1)S(1)}, u32[]{:S(2)}, u32[]{:S(2)}) collective-permute-start(bf16[128,2048]{1,0:T(8,128)(2,1)} %refs_1_.5), channel_id=1, source_target_pairs={{0,4},{4,0},{8,12},{12,8},{16,20},{20,16},{24,28},{28,24},{1,5},{5... | collective-permute-start | bytes 1572872 | tf_op jit(solution)/shard_map/ppermute | solution.py:36
  20.3 2.4 %copy-start.2 = (bf16[2048,1024]{1,0:T(8,128)(2,1)S(1)}, bf16[2048,1024]{1,0:T(8,128)(2,1)}, u32[]{:S(2)}) copy-start(bf16[2048,1024]{1,0:T(8,128)(2,1)} %refs_1_.7) | copy-start | bytes 12582916
  23.8 2.2 %copy-start.10 = (bf16[128,2048]{1,0:T(8,128)(2,1)S(1)}, bf16[128,2048]{1,0:T(8,128)(2,1)}, u32[]{:S(2)}) copy-start(bf16[128,2048]{1,0:T(8,128)(2,1)} %param.11) | copy-start | bytes 1572868
  25.4 2.0 %collective-permute-start.5 = (bf16[256,1024]{1,0:T(8,128)(2,1)S(1)}, bf16[256,1024]{1,0:T(8,128)(2,1)S(1)}, u32[]{:S(2)}, u32[]{:S(2)}) collective-permute-start(bf16[256,1024]{1,0:T(8,128)(2,1)S(1)} %shard_map.149.refs_2_.refs_1_), channel_id=1, source_target_pairs={{0,4},{4,0},{8,12},{12,8},{16,20},{20,16},{24,28},{28,24},{1,5},{5... | collective-permute-start | bytes 1572872 | tf_op jit(solution)/shard_map/ppermute | solution.py:36
  26.8 11.9 %collective-permute-start.7 = (bf16[128,1024]{1,0:T(8,128)(2,1)S(1)}, bf16[128,1024]{1,0:T(8,128)(2,1)S(1)}, u32[]{:S(2)}, u32[]{:S(2)}) collective-permute-start(bf16[128,1024]{1,0:T(8,128)(2,1)S(1)} %get-tuple-element.96), channel_id=1, source_target_pairs={{0,4},{4,0},{8,12},{12,8},{16,20},{20,16},{24,28},{28,24},{1,5},{5... | collective-permute-start | bytes 786440 | tf_op jit(solution)/shard_map/ppermute | solution.py:36
  30.6 5.7 %collective-permute-start.6 = (bf16[512,1024]{1,0:T(8,128)(2,1)S(1)}, bf16[512,1024]{1,0:T(8,128)(2,1)S(1)}, u32[]{:S(2)}, u32[]{:S(2)}) collective-permute-start(bf16[512,1024]{1,0:T(8,128)(2,1)S(1)} %get-tuple-element.104), channel_id=1, source_target_pairs={{0,4},{4,0},{8,12},{12,8},{16,20},{20,16},{24,28},{28,24},{1,5},{5... | collective-permute-start | bytes 3145736 | tf_op jit(solution)/shard_map/ppermute | solution.py:36
  31.6 20.5 %collective-permute-start.10 = (bf16[512,1024]{1,0:T(8,128)(2,1)S(1)}, bf16[512,1024]{1,0:T(8,128)(2,1)S(1)}, u32[]{:S(2)}, u32[]{:S(2)}) collective-permute-start(bf16[512,1024]{1,0:T(8,128)(2,1)S(1)} %convolution_convert_fusion.3.refs_2_), channel_id=1, source_target_pairs={{0,8},{4,20},{8,0},{12,28},{16,24},{20,4},{24,16},{28,12},{1,9},{5... | collective-permute-start | bytes 3145736 | tf_op jit(solution)/shard_map/ppermute | solution.py:36
  34.1 25.5 %collective-permute-start.12 = (bf16[512,1024]{1,0:T(8,128)(2,1)S(1)}, bf16[512,1024]{1,0:T(8,128)(2,1)S(1)}, u32[]{:S(2)}, u32[]{:S(2)}) collective-permute-start(bf16[512,1024]{1,0:T(8,128)(2,1)S(1)} %convolution_convert_fusion.2.refs_3_), channel_id=1, source_target_pairs={{0,1},{1,0},{2,3},{3,2},{4,5},{5,4},{6,7},{7,6},{8,9},{9,8},{10,11... | collective-permute-start | bytes 3145736 | tf_op jit(solution)/shard_map/ppermute | solution.py:36
  39.3 10.2 %collective-permute-start.8 = (bf16[128,1152]{1,0:T(8,128)(2,1)S(1)}, bf16[128,1152]{1,0:T(8,128)(2,1)S(1)}, u32[]{:S(2)}, u32[]{:S(2)}) collective-permute-start(bf16[128,1152]{1,0:T(8,128)(2,1)S(1)} %get-tuple-element.53), channel_id=1, source_target_pairs={{0,8},{4,20},{8,0},{12,28},{16,24},{20,4},{24,16},{28,12},{1,9},{5... | collective-permute-start | bytes 884744 | tf_op jit(solution)/shard_map/ppermute | solution.py:36
  43.0 22.6 %collective-permute-start.14 = (bf16[256,1024]{1,0:T(8,128)(2,1)S(1)}, bf16[256,1024]{1,0:T(8,128)(2,1)S(1)}, u32[]{:S(2)}, u32[]{:S(2)}) collective-permute-start(bf16[256,1024]{1,0:T(8,128)(2,1)S(1)} %get-tuple-element.59), channel_id=1, source_target_pairs={{0,8},{4,20},{8,0},{12,28},{16,24},{20,4},{24,16},{28,12},{1,9},{5... | collective-permute-start | bytes 1572872 | tf_op jit(solution)/shard_map/ppermute | solution.py:36
  44.6 5.7 %copy-start.5 = (bf16[128,2048]{1,0:T(8,128)(2,1)}, bf16[128,2048]{1,0:T(8,128)(2,1)S(1)}, u32[]{:S(2)}) copy-start(bf16[128,2048]{1,0:T(8,128)(2,1)S(1)} %pad_maximum_fusion.refs_7_) | copy-start | bytes 1572868
  50.2 6.0 %collective-permute-start.9 = (bf16[64,1152]{1,0:T(8,128)(2,1)S(1)}, bf16[64,1152]{1,0:T(8,128)(2,1)S(1)}, u32[]{:S(2)}, u32[]{:S(2)}) collective-permute-start(bf16[64,1152]{1,0:T(8,128)(2,1)S(1)} %get-tuple-element.56), channel_id=1, source_target_pairs={{0,16},{4,12},{8,24},{12,4},{16,0},{20,28},{24,8},{28,20},{1,17},{... | collective-permute-start | bytes 442376 | tf_op jit(solution)/shard_map/ppermute | solution.py:36
  52.8 14.9 %collective-permute-start.17 = (bf16[256,1024]{1,0:T(8,128)(2,1)S(1)}, bf16[256,1024]{1,0:T(8,128)(2,1)S(1)}, u32[]{:S(2)}, u32[]{:S(2)}) collective-permute-start(bf16[256,1024]{1,0:T(8,128)(2,1)S(1)} %get-tuple-element.63), channel_id=1, source_target_pairs={{0,16},{4,12},{8,24},{12,4},{16,0},{20,28},{24,8},{28,20},{1,17},{... | collective-permute-start | bytes 1572872 | tf_op jit(solution)/shard_map/ppermute | solution.py:36
  56.8 5.7 %collective-permute-start.11 = (bf16[64,1152]{1,0:T(8,128)(2,1)S(1)}, bf16[64,1152]{1,0:T(8,128)(2,1)S(1)}, u32[]{:S(2)}, u32[]{:S(2)}) collective-permute-start(bf16[64,1152]{1,0:T(8,128)(2,1)S(1)} %shard_map.158.refs_3_.refs_1_), channel_id=1, source_target_pairs={{0,1},{1,0},{2,3},{3,2},{4,5},{5,4},{6,7},{7,6},{8,9},{9,8},{10,11... | collective-permute-start | bytes 442376 | tf_op jit(solution)/shard_map/ppermute | solution.py:36
  60.4 11.1 %collective-permute-start.16 = (bf16[256,1024]{1,0:T(8,128)(2,1)S(1)}, bf16[256,1024]{1,0:T(8,128)(2,1)S(1)}, u32[]{:S(2)}, u32[]{:S(2)}) collective-permute-start(bf16[256,1024]{1,0:T(8,128)(2,1)S(1)} %get-tuple-element.62), channel_id=1, source_target_pairs={{0,8},{4,20},{8,0},{12,28},{16,24},{20,4},{24,16},{28,12},{1,9},{5... | collective-permute-start | bytes 1572872 | tf_op jit(solution)/shard_map/ppermute | solution.py:36
  63.1 10.2 %collective-permute-start.13 = (bf16[64,1152]{1,0:T(8,128)(2,1)S(1)}, bf16[64,1152]{1,0:T(8,128)(2,1)S(1)}, u32[]{:S(2)}, u32[]{:S(2)}) collective-permute-start(bf16[64,1152]{1,0:T(8,128)(2,1)S(1)} %shard_map.160.refs_3_.refs_1_), channel_id=1, source_target_pairs={{0,2},{1,3},{2,0},{3,1},{4,6},{5,7},{6,4},{7,5},{8,10},{9,11},{10,... | collective-permute-start | bytes 442376 | tf_op jit(solution)/shard_map/ppermute | solution.py:36
  66.2 6.4 %collective-permute-start.15 = (bf16[128,1024]{1,0:T(8,128)(2,1)S(1)}, bf16[128,1024]{1,0:T(8,128)(2,1)S(1)}, u32[]{:S(2)}, u32[]{:S(2)}) collective-permute-start(bf16[128,1024]{1,0:T(8,128)(2,1)S(1)} %get-tuple-element.61), channel_id=1, source_target_pairs={{0,16},{4,12},{8,24},{12,4},{16,0},{20,28},{24,8},{28,20},{1,17},{... | collective-permute-start | bytes 786440 | tf_op jit(solution)/shard_map/ppermute | solution.py:36
  68.4 13.3 %collective-permute-start.21 = (bf16[128,1024]{1,0:T(8,128)(2,1)S(1)}, bf16[128,1024]{1,0:T(8,128)(2,1)S(1)}, u32[]{:S(2)}, u32[]{:S(2)}) collective-permute-start(bf16[128,1024]{1,0:T(8,128)(2,1)S(1)} %get-tuple-element.69), channel_id=1, source_target_pairs={{0,1},{1,0},{2,3},{3,2},{4,5},{5,4},{6,7},{7,6},{8,9},{9,8},{10,11... | collective-permute-start | bytes 786440 | tf_op jit(solution)/shard_map/ppermute | solution.py:36
  72.2 6.4 %collective-permute-start.19 = (bf16[128,1024]{1,0:T(8,128)(2,1)S(1)}, bf16[128,1024]{1,0:T(8,128)(2,1)S(1)}, u32[]{:S(2)}, u32[]{:S(2)}) collective-permute-start(bf16[128,1024]{1,0:T(8,128)(2,1)S(1)} %get-tuple-element.67), channel_id=1, source_target_pairs={{0,16},{4,12},{8,24},{12,4},{16,0},{20,28},{24,8},{28,20},{1,17},{... | collective-permute-start | bytes 786440 | tf_op jit(solution)/shard_map/ppermute | solution.py:36
  73.9 6.3 %collective-permute-start.18 = (bf16[64,1152]{1,0:T(8,128)(2,1)S(1)}, bf16[64,1152]{1,0:T(8,128)(2,1)S(1)}, u32[]{:S(2)}, u32[]{:S(2)}) collective-permute-start(bf16[64,1152]{1,0:T(8,128)(2,1)S(1)} %shard_map.165.refs_3_.refs_1_), channel_id=1, source_target_pairs={{0,16},{4,12},{8,24},{12,4},{16,0},{20,28},{24,8},{28,20},{1,17},{... | collective-permute-start | bytes 442376 | tf_op jit(solution)/shard_map/ppermute | solution.py:36
  75.6 5.5 %collective-permute-start.22 = (bf16[64,1024]{1,0:T(8,128)(2,1)S(1)}, bf16[64,1024]{1,0:T(8,128)(2,1)S(1)}, u32[]{:S(2)}, u32[]{:S(2)}) collective-permute-start(bf16[64,1024]{1,0:T(8,128)(2,1)S(1)} %get-tuple-element.70), channel_id=1, source_target_pairs={{0,1},{1,0},{2,3},{3,2},{4,5},{5,4},{6,7},{7,6},{8,9},{9,8},{10,11... | collective-permute-start | bytes 393224 | tf_op jit(solution)/shard_map/ppermute | solution.py:36
  80.8 10.1 %collective-permute-start.20 = (bf16[128,1152]{1,0:T(8,128)(2,1)S(1)}, bf16[128,1152]{1,0:T(8,128)(2,1)S(1)}, u32[]{:S(2)}, u32[]{:S(2)}) collective-permute-start(bf16[128,1152]{1,0:T(8,128)(2,1)S(1)} %shard_map.167.refs_3_.refs_1_), channel_id=1, source_target_pairs={{0,8},{4,20},{8,0},{12,28},{16,24},{20,4},{24,16},{28,12},{1,9},{5... | collective-permute-start | bytes 884744 | tf_op jit(solution)/shard_map/ppermute | solution.py:36
  82.3 18.7 %collective-permute-start.24 = (bf16[64,1024]{1,0:T(8,128)(2,1)S(1)}, bf16[64,1024]{1,0:T(8,128)(2,1)S(1)}, u32[]{:S(2)}, u32[]{:S(2)}) collective-permute-start(bf16[64,1024]{1,0:T(8,128)(2,1)S(1)} %get-tuple-element.73), channel_id=1, source_target_pairs={{0,2},{1,3},{2,0},{3,1},{4,6},{5,7},{6,4},{7,5},{8,10},{9,11},{10,... | collective-permute-start | bytes 393224 | tf_op jit(solution)/shard_map/ppermute | solution.py:36
  87.9 10.9 %collective-permute-start.25 = (bf16[64,1024]{1,0:T(8,128)(2,1)S(1)}, bf16[64,1024]{1,0:T(8,128)(2,1)S(1)}, u32[]{:S(2)}, u32[]{:S(2)}) collective-permute-start(bf16[64,1024]{1,0:T(8,128)(2,1)S(1)} %get-tuple-element.74), channel_id=1, source_target_pairs={{0,2},{1,3},{2,0},{3,1},{4,6},{5,7},{6,4},{7,5},{8,10},{9,11},{10,... | collective-permute-start | bytes 393224 | tf_op jit(solution)/shard_map/ppermute | solution.py:36
  88.0 9.6 %collective-permute-start.26 = (bf16[32,1024]{1,0:T(8,128)(2,1)S(1)}, bf16[32,1024]{1,0:T(8,128)(2,1)S(1)}, u32[]{:S(2)}, u32[]{:S(2)}) collective-permute-start(bf16[32,1024]{1,0:T(8,128)(2,1)S(1)} %get-tuple-element.75), channel_id=1, source_target_pairs={{0,2},{1,3},{2,0},{3,1},{4,6},{5,7},{6,4},{7,5},{8,10},{9,11},{10,... | collective-permute-start | bytes 196616 | tf_op jit(solution)/shard_map/ppermute | solution.py:36
  91.5 11.8 %collective-permute-start.23 = (bf16[256,1152]{1,0:T(8,128)(2,1)S(1)}, bf16[256,1152]{1,0:T(8,128)(2,1)S(1)}, u32[]{:S(2)}, u32[]{:S(2)}) collective-permute-start(bf16[256,1152]{1,0:T(8,128)(2,1)S(1)} %shard_map.170.refs_3_.refs_1_), channel_id=1, source_target_pairs={{0,4},{4,0},{8,12},{12,8},{16,20},{20,16},{24,28},{28,24},{1,5},{5... | collective-permute-start | bytes 1769480 | tf_op jit(solution)/shard_map/ppermute | solution.py:36
  (7 other events, 8.3 us)
where the time goes:
time: 108 us
  starting transfers between devices  33.3 us (31%)
  Pallas kernels  28.6 us (26%)
  waiting for transfers between devices  21.9 us (20%)
  matrix products  12.7 us (12%)
  local copies, waits for them, and re-layouts  7.76 us (7%)
  other arithmetic  1.92 us (2%)
  between operations  1.41 us (1%)
    ppermute x27, starting transfers between devices, swap(): return lax.ppermute(value, axis, pairs)  33.3 us
    pallas_call x31, Pallas kernels, run(): pl.pallas_call(kernel, out_shape=tuple(outs), grid_spec=pltpu.PrefetchSca...  28.6 us
    ppermute x27, waiting for transfers between devices, swap(): return lax.ppermute(value, axis, pairs)  21.9 us
    unnamed x30, local copies, waits for them, and re-layouts  5.58 us
    dot_general x3, matrix products, times(): return jnp.dot(left, right, preferred_element_type=F32)  4.7 us
    dot_general x8, matrix products, inner(): lax.dot_general(left, right, (((0,), (0,)), ((), ())), preferred_element_...  4.61 us
    dot_general x3, matrix products, outer(): lax.dot_general(left, right, (((1,), (1,)), ((), ())), preferred_element_...  3.38 us
  transfers between devices with their start and end apart: 27, of which 10 were waited for; matrix products, arithmetic and copies ran while one was open for 16% of the time, Pallas kernels for 20%

commit v1 on v0

--- a/solution.py
+++ b/solution.py
@@ -10,6 +10,7 @@
 BF = jnp.bfloat16
 F32 = jnp.float32
 ROOM = 8 * 1024 * 1024
+WIDE = 24 * 1024 * 1024
 STEP = 6 * 1000 * 1000 * 1000
 VMEM = pltpu.VMEM
 
@@ -119,7 +120,7 @@
             both[pl.ds(start, patches), :] = value[:, j * width : (j + 1) * width]
 
 
-def hots_body(own, tp_count, share_count, height, core_at, numbers, ids_own, ids_other, prev, here, mine):
+def hots(own, tp_count, share_count, height, core_at, numbers, ids_own, ids_other, prev, here, mine):
     patches = ids_own.shape[1]
     plain = lax.broadcasted_iota(jnp.int32, (1, prev.shape[1]), 1)
     line = vocab_line(numbers, tp_count, share_count, height)
@@ -148,14 +149,26 @@
     return (row == source).astype(BF)
 
 
-def pick_up_body(tp_count, share_count, numbers, up, up_here, ups, ready):
+def prepare_body(
+    own, tp_count, share_count, height, core_at,
+    numbers, up, down, ids_own, ids_other,
+    prev, here, mine, up_here, down_here, ups, downs, ready,
+):
     chunk = ups.shape[2]
+    unit = chunk // tp_count
     half = chunk // 2
     copies = []
     for n in range(share_count):
         at = pl.ds(pl.multiple_of(numbers[tp_count + n] * chunk, chunk), chunk)
-        copies.append(pltpu.make_async_copy(up.at[:, at], ups.at[n], ready.at[n]))
+        copies.append(pltpu.make_async_copy(up.at[:, at], ups.at[n], ready.at[0, n]))
         copies[-1].start()
+    for n in range(share_count):
+        at = pl.ds(pl.multiple_of(numbers[tp_count + n] * chunk, chunk), chunk)
+        copies.append(pltpu.make_async_copy(down.at[at, :], downs.at[n], ready.at[1, n]))
+        copies[-1].start()
+    hots(
+        own, tp_count, share_count, height, core_at, numbers, ids_own, ids_other, prev, here, mine
+    )
     turn = turn_matrix(tp_count, chunk, numbers)
     for n in range(share_count):
         copies[n].wait()
@@ -163,19 +176,8 @@
         for z in range(2):
             first = (z * share_count + n) * half
             up_here[:, first : first + half] = value[:, z * half : (z + 1) * half]
-
-
-def pick_down_body(tp_count, share_count, numbers, down, down_here, downs, ready):
-    chunk = downs.shape[1]
-    unit = chunk // tp_count
-    half = chunk // 2
-    copies = []
     for n in range(share_count):
-        at = pl.ds(pl.multiple_of(numbers[tp_count + n] * chunk, chunk), chunk)
-        copies.append(pltpu.make_async_copy(down.at[at, :], downs.at[n], ready.at[n]))
-        copies[-1].start()
-    for n in range(share_count):
-        copies[n].wait()
+        copies[share_count + n].wait()
         for i, m in enumerate(sent_order(tp_count)):
             z, place = i // (tp_count // 2), i % (tp_count // 2)
             first = (z * share_count + n) * half + place * unit
@@ -238,28 +240,27 @@
     both[rows:, :] = second[...]
 
 
-def sort_out_body(numbers, place, sort):
-    vocab = (sort.shape[0] - 16) // 2
-    row = lax.broadcasted_iota(jnp.int32, (vocab, sort.shape[1]), 0)
-    sort[:vocab, :] = hot(row, place[:1, :])
-    sort[vocab : 2 * vocab, :] = hot(row, place[1:2, :])
-    sort[2 * vocab :, :] = place[2:, :].astype(F32).astype(BF)
-
-
-def tables_body(numbers, first, second, first_gain, second_gain, sort, glob, local, gain):
-    half = first.shape[0]
-    vocab = glob.shape[0]
-    tall = sort[: 2 * vocab]
-    value = times(tall[:, :half], first[...]) + times(tall[:, half:], second[...])
-    glob[...] = value[:vocab]
-    local[...] = value[vocab:]
-
-    @pl.when(pl.program_id(0) == 0)
-    def _():
-        flat = sort[2 * vocab :]
-        value = times(flat[:, :half], first_gain[...])
-        value = value + times(flat[:, half:], second_gain[...])
-        gain[...] = value[: gain.shape[0]]
+def tables_body(
+    share_count, first_share, height, numbers, first, second, first_gain, second_gain,
+    glob, local, gain,
+):
+    gains = None
+    for side, (value, line) in enumerate(((first, first_gain), (second, second_gain))):
+        for n in range(share_count):
+            start = numbers[first_share + side * share_count + n] * height
+            at = pl.ds(pl.multiple_of(start, height), height)
+            row = 2 * n * height
+            glob[at, :] = value[row : row + height, :].astype(F32)
+            local[at, :] = value[row + height : row + 2 * height, :].astype(F32)
+            term = line[row : row + 16, :].astype(F32)
+            gains = term if gains is None else gains + term
+    gain[...] = gains[: gain.shape[0]]
+
+
+def finals_body(numbers, *refs):
+    for i in range(len(refs) // 3):
+        kept, arrived, whole = refs[2 * i], refs[2 * i + 1], refs[len(refs) // 3 * 2 + i]
+        whole[...] = kept[...].astype(F32) + arrived[...].astype(F32)
 
 
 def on_device(
@@ -346,11 +347,25 @@
         [],
     )
     blocks = [swap(b, "tp", (m,)) if m else b for m, b in enumerate(blocks)]
-    prev_hot, prev_here, own_hot = call(
-        functools.partial(hots_body, own, tp_count, share_count, height, core_at),
-        [like(2 * rows, vocab, BF), like(2 * rows, vocab // 2, BF), like(rows, vocab, BF)],
-        [ids_own, ids_other],
+    far = pl.BlockSpec(memory_space=pltpu.HBM)
+    prev_hot, prev_here, own_hot, up_here, down_here = call(
+        functools.partial(prepare_body, own, tp_count, share_count, height, core_at),
+        [
+            like(2 * rows, vocab, BF),
+            like(2 * rows, vocab // 2, BF),
+            like(rows, vocab, BF),
+            like(width, hidden // 2, BF),
+            like(hidden // 2, width, BF),
+        ],
+        [up_weight, down_weight, ids_own, ids_other],
         [blocks[0]],
+        in_specs=[far, far, None, None],
+        scratch=[
+            VMEM((share_count, width, chunk), BF),
+            VMEM((share_count, chunk, width), BF),
+            pltpu.SemaphoreType.DMA((2, share_count)),
+        ],
+        room=WIDE,
     )
 
     def by_slot(value):
@@ -366,28 +381,11 @@
     scale = lax.rsqrt(jnp.mean(u_rows * u_rows, axis=1, keepdims=True) + 1e-05)
     normed = u_rows * scale
     r_rows = (normed * norm_gain).astype(BF)
-    far = pl.BlockSpec(memory_space=pltpu.HBM)
-    (up_here,) = call(
-        functools.partial(pick_up_body, tp_count, share_count),
-        [like(width, hidden // 2, BF)],
-        [up_weight],
-        [r_rows],
-        in_specs=[far],
-        scratch=[VMEM((share_count, width, chunk), BF), pltpu.SemaphoreType.DMA((share_count,))],
-    )
     a_rows = times(r_rows, up_here)
     sig = jax.nn.sigmoid(a_rows)
     h_rows = (a_rows * sig).astype(BF)
     slope = (sig * (1.0 + a_rows * (1.0 - sig))).astype(BF)
     h_rows, slope = lax.optimization_barrier((h_rows, slope))
-    (down_here,) = call(
-        functools.partial(pick_down_body, tp_count, share_count),
-        [like(hidden // 2, width, BF)],
-        [down_weight],
-        [h_rows],
-        in_specs=[far],
-        scratch=[VMEM((share_count, chunk, width), BF), pltpu.SemaphoreType.DMA((share_count,))],
-    )
     strip = chunk // 2
     h_rows = jnp.concatenate(
         [
@@ -402,7 +400,7 @@
         functools.partial(join_body, part, own, tp_count),
         [like(rows, width, BF)],
         blocks,
-        [h_rows, down_here],
+        [h_rows],
     )
     grad_other = core_swap(grad_own)
     own_hot = gate(own_hot, [grad_own])
@@ -431,19 +429,16 @@
         def __init__(self, kept, sent, steps):
             self.kept, self.steps, self.at = kept, steps, 0
             self.arrived = go(sent, self.steps[0])
-            self.left = len(self.steps)
+            self.left = len(self.steps) - 1
 
         def next(self, after):
             self.at += 1
             self.left -= 1
             rows, columns = self.kept.shape
             ins = [self.kept, self.arrived]
-            if self.left:
-                outs = [like(rows // 2, columns, self.kept.dtype)] * 2
-                self.kept, sent = step(add_body, outs, ins, after)
-                self.arrived = go(sent, self.steps[self.at])
-            else:
-                (self.kept,) = step(sum_body, [like(rows, columns, F32)], ins, after)
+            outs = [like(rows // 2, columns, self.kept.dtype)] * 2
+            self.kept, sent = step(add_body, outs, ins, after)
+            self.arrived = go(sent, self.steps[self.at])
             return self.kept
 
     class Table:
@@ -523,24 +518,7 @@
         [back[j * patches : (j + 1) * patches] for j in range(own)], axis=1
     )
 
-    all_numbers = jnp.stack(shares + others)
-    inside = jnp.arange(size)[None, :]
-    own_row = all_numbers[:, None] * height + inside
-    place = jnp.stack(
-        [
-            jnp.where(inside < height, own_row, -1).reshape(-1),
-            jnp.where(inside >= height, own_row - height, -1).reshape(-1),
-        ]
-        + [
-            jnp.broadcast_to(inside == line, own_row.shape).reshape(-1).astype(jnp.int32)
-            for line in range(16)
-        ]
-    ).astype(jnp.int32)
-    count = seq_count * size
-    (sort,) = call(
-        sort_out_body, [like(2 * vocab + 16, count, BF)], [place], [table.kept]
-    )
-    last = [up.kept, proj.kept, table.kept, down.kept, glob_out_grad, sort]
+    last = [up.kept, proj.kept, table.kept, down.kept, glob_out_grad]
     names = {"T": table, "D": down, "U": up, "P": proj}
     queue = [names[c] for c in "TDTUTPDUPTUTPDTPUTD"]
     for chain in queue + [table, proj, down, up] * 16:
@@ -553,25 +531,33 @@
     def columns(height):
         return pl.BlockSpec((height, wide), lambda n, s: (0, n))
 
+    count = table.kept.shape[0]
     lines = width // 128
-    beside = pl.BlockSpec((count // 2, 128), lambda n, s: (0, lines))
+    beside = pl.BlockSpec((count, 128), lambda n, s: (0, lines))
     emb_global_grad, emb_local_grad, gain_grad = call(
-        tables_body,
+        functools.partial(tables_body, share_count, tp_count, height),
         [like(vocab, width, F32), like(vocab, width, F32), like(lines, 128, F32)],
-        [table.kept, table.arrived, table.kept, table.arrived, sort],
+        [table.kept, table.arrived, table.kept, table.arrived],
         last,
         grid=parts,
-        in_specs=[columns(count // 2), columns(count // 2), beside, beside, None],
+        in_specs=[columns(count), columns(count), beside, beside],
         out_specs=[columns(vocab), columns(vocab), None],
+    )
+    ends = [down, up, proj]
+    down_grad, up_grad, proj_grad = call(
+        finals_body,
+        [like(*c.kept.shape, F32) for c in ends],
+        [x for c in ends for x in (c.kept, c.arrived)],
+        [emb_global_grad],
     )
     return (
         glob_out_grad,
         emb_global_grad,
         emb_local_grad,
         gain_grad.reshape(width),
-        proj.kept.T,
-        up.kept.T,
-        down.kept,
+        proj_grad.T,
+        up_grad.T,
+        down_grad,
     )
 
 

time: 108 us -> 110 us (1.019)
  waiting for transfers between devices: 21.9 us -> 30.9 us
  Pallas kernels: 28.6 us -> 21.9 us
    ppermute x27, waiting for transfers between devices: 21.9 us -> 30.9 us  [swap(): return lax.ppermute(value, axis, pairs)]
    pallas_call x31 -> x26, Pallas kernels: 28.6 us -> 21.9 us  [run(): pl.pallas_call(kernel, out_shape=tuple(outs), grid_spec=pltpu.PrefetchSca...]
    unnamed x30 -> x28, local copies, waits for them, and re-layouts: 5.58 us -> 8.22 us
    convert_element_type x16 -> x0, local copies, waits for them, and re-layouts: 1.26 us -> none  [on_device(): jnp.broadcast_to(inside == line, own_row.shape).reshape(-1)]
  transfers between devices with their start and end apart: 27 -> 27, of which waited for: 10 -> 11; matrix products, arithmetic and copies ran while one was open for 16% -> 13% of each run, Pallas kernels for 20% -> 18%
where the time goes in v1:
time: 110 us
  starting transfers between devices  33.1 us (30%)
  waiting for transfers between devices  30.9 us (28%)
  Pallas kernels  21.9 us (20%)
  matrix products  11.7 us (11%)
  local copies, waits for them, and re-layouts  8.76 us (8%)
  other arithmetic  2.04 us (2%)
  between operations  1.19 us (1%)
    ppermute x27, starting transfers between devices, swap(): return lax.ppermute(value, axis, pairs)  33.1 us
    ppermute x27, waiting for transfers between devices, swap(): return lax.ppermute(value, axis, pairs)  30.9 us
    pallas_call x26, Pallas kernels, run(): pl.pallas_call(kernel, out_shape=tuple(outs), grid_spec=pltpu.PrefetchSca...  21.9 us
    unnamed x28, local copies, waits for them, and re-layouts  8.22 us
    dot_general x8, matrix products, inner(): lax.dot_general(left, right, (((0,), (0,)), ((), ())), preferred_element_...  4.65 us
    dot_general x3, matrix products, times(): return jnp.dot(left, right, preferred_element_type=F32)  3.64 us
    dot_general x3, matrix products, outer(): lax.dot_general(left, right, (((1,), (1,)), ((), ())), preferred_element_...  3.36 us
  transfers between devices with their start and end apart: 27, of which 11 were waited for; matrix products, arithmetic and copies ran while one was open for 13% of the time, Pallas kernels for 18%

profile of v1, /device:TPU:0, one launch (start us, length us, event | category | flops | bytes accessed | tf_op | source)
XLA Modules:
  0.0 109.6 jit_solution(9541299720975906479)
XLA Ops:
  1.3 1.0 copy-done.5
  2.4 1.0 shard_map.144
  3.4 3.1 %collective-permute-start = (bf16[64,1024]{1,0:T(8,128)(2,1)S(1)}, bf16[64,1024]{1,0:T(8,128)(2,1)S(1)}, u32[]{:S(2)}, u32[]{:S(2)}) collective-permute-start(bf16[64,1024]{1,0:T(8,128)(2,1)S(1)} %get-tuple-element.49), channel_id=1, source_target_pairs={{0,1},{1,0},{2,3},{3,2},{4,5},{5,4},{6,7},{7,6},{8,9},{9,8},{10,11... | collective-permute-start | bytes 393224 | tf_op jit(solution)/shard_map/ppermute | solution.py:37
  6.5 2.6 %collective-permute-start.1 = (bf16[64,1024]{1,0:T(8,128)(2,1)S(1)}, bf16[64,1024]{1,0:T(8,128)(2,1)S(1)}, u32[]{:S(2)}, u32[]{:S(2)}) collective-permute-start(bf16[64,1024]{1,0:T(8,128)(2,1)S(1)} %get-tuple-element.50), channel_id=1, source_target_pairs={{0,2},{1,3},{2,0},{3,1},{4,6},{5,7},{6,4},{7,5},{8,10},{9,11},{10,... | collective-permute-start | bytes 393224 | tf_op jit(solution)/shard_map/ppermute | solution.py:37
  9.1 2.2 %copy-done.1 = bf16[1024,2048]{1,0:T(8,128)(2,1)S(1)} copy-done((bf16[1024,2048]{1,0:T(8,128)(2,1)S(1)}, bf16[1024,2048]{1,0:T(8,128)(2,1)}, u32[]{:S(2)}) %copy-start.1) | copy-done | bytes 4194328
  11.3 2.2 %copy-done.2 = bf16[2048,1024]{1,0:T(8,128)(2,1)S(1)} copy-done((bf16[2048,1024]{1,0:T(8,128)(2,1)S(1)}, bf16[2048,1024]{1,0:T(8,128)(2,1)}, u32[]{:S(2)}) %copy-start.2) | copy-done | bytes 4194328
  14.1 3.3 %shard_map.145 = (bf16[512,256]{1,0:T(8,128)(2,1)S(1)}, bf16[512,128]{1,0:T(8,128)(2,1)S(1)}, bf16[256,256]{1,0:T(8,128)(2,1)S(1)}, bf16[1024,1024]{1,0:T(8,128)(2,1)S(1)}, bf16[1024,1024]{1,0:T(8,128)(2,1)S(1)}) custom-call(s32[13]{0:T(128)S(1)} %stack.55.refs_0_, bf16[1024,2048]{1,0:T(8,128)(2,1)S(1)} %copy-done.1, bf16[2048,1024]{1,0:T(8,128)(2,1)S(1)} %copy-done.2, ...), custom_call_target="tpu_custom_call" | custom-call | tf_op jit(solution)/shard_map/pallas_call | solution.py:59
  19.1 1.4 %multiply_reduce_fusion.2 = (f32[512]{0:T(512)S(1)}, f32[512,1024]{1,0:T(8,128)S(1)}) fusion(f32[512,1024]{1,0:T(8,128)S(1)} %fusion.39, bf16[512,1024]{1,0:T(8,128)(2,1)S(1)} %shard_map.146, bf16[1024,1024]{1,0:T(8,128)(2,1)S(1)} %copy-done), kind=kOutput, calls=%fused_computation.9 | convolution fusion | flops 1075314176 | bytes 7342080 | tf_op jit(solution)/shard_map/dot_general | solution.py:31
  20.8 1.8 %multiply_convert_fusion.1 = (bf16[512,1024]{1,0:T(8,128)(2,1)S(1)}, bf16[512,1024]{1,0:T(8,128)(2,1)S(1)}) fusion(bf16[512,1024]{1,0:T(8,128)(2,1)S(1)} %multiply_convert_fusion.3, bf16[1024,1024]{1,0:T(8,128)(2,1)S(1)} %get-tuple-element.53), kind=kOutput, calls=%fused_computation.5 | convolution fusion | flops 1078984704 | bytes 5242880 | tf_op jit(solution)/shard_map/dot_general | solution.py:31
  26.4 1.3 %multiply_convert_fusion = bf16[512,1024]{1,0:T(8,128)(2,1)S(1)} fusion(bf16[512,1024]{1,0:T(8,128)(2,1)S(1)} %get-tuple-element.57, bf16[512,1024]{1,0:T(8,128)(2,1)S(1)} %shard_map.149, bf16[1024,1024]{1,0:T(8,128)(2,1)S(1)} %get-tuple-element.56), kind=kOutput, calls=%fused_computation.4 | convolution fusion | flops 1075314688 | bytes 5242880 | tf_op jit(solution)/shard_map/dot_general | solution.py:25
  27.8 1.3 %fusion.38 = (bf16[512,1024]{1,0:T(8,128)(2,1)S(1)}, f32[512,1024]{1,0:T(8,128)S(1)}) fusion(bf16[512,1024]{1,0:T(8,128)(2,1)S(1)} %multiply_convert_fusion, bf16[1024,1024]{1,0:T(8,128)(2,1)S(1)} %get-tuple-element.53), kind=kOutput, calls=%fused_computation.70 | convolution fusion | flops 1074266112 | bytes 6291456 | tf_op jit(solution)/shard_map/dot_general | solution.py:25
  30.0 1.8 %collective-permute-start.10 = (bf16[512,1024]{1,0:T(8,128)(2,1)S(1)}, bf16[512,1024]{1,0:T(8,128)(2,1)S(1)}, u32[]{:S(2)}, u32[]{:S(2)}) collective-permute-start(bf16[512,1024]{1,0:T(8,128)(2,1)S(1)} %convolution_convert_fusion.3.refs_2_), channel_id=1, source_target_pairs={{0,8},{4,20},{8,0},{12,28},{16,24},{20,4},{24,16},{28,12},{1,9},{5... | collective-permute-start | bytes 3145736 | tf_op jit(solution)/shard_map/ppermute | solution.py:37
  41.0 1.6 %collective-permute-start.14 = (bf16[256,1024]{1,0:T(8,128)(2,1)S(1)}, bf16[256,1024]{1,0:T(8,128)(2,1)S(1)}, u32[]{:S(2)}, u32[]{:S(2)}) collective-permute-start(bf16[256,1024]{1,0:T(8,128)(2,1)S(1)} %get-tuple-element.66), channel_id=1, source_target_pairs={{0,8},{4,20},{8,0},{12,28},{16,24},{20,4},{24,16},{28,12},{1,9},{5... | collective-permute-start | bytes 1572872 | tf_op jit(solution)/shard_map/ppermute | solution.py:37
  42.6 5.4 %collective-permute-done.8.refs_2_ = bf16[128,1152]{1,0:T(8,128)(2,1)S(1)} collective-permute-done((bf16[128,1152]{1,0:T(8,128)(2,1)S(1)}, bf16[128,1152]{1,0:T(8,128)(2,1)S(1)}, u32[]{:S(2)}, u32[]{:S(2)}) %collective-permute-start.8) | collective-permute-done | bytes 294944 | tf_op jit(solution)/shard_map/ppermute | solution.py:37
  48.7 1.8 %collective-permute-start.9 = (bf16[64,1152]{1,0:T(8,128)(2,1)S(1)}, bf16[64,1152]{1,0:T(8,128)(2,1)S(1)}, u32[]{:S(2)}, u32[]{:S(2)}) collective-permute-start(bf16[64,1152]{1,0:T(8,128)(2,1)S(1)} %get-tuple-element.63), channel_id=1, source_target_pairs={{0,16},{4,12},{8,24},{12,4},{16,0},{20,28},{24,8},{28,20},{1,17},{... | collective-permute-start | bytes 442376 | tf_op jit(solution)/shard_map/ppermute | solution.py:37
  51.6 3.0 %collective-permute-done.9.refs_2_ = bf16[64,1152]{1,0:T(8,128)(2,1)S(1)} collective-permute-done((bf16[64,1152]{1,0:T(8,128)(2,1)S(1)}, bf16[64,1152]{1,0:T(8,128)(2,1)S(1)}, u32[]{:S(2)}, u32[]{:S(2)}) %collective-permute-start.9) | collective-permute-done | bytes 147488 | tf_op jit(solution)/shard_map/ppermute | solution.py:37
  56.2 1.9 %collective-permute-done.12.refs_2_ = bf16[512,1024]{1,0:T(8,128)(2,1)S(1)} collective-permute-done((bf16[512,1024]{1,0:T(8,128)(2,1)S(1)}, bf16[512,1024]{1,0:T(8,128)(2,1)S(1)}, u32[]{:S(2)}, u32[]{:S(2)}) %collective-permute-start.12) | collective-permute-done | bytes 1048608 | tf_op jit(solution)/shard_map/ppermute | solution.py:37
  59.5 1.5 %collective-permute-done.11.refs_2_ = bf16[64,1152]{1,0:T(8,128)(2,1)S(1)} collective-permute-done((bf16[64,1152]{1,0:T(8,128)(2,1)S(1)}, bf16[64,1152]{1,0:T(8,128)(2,1)S(1)}, u32[]{:S(2)}, u32[]{:S(2)}) %collective-permute-start.11) | collective-permute-done | bytes 147488 | tf_op jit(solution)/shard_map/ppermute | solution.py:37
  61.5 2.5 %collective-permute-start.13 = (bf16[64,1152]{1,0:T(8,128)(2,1)S(1)}, bf16[64,1152]{1,0:T(8,128)(2,1)S(1)}, u32[]{:S(2)}, u32[]{:S(2)}) collective-permute-start(bf16[64,1152]{1,0:T(8,128)(2,1)S(1)} %shard_map.157.refs_3_.refs_1_), channel_id=1, source_target_pairs={{0,2},{1,3},{2,0},{3,1},{4,6},{5,7},{6,4},{7,5},{8,10},{9,11},{10,... | collective-permute-start | bytes 442376 | tf_op jit(solution)/shard_map/ppermute | solution.py:37
  64.7 1.4 %collective-permute-start.15 = (bf16[128,1024]{1,0:T(8,128)(2,1)S(1)}, bf16[128,1024]{1,0:T(8,128)(2,1)S(1)}, u32[]{:S(2)}, u32[]{:S(2)}) collective-permute-start(bf16[128,1024]{1,0:T(8,128)(2,1)S(1)} %get-tuple-element.68), channel_id=1, source_target_pairs={{0,16},{4,12},{8,24},{12,4},{16,0},{20,28},{24,8},{28,20},{1,17},{... | collective-permute-start | bytes 786440 | tf_op jit(solution)/shard_map/ppermute | solution.py:37
  66.8 1.8 %collective-permute-start.21 = (bf16[128,1024]{1,0:T(8,128)(2,1)S(1)}, bf16[128,1024]{1,0:T(8,128)(2,1)S(1)}, u32[]{:S(2)}, u32[]{:S(2)}) collective-permute-start(bf16[128,1024]{1,0:T(8,128)(2,1)S(1)} %get-tuple-element.76), channel_id=1, source_target_pairs={{0,1},{1,0},{2,3},{3,2},{4,5},{5,4},{6,7},{7,6},{8,9},{9,8},{10,11... | collective-permute-start | bytes 786440 | tf_op jit(solution)/shard_map/ppermute | solution.py:37
  68.6 1.4 %collective-permute-done.16.refs_2_ = bf16[256,1024]{1,0:T(8,128)(2,1)S(1)} collective-permute-done((bf16[256,1024]{1,0:T(8,128)(2,1)S(1)}, bf16[256,1024]{1,0:T(8,128)(2,1)S(1)}, u32[]{:S(2)}, u32[]{:S(2)}) %collective-permute-start.16) | collective-permute-done | bytes 524320 | tf_op jit(solution)/shard_map/ppermute | solution.py:37
  72.3 1.7 %collective-permute-start.18 = (bf16[64,1152]{1,0:T(8,128)(2,1)S(1)}, bf16[64,1152]{1,0:T(8,128)(2,1)S(1)}, u32[]{:S(2)}, u32[]{:S(2)}) collective-permute-start(bf16[64,1152]{1,0:T(8,128)(2,1)S(1)} %shard_map.162.refs_3_.refs_1_), channel_id=1, source_target_pairs={{0,16},{4,12},{8,24},{12,4},{16,0},{20,28},{24,8},{28,20},{1,17},{... | collective-permute-start | bytes 442376 | tf_op jit(solution)/shard_map/ppermute | solution.py:37
  74.0 1.5 %collective-permute-start.22 = (bf16[64,1024]{1,0:T(8,128)(2,1)S(1)}, bf16[64,1024]{1,0:T(8,128)(2,1)S(1)}, u32[]{:S(2)}, u32[]{:S(2)}) collective-permute-start(bf16[64,1024]{1,0:T(8,128)(2,1)S(1)} %get-tuple-element.77), channel_id=1, source_target_pairs={{0,1},{1,0},{2,3},{3,2},{4,5},{5,4},{6,7},{7,6},{8,9},{9,8},{10,11... | collective-permute-start | bytes 393224 | tf_op jit(solution)/shard_map/ppermute | solution.py:37
  75.5 1.6 %collective-permute-done.19.refs_2_ = bf16[128,1024]{1,0:T(8,128)(2,1)S(1)} collective-permute-done((bf16[128,1024]{1,0:T(8,128)(2,1)S(1)}, bf16[128,1024]{1,0:T(8,128)(2,1)S(1)}, u32[]{:S(2)}, u32[]{:S(2)}) %collective-permute-start.19) | collective-permute-done | bytes 262176 | tf_op jit(solution)/shard_map/ppermute | solution.py:37
  80.7 5.3 %collective-permute-done.20.refs_2_ = bf16[128,1152]{1,0:T(8,128)(2,1)S(1)} collective-permute-done((bf16[128,1152]{1,0:T(8,128)(2,1)S(1)}, bf16[128,1152]{1,0:T(8,128)(2,1)S(1)}, u32[]{:S(2)}, u32[]{:S(2)}) %collective-permute-start.20) | collective-permute-done | bytes 294944 | tf_op jit(solution)/shard_map/ppermute | solution.py:37
  86.7 5.3 %collective-permute-start.24 = (bf16[64,1024]{1,0:T(8,128)(2,1)S(1)}, bf16[64,1024]{1,0:T(8,128)(2,1)S(1)}, u32[]{:S(2)}, u32[]{:S(2)}) collective-permute-start(bf16[64,1024]{1,0:T(8,128)(2,1)S(1)} %get-tuple-element.83), channel_id=1, source_target_pairs={{0,2},{1,3},{2,0},{3,1},{4,6},{5,7},{6,4},{7,5},{8,10},{9,11},{10,... | collective-permute-start | bytes 393224 | tf_op jit(solution)/shard_map/ppermute | solution.py:37
  92.1 2.8 %collective-permute-start.26 = (bf16[32,1024]{1,0:T(8,128)(2,1)S(1)}, bf16[32,1024]{1,0:T(8,128)(2,1)S(1)}, u32[]{:S(2)}, u32[]{:S(2)}) collective-permute-start(bf16[32,1024]{1,0:T(8,128)(2,1)S(1)} %get-tuple-element.85), channel_id=1, source_target_pairs={{0,2},{1,3},{2,0},{3,1},{4,6},{5,7},{6,4},{7,5},{8,10},{9,11},{10,... | collective-permute-start | bytes 196616 | tf_op jit(solution)/shard_map/ppermute | solution.py:37
  94.9 2.6 %shard_map.168 = (f32[256,1024]{1,0:T(8,128)}, f32[256,1024]{1,0:T(8,128)}, f32[8,128]{1,0:T(8,128)}) custom-call(s32[13]{0:T(128)S(1)} %stack.55.refs_0_, bf16[256,1152]{1,0:T(8,128)(2,1)S(1)} %shard_map.167.refs_1_.refs_3_.refs_5_, bf16[256,1152]{1,0:T(8,128)(2,1)S(1)} %collective-permute-done.23.refs_2_.refs_4_, ...), custom_call_target="tpu_custom_call" | custom-call | tf_op jit(solution)/shard_map/pallas_call | solution.py:59
  97.5 9.4 %collective-permute-done.26.refs_6_ = bf16[32,1024]{1,0:T(8,128)(2,1)S(1)} collective-permute-done((bf16[32,1024]{1,0:T(8,128)(2,1)S(1)}, bf16[32,1024]{1,0:T(8,128)(2,1)S(1)}, u32[]{:S(2)}, u32[]{:S(2)}) %collective-permute-start.26) | collective-permute-done | bytes 65568 | tf_op jit(solution)/shard_map/ppermute | solution.py:37
  107.0 1.2 %copy-done.3 = f32[256,1024]{1,0:T(8,128)S(1)} copy-done((f32[256,1024]{1,0:T(8,128)S(1)}, f32[256,1024]{1,0:T(8,128)}, u32[]{:S(2)}) %copy-start.3) | copy-done | bytes 1048600
  108.2 1.4 %shard_map.169 = (f32[64,1024]{1,0:T(8,128)}, f32[64,1024]{1,0:T(8,128)}, f32[32,1024]{1,0:T(8,128)}) custom-call(s32[13]{0:T(128)S(1)} %stack.55.refs_0_, bf16[64,1024]{1,0:T(8,128)(2,1)S(1)} %get-tuple-element.79.refs_3_.refs_1_, bf16[64,1024]{1,0:T(8,128)(2,1)S(1)} %collective-permute-done.24.refs_2_, bf16[64,1024]{1,0:T(8,128)(2,1)S(1)} %get-tuple-element.75.refs_3_, ...), custom_call_target="tpu_custom_call" | custom-call | tf_op jit(solution)/shard_map/pallas_call | solution.py:59
  (102 shorter events, 30.3 us)
Async XLA Ops:
  0.6 18.5 %copy-start = (bf16[1024,1024]{1,0:T(8,128)(2,1)S(1)}, bf16[1024,1024]{1,0:T(8,128)(2,1)}, u32[]{:S(2)}) copy-start(bf16[1024,1024]{1,0:T(8,128)(2,1)} %param.13) | copy-start | bytes 6291460
  0.6 17.3 %collective-permute-start.3 = (bf16[128,2048]{1,0:T(8,128)(2,1)}, bf16[128,2048]{1,0:T(8,128)(2,1)S(1)}, u32[]{:S(2)}, u32[]{:S(2)}) collective-permute-start(bf16[128,2048]{1,0:T(8,128)(2,1)} %refs_1_.5), channel_id=1, source_target_pairs={{0,4},{4,0},{8,12},{12,8},{16,20},{20,16},{24,28},{28,24},{1,5},{5... | collective-permute-start | bytes 1572872 | tf_op jit(solution)/shard_map/ppermute | solution.py:37
  1.2 7.9 %collective-permute-start.4 = (s32[8,128]{1,0:T(8,128)}, s32[8,128]{1,0:T(8,128)S(1)}, u32[]{:S(2)}, u32[]{:S(2)}) collective-permute-start(s32[8,128]{1,0:T(8,128)} %bitcast.37), channel_id=1, source_target_pairs={{0,4},{4,0},{8,12},{12,8},{16,20},{20,16},{24,28},{28,24},{1,5},{5... | collective-permute-start | bytes 12296 | tf_op jit(solution)/shard_map/ppermute | solution.py:37
  3.4 19.8 %collective-permute-start = (bf16[64,1024]{1,0:T(8,128)(2,1)S(1)}, bf16[64,1024]{1,0:T(8,128)(2,1)S(1)}, u32[]{:S(2)}, u32[]{:S(2)}) collective-permute-start(bf16[64,1024]{1,0:T(8,128)(2,1)S(1)} %get-tuple-element.49), channel_id=1, source_target_pairs={{0,1},{1,0},{2,3},{3,2},{4,5},{5,4},{6,7},{7,6},{8,9},{9,8},{10,11... | collective-permute-start | bytes 393224 | tf_op jit(solution)/shard_map/ppermute | solution.py:37
  6.5 16.8 %collective-permute-start.1 = (bf16[64,1024]{1,0:T(8,128)(2,1)S(1)}, bf16[64,1024]{1,0:T(8,128)(2,1)S(1)}, u32[]{:S(2)}, u32[]{:S(2)}) collective-permute-start(bf16[64,1024]{1,0:T(8,128)(2,1)S(1)} %get-tuple-element.50), channel_id=1, source_target_pairs={{0,2},{1,3},{2,0},{3,1},{4,6},{5,7},{6,4},{7,5},{8,10},{9,11},{10,... | collective-permute-start | bytes 393224 | tf_op jit(solution)/shard_map/ppermute | solution.py:37
  9.1 14.2 %collective-permute-start.2 = (bf16[64,1024]{1,0:T(8,128)(2,1)S(1)}, bf16[64,1024]{1,0:T(8,128)(2,1)S(1)}, u32[]{:S(2)}, u32[]{:S(2)}) collective-permute-start(bf16[64,1024]{1,0:T(8,128)(2,1)S(1)} %get-tuple-element.51), channel_id=1, source_target_pairs={{0,3},{1,2},{2,1},{3,0},{4,7},{5,6},{6,5},{7,4},{8,11},{9,10},{10,... | collective-permute-start | bytes 393224 | tf_op jit(solution)/shard_map/ppermute | solution.py:37
  9.1 2.2 %copy-start.1 = (bf16[1024,2048]{1,0:T(8,128)(2,1)S(1)}, bf16[1024,2048]{1,0:T(8,128)(2,1)}, u32[]{:S(2)}) copy-start(bf16[1024,2048]{1,0:T(8,128)(2,1)} %refs_1_.4) | copy-start | bytes 12582916
  11.3 2.2 %copy-start.2 = (bf16[2048,1024]{1,0:T(8,128)(2,1)S(1)}, bf16[2048,1024]{1,0:T(8,128)(2,1)}, u32[]{:S(2)}) copy-start(bf16[2048,1024]{1,0:T(8,128)(2,1)} %refs_2_.1) | copy-start | bytes 12582916
  14.1 3.3 %copy-start.8 = (bf16[256,1024]{1,0:T(8,128)(2,1)S(1)}, bf16[256,1024]{1,0:T(8,128)(2,1)}, u32[]{:S(2)}) copy-start(bf16[256,1024]{1,0:T(8,128)(2,1)} %param.14) | copy-start | bytes 1572868
  23.9 2.0 %collective-permute-start.5 = (bf16[256,1024]{1,0:T(8,128)(2,1)S(1)}, bf16[256,1024]{1,0:T(8,128)(2,1)S(1)}, u32[]{:S(2)}, u32[]{:S(2)}) collective-permute-start(bf16[256,1024]{1,0:T(8,128)(2,1)S(1)} %shard_map.147.refs_2_.refs_1_), channel_id=1, source_target_pairs={{0,4},{4,0},{8,12},{12,8},{16,20},{20,16},{24,28},{28,24},{1,5},{5... | collective-permute-start | bytes 1572872 | tf_op jit(solution)/shard_map/ppermute | solution.py:37
  25.2 12.3 %collective-permute-start.7 = (bf16[128,1024]{1,0:T(8,128)(2,1)S(1)}, bf16[128,1024]{1,0:T(8,128)(2,1)S(1)}, u32[]{:S(2)}, u32[]{:S(2)}) collective-permute-start(bf16[128,1024]{1,0:T(8,128)(2,1)S(1)} %get-tuple-element.106), channel_id=1, source_target_pairs={{0,4},{4,0},{8,12},{12,8},{16,20},{20,16},{24,28},{28,24},{1,5},{5... | collective-permute-start | bytes 786440 | tf_op jit(solution)/shard_map/ppermute | solution.py:37
  29.1 5.7 %collective-permute-start.6 = (bf16[512,1024]{1,0:T(8,128)(2,1)S(1)}, bf16[512,1024]{1,0:T(8,128)(2,1)S(1)}, u32[]{:S(2)}, u32[]{:S(2)}) collective-permute-start(bf16[512,1024]{1,0:T(8,128)(2,1)S(1)} %get-tuple-element.112), channel_id=1, source_target_pairs={{0,4},{4,0},{8,12},{12,8},{16,20},{20,16},{24,28},{28,24},{1,5},{5... | collective-permute-start | bytes 3145736 | tf_op jit(solution)/shard_map/ppermute | solution.py:37
  30.0 20.5 %collective-permute-start.10 = (bf16[512,1024]{1,0:T(8,128)(2,1)S(1)}, bf16[512,1024]{1,0:T(8,128)(2,1)S(1)}, u32[]{:S(2)}, u32[]{:S(2)}) collective-permute-start(bf16[512,1024]{1,0:T(8,128)(2,1)S(1)} %convolution_convert_fusion.3.refs_2_), channel_id=1, source_target_pairs={{0,8},{4,20},{8,0},{12,28},{16,24},{20,4},{24,16},{28,12},{1,9},{5... | collective-permute-start | bytes 3145736 | tf_op jit(solution)/shard_map/ppermute | solution.py:37
  32.5 25.5 %collective-permute-start.12 = (bf16[512,1024]{1,0:T(8,128)(2,1)S(1)}, bf16[512,1024]{1,0:T(8,128)(2,1)S(1)}, u32[]{:S(2)}, u32[]{:S(2)}) collective-permute-start(bf16[512,1024]{1,0:T(8,128)(2,1)S(1)} %convolution_convert_fusion.2.refs_3_), channel_id=1, source_target_pairs={{0,1},{1,0},{2,3},{3,2},{4,5},{5,4},{6,7},{7,6},{8,9},{9,8},{10,11... | collective-permute-start | bytes 3145736 | tf_op jit(solution)/shard_map/ppermute | solution.py:37
  38.1 10.0 %collective-permute-start.8 = (bf16[128,1152]{1,0:T(8,128)(2,1)S(1)}, bf16[128,1152]{1,0:T(8,128)(2,1)S(1)}, u32[]{:S(2)}, u32[]{:S(2)}) collective-permute-start(bf16[128,1152]{1,0:T(8,128)(2,1)S(1)} %get-tuple-element.60), channel_id=1, source_target_pairs={{0,8},{4,20},{8,0},{12,28},{16,24},{20,4},{24,16},{28,12},{1,9},{5... | collective-permute-start | bytes 884744 | tf_op jit(solution)/shard_map/ppermute | solution.py:37
  41.0 23.0 %collective-permute-start.14 = (bf16[256,1024]{1,0:T(8,128)(2,1)S(1)}, bf16[256,1024]{1,0:T(8,128)(2,1)S(1)}, u32[]{:S(2)}, u32[]{:S(2)}) collective-permute-start(bf16[256,1024]{1,0:T(8,128)(2,1)S(1)} %get-tuple-element.66), channel_id=1, source_target_pairs={{0,8},{4,20},{8,0},{12,28},{16,24},{20,4},{24,16},{28,12},{1,9},{5... | collective-permute-start | bytes 1572872 | tf_op jit(solution)/shard_map/ppermute | solution.py:37
  42.6 6.1 %copy-start.6 = (bf16[128,2048]{1,0:T(8,128)(2,1)}, bf16[128,2048]{1,0:T(8,128)(2,1)S(1)}, u32[]{:S(2)}) copy-start(bf16[128,2048]{1,0:T(8,128)(2,1)S(1)} %pad_maximum_fusion.refs_7_) | copy-start | bytes 1572868
  48.7 6.0 %collective-permute-start.9 = (bf16[64,1152]{1,0:T(8,128)(2,1)S(1)}, bf16[64,1152]{1,0:T(8,128)(2,1)S(1)}, u32[]{:S(2)}, u32[]{:S(2)}) collective-permute-start(bf16[64,1152]{1,0:T(8,128)(2,1)S(1)} %get-tuple-element.63), channel_id=1, source_target_pairs={{0,16},{4,12},{8,24},{12,4},{16,0},{20,28},{24,8},{28,20},{1,17},{... | collective-permute-start | bytes 442376 | tf_op jit(solution)/shard_map/ppermute | solution.py:37
  51.3 14.9 %collective-permute-start.17 = (bf16[256,1024]{1,0:T(8,128)(2,1)S(1)}, bf16[256,1024]{1,0:T(8,128)(2,1)S(1)}, u32[]{:S(2)}, u32[]{:S(2)}) collective-permute-start(bf16[256,1024]{1,0:T(8,128)(2,1)S(1)} %get-tuple-element.70), channel_id=1, source_target_pairs={{0,16},{4,12},{8,24},{12,4},{16,0},{20,28},{24,8},{28,20},{1,17},{... | collective-permute-start | bytes 1572872 | tf_op jit(solution)/shard_map/ppermute | solution.py:37
  55.2 5.7 %collective-permute-start.11 = (bf16[64,1152]{1,0:T(8,128)(2,1)S(1)}, bf16[64,1152]{1,0:T(8,128)(2,1)S(1)}, u32[]{:S(2)}, u32[]{:S(2)}) collective-permute-start(bf16[64,1152]{1,0:T(8,128)(2,1)S(1)} %shard_map.155.refs_3_.refs_1_), channel_id=1, source_target_pairs={{0,1},{1,0},{2,3},{3,2},{4,5},{5,4},{6,7},{7,6},{8,9},{9,8},{10,11... | collective-permute-start | bytes 442376 | tf_op jit(solution)/shard_map/ppermute | solution.py:37
  58.9 11.1 %collective-permute-start.16 = (bf16[256,1024]{1,0:T(8,128)(2,1)S(1)}, bf16[256,1024]{1,0:T(8,128)(2,1)S(1)}, u32[]{:S(2)}, u32[]{:S(2)}) collective-permute-start(bf16[256,1024]{1,0:T(8,128)(2,1)S(1)} %get-tuple-element.69), channel_id=1, source_target_pairs={{0,8},{4,20},{8,0},{12,28},{16,24},{20,4},{24,16},{28,12},{1,9},{5... | collective-permute-start | bytes 1572872 | tf_op jit(solution)/shard_map/ppermute | solution.py:37
  61.5 10.2 %collective-permute-start.13 = (bf16[64,1152]{1,0:T(8,128)(2,1)S(1)}, bf16[64,1152]{1,0:T(8,128)(2,1)S(1)}, u32[]{:S(2)}, u32[]{:S(2)}) collective-permute-start(bf16[64,1152]{1,0:T(8,128)(2,1)S(1)} %shard_map.157.refs_3_.refs_1_), channel_id=1, source_target_pairs={{0,2},{1,3},{2,0},{3,1},{4,6},{5,7},{6,4},{7,5},{8,10},{9,11},{10,... | collective-permute-start | bytes 442376 | tf_op jit(solution)/shard_map/ppermute | solution.py:37
  64.7 6.4 %collective-permute-start.15 = (bf16[128,1024]{1,0:T(8,128)(2,1)S(1)}, bf16[128,1024]{1,0:T(8,128)(2,1)S(1)}, u32[]{:S(2)}, u32[]{:S(2)}) collective-permute-start(bf16[128,1024]{1,0:T(8,128)(2,1)S(1)} %get-tuple-element.68), channel_id=1, source_target_pairs={{0,16},{4,12},{8,24},{12,4},{16,0},{20,28},{24,8},{28,20},{1,17},{... | collective-permute-start | bytes 786440 | tf_op jit(solution)/shard_map/ppermute | solution.py:37
  66.8 13.3 %collective-permute-start.21 = (bf16[128,1024]{1,0:T(8,128)(2,1)S(1)}, bf16[128,1024]{1,0:T(8,128)(2,1)S(1)}, u32[]{:S(2)}, u32[]{:S(2)}) collective-permute-start(bf16[128,1024]{1,0:T(8,128)(2,1)S(1)} %get-tuple-element.76), channel_id=1, source_target_pairs={{0,1},{1,0},{2,3},{3,2},{4,5},{5,4},{6,7},{7,6},{8,9},{9,8},{10,11... | collective-permute-start | bytes 786440 | tf_op jit(solution)/shard_map/ppermute | solution.py:37
  70.6 6.4 %collective-permute-start.19 = (bf16[128,1024]{1,0:T(8,128)(2,1)S(1)}, bf16[128,1024]{1,0:T(8,128)(2,1)S(1)}, u32[]{:S(2)}, u32[]{:S(2)}) collective-permute-start(bf16[128,1024]{1,0:T(8,128)(2,1)S(1)} %get-tuple-element.74), channel_id=1, source_target_pairs={{0,16},{4,12},{8,24},{12,4},{16,0},{20,28},{24,8},{28,20},{1,17},{... | collective-permute-start | bytes 786440 | tf_op jit(solution)/shard_map/ppermute | solution.py:37
  72.3 6.3 %collective-permute-start.18 = (bf16[64,1152]{1,0:T(8,128)(2,1)S(1)}, bf16[64,1152]{1,0:T(8,128)(2,1)S(1)}, u32[]{:S(2)}, u32[]{:S(2)}) collective-permute-start(bf16[64,1152]{1,0:T(8,128)(2,1)S(1)} %shard_map.162.refs_3_.refs_1_), channel_id=1, source_target_pairs={{0,16},{4,12},{8,24},{12,4},{16,0},{20,28},{24,8},{28,20},{1,17},{... | collective-permute-start | bytes 442376 | tf_op jit(solution)/shard_map/ppermute | solution.py:37
  74.0 5.5 %collective-permute-start.22 = (bf16[64,1024]{1,0:T(8,128)(2,1)S(1)}, bf16[64,1024]{1,0:T(8,128)(2,1)S(1)}, u32[]{:S(2)}, u32[]{:S(2)}) collective-permute-start(bf16[64,1024]{1,0:T(8,128)(2,1)S(1)} %get-tuple-element.77), channel_id=1, source_target_pairs={{0,1},{1,0},{2,3},{3,2},{4,5},{5,4},{6,7},{7,6},{8,9},{9,8},{10,11... | collective-permute-start | bytes 393224 | tf_op jit(solution)/shard_map/ppermute | solution.py:37
  79.2 6.8 %collective-permute-start.20 = (bf16[128,1152]{1,0:T(8,128)(2,1)S(1)}, bf16[128,1152]{1,0:T(8,128)(2,1)S(1)}, u32[]{:S(2)}, u32[]{:S(2)}) collective-permute-start(bf16[128,1152]{1,0:T(8,128)(2,1)S(1)} %shard_map.164.refs_3_.refs_1_), channel_id=1, source_target_pairs={{0,8},{4,20},{8,0},{12,28},{16,24},{20,4},{24,16},{28,12},{1,9},{5... | collective-permute-start | bytes 884744 | tf_op jit(solution)/shard_map/ppermute | solution.py:37
  86.6 8.3 %collective-permute-start.23 = (bf16[256,1152]{1,0:T(8,128)(2,1)S(1)}, bf16[256,1152]{1,0:T(8,128)(2,1)S(1)}, u32[]{:S(2)}, u32[]{:S(2)}) collective-permute-start(bf16[256,1152]{1,0:T(8,128)(2,1)S(1)} %shard_map.167.refs_1_.refs_3_.refs_5_), channel_id=1, source_target_pairs={{0,4},{4,0},{8,12},{12,8},{16,20},{20,16},{24,28},{28,24},{1,5},{5... | collective-permute-start | bytes 1769480 | tf_op jit(solution)/shard_map/ppermute | solution.py:37
  86.7 20.3 %collective-permute-start.24 = (bf16[64,1024]{1,0:T(8,128)(2,1)S(1)}, bf16[64,1024]{1,0:T(8,128)(2,1)S(1)}, u32[]{:S(2)}, u32[]{:S(2)}) collective-permute-start(bf16[64,1024]{1,0:T(8,128)(2,1)S(1)} %get-tuple-element.83), channel_id=1, source_target_pairs={{0,2},{1,3},{2,0},{3,1},{4,6},{5,7},{6,4},{7,5},{8,10},{9,11},{10,... | collective-permute-start | bytes 393224 | tf_op jit(solution)/shard_map/ppermute | solution.py:37
  92.0 15.0 %collective-permute-start.25 = (bf16[64,1024]{1,0:T(8,128)(2,1)S(1)}, bf16[64,1024]{1,0:T(8,128)(2,1)S(1)}, u32[]{:S(2)}, u32[]{:S(2)}) collective-permute-start(bf16[64,1024]{1,0:T(8,128)(2,1)S(1)} %get-tuple-element.84), channel_id=1, source_target_pairs={{0,2},{1,3},{2,0},{3,1},{4,6},{5,7},{6,4},{7,5},{8,10},{9,11},{10,... | collective-permute-start | bytes 393224 | tf_op jit(solution)/shard_map/ppermute | solution.py:37
  92.1 14.9 %collective-permute-start.26 = (bf16[32,1024]{1,0:T(8,128)(2,1)S(1)}, bf16[32,1024]{1,0:T(8,128)(2,1)S(1)}, u32[]{:S(2)}, u32[]{:S(2)}) collective-permute-start(bf16[32,1024]{1,0:T(8,128)(2,1)S(1)} %get-tuple-element.85), channel_id=1, source_target_pairs={{0,2},{1,3},{2,0},{3,1},{4,6},{5,7},{6,4},{7,5},{8,10},{9,11},{10,... | collective-permute-start | bytes 196616 | tf_op jit(solution)/shard_map/ppermute | solution.py:37
  (6 other events, 6.9 us)

commit v2 on v1

--- a/solution.py
+++ b/solution.py
@@ -258,9 +258,11 @@
 
 
 def finals_body(numbers, *refs):
-    for i in range(len(refs) // 3):
-        kept, arrived, whole = refs[2 * i], refs[2 * i + 1], refs[len(refs) // 3 * 2 + i]
-        whole[...] = kept[...].astype(F32) + arrived[...].astype(F32)
+    count = len(refs) // 3
+    for i in range(count):
+        kept, arrived, total = refs[2 * i], refs[2 * i + 1], refs[2 * count + i]
+        total[...] = kept[...].astype(F32) + arrived[...].astype(F32)
+    refs[-1][...] = jnp.zeros(refs[-1].shape, F32)
 
 
 def on_device(
@@ -345,6 +347,7 @@
         [like(own * part, width, BF)] * tp_count,
         [out_grad],
         [],
+        flops=STEP,
     )
     blocks = [swap(b, "tp", (m,)) if m else b for m, b in enumerate(blocks)]
     far = pl.BlockSpec(memory_space=pltpu.HBM)
@@ -534,21 +537,23 @@
     count = table.kept.shape[0]
     lines = width // 128
     beside = pl.BlockSpec((count, 128), lambda n, s: (0, lines))
+    ends = [down, up, proj]
+    down_grad, up_grad, proj_grad, token = call(
+        finals_body,
+        [like(*c.kept.shape, F32) for c in ends] + [like(8, 128, F32)],
+        [x for c in ends for x in (c.kept, c.arrived)],
+        last,
+        flops=STEP,
+    )
     emb_global_grad, emb_local_grad, gain_grad = call(
         functools.partial(tables_body, share_count, tp_count, height),
         [like(vocab, width, F32), like(vocab, width, F32), like(lines, 128, F32)],
         [table.kept, table.arrived, table.kept, table.arrived],
-        last,
+        [token],
+        flops=STEP,
         grid=parts,
         in_specs=[columns(count), columns(count), beside, beside],
         out_specs=[columns(vocab), columns(vocab), None],
-    )
-    ends = [down, up, proj]
-    down_grad, up_grad, proj_grad = call(
-        finals_body,
-        [like(*c.kept.shape, F32) for c in ends],
-        [x for c in ends for x in (c.kept, c.arrived)],
-        [emb_global_grad],
     )
     return (
         glob_out_grad,

time: 110 us -> 99.6 us (0.905)
  waiting for transfers between devices: 30.9 us -> 22.3 us
  local copies, waits for them, and re-layouts: 8.76 us -> 6.85 us
    ppermute x27, waiting for transfers between devices: 30.9 us -> 22.3 us  [swap(): return lax.ppermute(value, axis, pairs)]
    unnamed x28 -> x26, local copies, waits for them, and re-layouts: 8.22 us -> 6.31 us
  transfers between devices with their start and end apart: 27 -> 27, of which waited for: 11 -> 10; matrix products, arithmetic and copies ran while one was open for 13% -> 15% of each run, Pallas kernels for 18% -> 19%
where the time goes in v2:
time: 99.6 us; the launch traced here: 99.4 us
  starting transfers between devices  33.5 us (34%)
  waiting for transfers between devices  22.3 us (22%)
  Pallas kernels  21.9 us (22%)
  matrix products  11.7 us (12%)
  local copies, waits for them, and re-layouts  6.85 us (7%)
  other arithmetic  2.04 us (2%)
  between operations  1.2 us (1%)
    ppermute x27, starting transfers between devices, swap(): return lax.ppermute(value, axis, pairs)  33.5 us
    ppermute x27, waiting for transfers between devices, swap(): return lax.ppermute(value, axis, pairs)  22.3 us
    pallas_call x26, Pallas kernels, run(): pl.pallas_call(kernel, out_shape=tuple(outs), grid_spec=pltpu.PrefetchSca...  21.9 us
    unnamed x26, local copies, waits for them, and re-layouts  6.31 us
    dot_general x8, matrix products, inner(): lax.dot_general(left, right, (((0,), (0,)), ((), ())), preferred_element_...  4.65 us
    dot_general x3, matrix products, times(): return jnp.dot(left, right, preferred_element_type=F32)  3.64 us
    dot_general x3, matrix products, outer(): lax.dot_general(left, right, (((1,), (1,)), ((), ())), preferred_element_...  3.36 us
  transfers between devices with their start and end apart: 27, of which 10 were waited for; matrix products, arithmetic and copies ran while one was open for 15% of the time, Pallas kernels for 19%

profile of v2, /device:TPU:0, one launch (start us, length us, event | category | flops | bytes accessed | tf_op | source)
XLA Modules:
  0.0 99.4 jit_solution(774377306059839983)
XLA Ops:
  1.3 1.0 %copy-done.6 = bf16[256,1024]{1,0:T(8,128)(2,1)S(1)} copy-done((bf16[256,1024]{1,0:T(8,128)(2,1)S(1)}, bf16[256,1024]{1,0:T(8,128)(2,1)}, u32[]{:S(2)}) %copy-start.6) | copy-done | bytes 524312
  2.4 1.0 %shard_map.144 = (bf16[64,1024]{1,0:T(8,128)(2,1)S(1)}, bf16[64,1024]{1,0:T(8,128)(2,1)S(1)}, bf16[64,1024]{1,0:T(8,128)(2,1)S(1)}, bf16[64,1024]{1,0:T(8,128)(2,1)S(1)}) custom-call(s32[13]{0:T(128)S(1)} %stack.55.refs_0_, bf16[256,1024]{1,0:T(8,128)(2,1)S(1)} %copy-done.6), custom_call_target="tpu_custom_call" | custom-call | flops 6000000000 | tf_op jit(solution)/shard_map/pallas_call | solution.py:59
  3.4 3.1 %collective-permute-start = (bf16[64,1024]{1,0:T(8,128)(2,1)S(1)}, bf16[64,1024]{1,0:T(8,128)(2,1)S(1)}, u32[]{:S(2)}, u32[]{:S(2)}) collective-permute-start(bf16[64,1024]{1,0:T(8,128)(2,1)S(1)} %get-tuple-element.50), channel_id=1, source_target_pairs={{0,1},{1,0},{2,3},{3,2},{4,5},{5,4},{6,7},{7,6},{8,9},{9,8},{10,11... | collective-permute-start | bytes 393224 | tf_op jit(solution)/shard_map/ppermute | solution.py:37
  6.5 2.6 %collective-permute-start.1 = (bf16[64,1024]{1,0:T(8,128)(2,1)S(1)}, bf16[64,1024]{1,0:T(8,128)(2,1)S(1)}, u32[]{:S(2)}, u32[]{:S(2)}) collective-permute-start(bf16[64,1024]{1,0:T(8,128)(2,1)S(1)} %get-tuple-element.51), channel_id=1, source_target_pairs={{0,2},{1,3},{2,0},{3,1},{4,6},{5,7},{6,4},{7,5},{8,10},{9,11},{10,... | collective-permute-start | bytes 393224 | tf_op jit(solution)/shard_map/ppermute | solution.py:37
  9.1 2.2 %copy-done.1 = bf16[1024,2048]{1,0:T(8,128)(2,1)S(1)} copy-done((bf16[1024,2048]{1,0:T(8,128)(2,1)S(1)}, bf16[1024,2048]{1,0:T(8,128)(2,1)}, u32[]{:S(2)}) %copy-start.1) | copy-done | bytes 4194328
  11.3 2.2 %copy-done.2 = bf16[2048,1024]{1,0:T(8,128)(2,1)S(1)} copy-done((bf16[2048,1024]{1,0:T(8,128)(2,1)S(1)}, bf16[2048,1024]{1,0:T(8,128)(2,1)}, u32[]{:S(2)}) %copy-start.2) | copy-done | bytes 4194328
  13.5 3.3 %shard_map.145 = (bf16[512,256]{1,0:T(8,128)(2,1)S(1)}, bf16[512,128]{1,0:T(8,128)(2,1)S(1)}, bf16[256,256]{1,0:T(8,128)(2,1)S(1)}, bf16[1024,1024]{1,0:T(8,128)(2,1)S(1)}, bf16[1024,1024]{1,0:T(8,128)(2,1)S(1)}) custom-call(s32[13]{0:T(128)S(1)} %stack.55.refs_0_, bf16[1024,2048]{1,0:T(8,128)(2,1)S(1)} %copy-done.1, bf16[2048,1024]{1,0:T(8,128)(2,1)S(1)} %copy-done.2, ...), custom_call_target="tpu_custom_call" | custom-call | tf_op jit(solution)/shard_map/pallas_call | solution.py:59
  18.5 1.4 %multiply_reduce_fusion.2 = (f32[512]{0:T(512)S(1)}, f32[512,1024]{1,0:T(8,128)S(1)}) fusion(f32[512,1024]{1,0:T(8,128)S(1)} %fusion.39, bf16[512,1024]{1,0:T(8,128)(2,1)S(1)} %shard_map.146, bf16[1024,1024]{1,0:T(8,128)(2,1)S(1)} %copy-done), kind=kOutput, calls=%fused_computation.9 | convolution fusion | flops 1075314176 | bytes 7342080 | tf_op jit(solution)/shard_map/dot_general | solution.py:31
  20.1 1.8 %multiply_convert_fusion.1 = (bf16[512,1024]{1,0:T(8,128)(2,1)S(1)}, bf16[512,1024]{1,0:T(8,128)(2,1)S(1)}) fusion(bf16[512,1024]{1,0:T(8,128)(2,1)S(1)} %multiply_convert_fusion.3, bf16[1024,1024]{1,0:T(8,128)(2,1)S(1)} %get-tuple-element.54), kind=kOutput, calls=%fused_computation.5 | convolution fusion | flops 1078984704 | bytes 5242880 | tf_op jit(solution)/shard_map/dot_general | solution.py:31
  25.8 1.3 %multiply_convert_fusion = bf16[512,1024]{1,0:T(8,128)(2,1)S(1)} fusion(bf16[512,1024]{1,0:T(8,128)(2,1)S(1)} %get-tuple-element.58, bf16[512,1024]{1,0:T(8,128)(2,1)S(1)} %shard_map.149, bf16[1024,1024]{1,0:T(8,128)(2,1)S(1)} %get-tuple-element.57), kind=kOutput, calls=%fused_computation.4 | convolution fusion | flops 1075314688 | bytes 5242880 | tf_op jit(solution)/shard_map/dot_general | solution.py:25
  27.1 1.3 %fusion.38 = (bf16[512,1024]{1,0:T(8,128)(2,1)S(1)}, f32[512,1024]{1,0:T(8,128)S(1)}) fusion(bf16[512,1024]{1,0:T(8,128)(2,1)S(1)} %multiply_convert_fusion, bf16[1024,1024]{1,0:T(8,128)(2,1)S(1)} %get-tuple-element.54), kind=kOutput, calls=%fused_computation.70 | convolution fusion | flops 1074266112 | bytes 6291456 | tf_op jit(solution)/shard_map/dot_general | solution.py:25
  29.3 1.8 %collective-permute-start.10 = (bf16[512,1024]{1,0:T(8,128)(2,1)S(1)}, bf16[512,1024]{1,0:T(8,128)(2,1)S(1)}, u32[]{:S(2)}, u32[]{:S(2)}) collective-permute-start(bf16[512,1024]{1,0:T(8,128)(2,1)S(1)} %convolution_convert_fusion.3.refs_2_), channel_id=1, source_target_pairs={{0,8},{4,20},{8,0},{12,28},{16,24},{20,4},{24,16},{28,12},{1,9},{5... | collective-permute-start | bytes 3145736 | tf_op jit(solution)/shard_map/ppermute | solution.py:37
  40.3 1.6 %collective-permute-start.14 = (bf16[256,1024]{1,0:T(8,128)(2,1)S(1)}, bf16[256,1024]{1,0:T(8,128)(2,1)S(1)}, u32[]{:S(2)}, u32[]{:S(2)}) collective-permute-start(bf16[256,1024]{1,0:T(8,128)(2,1)S(1)} %get-tuple-element.67), channel_id=1, source_target_pairs={{0,8},{4,20},{8,0},{12,28},{16,24},{20,4},{24,16},{28,12},{1,9},{5... | collective-permute-start | bytes 1572872 | tf_op jit(solution)/shard_map/ppermute | solution.py:37
  41.9 5.4 %collective-permute-done.8.refs_2_ = bf16[128,1152]{1,0:T(8,128)(2,1)S(1)} collective-permute-done((bf16[128,1152]{1,0:T(8,128)(2,1)S(1)}, bf16[128,1152]{1,0:T(8,128)(2,1)S(1)}, u32[]{:S(2)}, u32[]{:S(2)}) %collective-permute-start.8) | collective-permute-done | bytes 294944 | tf_op jit(solution)/shard_map/ppermute | solution.py:37
  48.0 1.8 %collective-permute-start.9 = (bf16[64,1152]{1,0:T(8,128)(2,1)S(1)}, bf16[64,1152]{1,0:T(8,128)(2,1)S(1)}, u32[]{:S(2)}, u32[]{:S(2)}) collective-permute-start(bf16[64,1152]{1,0:T(8,128)(2,1)S(1)} %get-tuple-element.64), channel_id=1, source_target_pairs={{0,16},{4,12},{8,24},{12,4},{16,0},{20,28},{24,8},{28,20},{1,17},{... | collective-permute-start | bytes 442376 | tf_op jit(solution)/shard_map/ppermute | solution.py:37
  50.9 3.0 %collective-permute-done.9.refs_2_ = bf16[64,1152]{1,0:T(8,128)(2,1)S(1)} collective-permute-done((bf16[64,1152]{1,0:T(8,128)(2,1)S(1)}, bf16[64,1152]{1,0:T(8,128)(2,1)S(1)}, u32[]{:S(2)}, u32[]{:S(2)}) %collective-permute-start.9) | collective-permute-done | bytes 147488 | tf_op jit(solution)/shard_map/ppermute | solution.py:37
  54.6 1.0 collective-permute-start.11
  55.5 1.9 %collective-permute-done.12.refs_2_ = bf16[512,1024]{1,0:T(8,128)(2,1)S(1)} collective-permute-done((bf16[512,1024]{1,0:T(8,128)(2,1)S(1)}, bf16[512,1024]{1,0:T(8,128)(2,1)S(1)}, u32[]{:S(2)}, u32[]{:S(2)}) %collective-permute-start.12) | collective-permute-done | bytes 1048608 | tf_op jit(solution)/shard_map/ppermute | solution.py:37
  58.8 1.5 %collective-permute-done.11.refs_2_ = bf16[64,1152]{1,0:T(8,128)(2,1)S(1)} collective-permute-done((bf16[64,1152]{1,0:T(8,128)(2,1)S(1)}, bf16[64,1152]{1,0:T(8,128)(2,1)S(1)}, u32[]{:S(2)}, u32[]{:S(2)}) %collective-permute-start.11) | collective-permute-done | bytes 147488 | tf_op jit(solution)/shard_map/ppermute | solution.py:37
  60.8 2.5 %collective-permute-start.13 = (bf16[64,1152]{1,0:T(8,128)(2,1)S(1)}, bf16[64,1152]{1,0:T(8,128)(2,1)S(1)}, u32[]{:S(2)}, u32[]{:S(2)}) collective-permute-start(bf16[64,1152]{1,0:T(8,128)(2,1)S(1)} %shard_map.157.refs_3_.refs_1_), channel_id=1, source_target_pairs={{0,2},{1,3},{2,0},{3,1},{4,6},{5,7},{6,4},{7,5},{8,10},{9,11},{10,... | collective-permute-start | bytes 442376 | tf_op jit(solution)/shard_map/ppermute | solution.py:37
  64.0 1.5 %collective-permute-start.15 = (bf16[128,1024]{1,0:T(8,128)(2,1)S(1)}, bf16[128,1024]{1,0:T(8,128)(2,1)S(1)}, u32[]{:S(2)}, u32[]{:S(2)}) collective-permute-start(bf16[128,1024]{1,0:T(8,128)(2,1)S(1)} %get-tuple-element.69), channel_id=1, source_target_pairs={{0,16},{4,12},{8,24},{12,4},{16,0},{20,28},{24,8},{28,20},{1,17},{... | collective-permute-start | bytes 786440 | tf_op jit(solution)/shard_map/ppermute | solution.py:37
  66.1 1.8 %collective-permute-start.21 = (bf16[128,1024]{1,0:T(8,128)(2,1)S(1)}, bf16[128,1024]{1,0:T(8,128)(2,1)S(1)}, u32[]{:S(2)}, u32[]{:S(2)}) collective-permute-start(bf16[128,1024]{1,0:T(8,128)(2,1)S(1)} %get-tuple-element.77), channel_id=1, source_target_pairs={{0,1},{1,0},{2,3},{3,2},{4,5},{5,4},{6,7},{7,6},{8,9},{9,8},{10,11... | collective-permute-start | bytes 786440 | tf_op jit(solution)/shard_map/ppermute | solution.py:37
  67.9 1.3 %collective-permute-done.16.refs_2_ = bf16[256,1024]{1,0:T(8,128)(2,1)S(1)} collective-permute-done((bf16[256,1024]{1,0:T(8,128)(2,1)S(1)}, bf16[256,1024]{1,0:T(8,128)(2,1)S(1)}, u32[]{:S(2)}, u32[]{:S(2)}) %collective-permute-start.16) | collective-permute-done | bytes 524320 | tf_op jit(solution)/shard_map/ppermute | solution.py:37
  71.7 1.7 %collective-permute-start.18 = (bf16[64,1152]{1,0:T(8,128)(2,1)S(1)}, bf16[64,1152]{1,0:T(8,128)(2,1)S(1)}, u32[]{:S(2)}, u32[]{:S(2)}) collective-permute-start(bf16[64,1152]{1,0:T(8,128)(2,1)S(1)} %shard_map.162.refs_3_.refs_1_), channel_id=1, source_target_pairs={{0,16},{4,12},{8,24},{12,4},{16,0},{20,28},{24,8},{28,20},{1,17},{... | collective-permute-start | bytes 442376 | tf_op jit(solution)/shard_map/ppermute | solution.py:37
  73.3 1.5 %collective-permute-start.22 = (bf16[64,1024]{1,0:T(8,128)(2,1)S(1)}, bf16[64,1024]{1,0:T(8,128)(2,1)S(1)}, u32[]{:S(2)}, u32[]{:S(2)}) collective-permute-start(bf16[64,1024]{1,0:T(8,128)(2,1)S(1)} %get-tuple-element.78), channel_id=1, source_target_pairs={{0,1},{1,0},{2,3},{3,2},{4,5},{5,4},{6,7},{7,6},{8,9},{9,8},{10,11... | collective-permute-start | bytes 393224 | tf_op jit(solution)/shard_map/ppermute | solution.py:37
  74.9 1.5 %collective-permute-done.19.refs_2_ = bf16[128,1024]{1,0:T(8,128)(2,1)S(1)} collective-permute-done((bf16[128,1024]{1,0:T(8,128)(2,1)S(1)}, bf16[128,1024]{1,0:T(8,128)(2,1)S(1)}, u32[]{:S(2)}, u32[]{:S(2)}) %collective-permute-start.19) | collective-permute-done | bytes 262176 | tf_op jit(solution)/shard_map/ppermute | solution.py:37
  77.0 1.0 collective-permute-done.18.refs_2_
  80.1 5.7 %collective-permute-start.24 = (bf16[64,1024]{1,0:T(8,128)(2,1)S(1)}, bf16[64,1024]{1,0:T(8,128)(2,1)S(1)}, u32[]{:S(2)}, u32[]{:S(2)}) collective-permute-start(bf16[64,1024]{1,0:T(8,128)(2,1)S(1)} %get-tuple-element.81), channel_id=1, source_target_pairs={{0,2},{1,3},{2,0},{3,1},{4,6},{5,7},{6,4},{7,5},{8,10},{9,11},{10,... | collective-permute-start | bytes 393224 | tf_op jit(solution)/shard_map/ppermute | solution.py:37
  85.8 2.8 %collective-permute-start.26 = (bf16[32,1024]{1,0:T(8,128)(2,1)S(1)}, bf16[32,1024]{1,0:T(8,128)(2,1)S(1)}, u32[]{:S(2)}, u32[]{:S(2)}) collective-permute-start(bf16[32,1024]{1,0:T(8,128)(2,1)S(1)} %get-tuple-element.83), channel_id=1, source_target_pairs={{0,2},{1,3},{2,0},{3,1},{4,6},{5,7},{6,4},{7,5},{8,10},{9,11},{10,... | collective-permute-start | bytes 196616 | tf_op jit(solution)/shard_map/ppermute | solution.py:37
  89.3 6.1 %collective-permute-done.26.refs_6_ = bf16[32,1024]{1,0:T(8,128)(2,1)S(1)} collective-permute-done((bf16[32,1024]{1,0:T(8,128)(2,1)S(1)}, bf16[32,1024]{1,0:T(8,128)(2,1)S(1)}, u32[]{:S(2)}, u32[]{:S(2)}) %collective-permute-start.26) | collective-permute-done | bytes 65568 | tf_op jit(solution)/shard_map/ppermute | solution.py:37
  95.4 1.4 %shard_map.168 = (f32[64,1024]{1,0:T(8,128)}, f32[64,1024]{1,0:T(8,128)}, f32[32,1024]{1,0:T(8,128)}, f32[8,128]{1,0:T(8,128)S(1)}) custom-call(s32[13]{0:T(128)S(1)} %stack.55.refs_0_, bf16[64,1024]{1,0:T(8,128)(2,1)S(1)} %get-tuple-element.80.refs_3_.refs_1_, bf16[64,1024]{1,0:T(8,128)(2,1)S(1)} %collective-permute-done.24.refs_2_, ...), custom_call_target="tpu_custom_call" | custom-call | flops 6000000000 | tf_op jit(solution)/shard_map/pallas_call | solution.py:59
  96.8 2.6 %shard_map.169 = (f32[256,1024]{1,0:T(8,128)}, f32[256,1024]{1,0:T(8,128)}, f32[8,128]{1,0:T(8,128)}) custom-call(s32[13]{0:T(128)S(1)} %stack.55.refs_0_, bf16[256,1152]{1,0:T(8,128)(2,1)S(1)} %shard_map.167.refs_7_.refs_1_.refs_3_, bf16[256,1152]{1,0:T(8,128)(2,1)S(1)} %collective-permute-done.23.refs_2_.refs_4_, ...), custom_call_target="tpu_custom_call" | custom-call | flops 6000000000 | tf_op jit(solution)/shard_map/pallas_call | solution.py:59
  (100 shorter events, 27.7 us)
Async XLA Ops:
  0.6 17.8 %copy-start = (bf16[1024,1024]{1,0:T(8,128)(2,1)S(1)}, bf16[1024,1024]{1,0:T(8,128)(2,1)}, u32[]{:S(2)}) copy-start(bf16[1024,1024]{1,0:T(8,128)(2,1)} %param.13) | copy-start | bytes 6291460
  0.6 8.4 %collective-permute-start.4 = (s32[8,128]{1,0:T(8,128)}, s32[8,128]{1,0:T(8,128)S(1)}, u32[]{:S(2)}, u32[]{:S(2)}) collective-permute-start(s32[8,128]{1,0:T(8,128)} %bitcast.37), channel_id=1, source_target_pairs={{0,4},{4,0},{8,12},{12,8},{16,20},{20,16},{24,28},{28,24},{1,5},{5... | collective-permute-start | bytes 12296 | tf_op jit(solution)/shard_map/ppermute | solution.py:37
  1.2 16.1 %collective-permute-start.3 = (bf16[128,2048]{1,0:T(8,128)(2,1)}, bf16[128,2048]{1,0:T(8,128)(2,1)S(1)}, u32[]{:S(2)}, u32[]{:S(2)}) collective-permute-start(bf16[128,2048]{1,0:T(8,128)(2,1)} %refs_1_.5), channel_id=1, source_target_pairs={{0,4},{4,0},{8,12},{12,8},{16,20},{20,16},{24,28},{28,24},{1,5},{5... | collective-permute-start | bytes 1572872 | tf_op jit(solution)/shard_map/ppermute | solution.py:37
  2.4 6.7 %copy-start.5 = (s32[128,8]{0,1:T(8,128)S(1)}, s32[128,8]{0,1:T(8,128)}, u32[]{:S(2)}) copy-start(s32[128,8]{0,1:T(8,128)} %param.9) | copy-start | bytes 12292
  3.4 19.1 %collective-permute-start = (bf16[64,1024]{1,0:T(8,128)(2,1)S(1)}, bf16[64,1024]{1,0:T(8,128)(2,1)S(1)}, u32[]{:S(2)}, u32[]{:S(2)}) collective-permute-start(bf16[64,1024]{1,0:T(8,128)(2,1)S(1)} %get-tuple-element.50), channel_id=1, source_target_pairs={{0,1},{1,0},{2,3},{3,2},{4,5},{5,4},{6,7},{7,6},{8,9},{9,8},{10,11... | collective-permute-start | bytes 393224 | tf_op jit(solution)/shard_map/ppermute | solution.py:37
  6.5 16.1 %collective-permute-start.1 = (bf16[64,1024]{1,0:T(8,128)(2,1)S(1)}, bf16[64,1024]{1,0:T(8,128)(2,1)S(1)}, u32[]{:S(2)}, u32[]{:S(2)}) collective-permute-start(bf16[64,1024]{1,0:T(8,128)(2,1)S(1)} %get-tuple-element.51), channel_id=1, source_target_pairs={{0,2},{1,3},{2,0},{3,1},{4,6},{5,7},{6,4},{7,5},{8,10},{9,11},{10,... | collective-permute-start | bytes 393224 | tf_op jit(solution)/shard_map/ppermute | solution.py:37
  9.1 13.5 %collective-permute-start.2 = (bf16[64,1024]{1,0:T(8,128)(2,1)S(1)}, bf16[64,1024]{1,0:T(8,128)(2,1)S(1)}, u32[]{:S(2)}, u32[]{:S(2)}) collective-permute-start(bf16[64,1024]{1,0:T(8,128)(2,1)S(1)} %get-tuple-element.52), channel_id=1, source_target_pairs={{0,3},{1,2},{2,1},{3,0},{4,7},{5,6},{6,5},{7,4},{8,11},{9,10},{10,... | collective-permute-start | bytes 393224 | tf_op jit(solution)/shard_map/ppermute | solution.py:37
  9.1 2.2 %copy-start.1 = (bf16[1024,2048]{1,0:T(8,128)(2,1)S(1)}, bf16[1024,2048]{1,0:T(8,128)(2,1)}, u32[]{:S(2)}) copy-start(bf16[1024,2048]{1,0:T(8,128)(2,1)} %refs_1_.4) | copy-start | bytes 12582916
  13.5 3.3 %copy-start.7 = (bf16[256,1024]{1,0:T(8,128)(2,1)S(1)}, bf16[256,1024]{1,0:T(8,128)(2,1)}, u32[]{:S(2)}) copy-start(bf16[256,1024]{1,0:T(8,128)(2,1)} %param.14) | copy-start | bytes 1572868
  23.2 2.0 %collective-permute-start.5 = (bf16[256,1024]{1,0:T(8,128)(2,1)S(1)}, bf16[256,1024]{1,0:T(8,128)(2,1)S(1)}, u32[]{:S(2)}, u32[]{:S(2)}) collective-permute-start(bf16[256,1024]{1,0:T(8,128)(2,1)S(1)} %shard_map.147.refs_2_.refs_1_), channel_id=1, source_target_pairs={{0,4},{4,0},{8,12},{12,8},{16,20},{20,16},{24,28},{28,24},{1,5},{5... | collective-permute-start | bytes 1572872 | tf_op jit(solution)/shard_map/ppermute | solution.py:37
  24.5 12.3 %collective-permute-start.7 = (bf16[128,1024]{1,0:T(8,128)(2,1)S(1)}, bf16[128,1024]{1,0:T(8,128)(2,1)S(1)}, u32[]{:S(2)}, u32[]{:S(2)}) collective-permute-start(bf16[128,1024]{1,0:T(8,128)(2,1)S(1)} %get-tuple-element.108), channel_id=1, source_target_pairs={{0,4},{4,0},{8,12},{12,8},{16,20},{20,16},{24,28},{28,24},{1,5},{5... | collective-permute-start | bytes 786440 | tf_op jit(solution)/shard_map/ppermute | solution.py:37
  28.4 5.7 %collective-permute-start.6 = (bf16[512,1024]{1,0:T(8,128)(2,1)S(1)}, bf16[512,1024]{1,0:T(8,128)(2,1)S(1)}, u32[]{:S(2)}, u32[]{:S(2)}) collective-permute-start(bf16[512,1024]{1,0:T(8,128)(2,1)S(1)} %get-tuple-element.114), channel_id=1, source_target_pairs={{0,4},{4,0},{8,12},{12,8},{16,20},{20,16},{24,28},{28,24},{1,5},{5... | collective-permute-start | bytes 3145736 | tf_op jit(solution)/shard_map/ppermute | solution.py:37
  29.3 20.5 %collective-permute-start.10 = (bf16[512,1024]{1,0:T(8,128)(2,1)S(1)}, bf16[512,1024]{1,0:T(8,128)(2,1)S(1)}, u32[]{:S(2)}, u32[]{:S(2)}) collective-permute-start(bf16[512,1024]{1,0:T(8,128)(2,1)S(1)} %convolution_convert_fusion.3.refs_2_), channel_id=1, source_target_pairs={{0,8},{4,20},{8,0},{12,28},{16,24},{20,4},{24,16},{28,12},{1,9},{5... | collective-permute-start | bytes 3145736 | tf_op jit(solution)/shard_map/ppermute | solution.py:37
  31.8 25.5 %collective-permute-start.12 = (bf16[512,1024]{1,0:T(8,128)(2,1)S(1)}, bf16[512,1024]{1,0:T(8,128)(2,1)S(1)}, u32[]{:S(2)}, u32[]{:S(2)}) collective-permute-start(bf16[512,1024]{1,0:T(8,128)(2,1)S(1)} %convolution_convert_fusion.2.refs_3_), channel_id=1, source_target_pairs={{0,1},{1,0},{2,3},{3,2},{4,5},{5,4},{6,7},{7,6},{8,9},{9,8},{10,11... | collective-permute-start | bytes 3145736 | tf_op jit(solution)/shard_map/ppermute | solution.py:37
  37.4 10.0 %collective-permute-start.8 = (bf16[128,1152]{1,0:T(8,128)(2,1)S(1)}, bf16[128,1152]{1,0:T(8,128)(2,1)S(1)}, u32[]{:S(2)}, u32[]{:S(2)}) collective-permute-start(bf16[128,1152]{1,0:T(8,128)(2,1)S(1)} %get-tuple-element.61), channel_id=1, source_target_pairs={{0,8},{4,20},{8,0},{12,28},{16,24},{20,4},{24,16},{28,12},{1,9},{5... | collective-permute-start | bytes 884744 | tf_op jit(solution)/shard_map/ppermute | solution.py:37
  40.3 23.0 %collective-permute-start.14 = (bf16[256,1024]{1,0:T(8,128)(2,1)S(1)}, bf16[256,1024]{1,0:T(8,128)(2,1)S(1)}, u32[]{:S(2)}, u32[]{:S(2)}) collective-permute-start(bf16[256,1024]{1,0:T(8,128)(2,1)S(1)} %get-tuple-element.67), channel_id=1, source_target_pairs={{0,8},{4,20},{8,0},{12,28},{16,24},{20,4},{24,16},{28,12},{1,9},{5... | collective-permute-start | bytes 1572872 | tf_op jit(solution)/shard_map/ppermute | solution.py:37
  41.9 6.1 %copy-start.4 = (bf16[128,2048]{1,0:T(8,128)(2,1)}, bf16[128,2048]{1,0:T(8,128)(2,1)S(1)}, u32[]{:S(2)}) copy-start(bf16[128,2048]{1,0:T(8,128)(2,1)S(1)} %pad_maximum_fusion.refs_7_) | copy-start | bytes 1572868
  48.0 6.0 %collective-permute-start.9 = (bf16[64,1152]{1,0:T(8,128)(2,1)S(1)}, bf16[64,1152]{1,0:T(8,128)(2,1)S(1)}, u32[]{:S(2)}, u32[]{:S(2)}) collective-permute-start(bf16[64,1152]{1,0:T(8,128)(2,1)S(1)} %get-tuple-element.64), channel_id=1, source_target_pairs={{0,16},{4,12},{8,24},{12,4},{16,0},{20,28},{24,8},{28,20},{1,17},{... | collective-permute-start | bytes 442376 | tf_op jit(solution)/shard_map/ppermute | solution.py:37
  50.6 14.9 %collective-permute-start.17 = (bf16[256,1024]{1,0:T(8,128)(2,1)S(1)}, bf16[256,1024]{1,0:T(8,128)(2,1)S(1)}, u32[]{:S(2)}, u32[]{:S(2)}) collective-permute-start(bf16[256,1024]{1,0:T(8,128)(2,1)S(1)} %get-tuple-element.71), channel_id=1, source_target_pairs={{0,16},{4,12},{8,24},{12,4},{16,0},{20,28},{24,8},{28,20},{1,17},{... | collective-permute-start | bytes 1572872 | tf_op jit(solution)/shard_map/ppermute | solution.py:37
  54.6 5.7 %collective-permute-start.11 = (bf16[64,1152]{1,0:T(8,128)(2,1)S(1)}, bf16[64,1152]{1,0:T(8,128)(2,1)S(1)}, u32[]{:S(2)}, u32[]{:S(2)}) collective-permute-start(bf16[64,1152]{1,0:T(8,128)(2,1)S(1)} %shard_map.155.refs_3_.refs_1_), channel_id=1, source_target_pairs={{0,1},{1,0},{2,3},{3,2},{4,5},{5,4},{6,7},{7,6},{8,9},{9,8},{10,11... | collective-permute-start | bytes 442376 | tf_op jit(solution)/shard_map/ppermute | solution.py:37
  58.2 11.1 %collective-permute-start.16 = (bf16[256,1024]{1,0:T(8,128)(2,1)S(1)}, bf16[256,1024]{1,0:T(8,128)(2,1)S(1)}, u32[]{:S(2)}, u32[]{:S(2)}) collective-permute-start(bf16[256,1024]{1,0:T(8,128)(2,1)S(1)} %get-tuple-element.70), channel_id=1, source_target_pairs={{0,8},{4,20},{8,0},{12,28},{16,24},{20,4},{24,16},{28,12},{1,9},{5... | collective-permute-start | bytes 1572872 | tf_op jit(solution)/shard_map/ppermute | solution.py:37
  60.8 10.2 %collective-permute-start.13 = (bf16[64,1152]{1,0:T(8,128)(2,1)S(1)}, bf16[64,1152]{1,0:T(8,128)(2,1)S(1)}, u32[]{:S(2)}, u32[]{:S(2)}) collective-permute-start(bf16[64,1152]{1,0:T(8,128)(2,1)S(1)} %shard_map.157.refs_3_.refs_1_), channel_id=1, source_target_pairs={{0,2},{1,3},{2,0},{3,1},{4,6},{5,7},{6,4},{7,5},{8,10},{9,11},{10,... | collective-permute-start | bytes 442376 | tf_op jit(solution)/shard_map/ppermute | solution.py:37
  64.0 6.4 %collective-permute-start.15 = (bf16[128,1024]{1,0:T(8,128)(2,1)S(1)}, bf16[128,1024]{1,0:T(8,128)(2,1)S(1)}, u32[]{:S(2)}, u32[]{:S(2)}) collective-permute-start(bf16[128,1024]{1,0:T(8,128)(2,1)S(1)} %get-tuple-element.69), channel_id=1, source_target_pairs={{0,16},{4,12},{8,24},{12,4},{16,0},{20,28},{24,8},{28,20},{1,17},{... | collective-permute-start | bytes 786440 | tf_op jit(solution)/shard_map/ppermute | solution.py:37
  66.1 13.3 %collective-permute-start.21 = (bf16[128,1024]{1,0:T(8,128)(2,1)S(1)}, bf16[128,1024]{1,0:T(8,128)(2,1)S(1)}, u32[]{:S(2)}, u32[]{:S(2)}) collective-permute-start(bf16[128,1024]{1,0:T(8,128)(2,1)S(1)} %get-tuple-element.77), channel_id=1, source_target_pairs={{0,1},{1,0},{2,3},{3,2},{4,5},{5,4},{6,7},{7,6},{8,9},{9,8},{10,11... | collective-permute-start | bytes 786440 | tf_op jit(solution)/shard_map/ppermute | solution.py:37
  69.9 6.4 %collective-permute-start.19 = (bf16[128,1024]{1,0:T(8,128)(2,1)S(1)}, bf16[128,1024]{1,0:T(8,128)(2,1)S(1)}, u32[]{:S(2)}, u32[]{:S(2)}) collective-permute-start(bf16[128,1024]{1,0:T(8,128)(2,1)S(1)} %get-tuple-element.75), channel_id=1, source_target_pairs={{0,16},{4,12},{8,24},{12,4},{16,0},{20,28},{24,8},{28,20},{1,17},{... | collective-permute-start | bytes 786440 | tf_op jit(solution)/shard_map/ppermute | solution.py:37
  71.7 6.3 %collective-permute-start.18 = (bf16[64,1152]{1,0:T(8,128)(2,1)S(1)}, bf16[64,1152]{1,0:T(8,128)(2,1)S(1)}, u32[]{:S(2)}, u32[]{:S(2)}) collective-permute-start(bf16[64,1152]{1,0:T(8,128)(2,1)S(1)} %shard_map.162.refs_3_.refs_1_), channel_id=1, source_target_pairs={{0,16},{4,12},{8,24},{12,4},{16,0},{20,28},{24,8},{28,20},{1,17},{... | collective-permute-start | bytes 442376 | tf_op jit(solution)/shard_map/ppermute | solution.py:37
  73.3 5.5 %collective-permute-start.22 = (bf16[64,1024]{1,0:T(8,128)(2,1)S(1)}, bf16[64,1024]{1,0:T(8,128)(2,1)S(1)}, u32[]{:S(2)}, u32[]{:S(2)}) collective-permute-start(bf16[64,1024]{1,0:T(8,128)(2,1)S(1)} %get-tuple-element.78), channel_id=1, source_target_pairs={{0,1},{1,0},{2,3},{3,2},{4,5},{5,4},{6,7},{7,6},{8,9},{9,8},{10,11... | collective-permute-start | bytes 393224 | tf_op jit(solution)/shard_map/ppermute | solution.py:37
  78.5 10.1 %collective-permute-start.20 = (bf16[128,1152]{1,0:T(8,128)(2,1)S(1)}, bf16[128,1152]{1,0:T(8,128)(2,1)S(1)}, u32[]{:S(2)}, u32[]{:S(2)}) collective-permute-start(bf16[128,1152]{1,0:T(8,128)(2,1)S(1)} %shard_map.164.refs_3_.refs_1_), channel_id=1, source_target_pairs={{0,8},{4,20},{8,0},{12,28},{16,24},{20,4},{24,16},{28,12},{1,9},{5... | collective-permute-start | bytes 884744 | tf_op jit(solution)/shard_map/ppermute | solution.py:37
  80.1 15.3 %collective-permute-start.24 = (bf16[64,1024]{1,0:T(8,128)(2,1)S(1)}, bf16[64,1024]{1,0:T(8,128)(2,1)S(1)}, u32[]{:S(2)}, u32[]{:S(2)}) collective-permute-start(bf16[64,1024]{1,0:T(8,128)(2,1)S(1)} %get-tuple-element.81), channel_id=1, source_target_pairs={{0,2},{1,3},{2,0},{3,1},{4,6},{5,7},{6,4},{7,5},{8,10},{9,11},{10,... | collective-permute-start | bytes 393224 | tf_op jit(solution)/shard_map/ppermute | solution.py:37
  85.7 9.7 %collective-permute-start.25 = (bf16[64,1024]{1,0:T(8,128)(2,1)S(1)}, bf16[64,1024]{1,0:T(8,128)(2,1)S(1)}, u32[]{:S(2)}, u32[]{:S(2)}) collective-permute-start(bf16[64,1024]{1,0:T(8,128)(2,1)S(1)} %get-tuple-element.82), channel_id=1, source_target_pairs={{0,2},{1,3},{2,0},{3,1},{4,6},{5,7},{6,4},{7,5},{8,10},{9,11},{10,... | collective-permute-start | bytes 393224 | tf_op jit(solution)/shard_map/ppermute | solution.py:37
  85.8 9.6 %collective-permute-start.26 = (bf16[32,1024]{1,0:T(8,128)(2,1)S(1)}, bf16[32,1024]{1,0:T(8,128)(2,1)S(1)}, u32[]{:S(2)}, u32[]{:S(2)}) collective-permute-start(bf16[32,1024]{1,0:T(8,128)(2,1)S(1)} %get-tuple-element.83), channel_id=1, source_target_pairs={{0,2},{1,3},{2,0},{3,1},{4,6},{5,7},{6,4},{7,5},{8,10},{9,11},{10,... | collective-permute-start | bytes 196616 | tf_op jit(solution)/shard_map/ppermute | solution.py:37
  89.2 7.5 %collective-permute-start.23 = (bf16[256,1152]{1,0:T(8,128)(2,1)S(1)}, bf16[256,1152]{1,0:T(8,128)(2,1)S(1)}, u32[]{:S(2)}, u32[]{:S(2)}) collective-permute-start(bf16[256,1152]{1,0:T(8,128)(2,1)S(1)} %shard_map.167.refs_7_.refs_1_.refs_3_), channel_id=1, source_target_pairs={{0,4},{4,0},{8,12},{12,8},{16,20},{20,16},{24,28},{28,24},{1,5},{5... | collective-permute-start | bytes 1769480 | tf_op jit(solution)/shard_map/ppermute | solution.py:37
  (5 other events, 7.2 us)

commit v3 on v0

--- a/solution.py
+++ b/solution.py
@@ -10,6 +10,8 @@
 BF = jnp.bfloat16
 F32 = jnp.float32
 ROOM = 8 * 1024 * 1024
+PARTS = 3
+ORDER = "TDTUPTDUPTFTT"
 STEP = 6 * 1000 * 1000 * 1000
 VMEM = pltpu.VMEM
 
@@ -165,31 +167,35 @@
             up_here[:, first : first + half] = value[:, z * half : (z + 1) * half]
 
 
-def pick_down_body(tp_count, share_count, numbers, down, down_here, downs, ready):
-    chunk = downs.shape[1]
+def pick_down_body(tp_count, share_count, numbers, down, down_here, ready):
+    chunk = down_here.shape[0] // share_count
     unit = chunk // tp_count
     half = chunk // 2
     copies = []
     for n in range(share_count):
-        at = pl.ds(pl.multiple_of(numbers[tp_count + n] * chunk, chunk), chunk)
-        copies.append(pltpu.make_async_copy(down.at[at, :], downs.at[n], ready.at[n]))
-        copies[-1].start()
-    for n in range(share_count):
-        copies[n].wait()
         for i, m in enumerate(sent_order(tp_count)):
             z, place = i // (tp_count // 2), i % (tp_count // 2)
             first = (z * share_count + n) * half + place * unit
-            start = pl.multiple_of(numbers[m] * unit, unit)
-            down_here[first : first + unit, :] = downs[n, pl.ds(start, unit), :]
+            start = numbers[tp_count + n] * chunk + numbers[m] * unit
+            source = down.at[pl.ds(pl.multiple_of(start, unit), unit), :]
+            target = down_here.at[pl.ds(first, unit), :]
+            copies.append(pltpu.make_async_copy(source, target, ready.at[n, i]))
+            copies[-1].start()
+    for copy in copies:
+        copy.wait()
 
 
 def split_body(tp_count, share, numbers, value, kept, sent):
     unit = share // tp_count
     half = kept.shape[0]
-    for n in range(value.shape[0] // share):
+    inner_shares = value.shape[0] // share // 2
+    inner_places = tp_count // 2
+    for n in range(2 * inner_shares):
         for i, m in enumerate(sent_order(tp_count)):
             at = pl.ds(n * share + pl.multiple_of(numbers[m] * unit, unit), unit)
-            place = n * share + i * unit
+            place = 2 * (n // inner_shares) + i // inner_places
+            place = place * inner_shares + n % inner_shares
+            place = (place * inner_places + i % inner_places) * unit
             target = kept if place < half else sent
             row = place % half
             target[row : row + unit, :] = value[at, :].astype(target.dtype)
@@ -232,34 +238,57 @@
     summed[...] = (kept[...].astype(F32) + arrived[...].astype(F32)).astype(summed.dtype)
 
 
-def stack_body(numbers, first, second, both):
+def stack_body(numbers, first, second, *parts):
     rows = first.shape[0]
-    both[:rows, :] = first[...]
-    both[rows:, :] = second[...]
-
-
-def sort_out_body(numbers, place, sort):
-    vocab = (sort.shape[0] - 16) // 2
-    row = lax.broadcasted_iota(jnp.int32, (vocab, sort.shape[1]), 0)
-    sort[:vocab, :] = hot(row, place[:1, :])
-    sort[vocab : 2 * vocab, :] = hot(row, place[1:2, :])
-    sort[2 * vocab :, :] = place[2:, :].astype(F32).astype(BF)
-
-
-def tables_body(numbers, first, second, first_gain, second_gain, sort, glob, local, gain):
-    half = first.shape[0]
-    vocab = glob.shape[0]
-    tall = sort[: 2 * vocab]
-    value = times(tall[:, :half], first[...]) + times(tall[:, half:], second[...])
-    glob[...] = value[:vocab]
-    local[...] = value[vocab:]
-
-    @pl.when(pl.program_id(0) == 0)
-    def _():
-        flat = sort[2 * vocab :]
-        value = times(flat[:, :half], first_gain[...])
-        value = value + times(flat[:, half:], second_gain[...])
-        gain[...] = value[: gain.shape[0]]
+    column = 0
+    for part in parts:
+        at = slice(column, column + part.shape[1])
+        part[:rows, :] = first[:, at]
+        part[rows:, :] = second[:, at]
+        column += part.shape[1]
+
+
+def tables_body(share_count, first_share, height, count, numbers, *refs):
+    sides = (refs[:count], refs[count : 2 * count])
+    glob, local, gain = refs[2 * count :]
+    width = glob.shape[1]
+    gains = None
+    for side, parts in enumerate(sides):
+        for n in range(share_count):
+            start = numbers[first_share + side * share_count + n] * height
+            at = pl.ds(pl.multiple_of(start, height), height)
+            row = 2 * n * height
+            column = 0
+            for part in parts:
+                inside = min(part.shape[1], width - column)
+                to = slice(column, column + inside)
+                glob[at, to] = part[row : row + height, :inside].astype(F32)
+                local[at, to] = part[row + height : row + 2 * height, :inside].astype(F32)
+                column += inside
+            term = parts[-1][row : row + 16, parts[-1].shape[1] - 128 :].astype(F32)
+            gains = term if gains is None else gains + term
+    gain[...] = gains[: gain.shape[0]]
+
+
+def last_body(numbers, *refs):
+    keep, send = refs[-2:]
+    row = 0
+    for i in range(len(refs) // 2 - 1):
+        kept, arrived = refs[2 * i], refs[2 * i + 1]
+        half = kept.shape[0] // 2
+        at = slice(row, row + half)
+        for target, part in ((keep, slice(0, half)), (send, slice(half, 2 * half))):
+            value = kept[part, :].astype(F32) + arrived[part, :].astype(F32)
+            target[at, :] = value.astype(target.dtype)
+        row += half
+
+
+def finals_body(numbers, kept, arrived, *wholes):
+    row = 0
+    for whole in wholes:
+        at = slice(row, row + whole.shape[0])
+        whole[...] = kept[at, :].astype(F32) + arrived[at, :].astype(F32)
+        row += whole.shape[0]
 
 
 def on_device(
@@ -344,8 +373,10 @@
         [like(own * part, width, BF)] * tp_count,
         [out_grad],
         [],
+        flops=STEP,
     )
     blocks = [swap(b, "tp", (m,)) if m else b for m, b in enumerate(blocks)]
+    far = pl.BlockSpec(memory_space=pltpu.HBM)
     prev_hot, prev_here, own_hot = call(
         functools.partial(hots_body, own, tp_count, share_count, height, core_at),
         [like(2 * rows, vocab, BF), like(2 * rows, vocab // 2, BF), like(rows, vocab, BF)],
@@ -366,7 +397,6 @@
     scale = lax.rsqrt(jnp.mean(u_rows * u_rows, axis=1, keepdims=True) + 1e-05)
     normed = u_rows * scale
     r_rows = (normed * norm_gain).astype(BF)
-    far = pl.BlockSpec(memory_space=pltpu.HBM)
     (up_here,) = call(
         functools.partial(pick_up_body, tp_count, share_count),
         [like(width, hidden // 2, BF)],
@@ -386,7 +416,7 @@
         [down_weight],
         [h_rows],
         in_specs=[far],
-        scratch=[VMEM((share_count, chunk, width), BF), pltpu.SemaphoreType.DMA((share_count,))],
+        scratch=[pltpu.SemaphoreType.DMA((share_count, tp_count))],
     )
     strip = chunk // 2
     h_rows = jnp.concatenate(
@@ -402,7 +432,7 @@
         functools.partial(join_body, part, own, tp_count),
         [like(rows, width, BF)],
         blocks,
-        [h_rows, down_here],
+        [h_rows],
     )
     grad_other = core_swap(grad_own)
     own_hot = gate(own_hot, [grad_own])
@@ -431,19 +461,16 @@
         def __init__(self, kept, sent, steps):
             self.kept, self.steps, self.at = kept, steps, 0
             self.arrived = go(sent, self.steps[0])
-            self.left = len(self.steps)
+            self.left = len(self.steps) - 2
 
         def next(self, after):
             self.at += 1
             self.left -= 1
             rows, columns = self.kept.shape
             ins = [self.kept, self.arrived]
-            if self.left:
-                outs = [like(rows // 2, columns, self.kept.dtype)] * 2
-                self.kept, sent = step(add_body, outs, ins, after)
-                self.arrived = go(sent, self.steps[self.at])
-            else:
-                (self.kept,) = step(sum_body, [like(rows, columns, F32)], ins, after)
+            outs = [like(rows // 2, columns, self.kept.dtype)] * 2
+            self.kept, sent = step(add_body, outs, ins, after)
+            self.arrived = go(sent, self.steps[self.at])
             return self.kept
 
     class Table:
@@ -465,14 +492,19 @@
             if last == "half" and kind == "half":
                 self.kept, sent = step(add_body, [like(rows // 2, columns, BF)] * 2, ins, after)
             elif last == "join":
-                (self.kept,) = step(stack_body, [like(2 * rows, columns, BF)], ins, after)
-                sent = self.kept
+                cut = columns // PARTS if hop is None else columns
+                outs = [like(2 * rows, cut, BF)] * (columns // cut)
+                self.parts = step(stack_body, outs, ins, after)
+                self.kept = sent = self.parts[0]
             else:
                 (self.kept,) = step(sum_body, [like(rows, columns, BF)], ins, after)
                 sent = self.kept
             self.at += 1
             self.left -= 1
-            self.arrived = core_swap(sent) if hop is None else go(sent, hop)
+            if hop is None:
+                self.arrived = [core_swap(part) for part in self.parts]
+            else:
+                self.arrived = go(sent, hop)
             return self.kept
 
     dh_rows = outer(out_rows, down_here)
@@ -516,62 +548,64 @@
         [value],
         [table.kept],
     )
-    proj = Chain(kept, sent, seq_steps + tp_steps)
+    proj = Chain(kept, sent, seq_steps[:1] + tp_steps[:1] + seq_steps[1:] + tp_steps[1:])
     du_own = lax.dynamic_slice_in_dim(du_rows, core * rows, rows, 0)
     back = outer(du_own, proj_weight).astype(BF)
     glob_out_grad = jnp.concatenate(
         [back[j * patches : (j + 1) * patches] for j in range(own)], axis=1
     )
 
-    all_numbers = jnp.stack(shares + others)
-    inside = jnp.arange(size)[None, :]
-    own_row = all_numbers[:, None] * height + inside
-    place = jnp.stack(
-        [
-            jnp.where(inside < height, own_row, -1).reshape(-1),
-            jnp.where(inside >= height, own_row - height, -1).reshape(-1),
-        ]
-        + [
-            jnp.broadcast_to(inside == line, own_row.shape).reshape(-1).astype(jnp.int32)
-            for line in range(16)
-        ]
-    ).astype(jnp.int32)
-    count = seq_count * size
-    (sort,) = call(
-        sort_out_body, [like(2 * vocab + 16, count, BF)], [place], [table.kept]
-    )
-    last = [up.kept, proj.kept, table.kept, down.kept, glob_out_grad, sort]
+    last = [up.kept, proj.kept, table.kept, down.kept, glob_out_grad]
     names = {"T": table, "D": down, "U": up, "P": proj}
-    queue = [names[c] for c in "TDTUTPDUPTUTPDTPUTD"]
-    for chain in queue + [table, proj, down, up] * 16:
-        if chain.left:
+    ends = [down, up, proj]
+    heights = [c.kept.shape[0] >> c.left + 1 for c in ends]
+    merged = None
+
+    def last_sums(after):
+        kind = down.kept.dtype if down.kept.dtype == proj.kept.dtype else F32
+        keep, sent = step(
+            last_body,
+            [like(sum(heights), width, kind)] * 2,
+            [x for c in ends for x in (c.kept, c.arrived)],
+            after,
+        )
+        return keep, go(sent, tp_steps[-1])
+
+    for name in ORDER:
+        chain = names.get(name)
+        if chain is not None and chain.left:
             last = [chain.next(last)]
-
-    parts = 4
-    wide = width // parts
-
-    def columns(height):
-        return pl.BlockSpec((height, wide), lambda n, s: (0, n))
+        elif name == "F":
+            while any(c.left for c in ends):
+                for c in ends:
+                    if c.left:
+                        last = [c.next(last)]
+            merged = last_sums(last)
+            last = [merged[0]]
+    while table.left:
+        last = [table.next(last)]
 
     lines = width // 128
-    beside = pl.BlockSpec((count // 2, 128), lambda n, s: (0, lines))
     emb_global_grad, emb_local_grad, gain_grad = call(
-        tables_body,
+        functools.partial(tables_body, share_count, tp_count, height, PARTS),
         [like(vocab, width, F32), like(vocab, width, F32), like(lines, 128, F32)],
-        [table.kept, table.arrived, table.kept, table.arrived, sort],
+        [*table.parts, *table.arrived],
         last,
-        grid=parts,
-        in_specs=[columns(count // 2), columns(count // 2), beside, beside, None],
-        out_specs=[columns(vocab), columns(vocab), None],
+    )
+    down_grad, up_grad, proj_grad = call(
+        finals_body,
+        [like(h, width, F32) for h in heights],
+        [*merged],
+        [gain_grad],
     )
     return (
         glob_out_grad,
         emb_global_grad,
         emb_local_grad,
         gain_grad.reshape(width),
-        proj.kept.T,
-        up.kept.T,
-        down.kept,
+        proj_grad.T,
+        up_grad.T,
+        down_grad,
     )
 
 

time: 108 us -> 100 us (0.926)
  waiting for transfers between devices: 21.9 us -> 27.6 us
  starting transfers between devices: 33.3 us -> 27.6 us
  local copies, waits for them, and re-layouts: 7.76 us -> 3.19 us
  Pallas kernels: 28.6 us -> 26 us
    ppermute x27, starting transfers between devices: 33.3 us -> 27.6 us  [swap(): return lax.ppermute(value, axis, pairs)]
    ppermute x27, waiting for transfers between devices: 21.9 us -> 27.6 us  [swap(): return lax.ppermute(value, axis, pairs)]
    unnamed x30 -> x26, local copies, waits for them, and re-layouts: 5.58 us -> 2.63 us
    pallas_call x31 -> x26, Pallas kernels: 28.6 us -> 26 us  [run(): pl.pallas_call(kernel, out_shape=tuple(outs), grid_spec=pltpu.PrefetchSca...]
    convert_element_type x16 -> x0, local copies, waits for them, and re-layouts: 1.26 us -> none  [on_device(): jnp.broadcast_to(inside == line, own_row.shape).reshape(-1)]
  transfers between devices with their start and end apart: 27 -> 27, of which waited for: 10 -> 14; matrix products, arithmetic and copies ran while one was open for 16% -> 15% of each run, Pallas kernels for 20% -> 22%
where the time goes in v3:
time: 100 us; the launch traced here: 99.9 us
  starting transfers between devices  27.6 us (28%)
  waiting for transfers between devices  27.6 us (28%)
  Pallas kernels  26 us (26%)
  matrix products  12.7 us (13%)
  local copies, waits for them, and re-layouts  3.19 us (3%)
  other arithmetic  1.78 us (2%)
  between operations  1.17 us (1%)
    ppermute x27, starting transfers between devices, swap(): return lax.ppermute(value, axis, pairs)  27.6 us
    ppermute x27, waiting for transfers between devices, swap(): return lax.ppermute(value, axis, pairs)  27.6 us
    pallas_call x26, Pallas kernels, run(): pl.pallas_call(kernel, out_shape=tuple(outs), grid_spec=pltpu.PrefetchSca...  26 us
    dot_general x3, matrix products, times(): return jnp.dot(left, right, preferred_element_type=F32)  4.7 us
    dot_general x8, matrix products, inner(): lax.dot_general(left, right, (((0,), (0,)), ((), ())), preferred_element_...  4.6 us
    dot_general x3, matrix products, outer(): lax.dot_general(left, right, (((1,), (1,)), ((), ())), preferred_element_...  3.38 us
    unnamed x26, local copies, waits for them, and re-layouts  2.63 us
  transfers between devices with their start and end apart: 27, of which 14 were waited for; matrix products, arithmetic and copies ran while one was open for 15% of the time, Pallas kernels for 22%

profile of v3, /device:TPU:0, one launch (start us, length us, event | category | flops | bytes accessed | tf_op | source)
XLA Modules:
  0.0 99.9 jit_solution(4884693939444415984)
XLA Ops:
  1.3 1.0 %copy-done.7 = bf16[256,1024]{1,0:T(8,128)(2,1)S(1)} copy-done((bf16[256,1024]{1,0:T(8,128)(2,1)S(1)}, bf16[256,1024]{1,0:T(8,128)(2,1)}, u32[]{:S(2)}) %copy-start.7) | copy-done | bytes 524312
  2.4 1.7 %shard_map.144 = (bf16[64,1024]{1,0:T(8,128)(2,1)S(1)}, bf16[64,1024]{1,0:T(8,128)(2,1)}, bf16[64,1024]{1,0:T(8,128)(2,1)}, bf16[64,1024]{1,0:T(8,128)(2,1)}) custom-call(s32[13]{0:T(128)S(1)} %stack.55.refs_0_, bf16[256,1024]{1,0:T(8,128)(2,1)S(1)} %copy-done.7), custom_call_target="tpu_custom_call" | custom-call | flops 6000000000 | tf_op jit(solution)/shard_map/pallas_call | solution.py:60
  4.1 3.0 %collective-permute-start = (bf16[64,1024]{1,0:T(8,128)(2,1)}, bf16[64,1024]{1,0:T(8,128)(2,1)S(1)}, u32[]{:S(2)}, u32[]{:S(2)}) collective-permute-start(bf16[64,1024]{1,0:T(8,128)(2,1)} %get-tuple-element.46), channel_id=1, source_target_pairs={{0,1},{1,0},{2,3},{3,2},{4,5},{5,4},{6,7},{7,6},{8,9},{9,8},{10,11... | collective-permute-start | bytes 393224 | tf_op jit(solution)/shard_map/ppermute | solution.py:38
  7.1 2.6 %collective-permute-start.1 = (bf16[64,1024]{1,0:T(8,128)(2,1)}, bf16[64,1024]{1,0:T(8,128)(2,1)S(1)}, u32[]{:S(2)}, u32[]{:S(2)}) collective-permute-start(bf16[64,1024]{1,0:T(8,128)(2,1)} %get-tuple-element.47), channel_id=1, source_target_pairs={{0,2},{1,3},{2,0},{3,1},{4,6},{5,7},{6,4},{7,5},{8,10},{9,11},{10,... | collective-permute-start | bytes 393224 | tf_op jit(solution)/shard_map/ppermute | solution.py:38
  10.6 1.5 %fusion.39 = f32[512,1024]{1,0:T(8,128)S(1)} fusion(bf16[512,256]{1,0:T(8,128)(2,1)S(1)} %get-tuple-element.49.refs_3_, bf16[256,1024]{1,0:T(8,128)(2,1)} %param.14), kind=kOutput, calls=%fused_computation.71 | convolution fusion | flops 268435456 | bytes 2883584 | tf_op jit(solution)/shard_map/dot_general | solution.py:32
  12.8 1.4 %multiply_reduce_fusion.2 = (f32[512]{0:T(512)S(1)}, f32[512,1024]{1,0:T(8,128)S(1)}) fusion(f32[512,1024]{1,0:T(8,128)S(1)} %fusion.39, bf16[512,1024]{1,0:T(8,128)(2,1)S(1)} %shard_map.146, bf16[1024,1024]{1,0:T(8,128)(2,1)S(1)} %copy-done), kind=kOutput, calls=%fused_computation.9 | convolution fusion | flops 1075314176 | bytes 7342080 | tf_op jit(solution)/shard_map/dot_general | solution.py:32
  14.9 2.6 %shard_map.147 = bf16[1024,1024]{1,0:T(8,128)(2,1)S(1)} custom-call(s32[13]{0:T(128)S(1)} %stack.55.refs_0_, bf16[1024,2048]{1,0:T(8,128)(2,1)S(1)} %copy-done.1, bf16[512,1024]{1,0:T(8,128)(2,1)S(1)} %multiply_convert_fusion.3.refs_2_), custom_call_target="tpu_custom_call" | custom-call | tf_op jit(solution)/shard_map/pallas_call | solution.py:60
  17.6 1.8 %multiply_convert_fusion.1 = (bf16[512,1024]{1,0:T(8,128)(2,1)S(1)}, bf16[512,1024]{1,0:T(8,128)(2,1)S(1)}) fusion(bf16[512,1024]{1,0:T(8,128)(2,1)S(1)} %multiply_convert_fusion.3.refs_2_, bf16[1024,1024]{1,0:T(8,128)(2,1)S(1)} %shard_map.147), kind=kOutput, calls=%fused_computation.5 | convolution fusion | flops 1078984704 | bytes 5242880 | tf_op jit(solution)/shard_map/dot_general | solution.py:32
  20.2 1.8 %shard_map.148.refs_2_.refs_1_ = bf16[256,1024]{1,0:T(8,128)(2,1)S(1)} custom-call(s32[13]{0:T(128)S(1)} %stack.55.refs_0_, bf16[64,1024]{1,0:T(8,128)(2,1)S(1)} %get-tuple-element.45.refs_3_.refs_1_, bf16[64,1024]{1,0:T(8,128)(2,1)S(1)} %collective-permute-done.refs_2_, bf16[64,1024]{1,0:T(8,128)(2,1)S(1)} %collective-permute-done.1.refs_3_, ...), custom_call_target="tpu_custom_call" | custom-call | tf_op jit(solution)/shard_map/pallas_call | solution.py:60
  23.0 3.7 %shard_map.151 = bf16[1024,1024]{1,0:T(8,128)(2,1)S(1)} custom-call(s32[13]{0:T(128)S(1)} %stack.55.refs_0_, bf16[2048,1024]{1,0:T(8,128)(2,1)S(1)} %copy-done.2, bf16[512,1024]{1,0:T(8,128)(2,1)S(1)} %get-tuple-element.50.refs_2_), custom_call_target="tpu_custom_call" | custom-call | tf_op jit(solution)/shard_map/pallas_call | solution.py:60
  28.2 1.3 %multiply_convert_fusion = bf16[512,1024]{1,0:T(8,128)(2,1)S(1)} fusion(bf16[512,1024]{1,0:T(8,128)(2,1)S(1)} %get-tuple-element.52, bf16[512,1024]{1,0:T(8,128)(2,1)S(1)} %shard_map.150, bf16[1024,1024]{1,0:T(8,128)(2,1)S(1)} %shard_map.151), kind=kOutput, calls=%fused_computation.4 | convolution fusion | flops 1075314688 | bytes 5242880 | tf_op jit(solution)/shard_map/dot_general | solution.py:26
  29.5 1.3 %fusion.38 = (bf16[512,1024]{1,0:T(8,128)(2,1)S(1)}, f32[512,1024]{1,0:T(8,128)S(1)}) fusion(bf16[512,1024]{1,0:T(8,128)(2,1)S(1)} %multiply_convert_fusion, bf16[1024,1024]{1,0:T(8,128)(2,1)S(1)} %shard_map.147), kind=kOutput, calls=%fused_computation.70 | convolution fusion | flops 1074266112 | bytes 6291456 | tf_op jit(solution)/shard_map/dot_general | solution.py:26
  31.6 1.6 %collective-permute-start.10 = (bf16[512,1024]{1,0:T(8,128)(2,1)S(1)}, bf16[512,1024]{1,0:T(8,128)(2,1)S(1)}, u32[]{:S(2)}, u32[]{:S(2)}) collective-permute-start(bf16[512,1024]{1,0:T(8,128)(2,1)S(1)} %convolution_convert_fusion.3.refs_2_), channel_id=1, source_target_pairs={{0,8},{4,20},{8,0},{12,28},{16,24},{20,4},{24,16},{28,12},{1,9},{5... | collective-permute-start | bytes 3145736 | tf_op jit(solution)/shard_map/ppermute | solution.py:38
  34.0 2.0 %collective-permute-start.13 = (bf16[512,1024]{1,0:T(8,128)(2,1)S(1)}, bf16[512,1024]{1,0:T(8,128)(2,1)S(1)}, u32[]{:S(2)}, u32[]{:S(2)}) collective-permute-start(bf16[512,1024]{1,0:T(8,128)(2,1)S(1)} %convolution_convert_fusion.2.refs_3_), channel_id=1, source_target_pairs={{0,1},{1,0},{2,3},{3,2},{4,5},{5,4},{6,7},{7,6},{8,9},{9,8},{10,11... | collective-permute-start | bytes 3145736 | tf_op jit(solution)/shard_map/ppermute | solution.py:38
  43.5 1.6 %collective-permute-start.12 = (bf16[256,1024]{1,0:T(8,128)(2,1)S(1)}, bf16[256,1024]{1,0:T(8,128)(2,1)S(1)}, u32[]{:S(2)}, u32[]{:S(2)}) collective-permute-start(bf16[256,1024]{1,0:T(8,128)(2,1)S(1)} %get-tuple-element.60), channel_id=1, source_target_pairs={{0,8},{4,20},{8,0},{12,28},{16,24},{20,4},{24,16},{28,12},{1,9},{5... | collective-permute-start | bytes 1572872 | tf_op jit(solution)/shard_map/ppermute | solution.py:38
  45.1 4.6 %collective-permute-done.8.refs_2_ = bf16[128,1152]{1,0:T(8,128)(2,1)S(1)} collective-permute-done((bf16[128,1152]{1,0:T(8,128)(2,1)S(1)}, bf16[128,1152]{1,0:T(8,128)(2,1)S(1)}, u32[]{:S(2)}, u32[]{:S(2)}) %collective-permute-start.8) | collective-permute-done | bytes 294944 | tf_op jit(solution)/shard_map/ppermute | solution.py:38
  50.3 1.7 %collective-permute-start.9 = (bf16[64,1152]{1,0:T(8,128)(2,1)S(1)}, bf16[64,1152]{1,0:T(8,128)(2,1)S(1)}, u32[]{:S(2)}, u32[]{:S(2)}) collective-permute-start(bf16[64,1152]{1,0:T(8,128)(2,1)S(1)} %get-tuple-element.58), channel_id=1, source_target_pairs={{0,16},{4,12},{8,24},{12,4},{16,0},{20,28},{24,8},{28,20},{1,17},{... | collective-permute-start | bytes 442376 | tf_op jit(solution)/shard_map/ppermute | solution.py:38
  53.2 3.1 %collective-permute-done.9.refs_2_ = bf16[64,1152]{1,0:T(8,128)(2,1)S(1)} collective-permute-done((bf16[64,1152]{1,0:T(8,128)(2,1)S(1)}, bf16[64,1152]{1,0:T(8,128)(2,1)S(1)}, u32[]{:S(2)}, u32[]{:S(2)}) %collective-permute-start.9) | collective-permute-done | bytes 147488 | tf_op jit(solution)/shard_map/ppermute | solution.py:38
  56.9 2.1 %collective-permute-start.11 = (bf16[64,1152]{1,0:T(8,128)(2,1)S(1)}, bf16[64,1152]{1,0:T(8,128)(2,1)S(1)}, u32[]{:S(2)}, u32[]{:S(2)}) collective-permute-start(bf16[64,1152]{1,0:T(8,128)(2,1)S(1)} %shard_map.157.refs_3_.refs_1_), channel_id=1, source_target_pairs={{0,1},{1,0},{2,3},{3,2},{4,5},{5,4},{6,7},{7,6},{8,9},{9,8},{10,11... | collective-permute-start | bytes 442376 | tf_op jit(solution)/shard_map/ppermute | solution.py:38
  60.4 1.0 collective-permute-start.16
  62.0 1.9 %collective-permute-start.15 = (bf16[128,1024]{1,0:T(8,128)(2,1)S(1)}, bf16[128,1024]{1,0:T(8,128)(2,1)S(1)}, u32[]{:S(2)}, u32[]{:S(2)}) collective-permute-start(bf16[128,1024]{1,0:T(8,128)(2,1)S(1)} %get-tuple-element.63), channel_id=1, source_target_pairs={{0,1},{1,0},{2,3},{3,2},{4,5},{5,4},{6,7},{7,6},{8,9},{9,8},{10,11... | collective-permute-start | bytes 786440 | tf_op jit(solution)/shard_map/ppermute | solution.py:38
  64.5 2.3 %collective-permute-start.14 = (bf16[64,1152]{1,0:T(8,128)(2,1)S(1)}, bf16[64,1152]{1,0:T(8,128)(2,1)S(1)}, u32[]{:S(2)}, u32[]{:S(2)}) collective-permute-start(bf16[64,1152]{1,0:T(8,128)(2,1)S(1)} %shard_map.160.refs_3_.refs_1_), channel_id=1, source_target_pairs={{0,2},{1,3},{2,0},{3,1},{4,6},{5,7},{6,4},{7,5},{8,10},{9,11},{10,... | collective-permute-start | bytes 442376 | tf_op jit(solution)/shard_map/ppermute | solution.py:38
  68.3 1.3 %collective-permute-done.16.refs_2_ = bf16[256,1024]{1,0:T(8,128)(2,1)S(1)} collective-permute-done((bf16[256,1024]{1,0:T(8,128)(2,1)S(1)}, bf16[256,1024]{1,0:T(8,128)(2,1)S(1)}, u32[]{:S(2)}, u32[]{:S(2)}) %collective-permute-start.16) | collective-permute-done | bytes 524320 | tf_op jit(solution)/shard_map/ppermute | solution.py:38
  70.3 1.0 %collective-permute-start.20 = (bf16[128,1024]{1,0:T(8,128)(2,1)S(1)}, bf16[128,1024]{1,0:T(8,128)(2,1)S(1)}, u32[]{:S(2)}, u32[]{:S(2)}) collective-permute-start(bf16[128,1024]{1,0:T(8,128)(2,1)S(1)} %get-tuple-element.70), channel_id=1, source_target_pairs={{0,16},{4,12},{8,24},{12,4},{16,0},{20,28},{24,8},{28,20},{1,17},{... | collective-permute-start | bytes 786440 | tf_op jit(solution)/shard_map/ppermute | solution.py:38
  71.3 3.2 %collective-permute-done.15.refs_2_ = bf16[128,1024]{1,0:T(8,128)(2,1)S(1)} collective-permute-done((bf16[128,1024]{1,0:T(8,128)(2,1)S(1)}, bf16[128,1024]{1,0:T(8,128)(2,1)S(1)}, u32[]{:S(2)}, u32[]{:S(2)}) %collective-permute-start.15) | collective-permute-done | bytes 262176 | tf_op jit(solution)/shard_map/ppermute | solution.py:38
  75.1 1.6 %collective-permute-start.21 = (bf16[64,1024]{1,0:T(8,128)(2,1)S(1)}, bf16[64,1024]{1,0:T(8,128)(2,1)S(1)}, u32[]{:S(2)}, u32[]{:S(2)}) collective-permute-start(bf16[64,1024]{1,0:T(8,128)(2,1)S(1)} %get-tuple-element.71), channel_id=1, source_target_pairs={{0,16},{4,12},{8,24},{12,4},{16,0},{20,28},{24,8},{28,20},{1,17},{... | collective-permute-start | bytes 393224 | tf_op jit(solution)/shard_map/ppermute | solution.py:38
  78.1 2.0 %collective-permute-done.21.refs_6_ = bf16[64,1024]{1,0:T(8,128)(2,1)S(1)} collective-permute-done((bf16[64,1024]{1,0:T(8,128)(2,1)S(1)}, bf16[64,1024]{1,0:T(8,128)(2,1)S(1)}, u32[]{:S(2)}, u32[]{:S(2)}) %collective-permute-start.21) | collective-permute-done | bytes 131104 | tf_op jit(solution)/shard_map/ppermute | solution.py:38
  80.8 2.7 %collective-permute-done.18.refs_2_ = bf16[64,1152]{1,0:T(8,128)(2,1)S(1)} collective-permute-done((bf16[64,1152]{1,0:T(8,128)(2,1)S(1)}, bf16[64,1152]{1,0:T(8,128)(2,1)S(1)}, u32[]{:S(2)}, u32[]{:S(2)}) %collective-permute-start.18) | collective-permute-done | bytes 147488 | tf_op jit(solution)/shard_map/ppermute | solution.py:38
  85.0 6.0 %collective-permute-done.22.refs_2_ = bf16[128,1152]{1,0:T(8,128)(2,1)S(1)} collective-permute-done((bf16[128,1152]{1,0:T(8,128)(2,1)S(1)}, bf16[128,1152]{1,0:T(8,128)(2,1)S(1)}, u32[]{:S(2)}, u32[]{:S(2)}) %collective-permute-start.22) | collective-permute-done | bytes 294944 | tf_op jit(solution)/shard_map/ppermute | solution.py:38
  93.6 2.0 %shard_map.168 = (f32[256,1024]{1,0:T(8,128)}, f32[256,1024]{1,0:T(8,128)}, f32[8,128]{1,0:T(8,128)}) custom-call(s32[13]{0:T(128)S(1)} %stack.55.refs_0_, bf16[256,384]{1,0:T(8,128)(2,1)S(1)} %get-tuple-element.73.refs_1_.refs_7_, bf16[256,384]{1,0:T(8,128)(2,1)S(1)} %get-tuple-element.74.refs_2_, bf16[256,384]{1,0:T(8,128)(2,1)S(1)} %get-tuple-element.75.refs_3_, ...), custom_call_target="tpu_custom_call" | custom-call | tf_op jit(solution)/shard_map/pallas_call | solution.py:60
  95.6 2.3 %collective-permute-done.26.refs_2_ = bf16[160,1024]{1,0:T(8,128)(2,1)S(1)} collective-permute-done((bf16[160,1024]{1,0:T(8,128)(2,1)S(1)}, bf16[160,1024]{1,0:T(8,128)(2,1)S(1)}, u32[]{:S(2)}, u32[]{:S(2)}) %collective-permute-start.26) | collective-permute-done | bytes 327712 | tf_op jit(solution)/shard_map/ppermute | solution.py:38
  98.5 1.4 %shard_map.169 = (f32[64,1024]{1,0:T(8,128)}, f32[64,1024]{1,0:T(8,128)}, f32[32,1024]{1,0:T(8,128)}) custom-call(s32[13]{0:T(128)S(1)} %stack.55.refs_0_, bf16[160,1024]{1,0:T(8,128)(2,1)S(1)} %get-tuple-element.72.refs_3_.refs_1_, bf16[160,1024]{1,0:T(8,128)(2,1)S(1)} %collective-permute-done.26.refs_2_, f32[8,128]{1,0:T(8,128)S(1)} %copy-done.5), custom_call_target="tpu_custom_call" | custom-call | tf_op jit(solution)/shard_map/pallas_call | solution.py:60
  (100 shorter events, 29.8 us)
Async XLA Ops:
  0.6 12.1 %copy-start = (bf16[1024,1024]{1,0:T(8,128)(2,1)S(1)}, bf16[1024,1024]{1,0:T(8,128)(2,1)}, u32[]{:S(2)}) copy-start(bf16[1024,1024]{1,0:T(8,128)(2,1)} %param.13) | copy-start | bytes 6291460
  0.6 9.0 %collective-permute-start.4 = (s32[8,128]{1,0:T(8,128)}, s32[8,128]{1,0:T(8,128)S(1)}, u32[]{:S(2)}, u32[]{:S(2)}) collective-permute-start(s32[8,128]{1,0:T(8,128)} %bitcast.38), channel_id=1, source_target_pairs={{0,4},{4,0},{8,12},{12,8},{16,20},{20,16},{24,28},{28,24},{1,5},{5... | collective-permute-start | bytes 12296 | tf_op jit(solution)/shard_map/ppermute | solution.py:38
  1.2 10.9 %collective-permute-start.3 = (bf16[128,2048]{1,0:T(8,128)(2,1)}, bf16[128,2048]{1,0:T(8,128)(2,1)S(1)}, u32[]{:S(2)}, u32[]{:S(2)}) collective-permute-start(bf16[128,2048]{1,0:T(8,128)(2,1)} %refs_1_.5), channel_id=1, source_target_pairs={{0,4},{4,0},{8,12},{12,8},{16,20},{20,16},{24,28},{28,24},{1,5},{5... | collective-permute-start | bytes 1572872 | tf_op jit(solution)/shard_map/ppermute | solution.py:38
  2.4 7.3 %copy-start.6 = (s32[128,8]{0,1:T(8,128)S(1)}, s32[128,8]{0,1:T(8,128)}, u32[]{:S(2)}) copy-start(s32[128,8]{0,1:T(8,128)} %param.9) | copy-start | bytes 12292
  4.1 8.0 %copy-start.3 = (bf16[128,2048]{1,0:T(8,128)(2,1)S(1)}, bf16[128,2048]{1,0:T(8,128)(2,1)}, u32[]{:S(2)}) copy-start(bf16[128,2048]{1,0:T(8,128)(2,1)} %refs_1_.5) | copy-start | bytes 1572868
  4.1 16.0 %collective-permute-start = (bf16[64,1024]{1,0:T(8,128)(2,1)}, bf16[64,1024]{1,0:T(8,128)(2,1)S(1)}, u32[]{:S(2)}, u32[]{:S(2)}) collective-permute-start(bf16[64,1024]{1,0:T(8,128)(2,1)} %get-tuple-element.46), channel_id=1, source_target_pairs={{0,1},{1,0},{2,3},{3,2},{4,5},{5,4},{6,7},{7,6},{8,9},{9,8},{10,11... | collective-permute-start | bytes 393224 | tf_op jit(solution)/shard_map/ppermute | solution.py:38
  7.1 13.1 %collective-permute-start.1 = (bf16[64,1024]{1,0:T(8,128)(2,1)}, bf16[64,1024]{1,0:T(8,128)(2,1)S(1)}, u32[]{:S(2)}, u32[]{:S(2)}) collective-permute-start(bf16[64,1024]{1,0:T(8,128)(2,1)} %get-tuple-element.47), channel_id=1, source_target_pairs={{0,2},{1,3},{2,0},{3,1},{4,6},{5,7},{6,4},{7,5},{8,10},{9,11},{10,... | collective-permute-start | bytes 393224 | tf_op jit(solution)/shard_map/ppermute | solution.py:38
  9.7 10.5 %collective-permute-start.2 = (bf16[64,1024]{1,0:T(8,128)(2,1)}, bf16[64,1024]{1,0:T(8,128)(2,1)}, u32[]{:S(2)}, u32[]{:S(2)}) collective-permute-start(bf16[64,1024]{1,0:T(8,128)(2,1)} %get-tuple-element.48), channel_id=1, source_target_pairs={{0,3},{1,2},{2,1},{3,0},{4,7},{5,6},{6,5},{7,4},{8,11},{9,10},{10,... | collective-permute-start | bytes 393224 | tf_op jit(solution)/shard_map/ppermute | solution.py:38
  20.0 2.9 %copy-start.2 = (bf16[2048,1024]{1,0:T(8,128)(2,1)S(1)}, bf16[2048,1024]{1,0:T(8,128)(2,1)}, u32[]{:S(2)}) copy-start(bf16[2048,1024]{1,0:T(8,128)(2,1)} %refs_1_.7) | copy-start | bytes 12582916
  22.0 5.6 %collective-permute-start.5 = (bf16[256,1024]{1,0:T(8,128)(2,1)S(1)}, bf16[256,1024]{1,0:T(8,128)(2,1)S(1)}, u32[]{:S(2)}, u32[]{:S(2)}) collective-permute-start(bf16[256,1024]{1,0:T(8,128)(2,1)S(1)} %shard_map.148.refs_2_.refs_1_), channel_id=1, source_target_pairs={{0,4},{4,0},{8,12},{12,8},{16,20},{20,16},{24,28},{28,24},{1,5},{5... | collective-permute-start | bytes 1572872 | tf_op jit(solution)/shard_map/ppermute | solution.py:38
  27.0 12.8 %collective-permute-start.7 = (bf16[128,1024]{1,0:T(8,128)(2,1)S(1)}, bf16[128,1024]{1,0:T(8,128)(2,1)S(1)}, u32[]{:S(2)}, u32[]{:S(2)}) collective-permute-start(bf16[128,1024]{1,0:T(8,128)(2,1)S(1)} %get-tuple-element.100), channel_id=1, source_target_pairs={{0,4},{4,0},{8,12},{12,8},{16,20},{20,16},{24,28},{28,24},{1,5},{5... | collective-permute-start | bytes 786440 | tf_op jit(solution)/shard_map/ppermute | solution.py:38
  30.8 6.7 %collective-permute-start.6 = (bf16[512,1024]{1,0:T(8,128)(2,1)S(1)}, bf16[512,1024]{1,0:T(8,128)(2,1)S(1)}, u32[]{:S(2)}, u32[]{:S(2)}) collective-permute-start(bf16[512,1024]{1,0:T(8,128)(2,1)S(1)} %get-tuple-element.106), channel_id=1, source_target_pairs={{0,4},{4,0},{8,12},{12,8},{16,20},{20,16},{24,28},{28,24},{1,5},{5... | collective-permute-start | bytes 3145736 | tf_op jit(solution)/shard_map/ppermute | solution.py:38
  31.6 20.3 %collective-permute-start.10 = (bf16[512,1024]{1,0:T(8,128)(2,1)S(1)}, bf16[512,1024]{1,0:T(8,128)(2,1)S(1)}, u32[]{:S(2)}, u32[]{:S(2)}) collective-permute-start(bf16[512,1024]{1,0:T(8,128)(2,1)S(1)} %convolution_convert_fusion.3.refs_2_), channel_id=1, source_target_pairs={{0,8},{4,20},{8,0},{12,28},{16,24},{20,4},{24,16},{28,12},{1,9},{5... | collective-permute-start | bytes 3145736 | tf_op jit(solution)/shard_map/ppermute | solution.py:38
  34.0 25.6 %collective-permute-start.13 = (bf16[512,1024]{1,0:T(8,128)(2,1)S(1)}, bf16[512,1024]{1,0:T(8,128)(2,1)S(1)}, u32[]{:S(2)}, u32[]{:S(2)}) collective-permute-start(bf16[512,1024]{1,0:T(8,128)(2,1)S(1)} %convolution_convert_fusion.2.refs_3_), channel_id=1, source_target_pairs={{0,1},{1,0},{2,3},{3,2},{4,5},{5,4},{6,7},{7,6},{8,9},{9,8},{10,11... | collective-permute-start | bytes 3145736 | tf_op jit(solution)/shard_map/ppermute | solution.py:38
  40.5 9.1 %collective-permute-start.8 = (bf16[128,1152]{1,0:T(8,128)(2,1)S(1)}, bf16[128,1152]{1,0:T(8,128)(2,1)S(1)}, u32[]{:S(2)}, u32[]{:S(2)}) collective-permute-start(bf16[128,1152]{1,0:T(8,128)(2,1)S(1)} %get-tuple-element.55), channel_id=1, source_target_pairs={{0,8},{4,20},{8,0},{12,28},{16,24},{20,4},{24,16},{28,12},{1,9},{5... | collective-permute-start | bytes 884744 | tf_op jit(solution)/shard_map/ppermute | solution.py:38
  43.5 17.9 %collective-permute-start.12 = (bf16[256,1024]{1,0:T(8,128)(2,1)S(1)}, bf16[256,1024]{1,0:T(8,128)(2,1)S(1)}, u32[]{:S(2)}, u32[]{:S(2)}) collective-permute-start(bf16[256,1024]{1,0:T(8,128)(2,1)S(1)} %get-tuple-element.60), channel_id=1, source_target_pairs={{0,8},{4,20},{8,0},{12,28},{16,24},{20,4},{24,16},{28,12},{1,9},{5... | collective-permute-start | bytes 1572872 | tf_op jit(solution)/shard_map/ppermute | solution.py:38
  45.1 5.2 %copy-start.4 = (bf16[128,2048]{1,0:T(8,128)(2,1)}, bf16[128,2048]{1,0:T(8,128)(2,1)S(1)}, u32[]{:S(2)}) copy-start(bf16[128,2048]{1,0:T(8,128)(2,1)S(1)} %pad_maximum_fusion.refs_7_) | copy-start | bytes 1572868
  50.3 6.1 %collective-permute-start.9 = (bf16[64,1152]{1,0:T(8,128)(2,1)S(1)}, bf16[64,1152]{1,0:T(8,128)(2,1)S(1)}, u32[]{:S(2)}, u32[]{:S(2)}) collective-permute-start(bf16[64,1152]{1,0:T(8,128)(2,1)S(1)} %get-tuple-element.58), channel_id=1, source_target_pairs={{0,16},{4,12},{8,24},{12,4},{16,0},{20,28},{24,8},{28,20},{1,17},{... | collective-permute-start | bytes 442376 | tf_op jit(solution)/shard_map/ppermute | solution.py:38
  52.7 14.1 %collective-permute-start.17 = (bf16[256,1024]{1,0:T(8,128)(2,1)S(1)}, bf16[256,1024]{1,0:T(8,128)(2,1)S(1)}, u32[]{:S(2)}, u32[]{:S(2)}) collective-permute-start(bf16[256,1024]{1,0:T(8,128)(2,1)S(1)} %get-tuple-element.65), channel_id=1, source_target_pairs={{0,16},{4,12},{8,24},{12,4},{16,0},{20,28},{24,8},{28,20},{1,17},{... | collective-permute-start | bytes 1572872 | tf_op jit(solution)/shard_map/ppermute | solution.py:38
  56.9 7.0 %collective-permute-start.11 = (bf16[64,1152]{1,0:T(8,128)(2,1)S(1)}, bf16[64,1152]{1,0:T(8,128)(2,1)S(1)}, u32[]{:S(2)}, u32[]{:S(2)}) collective-permute-start(bf16[64,1152]{1,0:T(8,128)(2,1)S(1)} %shard_map.157.refs_3_.refs_1_), channel_id=1, source_target_pairs={{0,1},{1,0},{2,3},{3,2},{4,5},{5,4},{6,7},{7,6},{8,9},{9,8},{10,11... | collective-permute-start | bytes 442376 | tf_op jit(solution)/shard_map/ppermute | solution.py:38
  60.4 9.2 %collective-permute-start.16 = (bf16[256,1024]{1,0:T(8,128)(2,1)S(1)}, bf16[256,1024]{1,0:T(8,128)(2,1)S(1)}, u32[]{:S(2)}, u32[]{:S(2)}) collective-permute-start(bf16[256,1024]{1,0:T(8,128)(2,1)S(1)} %get-tuple-element.64), channel_id=1, source_target_pairs={{0,8},{4,20},{8,0},{12,28},{16,24},{20,4},{24,16},{28,12},{1,9},{5... | collective-permute-start | bytes 1572872 | tf_op jit(solution)/shard_map/ppermute | solution.py:38
  62.0 12.5 %collective-permute-start.15 = (bf16[128,1024]{1,0:T(8,128)(2,1)S(1)}, bf16[128,1024]{1,0:T(8,128)(2,1)S(1)}, u32[]{:S(2)}, u32[]{:S(2)}) collective-permute-start(bf16[128,1024]{1,0:T(8,128)(2,1)S(1)} %get-tuple-element.63), channel_id=1, source_target_pairs={{0,1},{1,0},{2,3},{3,2},{4,5},{5,4},{6,7},{7,6},{8,9},{9,8},{10,11... | collective-permute-start | bytes 786440 | tf_op jit(solution)/shard_map/ppermute | solution.py:38
  64.5 12.2 %collective-permute-start.14 = (bf16[64,1152]{1,0:T(8,128)(2,1)S(1)}, bf16[64,1152]{1,0:T(8,128)(2,1)S(1)}, u32[]{:S(2)}, u32[]{:S(2)}) collective-permute-start(bf16[64,1152]{1,0:T(8,128)(2,1)S(1)} %shard_map.160.refs_3_.refs_1_), channel_id=1, source_target_pairs={{0,2},{1,3},{2,0},{3,1},{4,6},{5,7},{6,4},{7,5},{8,10},{9,11},{10,... | collective-permute-start | bytes 442376 | tf_op jit(solution)/shard_map/ppermute | solution.py:38
  67.5 10.6 %collective-permute-start.19 = (bf16[128,1024]{1,0:T(8,128)(2,1)S(1)}, bf16[128,1024]{1,0:T(8,128)(2,1)S(1)}, u32[]{:S(2)}, u32[]{:S(2)}) collective-permute-start(bf16[128,1024]{1,0:T(8,128)(2,1)S(1)} %get-tuple-element.69), channel_id=1, source_target_pairs={{0,1},{1,0},{2,3},{3,2},{4,5},{5,4},{6,7},{7,6},{8,9},{9,8},{10,11... | collective-permute-start | bytes 786440 | tf_op jit(solution)/shard_map/ppermute | solution.py:38
  70.3 9.8 %collective-permute-start.20 = (bf16[128,1024]{1,0:T(8,128)(2,1)S(1)}, bf16[128,1024]{1,0:T(8,128)(2,1)S(1)}, u32[]{:S(2)}, u32[]{:S(2)}) collective-permute-start(bf16[128,1024]{1,0:T(8,128)(2,1)S(1)} %get-tuple-element.70), channel_id=1, source_target_pairs={{0,16},{4,12},{8,24},{12,4},{16,0},{20,28},{24,8},{28,20},{1,17},{... | collective-permute-start | bytes 786440 | tf_op jit(solution)/shard_map/ppermute | solution.py:38
  75.1 5.0 %collective-permute-start.21 = (bf16[64,1024]{1,0:T(8,128)(2,1)S(1)}, bf16[64,1024]{1,0:T(8,128)(2,1)S(1)}, u32[]{:S(2)}, u32[]{:S(2)}) collective-permute-start(bf16[64,1024]{1,0:T(8,128)(2,1)S(1)} %get-tuple-element.71), channel_id=1, source_target_pairs={{0,16},{4,12},{8,24},{12,4},{16,0},{20,28},{24,8},{28,20},{1,17},{... | collective-permute-start | bytes 393224 | tf_op jit(solution)/shard_map/ppermute | solution.py:38
  77.3 6.3 %collective-permute-start.18 = (bf16[64,1152]{1,0:T(8,128)(2,1)S(1)}, bf16[64,1152]{1,0:T(8,128)(2,1)S(1)}, u32[]{:S(2)}, u32[]{:S(2)}) collective-permute-start(bf16[64,1152]{1,0:T(8,128)(2,1)S(1)} %shard_map.164.refs_7_.refs_1_), channel_id=1, source_target_pairs={{0,16},{4,12},{8,24},{12,4},{16,0},{20,28},{24,8},{28,20},{1,17},{... | collective-permute-start | bytes 442376 | tf_op jit(solution)/shard_map/ppermute | solution.py:38
  84.1 6.8 %collective-permute-start.22 = (bf16[128,1152]{1,0:T(8,128)(2,1)S(1)}, bf16[128,1152]{1,0:T(8,128)(2,1)S(1)}, u32[]{:S(2)}, u32[]{:S(2)}) collective-permute-start(bf16[128,1152]{1,0:T(8,128)(2,1)S(1)} %shard_map.166.refs_1_.refs_3_), channel_id=1, source_target_pairs={{0,8},{4,20},{8,0},{12,28},{16,24},{20,4},{24,16},{28,12},{1,9},{5... | collective-permute-start | bytes 884744 | tf_op jit(solution)/shard_map/ppermute | solution.py:38
  84.2 13.6 %collective-permute-start.26 = (bf16[160,1024]{1,0:T(8,128)(2,1)S(1)}, bf16[160,1024]{1,0:T(8,128)(2,1)S(1)}, u32[]{:S(2)}, u32[]{:S(2)}) collective-permute-start(bf16[160,1024]{1,0:T(8,128)(2,1)S(1)} %get-tuple-element.79), channel_id=1, source_target_pairs={{0,2},{1,3},{2,0},{3,1},{4,6},{5,7},{6,4},{7,5},{8,10},{9,11},{10,... | collective-permute-start | bytes 983048 | tf_op jit(solution)/shard_map/ppermute | solution.py:38
  91.5 1.5 %collective-permute-start.23 = (bf16[256,384]{1,0:T(8,128)(2,1)S(1)}, bf16[256,384]{1,0:T(8,128)(2,1)S(1)}, u32[]{:S(2)}, u32[]{:S(2)}) collective-permute-start(bf16[256,384]{1,0:T(8,128)(2,1)S(1)} %get-tuple-element.73.refs_1_.refs_7_), channel_id=1, source_target_pairs={{0,4},{4,0},{8,12},{12,8},{16,20},{20,16},{24,28},{28,24},{1,5},{5... | collective-permute-start | bytes 589832 | tf_op jit(solution)/shard_map/ppermute | solution.py:38
  91.6 1.7 %collective-permute-start.24 = (bf16[256,384]{1,0:T(8,128)(2,1)S(1)}, bf16[256,384]{1,0:T(8,128)(2,1)S(1)}, u32[]{:S(2)}, u32[]{:S(2)}) collective-permute-start(bf16[256,384]{1,0:T(8,128)(2,1)S(1)} %get-tuple-element.74.refs_2_), channel_id=1, source_target_pairs={{0,4},{4,0},{8,12},{12,8},{16,20},{20,16},{24,28},{28,24},{1,5},{5... | collective-permute-start | bytes 589832 | tf_op jit(solution)/shard_map/ppermute | solution.py:38
  92.1 1.5 %collective-permute-start.25 = (bf16[256,384]{1,0:T(8,128)(2,1)S(1)}, bf16[256,384]{1,0:T(8,128)(2,1)S(1)}, u32[]{:S(2)}, u32[]{:S(2)}) collective-permute-start(bf16[256,384]{1,0:T(8,128)(2,1)S(1)} %get-tuple-element.75.refs_3_), channel_id=1, source_target_pairs={{0,4},{4,0},{8,12},{12,8},{16,20},{20,16},{24,28},{28,24},{1,5},{5... | collective-permute-start | bytes 589832 | tf_op jit(solution)/shard_map/ppermute | solution.py:38
  (5 other events, 8.2 us)

commit v4 on v3

--- a/solution.py
+++ b/solution.py
@@ -167,22 +167,22 @@
             up_here[:, first : first + half] = value[:, z * half : (z + 1) * half]
 
 
-def pick_down_body(tp_count, share_count, numbers, down, down_here, ready):
-    chunk = down_here.shape[0] // share_count
+def pick_down_body(tp_count, share_count, numbers, down, down_here, downs, ready):
+    chunk = downs.shape[1]
     unit = chunk // tp_count
     half = chunk // 2
     copies = []
     for n in range(share_count):
+        at = pl.ds(pl.multiple_of(numbers[tp_count + n] * chunk, chunk), chunk)
+        copies.append(pltpu.make_async_copy(down.at[at, :], downs.at[n], ready.at[n]))
+        copies[-1].start()
+    for n in range(share_count):
+        copies[n].wait()
         for i, m in enumerate(sent_order(tp_count)):
             z, place = i // (tp_count // 2), i % (tp_count // 2)
             first = (z * share_count + n) * half + place * unit
-            start = numbers[tp_count + n] * chunk + numbers[m] * unit
-            source = down.at[pl.ds(pl.multiple_of(start, unit), unit), :]
-            target = down_here.at[pl.ds(first, unit), :]
-            copies.append(pltpu.make_async_copy(source, target, ready.at[n, i]))
-            copies[-1].start()
-    for copy in copies:
-        copy.wait()
+            start = pl.multiple_of(numbers[m] * unit, unit)
+            down_here[first : first + unit, :] = downs[n, pl.ds(start, unit), :]
 
 
 def split_body(tp_count, share, numbers, value, kept, sent):
@@ -238,14 +238,17 @@
     summed[...] = (kept[...].astype(F32) + arrived[...].astype(F32)).astype(summed.dtype)
 
 
-def stack_body(numbers, first, second, *parts):
-    rows = first.shape[0]
+def stack_body(count, numbers, *refs):
+    firsts, seconds, parts = refs[:count], refs[count : 2 * count], refs[2 * count :]
     column = 0
-    for part in parts:
+    for i, part in enumerate(parts):
+        first, second = firsts[min(i, count - 1)], seconds[min(i, count - 1)]
         at = slice(column, column + part.shape[1])
+        rows = first.shape[0]
         part[:rows, :] = first[:, at]
         part[rows:, :] = second[:, at]
-        column += part.shape[1]
+        if count == 1:
+            column += part.shape[1]
 
 
 def tables_body(share_count, first_share, height, count, numbers, *refs):
@@ -416,7 +419,7 @@
         [down_weight],
         [h_rows],
         in_specs=[far],
-        scratch=[pltpu.SemaphoreType.DMA((share_count, tp_count))],
+        scratch=[VMEM((share_count, chunk, width), BF), pltpu.SemaphoreType.DMA((share_count,))],
     )
     strip = chunk // 2
     h_rows = jnp.concatenate(
@@ -492,17 +495,24 @@
             if last == "half" and kind == "half":
                 self.kept, sent = step(add_body, [like(rows // 2, columns, BF)] * 2, ins, after)
             elif last == "join":
-                cut = columns // PARTS if hop is None else columns
-                outs = [like(2 * rows, cut, BF)] * (columns // cut)
-                self.parts = step(stack_body, outs, ins, after)
-                self.kept = sent = self.parts[0]
+                many = self.plan[self.at + 1 :]
+                cut = columns if len(many) > 2 or len(self.parts) > 1 else columns // PARTS
+                outs = [like(2 * rows, cut, BF)] * (PARTS if len(many) <= 2 else 1)
+                body = functools.partial(stack_body, len(self.parts))
+                build = step if len(many) > 2 else call
+                self.parts = build(body, outs, [*self.parts, *self.arrived], after)
+                self.kept = self.parts[0]
             else:
                 (self.kept,) = step(sum_body, [like(rows, columns, BF)], ins, after)
                 sent = self.kept
             self.at += 1
             self.left -= 1
-            if hop is None:
-                self.arrived = [core_swap(part) for part in self.parts]
+            if kind == "join":
+                if last != "join":
+                    self.parts = [sent]
+                self.arrived = [
+                    core_swap(part) if hop is None else go(part, hop) for part in self.parts
+                ]
             else:
                 self.arrived = go(sent, hop)
             return self.kept

time: 100 us -> 94.7 us (0.947)
  waiting for transfers between devices: 27.6 us -> 20.4 us
  starting transfers between devices: 27.6 us -> 31.4 us
  Pallas kernels: 26 us -> 23.4 us
    ppermute x27 -> x29, waiting for transfers between devices: 27.6 us -> 20.4 us  [swap(): return lax.ppermute(value, axis, pairs)]
    ppermute x27 -> x29, starting transfers between devices: 27.6 us -> 31.4 us  [swap(): return lax.ppermute(value, axis, pairs)]
    pallas_call x26, Pallas kernels: 26 us -> 23.4 us  [run(): pl.pallas_call(kernel, out_shape=tuple(outs), grid_spec=pltpu.PrefetchSca...]
  transfers between devices with their start and end apart: 27 -> 29, of which waited for: 14 -> 15; matrix products, arithmetic and copies ran while one was open for 15% -> 16% of each run, Pallas kernels for 22% -> 21%
where the time goes in v4:
time: 94.7 us; the launch traced here: 94 us
  starting transfers between devices  31.4 us (33%)
  Pallas kernels  23.4 us (25%)
  waiting for transfers between devices  20.4 us (22%)
  matrix products  12.7 us (13%)
  local copies, waits for them, and re-layouts  3.19 us (3%)
  other arithmetic  1.78 us (2%)
  between operations  1.16 us (1%)
    ppermute x29, starting transfers between devices, swap(): return lax.ppermute(value, axis, pairs)  31.4 us
    pallas_call x26, Pallas kernels, run(): pl.pallas_call(kernel, out_shape=tuple(outs), grid_spec=pltpu.PrefetchSca...  23.4 us
    ppermute x29, waiting for transfers between devices, swap(): return lax.ppermute(value, axis, pairs)  20.4 us
    dot_general x3, matrix products, times(): return jnp.dot(left, right, preferred_element_type=F32)  4.7 us
    dot_general x8, matrix products, inner(): lax.dot_general(left, right, (((0,), (0,)), ((), ())), preferred_element_...  4.59 us
    dot_general x3, matrix products, outer(): lax.dot_general(left, right, (((1,), (1,)), ((), ())), preferred_element_...  3.38 us
    unnamed x26, local copies, waits for them, and re-layouts  2.63 us
  transfers between devices with their start and end apart: 29, of which 15 were waited for; matrix products, arithmetic and copies ran while one was open for 16% of the time, Pallas kernels for 21%

profile of v4, /device:TPU:0, one launch (start us, length us, event | category | flops | bytes accessed | tf_op | source)
XLA Modules:
  0.0 94.0 jit_solution(14355851144154598766)
XLA Ops:
  1.3 1.0 %copy-done.7 = bf16[256,1024]{1,0:T(8,128)(2,1)S(1)} copy-done((bf16[256,1024]{1,0:T(8,128)(2,1)S(1)}, bf16[256,1024]{1,0:T(8,128)(2,1)}, u32[]{:S(2)}) %copy-start.7) | copy-done | bytes 524312
  2.4 1.7 %shard_map.144 = (bf16[64,1024]{1,0:T(8,128)(2,1)S(1)}, bf16[64,1024]{1,0:T(8,128)(2,1)}, bf16[64,1024]{1,0:T(8,128)(2,1)}, bf16[64,1024]{1,0:T(8,128)(2,1)}) custom-call(s32[13]{0:T(128)S(1)} %stack.55.refs_0_, bf16[256,1024]{1,0:T(8,128)(2,1)S(1)} %copy-done.7), custom_call_target="tpu_custom_call" | custom-call | flops 6000000000 | tf_op jit(solution)/shard_map/pallas_call | solution.py:60
  4.1 3.0 %collective-permute-start = (bf16[64,1024]{1,0:T(8,128)(2,1)}, bf16[64,1024]{1,0:T(8,128)(2,1)S(1)}, u32[]{:S(2)}, u32[]{:S(2)}) collective-permute-start(bf16[64,1024]{1,0:T(8,128)(2,1)} %get-tuple-element.49), channel_id=1, source_target_pairs={{0,1},{1,0},{2,3},{3,2},{4,5},{5,4},{6,7},{7,6},{8,9},{9,8},{10,11... | collective-permute-start | bytes 393224 | tf_op jit(solution)/shard_map/ppermute | solution.py:38
  7.1 2.6 %collective-permute-start.1 = (bf16[64,1024]{1,0:T(8,128)(2,1)}, bf16[64,1024]{1,0:T(8,128)(2,1)S(1)}, u32[]{:S(2)}, u32[]{:S(2)}) collective-permute-start(bf16[64,1024]{1,0:T(8,128)(2,1)} %get-tuple-element.50), channel_id=1, source_target_pairs={{0,2},{1,3},{2,0},{3,1},{4,6},{5,7},{6,4},{7,5},{8,10},{9,11},{10,... | collective-permute-start | bytes 393224 | tf_op jit(solution)/shard_map/ppermute | solution.py:38
  10.6 1.5 %fusion.39 = f32[512,1024]{1,0:T(8,128)S(1)} fusion(bf16[512,256]{1,0:T(8,128)(2,1)S(1)} %get-tuple-element.52.refs_3_, bf16[256,1024]{1,0:T(8,128)(2,1)} %param.14), kind=kOutput, calls=%fused_computation.71 | convolution fusion | flops 268435456 | bytes 2883584 | tf_op jit(solution)/shard_map/dot_general | solution.py:32
  12.8 1.4 %multiply_reduce_fusion.2 = (f32[512]{0:T(512)S(1)}, f32[512,1024]{1,0:T(8,128)S(1)}) fusion(f32[512,1024]{1,0:T(8,128)S(1)} %fusion.39, bf16[512,1024]{1,0:T(8,128)(2,1)S(1)} %shard_map.146, bf16[1024,1024]{1,0:T(8,128)(2,1)S(1)} %copy-done), kind=kOutput, calls=%fused_computation.9 | convolution fusion | flops 1075314176 | bytes 7342080 | tf_op jit(solution)/shard_map/dot_general | solution.py:32
  14.9 2.6 %shard_map.147 = bf16[1024,1024]{1,0:T(8,128)(2,1)S(1)} custom-call(s32[13]{0:T(128)S(1)} %stack.55.refs_0_, bf16[1024,2048]{1,0:T(8,128)(2,1)S(1)} %copy-done.1, bf16[512,1024]{1,0:T(8,128)(2,1)S(1)} %multiply_convert_fusion.3.refs_2_), custom_call_target="tpu_custom_call" | custom-call | tf_op jit(solution)/shard_map/pallas_call | solution.py:60
  17.6 1.8 %multiply_convert_fusion.1 = (bf16[512,1024]{1,0:T(8,128)(2,1)S(1)}, bf16[512,1024]{1,0:T(8,128)(2,1)S(1)}) fusion(bf16[512,1024]{1,0:T(8,128)(2,1)S(1)} %multiply_convert_fusion.3.refs_2_, bf16[1024,1024]{1,0:T(8,128)(2,1)S(1)} %shard_map.147), kind=kOutput, calls=%fused_computation.5 | convolution fusion | flops 1078984704 | bytes 5242880 | tf_op jit(solution)/shard_map/dot_general | solution.py:32
  20.2 1.8 %shard_map.148.refs_2_.refs_1_ = bf16[256,1024]{1,0:T(8,128)(2,1)S(1)} custom-call(s32[13]{0:T(128)S(1)} %stack.55.refs_0_, bf16[64,1024]{1,0:T(8,128)(2,1)S(1)} %get-tuple-element.48.refs_3_.refs_1_, bf16[64,1024]{1,0:T(8,128)(2,1)S(1)} %collective-permute-done.refs_2_, bf16[64,1024]{1,0:T(8,128)(2,1)S(1)} %collective-permute-done.1.refs_3_, ...), custom_call_target="tpu_custom_call" | custom-call | tf_op jit(solution)/shard_map/pallas_call | solution.py:60
  23.0 1.1 %shard_map.151 = bf16[1024,1024]{1,0:T(8,128)(2,1)S(1)} custom-call(s32[13]{0:T(128)S(1)} %stack.55.refs_0_, bf16[2048,1024]{1,0:T(8,128)(2,1)S(1)} %copy-done.2, bf16[512,1024]{1,0:T(8,128)(2,1)S(1)} %get-tuple-element.53.refs_2_), custom_call_target="tpu_custom_call" | custom-call | tf_op jit(solution)/shard_map/pallas_call | solution.py:60
  25.6 1.3 %multiply_convert_fusion = bf16[512,1024]{1,0:T(8,128)(2,1)S(1)} fusion(bf16[512,1024]{1,0:T(8,128)(2,1)S(1)} %get-tuple-element.55, bf16[512,1024]{1,0:T(8,128)(2,1)S(1)} %shard_map.150, bf16[1024,1024]{1,0:T(8,128)(2,1)S(1)} %shard_map.151), kind=kOutput, calls=%fused_computation.4 | convolution fusion | flops 1075314688 | bytes 5242880 | tf_op jit(solution)/shard_map/dot_general | solution.py:26
  26.9 1.3 %fusion.38 = (bf16[512,1024]{1,0:T(8,128)(2,1)S(1)}, f32[512,1024]{1,0:T(8,128)S(1)}) fusion(bf16[512,1024]{1,0:T(8,128)(2,1)S(1)} %multiply_convert_fusion, bf16[1024,1024]{1,0:T(8,128)(2,1)S(1)} %shard_map.147), kind=kOutput, calls=%fused_computation.70 | convolution fusion | flops 1074266112 | bytes 6291456 | tf_op jit(solution)/shard_map/dot_general | solution.py:26
  29.0 1.6 %collective-permute-start.10 = (bf16[512,1024]{1,0:T(8,128)(2,1)S(1)}, bf16[512,1024]{1,0:T(8,128)(2,1)S(1)}, u32[]{:S(2)}, u32[]{:S(2)}) collective-permute-start(bf16[512,1024]{1,0:T(8,128)(2,1)S(1)} %convolution_convert_fusion.3.refs_2_), channel_id=1, source_target_pairs={{0,8},{4,20},{8,0},{12,28},{16,24},{20,4},{24,16},{28,12},{1,9},{5... | collective-permute-start | bytes 3145736 | tf_op jit(solution)/shard_map/ppermute | solution.py:38
  31.4 2.0 %collective-permute-start.13 = (bf16[512,1024]{1,0:T(8,128)(2,1)S(1)}, bf16[512,1024]{1,0:T(8,128)(2,1)S(1)}, u32[]{:S(2)}, u32[]{:S(2)}) collective-permute-start(bf16[512,1024]{1,0:T(8,128)(2,1)S(1)} %convolution_convert_fusion.2.refs_3_), channel_id=1, source_target_pairs={{0,1},{1,0},{2,3},{3,2},{4,5},{5,4},{6,7},{7,6},{8,9},{9,8},{10,11... | collective-permute-start | bytes 3145736 | tf_op jit(solution)/shard_map/ppermute | solution.py:38
  40.9 1.6 %collective-permute-start.12 = (bf16[256,1024]{1,0:T(8,128)(2,1)S(1)}, bf16[256,1024]{1,0:T(8,128)(2,1)S(1)}, u32[]{:S(2)}, u32[]{:S(2)}) collective-permute-start(bf16[256,1024]{1,0:T(8,128)(2,1)S(1)} %get-tuple-element.63), channel_id=1, source_target_pairs={{0,8},{4,20},{8,0},{12,28},{16,24},{20,4},{24,16},{28,12},{1,9},{5... | collective-permute-start | bytes 1572872 | tf_op jit(solution)/shard_map/ppermute | solution.py:38
  42.5 4.6 %collective-permute-done.8.refs_2_ = bf16[128,1152]{1,0:T(8,128)(2,1)S(1)} collective-permute-done((bf16[128,1152]{1,0:T(8,128)(2,1)S(1)}, bf16[128,1152]{1,0:T(8,128)(2,1)S(1)}, u32[]{:S(2)}, u32[]{:S(2)}) %collective-permute-start.8) | collective-permute-done | bytes 294944 | tf_op jit(solution)/shard_map/ppermute | solution.py:38
  47.7 1.7 %collective-permute-start.9 = (bf16[64,1152]{1,0:T(8,128)(2,1)S(1)}, bf16[64,1152]{1,0:T(8,128)(2,1)S(1)}, u32[]{:S(2)}, u32[]{:S(2)}) collective-permute-start(bf16[64,1152]{1,0:T(8,128)(2,1)S(1)} %get-tuple-element.61), channel_id=1, source_target_pairs={{0,16},{4,12},{8,24},{12,4},{16,0},{20,28},{24,8},{28,20},{1,17},{... | collective-permute-start | bytes 442376 | tf_op jit(solution)/shard_map/ppermute | solution.py:38
  50.6 3.1 %collective-permute-done.9.refs_2_ = bf16[64,1152]{1,0:T(8,128)(2,1)S(1)} collective-permute-done((bf16[64,1152]{1,0:T(8,128)(2,1)S(1)}, bf16[64,1152]{1,0:T(8,128)(2,1)S(1)}, u32[]{:S(2)}, u32[]{:S(2)}) %collective-permute-start.9) | collective-permute-done | bytes 147488 | tf_op jit(solution)/shard_map/ppermute | solution.py:38
  54.3 2.1 %collective-permute-start.11 = (bf16[64,1152]{1,0:T(8,128)(2,1)S(1)}, bf16[64,1152]{1,0:T(8,128)(2,1)S(1)}, u32[]{:S(2)}, u32[]{:S(2)}) collective-permute-start(bf16[64,1152]{1,0:T(8,128)(2,1)S(1)} %shard_map.157.refs_3_.refs_1_), channel_id=1, source_target_pairs={{0,1},{1,0},{2,3},{3,2},{4,5},{5,4},{6,7},{7,6},{8,9},{9,8},{10,11... | collective-permute-start | bytes 442376 | tf_op jit(solution)/shard_map/ppermute | solution.py:38
  59.4 1.9 %collective-permute-start.15 = (bf16[128,1024]{1,0:T(8,128)(2,1)S(1)}, bf16[128,1024]{1,0:T(8,128)(2,1)S(1)}, u32[]{:S(2)}, u32[]{:S(2)}) collective-permute-start(bf16[128,1024]{1,0:T(8,128)(2,1)S(1)} %get-tuple-element.66), channel_id=1, source_target_pairs={{0,1},{1,0},{2,3},{3,2},{4,5},{5,4},{6,7},{7,6},{8,9},{9,8},{10,11... | collective-permute-start | bytes 786440 | tf_op jit(solution)/shard_map/ppermute | solution.py:38
  61.9 2.3 %collective-permute-start.14 = (bf16[64,1152]{1,0:T(8,128)(2,1)S(1)}, bf16[64,1152]{1,0:T(8,128)(2,1)S(1)}, u32[]{:S(2)}, u32[]{:S(2)}) collective-permute-start(bf16[64,1152]{1,0:T(8,128)(2,1)S(1)} %shard_map.160.refs_3_.refs_1_), channel_id=1, source_target_pairs={{0,2},{1,3},{2,0},{3,1},{4,6},{5,7},{6,4},{7,5},{8,10},{9,11},{10,... | collective-permute-start | bytes 442376 | tf_op jit(solution)/shard_map/ppermute | solution.py:38
  65.7 1.3 %collective-permute-done.16.refs_2_ = bf16[256,1024]{1,0:T(8,128)(2,1)S(1)} collective-permute-done((bf16[256,1024]{1,0:T(8,128)(2,1)S(1)}, bf16[256,1024]{1,0:T(8,128)(2,1)S(1)}, u32[]{:S(2)}, u32[]{:S(2)}) %collective-permute-start.16) | collective-permute-done | bytes 524320 | tf_op jit(solution)/shard_map/ppermute | solution.py:38
  68.7 3.2 %collective-permute-done.15.refs_2_ = bf16[128,1024]{1,0:T(8,128)(2,1)S(1)} collective-permute-done((bf16[128,1024]{1,0:T(8,128)(2,1)S(1)}, bf16[128,1024]{1,0:T(8,128)(2,1)S(1)}, u32[]{:S(2)}, u32[]{:S(2)}) %collective-permute-start.15) | collective-permute-done | bytes 262176 | tf_op jit(solution)/shard_map/ppermute | solution.py:38
  72.5 1.6 %collective-permute-start.21 = (bf16[64,1024]{1,0:T(8,128)(2,1)S(1)}, bf16[64,1024]{1,0:T(8,128)(2,1)S(1)}, u32[]{:S(2)}, u32[]{:S(2)}) collective-permute-start(bf16[64,1024]{1,0:T(8,128)(2,1)S(1)} %get-tuple-element.74), channel_id=1, source_target_pairs={{0,16},{4,12},{8,24},{12,4},{16,0},{20,28},{24,8},{28,20},{1,17},{... | collective-permute-start | bytes 393224 | tf_op jit(solution)/shard_map/ppermute | solution.py:38
  75.5 2.0 %collective-permute-done.21.refs_6_ = bf16[64,1024]{1,0:T(8,128)(2,1)S(1)} collective-permute-done((bf16[64,1024]{1,0:T(8,128)(2,1)S(1)}, bf16[64,1024]{1,0:T(8,128)(2,1)S(1)}, u32[]{:S(2)}, u32[]{:S(2)}) %collective-permute-start.21) | collective-permute-done | bytes 131104 | tf_op jit(solution)/shard_map/ppermute | solution.py:38
  78.2 1.6 %collective-permute-start.28 = (bf16[160,1024]{1,0:T(8,128)(2,1)S(1)}, bf16[160,1024]{1,0:T(8,128)(2,1)S(1)}, u32[]{:S(2)}, u32[]{:S(2)}) collective-permute-start(bf16[160,1024]{1,0:T(8,128)(2,1)S(1)} %get-tuple-element.85), channel_id=1, source_target_pairs={{0,2},{1,3},{2,0},{3,1},{4,6},{5,7},{6,4},{7,5},{8,10},{9,11},{10,... | collective-permute-start | bytes 983048 | tf_op jit(solution)/shard_map/ppermute | solution.py:38
  80.5 1.1 %collective-permute-start.22 = (bf16[128,384]{1,0:T(8,128)(2,1)S(1)}, bf16[128,384]{1,0:T(8,128)(2,1)S(1)}, u32[]{:S(2)}, u32[]{:S(2)}) collective-permute-start(bf16[128,384]{1,0:T(8,128)(2,1)S(1)} %get-tuple-element.76.refs_1_.refs_7_), channel_id=1, source_target_pairs={{0,8},{4,20},{8,0},{12,28},{16,24},{20,4},{24,16},{28,12},{1,9},{5... | collective-permute-start | bytes 294920 | tf_op jit(solution)/shard_map/ppermute | solution.py:38
  83.6 1.6 %collective-permute-done.22.refs_4_ = bf16[128,384]{1,0:T(8,128)(2,1)S(1)} collective-permute-done((bf16[128,384]{1,0:T(8,128)(2,1)S(1)}, bf16[128,384]{1,0:T(8,128)(2,1)S(1)}, u32[]{:S(2)}, u32[]{:S(2)}) %collective-permute-start.22) | collective-permute-done | bytes 98336 | tf_op jit(solution)/shard_map/ppermute | solution.py:38
  85.1 1.1 %collective-permute-done.23.refs_5_ = bf16[128,384]{1,0:T(8,128)(2,1)S(1)} collective-permute-done((bf16[128,384]{1,0:T(8,128)(2,1)S(1)}, bf16[128,384]{1,0:T(8,128)(2,1)S(1)}, u32[]{:S(2)}, u32[]{:S(2)}) %collective-permute-start.23) | collective-permute-done | bytes 98336 | tf_op jit(solution)/shard_map/ppermute | solution.py:38
  86.2 1.1 %collective-permute-done.24.refs_6_ = bf16[128,384]{1,0:T(8,128)(2,1)S(1)} collective-permute-done((bf16[128,384]{1,0:T(8,128)(2,1)S(1)}, bf16[128,384]{1,0:T(8,128)(2,1)S(1)}, u32[]{:S(2)}, u32[]{:S(2)}) %collective-permute-start.24) | collective-permute-done | bytes 98336 | tf_op jit(solution)/shard_map/ppermute | solution.py:38
  89.9 2.0 %shard_map.168 = (f32[256,1024]{1,0:T(8,128)}, f32[256,1024]{1,0:T(8,128)}, f32[8,128]{1,0:T(8,128)}) custom-call(s32[13]{0:T(128)S(1)} %stack.55.refs_0_, bf16[256,384]{1,0:T(8,128)(2,1)S(1)} %get-tuple-element.79.refs_1_.refs_7_, bf16[256,384]{1,0:T(8,128)(2,1)S(1)} %get-tuple-element.80.refs_2_, bf16[256,384]{1,0:T(8,128)(2,1)S(1)} %get-tuple-element.81.refs_3_, ...), custom_call_target="tpu_custom_call" | custom-call | tf_op jit(solution)/shard_map/pallas_call | solution.py:60
  92.6 1.4 %shard_map.169 = (f32[64,1024]{1,0:T(8,128)}, f32[64,1024]{1,0:T(8,128)}, f32[32,1024]{1,0:T(8,128)}) custom-call(s32[13]{0:T(128)S(1)} %stack.55.refs_0_, bf16[160,1024]{1,0:T(8,128)(2,1)S(1)} %get-tuple-element.75.refs_3_.refs_1_, bf16[160,1024]{1,0:T(8,128)(2,1)S(1)} %collective-permute-done.28.refs_2_, f32[8,128]{1,0:T(8,128)S(1)} %copy-done.5), custom_call_target="tpu_custom_call" | custom-call | tf_op jit(solution)/shard_map/pallas_call | solution.py:60
  (104 shorter events, 33.1 us)
Async XLA Ops:
  0.6 12.1 %copy-start = (bf16[1024,1024]{1,0:T(8,128)(2,1)S(1)}, bf16[1024,1024]{1,0:T(8,128)(2,1)}, u32[]{:S(2)}) copy-start(bf16[1024,1024]{1,0:T(8,128)(2,1)} %param.13) | copy-start | bytes 6291460
  0.6 9.0 %collective-permute-start.4 = (s32[8,128]{1,0:T(8,128)}, s32[8,128]{1,0:T(8,128)S(1)}, u32[]{:S(2)}, u32[]{:S(2)}) collective-permute-start(s32[8,128]{1,0:T(8,128)} %bitcast.38), channel_id=1, source_target_pairs={{0,4},{4,0},{8,12},{12,8},{16,20},{20,16},{24,28},{28,24},{1,5},{5... | collective-permute-start | bytes 12296 | tf_op jit(solution)/shard_map/ppermute | solution.py:38
  1.2 10.9 %collective-permute-start.3 = (bf16[128,2048]{1,0:T(8,128)(2,1)}, bf16[128,2048]{1,0:T(8,128)(2,1)S(1)}, u32[]{:S(2)}, u32[]{:S(2)}) collective-permute-start(bf16[128,2048]{1,0:T(8,128)(2,1)} %refs_1_.5), channel_id=1, source_target_pairs={{0,4},{4,0},{8,12},{12,8},{16,20},{20,16},{24,28},{28,24},{1,5},{5... | collective-permute-start | bytes 1572872 | tf_op jit(solution)/shard_map/ppermute | solution.py:38
  2.4 7.3 %copy-start.6 = (s32[128,8]{0,1:T(8,128)S(1)}, s32[128,8]{0,1:T(8,128)}, u32[]{:S(2)}) copy-start(s32[128,8]{0,1:T(8,128)} %param.9) | copy-start | bytes 12292
  4.1 8.0 %copy-start.3 = (bf16[128,2048]{1,0:T(8,128)(2,1)S(1)}, bf16[128,2048]{1,0:T(8,128)(2,1)}, u32[]{:S(2)}) copy-start(bf16[128,2048]{1,0:T(8,128)(2,1)} %refs_1_.5) | copy-start | bytes 1572868
  4.1 16.0 %collective-permute-start = (bf16[64,1024]{1,0:T(8,128)(2,1)}, bf16[64,1024]{1,0:T(8,128)(2,1)S(1)}, u32[]{:S(2)}, u32[]{:S(2)}) collective-permute-start(bf16[64,1024]{1,0:T(8,128)(2,1)} %get-tuple-element.49), channel_id=1, source_target_pairs={{0,1},{1,0},{2,3},{3,2},{4,5},{5,4},{6,7},{7,6},{8,9},{9,8},{10,11... | collective-permute-start | bytes 393224 | tf_op jit(solution)/shard_map/ppermute | solution.py:38
  7.1 13.1 %collective-permute-start.1 = (bf16[64,1024]{1,0:T(8,128)(2,1)}, bf16[64,1024]{1,0:T(8,128)(2,1)S(1)}, u32[]{:S(2)}, u32[]{:S(2)}) collective-permute-start(bf16[64,1024]{1,0:T(8,128)(2,1)} %get-tuple-element.50), channel_id=1, source_target_pairs={{0,2},{1,3},{2,0},{3,1},{4,6},{5,7},{6,4},{7,5},{8,10},{9,11},{10,... | collective-permute-start | bytes 393224 | tf_op jit(solution)/shard_map/ppermute | solution.py:38
  9.7 10.5 %collective-permute-start.2 = (bf16[64,1024]{1,0:T(8,128)(2,1)}, bf16[64,1024]{1,0:T(8,128)(2,1)}, u32[]{:S(2)}, u32[]{:S(2)}) collective-permute-start(bf16[64,1024]{1,0:T(8,128)(2,1)} %get-tuple-element.51), channel_id=1, source_target_pairs={{0,3},{1,2},{2,1},{3,0},{4,7},{5,6},{6,5},{7,4},{8,11},{9,10},{10,... | collective-permute-start | bytes 393224 | tf_op jit(solution)/shard_map/ppermute | solution.py:38
  22.0 3.0 %collective-permute-start.5 = (bf16[256,1024]{1,0:T(8,128)(2,1)S(1)}, bf16[256,1024]{1,0:T(8,128)(2,1)S(1)}, u32[]{:S(2)}, u32[]{:S(2)}) collective-permute-start(bf16[256,1024]{1,0:T(8,128)(2,1)S(1)} %shard_map.148.refs_2_.refs_1_), channel_id=1, source_target_pairs={{0,4},{4,0},{8,12},{12,8},{16,20},{20,16},{24,28},{28,24},{1,5},{5... | collective-permute-start | bytes 1572872 | tf_op jit(solution)/shard_map/ppermute | solution.py:38
  24.4 12.8 %collective-permute-start.7 = (bf16[128,1024]{1,0:T(8,128)(2,1)S(1)}, bf16[128,1024]{1,0:T(8,128)(2,1)S(1)}, u32[]{:S(2)}, u32[]{:S(2)}) collective-permute-start(bf16[128,1024]{1,0:T(8,128)(2,1)S(1)} %get-tuple-element.106), channel_id=1, source_target_pairs={{0,4},{4,0},{8,12},{12,8},{16,20},{20,16},{24,28},{28,24},{1,5},{5... | collective-permute-start | bytes 786440 | tf_op jit(solution)/shard_map/ppermute | solution.py:38
  28.2 6.7 %collective-permute-start.6 = (bf16[512,1024]{1,0:T(8,128)(2,1)S(1)}, bf16[512,1024]{1,0:T(8,128)(2,1)S(1)}, u32[]{:S(2)}, u32[]{:S(2)}) collective-permute-start(bf16[512,1024]{1,0:T(8,128)(2,1)S(1)} %get-tuple-element.112), channel_id=1, source_target_pairs={{0,4},{4,0},{8,12},{12,8},{16,20},{20,16},{24,28},{28,24},{1,5},{5... | collective-permute-start | bytes 3145736 | tf_op jit(solution)/shard_map/ppermute | solution.py:38
  29.0 20.3 %collective-permute-start.10 = (bf16[512,1024]{1,0:T(8,128)(2,1)S(1)}, bf16[512,1024]{1,0:T(8,128)(2,1)S(1)}, u32[]{:S(2)}, u32[]{:S(2)}) collective-permute-start(bf16[512,1024]{1,0:T(8,128)(2,1)S(1)} %convolution_convert_fusion.3.refs_2_), channel_id=1, source_target_pairs={{0,8},{4,20},{8,0},{12,28},{16,24},{20,4},{24,16},{28,12},{1,9},{5... | collective-permute-start | bytes 3145736 | tf_op jit(solution)/shard_map/ppermute | solution.py:38
  31.4 25.6 %collective-permute-start.13 = (bf16[512,1024]{1,0:T(8,128)(2,1)S(1)}, bf16[512,1024]{1,0:T(8,128)(2,1)S(1)}, u32[]{:S(2)}, u32[]{:S(2)}) collective-permute-start(bf16[512,1024]{1,0:T(8,128)(2,1)S(1)} %convolution_convert_fusion.2.refs_3_), channel_id=1, source_target_pairs={{0,1},{1,0},{2,3},{3,2},{4,5},{5,4},{6,7},{7,6},{8,9},{9,8},{10,11... | collective-permute-start | bytes 3145736 | tf_op jit(solution)/shard_map/ppermute | solution.py:38
  37.9 9.1 %collective-permute-start.8 = (bf16[128,1152]{1,0:T(8,128)(2,1)S(1)}, bf16[128,1152]{1,0:T(8,128)(2,1)S(1)}, u32[]{:S(2)}, u32[]{:S(2)}) collective-permute-start(bf16[128,1152]{1,0:T(8,128)(2,1)S(1)} %get-tuple-element.58), channel_id=1, source_target_pairs={{0,8},{4,20},{8,0},{12,28},{16,24},{20,4},{24,16},{28,12},{1,9},{5... | collective-permute-start | bytes 884744 | tf_op jit(solution)/shard_map/ppermute | solution.py:38
  40.9 17.9 %collective-permute-start.12 = (bf16[256,1024]{1,0:T(8,128)(2,1)S(1)}, bf16[256,1024]{1,0:T(8,128)(2,1)S(1)}, u32[]{:S(2)}, u32[]{:S(2)}) collective-permute-start(bf16[256,1024]{1,0:T(8,128)(2,1)S(1)} %get-tuple-element.63), channel_id=1, source_target_pairs={{0,8},{4,20},{8,0},{12,28},{16,24},{20,4},{24,16},{28,12},{1,9},{5... | collective-permute-start | bytes 1572872 | tf_op jit(solution)/shard_map/ppermute | solution.py:38
  47.7 6.1 %collective-permute-start.9 = (bf16[64,1152]{1,0:T(8,128)(2,1)S(1)}, bf16[64,1152]{1,0:T(8,128)(2,1)S(1)}, u32[]{:S(2)}, u32[]{:S(2)}) collective-permute-start(bf16[64,1152]{1,0:T(8,128)(2,1)S(1)} %get-tuple-element.61), channel_id=1, source_target_pairs={{0,16},{4,12},{8,24},{12,4},{16,0},{20,28},{24,8},{28,20},{1,17},{... | collective-permute-start | bytes 442376 | tf_op jit(solution)/shard_map/ppermute | solution.py:38
  50.1 14.1 %collective-permute-start.17 = (bf16[256,1024]{1,0:T(8,128)(2,1)S(1)}, bf16[256,1024]{1,0:T(8,128)(2,1)S(1)}, u32[]{:S(2)}, u32[]{:S(2)}) collective-permute-start(bf16[256,1024]{1,0:T(8,128)(2,1)S(1)} %get-tuple-element.68), channel_id=1, source_target_pairs={{0,16},{4,12},{8,24},{12,4},{16,0},{20,28},{24,8},{28,20},{1,17},{... | collective-permute-start | bytes 1572872 | tf_op jit(solution)/shard_map/ppermute | solution.py:38
  54.3 7.0 %collective-permute-start.11 = (bf16[64,1152]{1,0:T(8,128)(2,1)S(1)}, bf16[64,1152]{1,0:T(8,128)(2,1)S(1)}, u32[]{:S(2)}, u32[]{:S(2)}) collective-permute-start(bf16[64,1152]{1,0:T(8,128)(2,1)S(1)} %shard_map.157.refs_3_.refs_1_), channel_id=1, source_target_pairs={{0,1},{1,0},{2,3},{3,2},{4,5},{5,4},{6,7},{7,6},{8,9},{9,8},{10,11... | collective-permute-start | bytes 442376 | tf_op jit(solution)/shard_map/ppermute | solution.py:38
  57.8 9.2 %collective-permute-start.16 = (bf16[256,1024]{1,0:T(8,128)(2,1)S(1)}, bf16[256,1024]{1,0:T(8,128)(2,1)S(1)}, u32[]{:S(2)}, u32[]{:S(2)}) collective-permute-start(bf16[256,1024]{1,0:T(8,128)(2,1)S(1)} %get-tuple-element.67), channel_id=1, source_target_pairs={{0,8},{4,20},{8,0},{12,28},{16,24},{20,4},{24,16},{28,12},{1,9},{5... | collective-permute-start | bytes 1572872 | tf_op jit(solution)/shard_map/ppermute | solution.py:38
  59.4 12.5 %collective-permute-start.15 = (bf16[128,1024]{1,0:T(8,128)(2,1)S(1)}, bf16[128,1024]{1,0:T(8,128)(2,1)S(1)}, u32[]{:S(2)}, u32[]{:S(2)}) collective-permute-start(bf16[128,1024]{1,0:T(8,128)(2,1)S(1)} %get-tuple-element.66), channel_id=1, source_target_pairs={{0,1},{1,0},{2,3},{3,2},{4,5},{5,4},{6,7},{7,6},{8,9},{9,8},{10,11... | collective-permute-start | bytes 786440 | tf_op jit(solution)/shard_map/ppermute | solution.py:38
  61.9 12.2 %collective-permute-start.14 = (bf16[64,1152]{1,0:T(8,128)(2,1)S(1)}, bf16[64,1152]{1,0:T(8,128)(2,1)S(1)}, u32[]{:S(2)}, u32[]{:S(2)}) collective-permute-start(bf16[64,1152]{1,0:T(8,128)(2,1)S(1)} %shard_map.160.refs_3_.refs_1_), channel_id=1, source_target_pairs={{0,2},{1,3},{2,0},{3,1},{4,6},{5,7},{6,4},{7,5},{8,10},{9,11},{10,... | collective-permute-start | bytes 442376 | tf_op jit(solution)/shard_map/ppermute | solution.py:38
  64.9 10.6 %collective-permute-start.19 = (bf16[128,1024]{1,0:T(8,128)(2,1)S(1)}, bf16[128,1024]{1,0:T(8,128)(2,1)S(1)}, u32[]{:S(2)}, u32[]{:S(2)}) collective-permute-start(bf16[128,1024]{1,0:T(8,128)(2,1)S(1)} %get-tuple-element.72), channel_id=1, source_target_pairs={{0,1},{1,0},{2,3},{3,2},{4,5},{5,4},{6,7},{7,6},{8,9},{9,8},{10,11... | collective-permute-start | bytes 786440 | tf_op jit(solution)/shard_map/ppermute | solution.py:38
  67.7 9.8 %collective-permute-start.20 = (bf16[128,1024]{1,0:T(8,128)(2,1)S(1)}, bf16[128,1024]{1,0:T(8,128)(2,1)S(1)}, u32[]{:S(2)}, u32[]{:S(2)}) collective-permute-start(bf16[128,1024]{1,0:T(8,128)(2,1)S(1)} %get-tuple-element.73), channel_id=1, source_target_pairs={{0,16},{4,12},{8,24},{12,4},{16,0},{20,28},{24,8},{28,20},{1,17},{... | collective-permute-start | bytes 786440 | tf_op jit(solution)/shard_map/ppermute | solution.py:38
  72.5 5.0 %collective-permute-start.21 = (bf16[64,1024]{1,0:T(8,128)(2,1)S(1)}, bf16[64,1024]{1,0:T(8,128)(2,1)S(1)}, u32[]{:S(2)}, u32[]{:S(2)}) collective-permute-start(bf16[64,1024]{1,0:T(8,128)(2,1)S(1)} %get-tuple-element.74), channel_id=1, source_target_pairs={{0,16},{4,12},{8,24},{12,4},{16,0},{20,28},{24,8},{28,20},{1,17},{... | collective-permute-start | bytes 393224 | tf_op jit(solution)/shard_map/ppermute | solution.py:38
  74.7 5.2 %collective-permute-start.18 = (bf16[64,1152]{1,0:T(8,128)(2,1)S(1)}, bf16[64,1152]{1,0:T(8,128)(2,1)S(1)}, u32[]{:S(2)}, u32[]{:S(2)}) collective-permute-start(bf16[64,1152]{1,0:T(8,128)(2,1)S(1)} %shard_map.164.refs_7_.refs_1_), channel_id=1, source_target_pairs={{0,16},{4,12},{8,24},{12,4},{16,0},{20,28},{24,8},{28,20},{1,17},{... | collective-permute-start | bytes 442376 | tf_op jit(solution)/shard_map/ppermute | solution.py:38
  78.2 13.7 %collective-permute-start.28 = (bf16[160,1024]{1,0:T(8,128)(2,1)S(1)}, bf16[160,1024]{1,0:T(8,128)(2,1)S(1)}, u32[]{:S(2)}, u32[]{:S(2)}) collective-permute-start(bf16[160,1024]{1,0:T(8,128)(2,1)S(1)} %get-tuple-element.85), channel_id=1, source_target_pairs={{0,2},{1,3},{2,0},{3,1},{4,6},{5,7},{6,4},{7,5},{8,10},{9,11},{10,... | collective-permute-start | bytes 983048 | tf_op jit(solution)/shard_map/ppermute | solution.py:38
  80.5 4.7 %collective-permute-start.22 = (bf16[128,384]{1,0:T(8,128)(2,1)S(1)}, bf16[128,384]{1,0:T(8,128)(2,1)S(1)}, u32[]{:S(2)}, u32[]{:S(2)}) collective-permute-start(bf16[128,384]{1,0:T(8,128)(2,1)S(1)} %get-tuple-element.76.refs_1_.refs_7_), channel_id=1, source_target_pairs={{0,8},{4,20},{8,0},{12,28},{16,24},{20,4},{24,16},{28,12},{1,9},{5... | collective-permute-start | bytes 294920 | tf_op jit(solution)/shard_map/ppermute | solution.py:38
  81.6 4.6 %collective-permute-start.23 = (bf16[128,384]{1,0:T(8,128)(2,1)S(1)}, bf16[128,384]{1,0:T(8,128)(2,1)S(1)}, u32[]{:S(2)}, u32[]{:S(2)}) collective-permute-start(bf16[128,384]{1,0:T(8,128)(2,1)S(1)} %get-tuple-element.77.refs_2_), channel_id=1, source_target_pairs={{0,8},{4,20},{8,0},{12,28},{16,24},{20,4},{24,16},{28,12},{1,9},{5... | collective-permute-start | bytes 294920 | tf_op jit(solution)/shard_map/ppermute | solution.py:38
  82.6 4.7 %collective-permute-start.24 = (bf16[128,384]{1,0:T(8,128)(2,1)S(1)}, bf16[128,384]{1,0:T(8,128)(2,1)S(1)}, u32[]{:S(2)}, u32[]{:S(2)}) collective-permute-start(bf16[128,384]{1,0:T(8,128)(2,1)S(1)} %get-tuple-element.78.refs_3_), channel_id=1, source_target_pairs={{0,8},{4,20},{8,0},{12,28},{16,24},{20,4},{24,16},{28,12},{1,9},{5... | collective-permute-start | bytes 294920 | tf_op jit(solution)/shard_map/ppermute | solution.py:38
  87.8 1.5 %collective-permute-start.25 = (bf16[256,384]{1,0:T(8,128)(2,1)S(1)}, bf16[256,384]{1,0:T(8,128)(2,1)S(1)}, u32[]{:S(2)}, u32[]{:S(2)}) collective-permute-start(bf16[256,384]{1,0:T(8,128)(2,1)S(1)} %get-tuple-element.79.refs_1_.refs_7_), channel_id=1, source_target_pairs={{0,4},{4,0},{8,12},{12,8},{16,20},{20,16},{24,28},{28,24},{1,5},{5... | collective-permute-start | bytes 589832 | tf_op jit(solution)/shard_map/ppermute | solution.py:38
  87.9 1.7 %collective-permute-start.26 = (bf16[256,384]{1,0:T(8,128)(2,1)S(1)}, bf16[256,384]{1,0:T(8,128)(2,1)S(1)}, u32[]{:S(2)}, u32[]{:S(2)}) collective-permute-start(bf16[256,384]{1,0:T(8,128)(2,1)S(1)} %get-tuple-element.80.refs_2_), channel_id=1, source_target_pairs={{0,4},{4,0},{8,12},{12,8},{16,20},{20,16},{24,28},{28,24},{1,5},{5... | collective-permute-start | bytes 589832 | tf_op jit(solution)/shard_map/ppermute | solution.py:38
  88.4 1.5 %collective-permute-start.27 = (bf16[256,384]{1,0:T(8,128)(2,1)S(1)}, bf16[256,384]{1,0:T(8,128)(2,1)S(1)}, u32[]{:S(2)}, u32[]{:S(2)}) collective-permute-start(bf16[256,384]{1,0:T(8,128)(2,1)S(1)} %get-tuple-element.81.refs_3_), channel_id=1, source_target_pairs={{0,4},{4,0},{8,12},{12,8},{16,20},{20,16},{24,28},{28,24},{1,5},{5... | collective-permute-start | bytes 589832 | tf_op jit(solution)/shard_map/ppermute | solution.py:38
  (7 other events, 16.3 us)

commit v5 on v4

--- a/solution.py
+++ b/solution.py
@@ -74,21 +74,27 @@
     )(numbers, *ins, *after)
 
 
-def sort_body(patch, part, own, numbers, grad, *blocks):
+def sort_body(patch, part, own, masks, numbers, grad, *blocks):
     size = own * part
     row = lax.broadcasted_iota(jnp.int32, (size, grad.shape[0]), 0)
     source = lax.broadcasted_iota(jnp.int32, (size, grad.shape[0]), 1)
-    for m, block in enumerate(blocks):
+    for m, block in zip(masks, blocks):
         wanted = (row % part) * patch + numbers[m] * own + row // part
         block[...] = times((source == wanted).astype(BF), grad[...]).astype(BF)
 
 
-def join_body(part, own, count, numbers, *refs):
-    blocks, joined = refs[:-1], refs[-1]
+def join_body(part, own, count, share_count, height, numbers, ids_own, *refs):
+    blocks, joined, mine = refs[:-2], refs[-2], refs[-1]
     for m, block in enumerate(blocks):
         for j in range(own):
             start = pl.multiple_of((j * count + numbers[m]) * part, part)
             joined[pl.ds(start, part), :] = block[j * part : (j + 1) * part, :]
+    line = vocab_line(numbers, count, 2 * share_count, height)
+    ids = ids_own[...].T
+    patches = ids.shape[0]
+    for j in range(own):
+        wanted = id_of(ids, numbers[0] * own + j)
+        mine[j * patches : (j + 1) * patches, :] = hot(wanted, line)
 
 
 def sent_order(count):
@@ -121,11 +127,10 @@
             both[pl.ds(start, patches), :] = value[:, j * width : (j + 1) * width]
 
 
-def hots_body(own, tp_count, share_count, height, core_at, numbers, ids_own, ids_other, prev, here, mine):
+def hots_body(own, tp_count, share_count, height, core_at, numbers, ids_own, ids_other, prev, here):
     patches = ids_own.shape[1]
     plain = lax.broadcasted_iota(jnp.int32, (1, prev.shape[1]), 1)
     line = vocab_line(numbers, tp_count, share_count, height)
-    both = vocab_line(numbers, tp_count, 2 * share_count, height)
     core = numbers[core_at]
     for side, which in ((core, ids_own), (1 - core, ids_other)):
         ids = which[...].T
@@ -135,9 +140,6 @@
             before = id_of(ids, numbers[0] * own + j - 1)
             prev[at, :] = hot(before, plain)
             here[at, :] = hot(before, line)
-            if which is ids_own:
-                wanted = id_of(ids, numbers[0] * own + j)
-                mine[j * patches : (j + 1) * patches, :] = hot(wanted, both)
 
 
 def turn_matrix(tp_count, chunk, numbers):
@@ -222,10 +224,6 @@
         rows = [mine[:, i * 128 : (i + 1) * 128] for i in range(lines)]
         rows.append(jnp.zeros((16 - lines, 128), F32))
         target[first : first + 16, width:] = jnp.concatenate(rows, axis=0).astype(BF)
-
-
-def gate_body(numbers, value, same):
-    pass
 
 
 def add_body(numbers, kept, arrived, keep, send):
@@ -355,34 +353,26 @@
             return swap(value, "seq", (1 << walks[0][k], 1 << walks[1][k]))
         return swap(value, "tp", (1 << k,))
 
-    def gate(value, after):
-        there = pl.BlockSpec(memory_space=pl.ANY)
-        (value,) = call(
-            gate_body,
-            [like(*value.shape, value.dtype)],
-            [value],
-            after,
-            in_specs=[there],
-            out_specs=[there],
-            alias={1: 0},
-        )
-        return value
-
     ids_own = byte_ids.T
     ids_other = core_swap(ids_own)
     out_other = core_swap(global_out)
-    blocks = call(
-        functools.partial(sort_body, patch, part, own),
-        [like(own * part, width, BF)] * tp_count,
-        [out_grad],
-        [],
-        flops=STEP,
-    )
-    blocks = [swap(b, "tp", (m,)) if m else b for m, b in enumerate(blocks)]
+    blocks, first_rows = {}, []
+    for masks in (list(range(2, tp_count)), [1, 0]):
+        sorted_rows = call(
+            functools.partial(sort_body, patch, part, own, masks),
+            [like(own * part, width, BF)] * len(masks),
+            [out_grad],
+            first_rows,
+            flops=STEP,
+        )
+        first_rows = sorted_rows[:1]
+        for m, value in zip(masks, sorted_rows):
+            blocks[m] = swap(value, "tp", (m,)) if m else value
+    blocks = [blocks[m] for m in range(tp_count)]
     far = pl.BlockSpec(memory_space=pltpu.HBM)
-    prev_hot, prev_here, own_hot = call(
+    prev_hot, prev_here = call(
         functools.partial(hots_body, own, tp_count, share_count, height, core_at),
-        [like(2 * rows, vocab, BF), like(2 * rows, vocab // 2, BF), like(rows, vocab, BF)],
+        [like(2 * rows, vocab, BF), like(2 * rows, vocab // 2, BF)],
         [ids_own, ids_other],
         [blocks[0]],
     )
@@ -396,7 +386,8 @@
         [global_out, out_other],
         [prev_hot],
     )
-    u_rows = times(slot_in, proj_weight) + times(prev_hot, emb_local)
+    before = jnp.dot(prev_hot, emb_local, preferred_element_type=BF)
+    u_rows = times(slot_in, proj_weight) + before.astype(F32)
     scale = lax.rsqrt(jnp.mean(u_rows * u_rows, axis=1, keepdims=True) + 1e-05)
     normed = u_rows * scale
     r_rows = (normed * norm_gain).astype(BF)
@@ -408,7 +399,15 @@
         in_specs=[far],
         scratch=[VMEM((share_count, width, chunk), BF), pltpu.SemaphoreType.DMA((share_count,))],
     )
-    a_rows = times(r_rows, up_here)
+    grad_own, own_hot = call(
+        functools.partial(join_body, part, own, tp_count, share_count, height),
+        [like(rows, width, BF), like(rows, vocab, BF)],
+        [ids_own, *blocks],
+        [up_here],
+        numbers=numbers,
+    )
+    up_later, _ = lax.optimization_barrier((up_here, grad_own))
+    a_rows = times(r_rows, up_later)
     sig = jax.nn.sigmoid(a_rows)
     h_rows = (a_rows * sig).astype(BF)
     slope = (sig * (1.0 + a_rows * (1.0 - sig))).astype(BF)
@@ -431,14 +430,7 @@
         axis=1,
     )
 
-    (grad_own,) = call(
-        functools.partial(join_body, part, own, tp_count),
-        [like(rows, width, BF)],
-        blocks,
-        [h_rows],
-    )
     grad_other = core_swap(grad_own)
-    own_hot = gate(own_hot, [grad_own])
     glob = [
         inner(own_hot[j * patches : (j + 1) * patches], value)
         for j, value in enumerate(by_slot(global_in_grad))
@@ -529,7 +521,7 @@
     up_sent = inner(da_rows[:, half:], r_rows).astype(kind)
     down = Chain(down_kept, down_sent, seq_steps + tp_steps)
     up = Chain(up_kept, up_sent, tp_steps[:1] + seq_steps + tp_steps[1:])
-    dr_more = gate(core_swap(dr_sent), [down_sent, up_sent])
+    dr_more = core_swap(dr_sent)
     dr_rows = dr_part + dr_more.astype(F32)
 
     gain_part = jnp.sum(dr_rows * normed, axis=0, keepdims=True)
@@ -559,7 +551,8 @@
         [table.kept],
     )
     proj = Chain(kept, sent, seq_steps[:1] + tp_steps[:1] + seq_steps[1:] + tp_steps[1:])
-    du_own = lax.dynamic_slice_in_dim(du_rows, core * rows, rows, 0)
+    du_later, _ = lax.optimization_barrier((du_rows, proj.kept))
+    du_own = lax.dynamic_slice_in_dim(du_later, core * rows, rows, 0)
     back = outer(du_own, proj_weight).astype(BF)
     glob_out_grad = jnp.concatenate(
         [back[j * patches : (j + 1) * patches] for j in range(own)], axis=1

time: 94.7 us -> 96.7 us (1.021)
  waiting for transfers between devices: 20.4 us -> 22.3 us
  starting transfers between devices: 31.4 us -> 30.4 us
    ppermute x29, waiting for transfers between devices: 20.4 us -> 22.3 us  [swap(): return lax.ppermute(value, axis, pairs)]
    dot_general x0 -> x1, matrix products: none -> 1.48 us  [on_device(): before = jnp.dot(prev_hot, emb_local, preferred_element_type=BF)]
    dot_general x3 -> x2, matrix products: 4.7 us -> 3.22 us  [times(): return jnp.dot(left, right, preferred_element_type=F32)]
    ppermute x29, starting transfers between devices: 31.4 us -> 30.4 us  [swap(): return lax.ppermute(value, axis, pairs)]
    unnamed x26 -> x20, local copies, waits for them, and re-layouts: 2.63 us -> 3.37 us
    pallas_call x26 -> x25, Pallas kernels: 23.4 us -> 23.4 us  [run(): pl.pallas_call(kernel, out_shape=tuple(outs), grid_spec=pltpu.PrefetchSca...]
  transfers between devices with their start and end apart: 29 -> 29, of which waited for: 15 -> 15; matrix products, arithmetic and copies ran while one was open for 16% -> 16% of each run, Pallas kernels for 21% -> 20%
where the time goes in v5:
time: 96.7 us; the launch traced here: 95.5 us
  starting transfers between devices  30.4 us (31%)
  Pallas kernels  23.4 us (24%)
  waiting for transfers between devices  22.3 us (23%)
  matrix products  12.7 us (13%)
  local copies, waits for them, and re-layouts  3.88 us (4%)
  other arithmetic  1.78 us (2%)
  between operations  1.13 us (1%)
    ppermute x29, starting transfers between devices, swap(): return lax.ppermute(value, axis, pairs)  30.4 us
    pallas_call x25, Pallas kernels, run(): pl.pallas_call(kernel, out_shape=tuple(outs), grid_spec=pltpu.PrefetchSca...  23.4 us
    ppermute x29, waiting for transfers between devices, swap(): return lax.ppermute(value, axis, pairs)  22.3 us
    dot_general x8, matrix products, inner(): lax.dot_general(left, right, (((0,), (0,)), ((), ())), preferred_element_...  4.6 us
    dot_general x3, matrix products, outer(): lax.dot_general(left, right, (((1,), (1,)), ((), ())), preferred_element_...  3.38 us
    unnamed x20, local copies, waits for them, and re-layouts  3.37 us
    dot_general x2, matrix products, times(): return jnp.dot(left, right, preferred_element_type=F32)  3.22 us
  transfers between devices with their start and end apart: 29, of which 15 were waited for; matrix products, arithmetic and copies ran while one was open for 16% of the time, Pallas kernels for 20%

profile of v5, /device:TPU:0, one launch (start us, length us, event | category | flops | bytes accessed | tf_op | source)
XLA Modules:
  0.0 95.5 jit_solution(15466582875849186392)
XLA Ops:
  0.8 1.2 %copy-done.7 = bf16[256,1024]{1,0:T(8,128)(2,1)S(1)} copy-done((bf16[256,1024]{1,0:T(8,128)(2,1)S(1)}, bf16[256,1024]{1,0:T(8,128)(2,1)}, u32[]{:S(2)}) %copy-start.7) | copy-done | bytes 524312
  1.9 1.5 %shard_map.144 = (bf16[64,1024]{1,0:T(8,128)(2,1)}, bf16[64,1024]{1,0:T(8,128)(2,1)}) custom-call(s32[13]{0:T(128)S(1)} %stack.55.refs_0_, bf16[256,1024]{1,0:T(8,128)(2,1)S(1)} %copy-done.7), custom_call_target="tpu_custom_call" | custom-call | flops 6000000000 | tf_op jit(solution)/shard_map/pallas_call | solution.py:60
  3.4 4.0 %collective-permute-start.1 = (bf16[64,1024]{1,0:T(8,128)(2,1)}, bf16[64,1024]{1,0:T(8,128)(2,1)S(1)}, u32[]{:S(2)}, u32[]{:S(2)}) collective-permute-start(bf16[64,1024]{1,0:T(8,128)(2,1)} %get-tuple-element.51.refs_2_), channel_id=1, source_target_pairs={{0,2},{1,3},{2,0},{3,1},{4,6},{5,7},{6,4},{7,5},{8,10},{9,11},{10,... | collective-permute-start | bytes 393224 | tf_op jit(solution)/shard_map/ppermute | solution.py:38
  8.0 1.4 %shard_map.145 = (bf16[64,1024]{1,0:T(8,128)(2,1)}, bf16[64,1024]{1,0:T(8,128)(2,1)S(1)}) custom-call(s32[13]{0:T(128)S(1)} %stack.55.refs_0_, bf16[256,1024]{1,0:T(8,128)(2,1)S(1)} %copy-done.7, bf16[64,1024]{1,0:T(8,128)(2,1)} %get-tuple-element.51.refs_2_), custom_call_target="tpu_custom_call" | custom-call | flops 6000000000 | tf_op jit(solution)/shard_map/pallas_call | solution.py:60
  9.4 1.6 %collective-permute-start = (bf16[64,1024]{1,0:T(8,128)(2,1)}, bf16[64,1024]{1,0:T(8,128)(2,1)S(1)}, u32[]{:S(2)}, u32[]{:S(2)}) collective-permute-start(bf16[64,1024]{1,0:T(8,128)(2,1)} %get-tuple-element.53), channel_id=1, source_target_pairs={{0,1},{1,0},{2,3},{3,2},{4,5},{5,4},{6,7},{7,6},{8,9},{9,8},{10,11... | collective-permute-start | bytes 393224 | tf_op jit(solution)/shard_map/ppermute | solution.py:38
  11.9 1.5 %fusion.39 = bf16[512,1024]{1,0:T(8,128)(2,1)S(1)} fusion(bf16[512,256]{1,0:T(8,128)(2,1)S(1)} %get-tuple-element.55.refs_3_, bf16[256,1024]{1,0:T(8,128)(2,1)} %param.14), kind=kOutput, calls=%fused_computation.63 | convolution fusion | flops 268435456 | bytes 1835008 | tf_op jit(solution)/shard_map/dot_general | solution.py:389
  14.0 1.4 %multiply_reduce_fusion.2 = (f32[512]{0:T(512)S(1)}, f32[512,1024]{1,0:T(8,128)S(1)}) fusion(bf16[512,1024]{1,0:T(8,128)(2,1)S(1)} %fusion.39, bf16[512,1024]{1,0:T(8,128)(2,1)S(1)} %shard_map.147, bf16[1024,1024]{1,0:T(8,128)(2,1)S(1)} %copy-done), kind=kOutput, calls=%fused_computation.9 | convolution fusion | flops 1075838464 | bytes 6293504 | tf_op jit(solution)/shard_map/dot_general | solution.py:32
  16.2 2.6 %shard_map.148.refs_6_ = bf16[1024,1024]{1,0:T(8,128)(2,1)S(1)} custom-call(s32[13]{0:T(128)S(1)} %stack.55.refs_0_, bf16[1024,2048]{1,0:T(8,128)(2,1)S(1)} %copy-done.1, bf16[512,1024]{1,0:T(8,128)(2,1)S(1)} %multiply_convert_fusion.3.refs_2_), custom_call_target="tpu_custom_call" | custom-call | tf_op jit(solution)/shard_map/pallas_call | solution.py:60
  19.4 1.7 %shard_map.149 = (bf16[256,1024]{1,0:T(8,128)(2,1)S(1)}, bf16[256,256]{1,0:T(8,128)(2,1)S(1)}) custom-call(s32[13]{0:T(128)S(1)} %stack.55.refs_0_, s32[8,128]{1,0:T(8,128)S(1)} %bitcast.38, bf16[64,1024]{1,0:T(8,128)(2,1)S(1)} %get-tuple-element.52.refs_3_.refs_2_, bf16[64,1024]{1,0:T(8,128)(2,1)S(1)} %collective-permute-done.refs_3_, ...), custom_call_target="tpu_custom_call" | custom-call | tf_op jit(solution)/shard_map/pallas_call | solution.py:60
  21.3 1.8 %multiply_convert_fusion.1 = (bf16[512,1024]{1,0:T(8,128)(2,1)S(1)}, bf16[512,1024]{1,0:T(8,128)(2,1)S(1)}) fusion(bf16[512,1024]{1,0:T(8,128)(2,1)S(1)} %multiply_convert_fusion.3.refs_2_, bf16[1024,1024]{1,0:T(8,128)(2,1)S(1)} %shard_map.148.refs_6_), kind=kOutput, calls=%fused_computation.5 | convolution fusion | flops 1078984704 | bytes 5242880 | tf_op jit(solution)/shard_map/dot_general | solution.py:32
  27.2 1.3 %multiply_convert_fusion = bf16[512,1024]{1,0:T(8,128)(2,1)S(1)} fusion(bf16[512,1024]{1,0:T(8,128)(2,1)S(1)} %get-tuple-element.60, bf16[512,1024]{1,0:T(8,128)(2,1)S(1)} %shard_map.150, bf16[1024,1024]{1,0:T(8,128)(2,1)S(1)} %shard_map.151), kind=kOutput, calls=%fused_computation.4 | convolution fusion | flops 1075314688 | bytes 5242880 | tf_op jit(solution)/shard_map/dot_general | solution.py:26
  28.5 1.3 %fusion.38 = (bf16[512,1024]{1,0:T(8,128)(2,1)S(1)}, f32[512,1024]{1,0:T(8,128)S(1)}) fusion(bf16[512,1024]{1,0:T(8,128)(2,1)S(1)} %multiply_convert_fusion, bf16[1024,1024]{1,0:T(8,128)(2,1)S(1)} %shard_map.148.refs_6_), kind=kOutput, calls=%fused_computation.62 | convolution fusion | flops 1074266112 | bytes 6291456 | tf_op jit(solution)/shard_map/dot_general | solution.py:26
  31.1 1.7 %collective-permute-start.10 = (bf16[512,1024]{1,0:T(8,128)(2,1)S(1)}, bf16[512,1024]{1,0:T(8,128)(2,1)S(1)}, u32[]{:S(2)}, u32[]{:S(2)}) collective-permute-start(bf16[512,1024]{1,0:T(8,128)(2,1)S(1)} %convolution_convert_fusion.1), channel_id=1, source_target_pairs={{0,8},{4,20},{8,0},{12,28},{16,24},{20,4},{24,16},{28,12},{1,9},{5... | collective-permute-start | bytes 3145736 | tf_op jit(solution)/shard_map/ppermute | solution.py:38
  41.5 1.6 %collective-permute-start.12 = (bf16[256,1024]{1,0:T(8,128)(2,1)S(1)}, bf16[256,1024]{1,0:T(8,128)(2,1)S(1)}, u32[]{:S(2)}, u32[]{:S(2)}) collective-permute-start(bf16[256,1024]{1,0:T(8,128)(2,1)S(1)} %get-tuple-element.69), channel_id=1, source_target_pairs={{0,8},{4,20},{8,0},{12,28},{16,24},{20,4},{24,16},{28,12},{1,9},{5... | collective-permute-start | bytes 1572872 | tf_op jit(solution)/shard_map/ppermute | solution.py:38
  43.1 6.0 %collective-permute-done.8.refs_2_ = bf16[128,1152]{1,0:T(8,128)(2,1)S(1)} collective-permute-done((bf16[128,1152]{1,0:T(8,128)(2,1)S(1)}, bf16[128,1152]{1,0:T(8,128)(2,1)S(1)}, u32[]{:S(2)}, u32[]{:S(2)}) %collective-permute-start.8) | collective-permute-done | bytes 294944 | tf_op jit(solution)/shard_map/ppermute | solution.py:38
  49.8 1.7 %collective-permute-start.9 = (bf16[64,1152]{1,0:T(8,128)(2,1)S(1)}, bf16[64,1152]{1,0:T(8,128)(2,1)S(1)}, u32[]{:S(2)}, u32[]{:S(2)}) collective-permute-start(bf16[64,1152]{1,0:T(8,128)(2,1)S(1)} %get-tuple-element.67), channel_id=1, source_target_pairs={{0,16},{4,12},{8,24},{12,4},{16,0},{20,28},{24,8},{28,20},{1,17},{... | collective-permute-start | bytes 442376 | tf_op jit(solution)/shard_map/ppermute | solution.py:38
  52.7 2.7 %collective-permute-done.9.refs_2_ = bf16[64,1152]{1,0:T(8,128)(2,1)S(1)} collective-permute-done((bf16[64,1152]{1,0:T(8,128)(2,1)S(1)}, bf16[64,1152]{1,0:T(8,128)(2,1)S(1)}, u32[]{:S(2)}, u32[]{:S(2)}) %collective-permute-start.9) | collective-permute-done | bytes 147488 | tf_op jit(solution)/shard_map/ppermute | solution.py:38
  56.0 1.1 %collective-permute-start.11 = (bf16[64,1152]{1,0:T(8,128)(2,1)S(1)}, bf16[64,1152]{1,0:T(8,128)(2,1)S(1)}, u32[]{:S(2)}, u32[]{:S(2)}) collective-permute-start(bf16[64,1152]{1,0:T(8,128)(2,1)S(1)} %shard_map.156.refs_3_.refs_1_), channel_id=1, source_target_pairs={{0,1},{1,0},{2,3},{3,2},{4,5},{5,4},{6,7},{7,6},{8,9},{9,8},{10,11... | collective-permute-start | bytes 442376 | tf_op jit(solution)/shard_map/ppermute | solution.py:38
  57.1 1.6 %collective-permute-done.13.refs_2_ = bf16[512,1024]{1,0:T(8,128)(2,1)S(1)} collective-permute-done((bf16[512,1024]{1,0:T(8,128)(2,1)S(1)}, bf16[512,1024]{1,0:T(8,128)(2,1)S(1)}, u32[]{:S(2)}, u32[]{:S(2)}) %collective-permute-start.13) | collective-permute-done | bytes 1048608 | tf_op jit(solution)/shard_map/ppermute | solution.py:38
  59.5 1.4 %collective-permute-start.16 = (bf16[256,1024]{1,0:T(8,128)(2,1)S(1)}, bf16[256,1024]{1,0:T(8,128)(2,1)S(1)}, u32[]{:S(2)}, u32[]{:S(2)}) collective-permute-start(bf16[256,1024]{1,0:T(8,128)(2,1)S(1)} %get-tuple-element.73), channel_id=1, source_target_pairs={{0,8},{4,20},{8,0},{12,28},{16,24},{20,4},{24,16},{28,12},{1,9},{5... | collective-permute-start | bytes 1572872 | tf_op jit(solution)/shard_map/ppermute | solution.py:38
  63.1 2.8 %collective-permute-start.14 = (bf16[64,1152]{1,0:T(8,128)(2,1)S(1)}, bf16[64,1152]{1,0:T(8,128)(2,1)S(1)}, u32[]{:S(2)}, u32[]{:S(2)}) collective-permute-start(bf16[64,1152]{1,0:T(8,128)(2,1)S(1)} %shard_map.159.refs_3_.refs_1_), channel_id=1, source_target_pairs={{0,2},{1,3},{2,0},{3,1},{4,6},{5,7},{6,4},{7,5},{8,10},{9,11},{10,... | collective-permute-start | bytes 442376 | tf_op jit(solution)/shard_map/ppermute | solution.py:38
  66.6 1.3 %collective-permute-start.19 = (bf16[128,1024]{1,0:T(8,128)(2,1)S(1)}, bf16[128,1024]{1,0:T(8,128)(2,1)S(1)}, u32[]{:S(2)}, u32[]{:S(2)}) collective-permute-start(bf16[128,1024]{1,0:T(8,128)(2,1)S(1)} %get-tuple-element.78), channel_id=1, source_target_pairs={{0,1},{1,0},{2,3},{3,2},{4,5},{5,4},{6,7},{7,6},{8,9},{9,8},{10,11... | collective-permute-start | bytes 786440 | tf_op jit(solution)/shard_map/ppermute | solution.py:38
  70.0 2.8 %collective-permute-done.15.refs_2_ = bf16[128,1024]{1,0:T(8,128)(2,1)S(1)} collective-permute-done((bf16[128,1024]{1,0:T(8,128)(2,1)S(1)}, bf16[128,1024]{1,0:T(8,128)(2,1)S(1)}, u32[]{:S(2)}, u32[]{:S(2)}) %collective-permute-start.15) | collective-permute-done | bytes 262176 | tf_op jit(solution)/shard_map/ppermute | solution.py:38
  73.4 1.6 %collective-permute-start.21 = (bf16[64,1024]{1,0:T(8,128)(2,1)S(1)}, bf16[64,1024]{1,0:T(8,128)(2,1)S(1)}, u32[]{:S(2)}, u32[]{:S(2)}) collective-permute-start(bf16[64,1024]{1,0:T(8,128)(2,1)S(1)} %get-tuple-element.80), channel_id=1, source_target_pairs={{0,16},{4,12},{8,24},{12,4},{16,0},{20,28},{24,8},{28,20},{1,17},{... | collective-permute-start | bytes 393224 | tf_op jit(solution)/shard_map/ppermute | solution.py:38
  76.3 2.1 %collective-permute-done.21.refs_6_ = bf16[64,1024]{1,0:T(8,128)(2,1)S(1)} collective-permute-done((bf16[64,1024]{1,0:T(8,128)(2,1)S(1)}, bf16[64,1024]{1,0:T(8,128)(2,1)S(1)}, u32[]{:S(2)}, u32[]{:S(2)}) %collective-permute-start.21) | collective-permute-done | bytes 131104 | tf_op jit(solution)/shard_map/ppermute | solution.py:38
  79.1 1.9 %collective-permute-start.28 = (bf16[160,1024]{1,0:T(8,128)(2,1)S(1)}, bf16[160,1024]{1,0:T(8,128)(2,1)S(1)}, u32[]{:S(2)}, u32[]{:S(2)}) collective-permute-start(bf16[160,1024]{1,0:T(8,128)(2,1)S(1)} %get-tuple-element.91), channel_id=1, source_target_pairs={{0,2},{1,3},{2,0},{3,1},{4,6},{5,7},{6,4},{7,5},{8,10},{9,11},{10,... | collective-permute-start | bytes 983048 | tf_op jit(solution)/shard_map/ppermute | solution.py:38
  81.6 1.2 %collective-permute-start.22 = (bf16[128,384]{1,0:T(8,128)(2,1)S(1)}, bf16[128,384]{1,0:T(8,128)(2,1)S(1)}, u32[]{:S(2)}, u32[]{:S(2)}) collective-permute-start(bf16[128,384]{1,0:T(8,128)(2,1)S(1)} %get-tuple-element.82.refs_1_.refs_7_), channel_id=1, source_target_pairs={{0,8},{4,20},{8,0},{12,28},{16,24},{20,4},{24,16},{28,12},{1,9},{5... | collective-permute-start | bytes 294920 | tf_op jit(solution)/shard_map/ppermute | solution.py:38
  83.7 1.1 %collective-permute-start.24 = (bf16[128,384]{1,0:T(8,128)(2,1)S(1)}, bf16[128,384]{1,0:T(8,128)(2,1)S(1)}, u32[]{:S(2)}, u32[]{:S(2)}) collective-permute-start(bf16[128,384]{1,0:T(8,128)(2,1)S(1)} %get-tuple-element.84.refs_3_), channel_id=1, source_target_pairs={{0,8},{4,20},{8,0},{12,28},{16,24},{20,4},{24,16},{28,12},{1,9},{5... | collective-permute-start | bytes 294920 | tf_op jit(solution)/shard_map/ppermute | solution.py:38
  84.8 1.5 %collective-permute-done.22.refs_4_ = bf16[128,384]{1,0:T(8,128)(2,1)S(1)} collective-permute-done((bf16[128,384]{1,0:T(8,128)(2,1)S(1)}, bf16[128,384]{1,0:T(8,128)(2,1)S(1)}, u32[]{:S(2)}, u32[]{:S(2)}) %collective-permute-start.22) | collective-permute-done | bytes 98336 | tf_op jit(solution)/shard_map/ppermute | solution.py:38
  86.3 1.1 %collective-permute-done.23.refs_5_ = bf16[128,384]{1,0:T(8,128)(2,1)S(1)} collective-permute-done((bf16[128,384]{1,0:T(8,128)(2,1)S(1)}, bf16[128,384]{1,0:T(8,128)(2,1)S(1)}, u32[]{:S(2)}, u32[]{:S(2)}) %collective-permute-start.23) | collective-permute-done | bytes 98336 | tf_op jit(solution)/shard_map/ppermute | solution.py:38
  91.1 2.0 %shard_map.167 = (f32[256,1024]{1,0:T(8,128)}, f32[256,1024]{1,0:T(8,128)}, f32[8,128]{1,0:T(8,128)}) custom-call(s32[13]{0:T(128)S(1)} %stack.55.refs_0_, bf16[256,384]{1,0:T(8,128)(2,1)S(1)} %get-tuple-element.85.refs_1_.refs_7_, bf16[256,384]{1,0:T(8,128)(2,1)S(1)} %get-tuple-element.86.refs_2_, bf16[256,384]{1,0:T(8,128)(2,1)S(1)} %get-tuple-element.87.refs_3_, ...), custom_call_target="tpu_custom_call" | custom-call | tf_op jit(solution)/shard_map/pallas_call | solution.py:60
  94.1 1.4 %shard_map.168 = (f32[64,1024]{1,0:T(8,128)}, f32[64,1024]{1,0:T(8,128)}, f32[32,1024]{1,0:T(8,128)}) custom-call(s32[13]{0:T(128)S(1)} %stack.55.refs_0_, bf16[160,1024]{1,0:T(8,128)(2,1)S(1)} %get-tuple-element.81.refs_3_.refs_1_, bf16[160,1024]{1,0:T(8,128)(2,1)S(1)} %collective-permute-done.28.refs_2_, f32[8,128]{1,0:T(8,128)S(1)} %copy-done.6), custom_call_target="tpu_custom_call" | custom-call | tf_op jit(solution)/shard_map/pallas_call | solution.py:60
  (96 shorter events, 34.5 us)
Async XLA Ops:
  0.6 13.3 %copy-start = (bf16[1024,1024]{1,0:T(8,128)(2,1)S(1)}, bf16[1024,1024]{1,0:T(8,128)(2,1)}, u32[]{:S(2)}) copy-start(bf16[1024,1024]{1,0:T(8,128)(2,1)} %param.13) | copy-start | bytes 6291460
  1.9 5.5 %copy-start.3 = (bf16[128,2048]{1,0:T(8,128)(2,1)S(1)}, bf16[128,2048]{1,0:T(8,128)(2,1)}, u32[]{:S(2)}) copy-start(bf16[128,2048]{1,0:T(8,128)(2,1)} %refs_1_.7) | copy-start | bytes 1572868
  3.4 16.0 %collective-permute-start.1 = (bf16[64,1024]{1,0:T(8,128)(2,1)}, bf16[64,1024]{1,0:T(8,128)(2,1)S(1)}, u32[]{:S(2)}, u32[]{:S(2)}) collective-permute-start(bf16[64,1024]{1,0:T(8,128)(2,1)} %get-tuple-element.51.refs_2_), channel_id=1, source_target_pairs={{0,2},{1,3},{2,0},{3,1},{4,6},{5,7},{6,4},{7,5},{8,10},{9,11},{10,... | collective-permute-start | bytes 393224 | tf_op jit(solution)/shard_map/ppermute | solution.py:38
  7.5 3.5 %collective-permute-start.4 = (s32[8,128]{1,0:T(8,128)S(1)}, s32[8,128]{1,0:T(8,128)S(1)}, u32[]{:S(2)}, u32[]{:S(2)}) collective-permute-start(s32[8,128]{1,0:T(8,128)S(1)} %bitcast.36), channel_id=1, source_target_pairs={{0,4},{4,0},{8,12},{12,8},{16,20},{20,16},{24,28},{28,24},{1,5},{5... | collective-permute-start | bytes 12296 | tf_op jit(solution)/shard_map/ppermute | solution.py:38
  7.5 5.9 %collective-permute-start.3 = (bf16[128,2048]{1,0:T(8,128)(2,1)S(1)}, bf16[128,2048]{1,0:T(8,128)(2,1)S(1)}, u32[]{:S(2)}, u32[]{:S(2)}) collective-permute-start(bf16[128,2048]{1,0:T(8,128)(2,1)S(1)} %copy-done.3), channel_id=1, source_target_pairs={{0,4},{4,0},{8,12},{12,8},{16,20},{20,16},{24,28},{28,24},{1,5},{5... | collective-permute-start | bytes 1572872 | tf_op jit(solution)/shard_map/ppermute | solution.py:38
  9.4 10.0 %collective-permute-start = (bf16[64,1024]{1,0:T(8,128)(2,1)}, bf16[64,1024]{1,0:T(8,128)(2,1)S(1)}, u32[]{:S(2)}, u32[]{:S(2)}) collective-permute-start(bf16[64,1024]{1,0:T(8,128)(2,1)} %get-tuple-element.53), channel_id=1, source_target_pairs={{0,1},{1,0},{2,3},{3,2},{4,5},{5,4},{6,7},{7,6},{8,9},{9,8},{10,11... | collective-permute-start | bytes 393224 | tf_op jit(solution)/shard_map/ppermute | solution.py:38
  11.0 8.4 %collective-permute-start.2 = (bf16[64,1024]{1,0:T(8,128)(2,1)}, bf16[64,1024]{1,0:T(8,128)(2,1)}, u32[]{:S(2)}, u32[]{:S(2)}) collective-permute-start(bf16[64,1024]{1,0:T(8,128)(2,1)} %get-tuple-element.54), channel_id=1, source_target_pairs={{0,3},{1,2},{2,1},{3,0},{4,7},{5,6},{6,5},{7,4},{8,11},{9,10},{10,... | collective-permute-start | bytes 393224 | tf_op jit(solution)/shard_map/ppermute | solution.py:38
  21.2 5.4 %collective-permute-start.5 = (bf16[256,1024]{1,0:T(8,128)(2,1)S(1)}, bf16[256,1024]{1,0:T(8,128)(2,1)S(1)}, u32[]{:S(2)}, u32[]{:S(2)}) collective-permute-start(bf16[256,1024]{1,0:T(8,128)(2,1)S(1)} %get-tuple-element.56.refs_1_), channel_id=1, source_target_pairs={{0,4},{4,0},{8,12},{12,8},{16,20},{20,16},{24,28},{28,24},{1,5},{5... | collective-permute-start | bytes 1572872 | tf_op jit(solution)/shard_map/ppermute | solution.py:38
  23.8 14.9 %collective-permute-start.7 = (bf16[128,1024]{1,0:T(8,128)(2,1)S(1)}, bf16[128,1024]{1,0:T(8,128)(2,1)S(1)}, u32[]{:S(2)}, u32[]{:S(2)}) collective-permute-start(bf16[128,1024]{1,0:T(8,128)(2,1)S(1)} %get-tuple-element.113), channel_id=1, source_target_pairs={{0,4},{4,0},{8,12},{12,8},{16,20},{20,16},{24,28},{28,24},{1,5},{5... | collective-permute-start | bytes 786440 | tf_op jit(solution)/shard_map/ppermute | solution.py:38
  29.8 6.2 %collective-permute-start.6 = (bf16[512,1024]{1,0:T(8,128)(2,1)S(1)}, bf16[512,1024]{1,0:T(8,128)(2,1)S(1)}, u32[]{:S(2)}, u32[]{:S(2)}) collective-permute-start(bf16[512,1024]{1,0:T(8,128)(2,1)S(1)} %get-tuple-element.117), channel_id=1, source_target_pairs={{0,4},{4,0},{8,12},{12,8},{16,20},{20,16},{24,28},{28,24},{1,5},{5... | collective-permute-start | bytes 3145736 | tf_op jit(solution)/shard_map/ppermute | solution.py:38
  31.1 20.4 %collective-permute-start.10 = (bf16[512,1024]{1,0:T(8,128)(2,1)S(1)}, bf16[512,1024]{1,0:T(8,128)(2,1)S(1)}, u32[]{:S(2)}, u32[]{:S(2)}) collective-permute-start(bf16[512,1024]{1,0:T(8,128)(2,1)S(1)} %convolution_convert_fusion.1), channel_id=1, source_target_pairs={{0,8},{4,20},{8,0},{12,28},{16,24},{20,4},{24,16},{28,12},{1,9},{5... | collective-permute-start | bytes 3145736 | tf_op jit(solution)/shard_map/ppermute | solution.py:38
  33.6 25.1 %collective-permute-start.13 = (bf16[512,1024]{1,0:T(8,128)(2,1)S(1)}, bf16[512,1024]{1,0:T(8,128)(2,1)S(1)}, u32[]{:S(2)}, u32[]{:S(2)}) collective-permute-start(bf16[512,1024]{1,0:T(8,128)(2,1)S(1)} %convolution_convert_fusion), channel_id=1, source_target_pairs={{0,1},{1,0},{2,3},{3,2},{4,5},{5,4},{6,7},{7,6},{8,9},{9,8},{10,11... | collective-permute-start | bytes 3145736 | tf_op jit(solution)/shard_map/ppermute | solution.py:38
  40.1 9.1 %collective-permute-start.8 = (bf16[128,1152]{1,0:T(8,128)(2,1)S(1)}, bf16[128,1152]{1,0:T(8,128)(2,1)S(1)}, u32[]{:S(2)}, u32[]{:S(2)}) collective-permute-start(bf16[128,1152]{1,0:T(8,128)(2,1)S(1)} %get-tuple-element.65), channel_id=1, source_target_pairs={{0,8},{4,20},{8,0},{12,28},{16,24},{20,4},{24,16},{28,12},{1,9},{5... | collective-permute-start | bytes 884744 | tf_op jit(solution)/shard_map/ppermute | solution.py:38
  41.5 19.4 %collective-permute-start.12 = (bf16[256,1024]{1,0:T(8,128)(2,1)S(1)}, bf16[256,1024]{1,0:T(8,128)(2,1)S(1)}, u32[]{:S(2)}, u32[]{:S(2)}) collective-permute-start(bf16[256,1024]{1,0:T(8,128)(2,1)S(1)} %get-tuple-element.69), channel_id=1, source_target_pairs={{0,8},{4,20},{8,0},{12,28},{16,24},{20,4},{24,16},{28,12},{1,9},{5... | collective-permute-start | bytes 1572872 | tf_op jit(solution)/shard_map/ppermute | solution.py:38
  43.1 6.7 %copy-start.4 = (bf16[128,2048]{1,0:T(8,128)(2,1)}, bf16[128,2048]{1,0:T(8,128)(2,1)S(1)}, u32[]{:S(2)}) copy-start(bf16[128,2048]{1,0:T(8,128)(2,1)S(1)} %pad_maximum_fusion.refs_7_) | copy-start | bytes 1572868
  49.8 5.6 %collective-permute-start.9 = (bf16[64,1152]{1,0:T(8,128)(2,1)S(1)}, bf16[64,1152]{1,0:T(8,128)(2,1)S(1)}, u32[]{:S(2)}, u32[]{:S(2)}) collective-permute-start(bf16[64,1152]{1,0:T(8,128)(2,1)S(1)} %get-tuple-element.67), channel_id=1, source_target_pairs={{0,16},{4,12},{8,24},{12,4},{16,0},{20,28},{24,8},{28,20},{1,17},{... | collective-permute-start | bytes 442376 | tf_op jit(solution)/shard_map/ppermute | solution.py:38
  52.3 13.6 %collective-permute-start.17 = (bf16[256,1024]{1,0:T(8,128)(2,1)S(1)}, bf16[256,1024]{1,0:T(8,128)(2,1)S(1)}, u32[]{:S(2)}, u32[]{:S(2)}) collective-permute-start(bf16[256,1024]{1,0:T(8,128)(2,1)S(1)} %get-tuple-element.74), channel_id=1, source_target_pairs={{0,16},{4,12},{8,24},{12,4},{16,0},{20,28},{24,8},{28,20},{1,17},{... | collective-permute-start | bytes 1572872 | tf_op jit(solution)/shard_map/ppermute | solution.py:38
  56.0 6.5 %collective-permute-start.11 = (bf16[64,1152]{1,0:T(8,128)(2,1)S(1)}, bf16[64,1152]{1,0:T(8,128)(2,1)S(1)}, u32[]{:S(2)}, u32[]{:S(2)}) collective-permute-start(bf16[64,1152]{1,0:T(8,128)(2,1)S(1)} %shard_map.156.refs_3_.refs_1_), channel_id=1, source_target_pairs={{0,1},{1,0},{2,3},{3,2},{4,5},{5,4},{6,7},{7,6},{8,9},{9,8},{10,11... | collective-permute-start | bytes 442376 | tf_op jit(solution)/shard_map/ppermute | solution.py:38
  59.5 9.2 %collective-permute-start.16 = (bf16[256,1024]{1,0:T(8,128)(2,1)S(1)}, bf16[256,1024]{1,0:T(8,128)(2,1)S(1)}, u32[]{:S(2)}, u32[]{:S(2)}) collective-permute-start(bf16[256,1024]{1,0:T(8,128)(2,1)S(1)} %get-tuple-element.73), channel_id=1, source_target_pairs={{0,8},{4,20},{8,0},{12,28},{16,24},{20,4},{24,16},{28,12},{1,9},{5... | collective-permute-start | bytes 1572872 | tf_op jit(solution)/shard_map/ppermute | solution.py:38
  61.6 11.2 %collective-permute-start.15 = (bf16[128,1024]{1,0:T(8,128)(2,1)S(1)}, bf16[128,1024]{1,0:T(8,128)(2,1)S(1)}, u32[]{:S(2)}, u32[]{:S(2)}) collective-permute-start(bf16[128,1024]{1,0:T(8,128)(2,1)S(1)} %get-tuple-element.72), channel_id=1, source_target_pairs={{0,1},{1,0},{2,3},{3,2},{4,5},{5,4},{6,7},{7,6},{8,9},{9,8},{10,11... | collective-permute-start | bytes 786440 | tf_op jit(solution)/shard_map/ppermute | solution.py:38
  63.1 11.9 %collective-permute-start.14 = (bf16[64,1152]{1,0:T(8,128)(2,1)S(1)}, bf16[64,1152]{1,0:T(8,128)(2,1)S(1)}, u32[]{:S(2)}, u32[]{:S(2)}) collective-permute-start(bf16[64,1152]{1,0:T(8,128)(2,1)S(1)} %shard_map.159.refs_3_.refs_1_), channel_id=1, source_target_pairs={{0,2},{1,3},{2,0},{3,1},{4,6},{5,7},{6,4},{7,5},{8,10},{9,11},{10,... | collective-permute-start | bytes 442376 | tf_op jit(solution)/shard_map/ppermute | solution.py:38
  66.6 9.7 %collective-permute-start.19 = (bf16[128,1024]{1,0:T(8,128)(2,1)S(1)}, bf16[128,1024]{1,0:T(8,128)(2,1)S(1)}, u32[]{:S(2)}, u32[]{:S(2)}) collective-permute-start(bf16[128,1024]{1,0:T(8,128)(2,1)S(1)} %get-tuple-element.78), channel_id=1, source_target_pairs={{0,1},{1,0},{2,3},{3,2},{4,5},{5,4},{6,7},{7,6},{8,9},{9,8},{10,11... | collective-permute-start | bytes 786440 | tf_op jit(solution)/shard_map/ppermute | solution.py:38
  69.4 9.1 %collective-permute-start.20 = (bf16[128,1024]{1,0:T(8,128)(2,1)S(1)}, bf16[128,1024]{1,0:T(8,128)(2,1)S(1)}, u32[]{:S(2)}, u32[]{:S(2)}) collective-permute-start(bf16[128,1024]{1,0:T(8,128)(2,1)S(1)} %get-tuple-element.79), channel_id=1, source_target_pairs={{0,16},{4,12},{8,24},{12,4},{16,0},{20,28},{24,8},{28,20},{1,17},{... | collective-permute-start | bytes 786440 | tf_op jit(solution)/shard_map/ppermute | solution.py:38
  73.4 5.0 %collective-permute-start.21 = (bf16[64,1024]{1,0:T(8,128)(2,1)S(1)}, bf16[64,1024]{1,0:T(8,128)(2,1)S(1)}, u32[]{:S(2)}, u32[]{:S(2)}) collective-permute-start(bf16[64,1024]{1,0:T(8,128)(2,1)S(1)} %get-tuple-element.80), channel_id=1, source_target_pairs={{0,16},{4,12},{8,24},{12,4},{16,0},{20,28},{24,8},{28,20},{1,17},{... | collective-permute-start | bytes 393224 | tf_op jit(solution)/shard_map/ppermute | solution.py:38
  75.6 5.5 %collective-permute-start.18 = (bf16[64,1152]{1,0:T(8,128)(2,1)S(1)}, bf16[64,1152]{1,0:T(8,128)(2,1)S(1)}, u32[]{:S(2)}, u32[]{:S(2)}) collective-permute-start(bf16[64,1152]{1,0:T(8,128)(2,1)S(1)} %shard_map.163.refs_7_.refs_1_), channel_id=1, source_target_pairs={{0,16},{4,12},{8,24},{12,4},{16,0},{20,28},{24,8},{28,20},{1,17},{... | collective-permute-start | bytes 442376 | tf_op jit(solution)/shard_map/ppermute | solution.py:38
  79.1 14.3 %collective-permute-start.28 = (bf16[160,1024]{1,0:T(8,128)(2,1)S(1)}, bf16[160,1024]{1,0:T(8,128)(2,1)S(1)}, u32[]{:S(2)}, u32[]{:S(2)}) collective-permute-start(bf16[160,1024]{1,0:T(8,128)(2,1)S(1)} %get-tuple-element.91), channel_id=1, source_target_pairs={{0,2},{1,3},{2,0},{3,1},{4,6},{5,7},{6,4},{7,5},{8,10},{9,11},{10,... | collective-permute-start | bytes 983048 | tf_op jit(solution)/shard_map/ppermute | solution.py:38
  81.6 4.7 %collective-permute-start.22 = (bf16[128,384]{1,0:T(8,128)(2,1)S(1)}, bf16[128,384]{1,0:T(8,128)(2,1)S(1)}, u32[]{:S(2)}, u32[]{:S(2)}) collective-permute-start(bf16[128,384]{1,0:T(8,128)(2,1)S(1)} %get-tuple-element.82.refs_1_.refs_7_), channel_id=1, source_target_pairs={{0,8},{4,20},{8,0},{12,28},{16,24},{20,4},{24,16},{28,12},{1,9},{5... | collective-permute-start | bytes 294920 | tf_op jit(solution)/shard_map/ppermute | solution.py:38
  82.8 4.6 %collective-permute-start.23 = (bf16[128,384]{1,0:T(8,128)(2,1)S(1)}, bf16[128,384]{1,0:T(8,128)(2,1)S(1)}, u32[]{:S(2)}, u32[]{:S(2)}) collective-permute-start(bf16[128,384]{1,0:T(8,128)(2,1)S(1)} %get-tuple-element.83.refs_2_), channel_id=1, source_target_pairs={{0,8},{4,20},{8,0},{12,28},{16,24},{20,4},{24,16},{28,12},{1,9},{5... | collective-permute-start | bytes 294920 | tf_op jit(solution)/shard_map/ppermute | solution.py:38
  83.7 4.8 %collective-permute-start.24 = (bf16[128,384]{1,0:T(8,128)(2,1)S(1)}, bf16[128,384]{1,0:T(8,128)(2,1)S(1)}, u32[]{:S(2)}, u32[]{:S(2)}) collective-permute-start(bf16[128,384]{1,0:T(8,128)(2,1)S(1)} %get-tuple-element.84.refs_3_), channel_id=1, source_target_pairs={{0,8},{4,20},{8,0},{12,28},{16,24},{20,4},{24,16},{28,12},{1,9},{5... | collective-permute-start | bytes 294920 | tf_op jit(solution)/shard_map/ppermute | solution.py:38
  89.1 1.5 %collective-permute-start.25 = (bf16[256,384]{1,0:T(8,128)(2,1)S(1)}, bf16[256,384]{1,0:T(8,128)(2,1)S(1)}, u32[]{:S(2)}, u32[]{:S(2)}) collective-permute-start(bf16[256,384]{1,0:T(8,128)(2,1)S(1)} %get-tuple-element.85.refs_1_.refs_7_), channel_id=1, source_target_pairs={{0,4},{4,0},{8,12},{12,8},{16,20},{20,16},{24,28},{28,24},{1,5},{5... | collective-permute-start | bytes 589832 | tf_op jit(solution)/shard_map/ppermute | solution.py:38
  89.1 1.7 %collective-permute-start.26 = (bf16[256,384]{1,0:T(8,128)(2,1)S(1)}, bf16[256,384]{1,0:T(8,128)(2,1)S(1)}, u32[]{:S(2)}, u32[]{:S(2)}) collective-permute-start(bf16[256,384]{1,0:T(8,128)(2,1)S(1)} %get-tuple-element.86.refs_2_), channel_id=1, source_target_pairs={{0,4},{4,0},{8,12},{12,8},{16,20},{20,16},{24,28},{28,24},{1,5},{5... | collective-permute-start | bytes 589832 | tf_op jit(solution)/shard_map/ppermute | solution.py:38
  89.6 1.5 %collective-permute-start.27 = (bf16[256,384]{1,0:T(8,128)(2,1)S(1)}, bf16[256,384]{1,0:T(8,128)(2,1)S(1)}, u32[]{:S(2)}, u32[]{:S(2)}) collective-permute-start(bf16[256,384]{1,0:T(8,128)(2,1)S(1)} %get-tuple-element.87.refs_3_), channel_id=1, source_target_pairs={{0,4},{4,0},{8,12},{12,8},{16,20},{20,16},{24,28},{28,24},{1,5},{5... | collective-permute-start | bytes 589832 | tf_op jit(solution)/shard_map/ppermute | solution.py:38
  (7 other events, 15.1 us)

commit v6 on v5

--- a/solution.py
+++ b/solution.py
@@ -74,11 +74,11 @@
     )(numbers, *ins, *after)
 
 
-def sort_body(patch, part, own, masks, numbers, grad, *blocks):
+def sort_body(patch, part, own, numbers, grad, *blocks):
     size = own * part
     row = lax.broadcasted_iota(jnp.int32, (size, grad.shape[0]), 0)
     source = lax.broadcasted_iota(jnp.int32, (size, grad.shape[0]), 1)
-    for m, block in zip(masks, blocks):
+    for m, block in enumerate(blocks):
         wanted = (row % part) * patch + numbers[m] * own + row // part
         block[...] = times((source == wanted).astype(BF), grad[...]).astype(BF)
 
@@ -356,19 +356,14 @@
     ids_own = byte_ids.T
     ids_other = core_swap(ids_own)
     out_other = core_swap(global_out)
-    blocks, first_rows = {}, []
-    for masks in (list(range(2, tp_count)), [1, 0]):
-        sorted_rows = call(
-            functools.partial(sort_body, patch, part, own, masks),
-            [like(own * part, width, BF)] * len(masks),
-            [out_grad],
-            first_rows,
-            flops=STEP,
-        )
-        first_rows = sorted_rows[:1]
-        for m, value in zip(masks, sorted_rows):
-            blocks[m] = swap(value, "tp", (m,)) if m else value
-    blocks = [blocks[m] for m in range(tp_count)]
+    blocks = call(
+        functools.partial(sort_body, patch, part, own),
+        [like(own * part, width, BF)] * tp_count,
+        [out_grad],
+        [],
+        flops=STEP,
+    )
+    blocks = [swap(b, "tp", (m,)) if m else b for m, b in enumerate(blocks)]
     far = pl.BlockSpec(memory_space=pltpu.HBM)
     prev_hot, prev_here = call(
         functools.partial(hots_body, own, tp_count, share_count, height, core_at),
@@ -399,15 +394,7 @@
         in_specs=[far],
         scratch=[VMEM((share_count, width, chunk), BF), pltpu.SemaphoreType.DMA((share_count,))],
     )
-    grad_own, own_hot = call(
-        functools.partial(join_body, part, own, tp_count, share_count, height),
-        [like(rows, width, BF), like(rows, vocab, BF)],
-        [ids_own, *blocks],
-        [up_here],
-        numbers=numbers,
-    )
-    up_later, _ = lax.optimization_barrier((up_here, grad_own))
-    a_rows = times(r_rows, up_later)
+    a_rows = times(r_rows, up_here)
     sig = jax.nn.sigmoid(a_rows)
     h_rows = (a_rows * sig).astype(BF)
     slope = (sig * (1.0 + a_rows * (1.0 - sig))).astype(BF)
@@ -430,6 +417,13 @@
         axis=1,
     )
 
+    grad_own, own_hot = call(
+        functools.partial(join_body, part, own, tp_count, share_count, height),
+        [like(rows, width, BF), like(rows, vocab, BF)],
+        [ids_own, *blocks],
+        [h_rows],
+        numbers=numbers,
+    )
     grad_other = core_swap(grad_own)
     glob = [
         inner(own_hot[j * patches : (j + 1) * patches], value)
@@ -456,7 +450,7 @@
         def __init__(self, kept, sent, steps):
             self.kept, self.steps, self.at = kept, steps, 0
             self.arrived = go(sent, self.steps[0])
-            self.left = len(self.steps) - 2
+            self.left = self.first = len(self.steps) - 2
 
         def next(self, after):
             self.at += 1
@@ -540,8 +534,9 @@
     table = Table(kept, sent)
     share = width // seq_count
     kind = BF if share // tp_count % 16 == 0 else F32
+    du_later, _ = lax.optimization_barrier((du_rows, table.kept))
     du_here = jnp.concatenate(
-        [lax.dynamic_slice_in_dim(du_rows, s * share, share, 1) for s in shares], axis=1
+        [lax.dynamic_slice_in_dim(du_later, s * share, share, 1) for s in shares], axis=1
     )
     value = inner(du_here, slot_in)
     kept, sent = call(
@@ -551,14 +546,7 @@
         [table.kept],
     )
     proj = Chain(kept, sent, seq_steps[:1] + tp_steps[:1] + seq_steps[1:] + tp_steps[1:])
-    du_later, _ = lax.optimization_barrier((du_rows, proj.kept))
-    du_own = lax.dynamic_slice_in_dim(du_later, core * rows, rows, 0)
-    back = outer(du_own, proj_weight).astype(BF)
-    glob_out_grad = jnp.concatenate(
-        [back[j * patches : (j + 1) * patches] for j in range(own)], axis=1
-    )
-
-    last = [up.kept, proj.kept, table.kept, down.kept, glob_out_grad]
+    last = [up.kept, proj.kept, table.kept, down.kept]
     names = {"T": table, "D": down, "U": up, "P": proj}
     ends = [down, up, proj]
     heights = [c.kept.shape[0] >> c.left + 1 for c in ends]
@@ -574,10 +562,22 @@
         )
         return keep, go(sent, tp_steps[-1])
 
+    def spread(after):
+        du_own, _ = lax.optimization_barrier((du_rows, after))
+        du_own = lax.dynamic_slice_in_dim(du_own, core * rows, rows, 0)
+        back = outer(du_own, proj_weight).astype(BF)
+        return jnp.concatenate(
+            [back[j * patches : (j + 1) * patches] for j in range(own)], axis=1
+        )
+
+    glob_out_grad = None
     for name in ORDER:
         chain = names.get(name)
         if chain is not None and chain.left:
             last = [chain.next(last)]
+            if chain is up and glob_out_grad is None and up.left <= max(0, up.first - 2):
+                glob_out_grad = spread(up.kept)
+                last.append(glob_out_grad)
         elif name == "F":
             while any(c.left for c in ends):
                 for c in ends:

time: 96.7 us -> 96.4 us (level); the launches traced: 95.5 us -> 96.2 us
  waiting for transfers between devices: 22.3 us -> 24.1 us
  Pallas kernels: 23.4 us -> 22.4 us
    ppermute x29, waiting for transfers between devices: 22.3 us -> 24.1 us  [swap(): return lax.ppermute(value, axis, pairs)]
    pallas_call x25 -> x24, Pallas kernels: 23.4 us -> 22.4 us  [run(): pl.pallas_call(kernel, out_shape=tuple(outs), grid_spec=pltpu.PrefetchSca...]
    unnamed x20 -> x26, local copies, waits for them, and re-layouts: 3.37 us -> 2.63 us
where the time goes in v6:
time: 96.4 us; the launch traced here: 96.2 us
  starting transfers between devices  31.1 us (32%)
  waiting for transfers between devices  24.1 us (25%)
  Pallas kernels  22.4 us (23%)
  matrix products  12.6 us (13%)
  local copies, waits for them, and re-layouts  3.18 us (3%)
  other arithmetic  1.67 us (2%)
  between operations  1.14 us (1%)
    ppermute x29, starting transfers between devices, swap(): return lax.ppermute(value, axis, pairs)  31.1 us
    ppermute x29, waiting for transfers between devices, swap(): return lax.ppermute(value, axis, pairs)  24.1 us
    pallas_call x24, Pallas kernels, run(): pl.pallas_call(kernel, out_shape=tuple(outs), grid_spec=pltpu.PrefetchSca...  22.4 us
    dot_general x8, matrix products, inner(): lax.dot_general(left, right, (((0,), (0,)), ((), ())), preferred_element_...  4.63 us
    dot_general x3, matrix products, outer(): lax.dot_general(left, right, (((1,), (1,)), ((), ())), preferred_element_...  3.32 us
    dot_general x2, matrix products, times(): return jnp.dot(left, right, preferred_element_type=F32)  3.21 us
    unnamed x26, local copies, waits for them, and re-layouts  2.63 us
  transfers between devices with their start and end apart: 29, of which 15 were waited for; matrix products, arithmetic and copies ran while one was open for 16% of the time, Pallas kernels for 20%

profile of v6, /device:TPU:0, one launch (start us, length us, event | category | flops | bytes accessed | tf_op | source)
XLA Modules:
  0.0 96.2 jit_solution(985055666550865107)
XLA Ops:
  2.4 1.7 %shard_map.144 = (bf16[64,1024]{1,0:T(8,128)(2,1)S(1)}, bf16[64,1024]{1,0:T(8,128)(2,1)}, bf16[64,1024]{1,0:T(8,128)(2,1)}, bf16[64,1024]{1,0:T(8,128)(2,1)}) custom-call(s32[13]{0:T(128)S(1)} %stack.55.refs_0_, bf16[256,1024]{1,0:T(8,128)(2,1)S(1)} %copy-done.7), custom_call_target="tpu_custom_call" | custom-call | flops 6000000000 | tf_op jit(solution)/shard_map/pallas_call | solution.py:60
  4.1 3.0 %collective-permute-start = (bf16[64,1024]{1,0:T(8,128)(2,1)}, bf16[64,1024]{1,0:T(8,128)(2,1)S(1)}, u32[]{:S(2)}, u32[]{:S(2)}) collective-permute-start(bf16[64,1024]{1,0:T(8,128)(2,1)} %get-tuple-element.52), channel_id=1, source_target_pairs={{0,1},{1,0},{2,3},{3,2},{4,5},{5,4},{6,7},{7,6},{8,9},{9,8},{10,11... | collective-permute-start | bytes 393224 | tf_op jit(solution)/shard_map/ppermute | solution.py:38
  7.1 2.6 %collective-permute-start.1 = (bf16[64,1024]{1,0:T(8,128)(2,1)}, bf16[64,1024]{1,0:T(8,128)(2,1)S(1)}, u32[]{:S(2)}, u32[]{:S(2)}) collective-permute-start(bf16[64,1024]{1,0:T(8,128)(2,1)} %get-tuple-element.53), channel_id=1, source_target_pairs={{0,2},{1,3},{2,0},{3,1},{4,6},{5,7},{6,4},{7,5},{8,10},{9,11},{10,... | collective-permute-start | bytes 393224 | tf_op jit(solution)/shard_map/ppermute | solution.py:38
  10.5 1.5 %fusion.39 = bf16[512,1024]{1,0:T(8,128)(2,1)S(1)} fusion(bf16[512,256]{1,0:T(8,128)(2,1)S(1)} %get-tuple-element.55.refs_3_, bf16[256,1024]{1,0:T(8,128)(2,1)} %param.14), kind=kOutput, calls=%fused_computation.71 | convolution fusion | flops 268435456 | bytes 1835008 | tf_op jit(solution)/shard_map/dot_general | solution.py:384
  12.7 1.4 %multiply_reduce_fusion.2 = (f32[512]{0:T(512)S(1)}, f32[512,1024]{1,0:T(8,128)S(1)}) fusion(bf16[512,1024]{1,0:T(8,128)(2,1)S(1)} %fusion.39, bf16[512,1024]{1,0:T(8,128)(2,1)S(1)} %shard_map.146, bf16[1024,1024]{1,0:T(8,128)(2,1)S(1)} %copy-done), kind=kOutput, calls=%fused_computation.9 | convolution fusion | flops 1075838464 | bytes 6293504 | tf_op jit(solution)/shard_map/dot_general | solution.py:32
  14.9 2.6 %shard_map.147 = bf16[1024,1024]{1,0:T(8,128)(2,1)S(1)} custom-call(s32[13]{0:T(128)S(1)} %stack.55.refs_0_, bf16[1024,2048]{1,0:T(8,128)(2,1)S(1)} %copy-done.1, bf16[512,1024]{1,0:T(8,128)(2,1)S(1)} %multiply_convert_fusion.3.refs_2_), custom_call_target="tpu_custom_call" | custom-call | tf_op jit(solution)/shard_map/pallas_call | solution.py:60
  17.5 1.8 %multiply_convert_fusion.1 = (bf16[512,1024]{1,0:T(8,128)(2,1)S(1)}, bf16[512,1024]{1,0:T(8,128)(2,1)S(1)}) fusion(bf16[512,1024]{1,0:T(8,128)(2,1)S(1)} %multiply_convert_fusion.3.refs_2_, bf16[1024,1024]{1,0:T(8,128)(2,1)S(1)} %shard_map.147), kind=kOutput, calls=%fused_computation.5 | convolution fusion | flops 1078984704 | bytes 5242880 | tf_op jit(solution)/shard_map/dot_general | solution.py:32
  20.2 2.0 %shard_map.148 = (bf16[256,1024]{1,0:T(8,128)(2,1)S(1)}, bf16[256,256]{1,0:T(8,128)(2,1)S(1)}) custom-call(s32[13]{0:T(128)S(1)} %stack.55.refs_0_, s32[8,128]{1,0:T(8,128)S(1)} %bitcast.38, bf16[64,1024]{1,0:T(8,128)(2,1)S(1)} %get-tuple-element.51.refs_3_.refs_2_, bf16[64,1024]{1,0:T(8,128)(2,1)S(1)} %collective-permute-done.refs_3_, ...), custom_call_target="tpu_custom_call" | custom-call | tf_op jit(solution)/shard_map/pallas_call | solution.py:60
  25.2 1.3 %multiply_convert_fusion = bf16[512,1024]{1,0:T(8,128)(2,1)S(1)} fusion(bf16[512,1024]{1,0:T(8,128)(2,1)S(1)} %get-tuple-element.59, bf16[512,1024]{1,0:T(8,128)(2,1)S(1)} %shard_map.149, bf16[1024,1024]{1,0:T(8,128)(2,1)S(1)} %shard_map.150), kind=kOutput, calls=%fused_computation.4 | convolution fusion | flops 1075314688 | bytes 5242880 | tf_op jit(solution)/shard_map/dot_general | solution.py:26
  26.5 1.3 %fusion.38 = (bf16[512,1024]{1,0:T(8,128)(2,1)S(1)}, f32[512,1024]{1,0:T(8,128)S(1)}) fusion(bf16[512,1024]{1,0:T(8,128)(2,1)S(1)} %multiply_convert_fusion, bf16[1024,1024]{1,0:T(8,128)(2,1)S(1)} %shard_map.147), kind=kOutput, calls=%fused_computation.70 | convolution fusion | flops 1074266112 | bytes 6291456 | tf_op jit(solution)/shard_map/dot_general | solution.py:26
  28.6 2.2 %collective-permute-start.7 = (bf16[512,1024]{1,0:T(8,128)(2,1)S(1)}, bf16[512,1024]{1,0:T(8,128)(2,1)S(1)}, u32[]{:S(2)}, u32[]{:S(2)}) collective-permute-start(bf16[512,1024]{1,0:T(8,128)(2,1)S(1)} %convolution_convert_fusion.2), channel_id=1, source_target_pairs={{0,1},{1,0},{2,3},{3,2},{4,5},{5,4},{6,7},{7,6},{8,9},{9,8},{10,11... | collective-permute-start | bytes 3145736 | tf_op jit(solution)/shard_map/ppermute | solution.py:38
  31.5 1.6 %collective-permute-start.11 = (bf16[512,1024]{1,0:T(8,128)(2,1)S(1)}, bf16[512,1024]{1,0:T(8,128)(2,1)S(1)}, u32[]{:S(2)}, u32[]{:S(2)}) collective-permute-start(bf16[512,1024]{1,0:T(8,128)(2,1)S(1)} %convolution_convert_fusion), channel_id=1, source_target_pairs={{0,8},{4,20},{8,0},{12,28},{16,24},{20,4},{24,16},{28,12},{1,9},{5... | collective-permute-start | bytes 3145736 | tf_op jit(solution)/shard_map/ppermute | solution.py:38
  39.1 1.6 %collective-permute-start.15 = (bf16[256,1024]{1,0:T(8,128)(2,1)S(1)}, bf16[256,1024]{1,0:T(8,128)(2,1)S(1)}, u32[]{:S(2)}, u32[]{:S(2)}) collective-permute-start(bf16[256,1024]{1,0:T(8,128)(2,1)S(1)} %get-tuple-element.71), channel_id=1, source_target_pairs={{0,8},{4,20},{8,0},{12,28},{16,24},{20,4},{24,16},{28,12},{1,9},{5... | collective-permute-start | bytes 1572872 | tf_op jit(solution)/shard_map/ppermute | solution.py:38
  40.6 8.9 %collective-permute-done.9.refs_2_ = bf16[128,1152]{1,0:T(8,128)(2,1)S(1)} collective-permute-done((bf16[128,1152]{1,0:T(8,128)(2,1)S(1)}, bf16[128,1152]{1,0:T(8,128)(2,1)S(1)}, u32[]{:S(2)}, u32[]{:S(2)}) %collective-permute-start.9) | collective-permute-done | bytes 294944 | tf_op jit(solution)/shard_map/ppermute | solution.py:38
  50.2 1.6 %collective-permute-start.10 = (bf16[64,1152]{1,0:T(8,128)(2,1)S(1)}, bf16[64,1152]{1,0:T(8,128)(2,1)S(1)}, u32[]{:S(2)}, u32[]{:S(2)}) collective-permute-start(bf16[64,1152]{1,0:T(8,128)(2,1)S(1)} %get-tuple-element.66), channel_id=1, source_target_pairs={{0,16},{4,12},{8,24},{12,4},{16,0},{20,28},{24,8},{28,20},{1,17},{... | collective-permute-start | bytes 442376 | tf_op jit(solution)/shard_map/ppermute | solution.py:38
  53.1 2.9 %collective-permute-done.10.refs_2_ = bf16[64,1152]{1,0:T(8,128)(2,1)S(1)} collective-permute-done((bf16[64,1152]{1,0:T(8,128)(2,1)S(1)}, bf16[64,1152]{1,0:T(8,128)(2,1)S(1)}, u32[]{:S(2)}, u32[]{:S(2)}) %collective-permute-start.10) | collective-permute-done | bytes 147488 | tf_op jit(solution)/shard_map/ppermute | solution.py:38
  57.8 1.6 %collective-permute-start.12 = (bf16[256,1024]{1,0:T(8,128)(2,1)S(1)}, bf16[256,1024]{1,0:T(8,128)(2,1)S(1)}, u32[]{:S(2)}, u32[]{:S(2)}) collective-permute-start(bf16[256,1024]{1,0:T(8,128)(2,1)S(1)} %get-tuple-element.69), channel_id=1, source_target_pairs={{0,8},{4,20},{8,0},{12,28},{16,24},{20,4},{24,16},{28,12},{1,9},{5... | collective-permute-start | bytes 1572872 | tf_op jit(solution)/shard_map/ppermute | solution.py:38
  60.0 1.8 %collective-permute-start.17 = (bf16[128,1024]{1,0:T(8,128)(2,1)S(1)}, bf16[128,1024]{1,0:T(8,128)(2,1)S(1)}, u32[]{:S(2)}, u32[]{:S(2)}) collective-permute-start(bf16[128,1024]{1,0:T(8,128)(2,1)S(1)} %get-tuple-element.76), channel_id=1, source_target_pairs={{0,1},{1,0},{2,3},{3,2},{4,5},{5,4},{6,7},{7,6},{8,9},{9,8},{10,11... | collective-permute-start | bytes 786440 | tf_op jit(solution)/shard_map/ppermute | solution.py:38
  62.7 2.1 %collective-permute-start.16 = (bf16[64,1152]{1,0:T(8,128)(2,1)S(1)}, bf16[64,1152]{1,0:T(8,128)(2,1)S(1)}, u32[]{:S(2)}, u32[]{:S(2)}) collective-permute-start(bf16[64,1152]{1,0:T(8,128)(2,1)S(1)} %shard_map.158.refs_3_.refs_1_), channel_id=1, source_target_pairs={{0,2},{1,3},{2,0},{3,1},{4,6},{5,7},{6,4},{7,5},{8,10},{9,11},{10,... | collective-permute-start | bytes 442376 | tf_op jit(solution)/shard_map/ppermute | solution.py:38
  66.3 1.6 %collective-permute-done.12.refs_2_ = bf16[256,1024]{1,0:T(8,128)(2,1)S(1)} collective-permute-done((bf16[256,1024]{1,0:T(8,128)(2,1)S(1)}, bf16[256,1024]{1,0:T(8,128)(2,1)S(1)}, u32[]{:S(2)}, u32[]{:S(2)}) %collective-permute-start.12) | collective-permute-done | bytes 524320 | tf_op jit(solution)/shard_map/ppermute | solution.py:38
  69.5 1.6 %collective-permute-start.20 = (bf16[128,1024]{1,0:T(8,128)(2,1)S(1)}, bf16[128,1024]{1,0:T(8,128)(2,1)S(1)}, u32[]{:S(2)}, u32[]{:S(2)}) collective-permute-start(bf16[128,1024]{1,0:T(8,128)(2,1)S(1)} %get-tuple-element.79), channel_id=1, source_target_pairs={{0,16},{4,12},{8,24},{12,4},{16,0},{20,28},{24,8},{28,20},{1,17},{... | collective-permute-start | bytes 786440 | tf_op jit(solution)/shard_map/ppermute | solution.py:38
  71.1 1.4 %collective-permute-done.17.refs_2_ = bf16[128,1024]{1,0:T(8,128)(2,1)S(1)} collective-permute-done((bf16[128,1024]{1,0:T(8,128)(2,1)S(1)}, bf16[128,1024]{1,0:T(8,128)(2,1)S(1)}, u32[]{:S(2)}, u32[]{:S(2)}) %collective-permute-start.17) | collective-permute-done | bytes 262176 | tf_op jit(solution)/shard_map/ppermute | solution.py:38
  73.1 1.6 %collective-permute-start.21 = (bf16[64,1024]{1,0:T(8,128)(2,1)S(1)}, bf16[64,1024]{1,0:T(8,128)(2,1)S(1)}, u32[]{:S(2)}, u32[]{:S(2)}) collective-permute-start(bf16[64,1024]{1,0:T(8,128)(2,1)S(1)} %get-tuple-element.80), channel_id=1, source_target_pairs={{0,16},{4,12},{8,24},{12,4},{16,0},{20,28},{24,8},{28,20},{1,17},{... | collective-permute-start | bytes 393224 | tf_op jit(solution)/shard_map/ppermute | solution.py:38
  76.3 1.8 %collective-permute-done.21.refs_6_ = bf16[64,1024]{1,0:T(8,128)(2,1)S(1)} collective-permute-done((bf16[64,1024]{1,0:T(8,128)(2,1)S(1)}, bf16[64,1024]{1,0:T(8,128)(2,1)S(1)}, u32[]{:S(2)}, u32[]{:S(2)}) %collective-permute-start.21) | collective-permute-done | bytes 131104 | tf_op jit(solution)/shard_map/ppermute | solution.py:38
  78.8 1.6 %collective-permute-start.28 = (bf16[160,1024]{1,0:T(8,128)(2,1)S(1)}, bf16[160,1024]{1,0:T(8,128)(2,1)S(1)}, u32[]{:S(2)}, u32[]{:S(2)}) collective-permute-start(bf16[160,1024]{1,0:T(8,128)(2,1)S(1)} %get-tuple-element.91), channel_id=1, source_target_pairs={{0,2},{1,3},{2,0},{3,1},{4,6},{5,7},{6,4},{7,5},{8,10},{9,11},{10,... | collective-permute-start | bytes 983048 | tf_op jit(solution)/shard_map/ppermute | solution.py:38
  81.0 1.5 %collective-permute-start.22 = (bf16[128,384]{1,0:T(8,128)(2,1)S(1)}, bf16[128,384]{1,0:T(8,128)(2,1)S(1)}, u32[]{:S(2)}, u32[]{:S(2)}) collective-permute-start(bf16[128,384]{1,0:T(8,128)(2,1)S(1)} %get-tuple-element.82.refs_1_.refs_7_), channel_id=1, source_target_pairs={{0,8},{4,20},{8,0},{12,28},{16,24},{20,4},{24,16},{28,12},{1,9},{5... | collective-permute-start | bytes 294920 | tf_op jit(solution)/shard_map/ppermute | solution.py:38
  83.1 1.4 %collective-permute-start.24 = (bf16[128,384]{1,0:T(8,128)(2,1)S(1)}, bf16[128,384]{1,0:T(8,128)(2,1)S(1)}, u32[]{:S(2)}, u32[]{:S(2)}) collective-permute-start(bf16[128,384]{1,0:T(8,128)(2,1)S(1)} %get-tuple-element.84.refs_3_), channel_id=1, source_target_pairs={{0,8},{4,20},{8,0},{12,28},{16,24},{20,4},{24,16},{28,12},{1,9},{5... | collective-permute-start | bytes 294920 | tf_op jit(solution)/shard_map/ppermute | solution.py:38
  84.5 1.2 %collective-permute-done.22.refs_4_ = bf16[128,384]{1,0:T(8,128)(2,1)S(1)} collective-permute-done((bf16[128,384]{1,0:T(8,128)(2,1)S(1)}, bf16[128,384]{1,0:T(8,128)(2,1)S(1)}, u32[]{:S(2)}, u32[]{:S(2)}) %collective-permute-start.22) | collective-permute-done | bytes 98336 | tf_op jit(solution)/shard_map/ppermute | solution.py:38
  85.7 1.4 %collective-permute-done.23.refs_5_ = bf16[128,384]{1,0:T(8,128)(2,1)S(1)} collective-permute-done((bf16[128,384]{1,0:T(8,128)(2,1)S(1)}, bf16[128,384]{1,0:T(8,128)(2,1)S(1)}, u32[]{:S(2)}, u32[]{:S(2)}) %collective-permute-start.23) | collective-permute-done | bytes 98336 | tf_op jit(solution)/shard_map/ppermute | solution.py:38
  90.8 2.0 %shard_map.166 = (f32[256,1024]{1,0:T(8,128)}, f32[256,1024]{1,0:T(8,128)}, f32[8,128]{1,0:T(8,128)}) custom-call(s32[13]{0:T(128)S(1)} %stack.55.refs_0_, bf16[256,384]{1,0:T(8,128)(2,1)S(1)} %get-tuple-element.85.refs_1_.refs_7_, bf16[256,384]{1,0:T(8,128)(2,1)S(1)} %get-tuple-element.86.refs_2_, bf16[256,384]{1,0:T(8,128)(2,1)S(1)} %get-tuple-element.87.refs_3_, ...), custom_call_target="tpu_custom_call" | custom-call | tf_op jit(solution)/shard_map/pallas_call | solution.py:60
  92.8 1.3 %collective-permute-done.28.refs_2_ = bf16[160,1024]{1,0:T(8,128)(2,1)S(1)} collective-permute-done((bf16[160,1024]{1,0:T(8,128)(2,1)S(1)}, bf16[160,1024]{1,0:T(8,128)(2,1)S(1)}, u32[]{:S(2)}, u32[]{:S(2)}) %collective-permute-start.28) | collective-permute-done | bytes 327712 | tf_op jit(solution)/shard_map/ppermute | solution.py:38
  94.8 1.4 %shard_map.167 = (f32[64,1024]{1,0:T(8,128)}, f32[64,1024]{1,0:T(8,128)}, f32[32,1024]{1,0:T(8,128)}) custom-call(s32[13]{0:T(128)S(1)} %stack.55.refs_0_, bf16[160,1024]{1,0:T(8,128)(2,1)S(1)} %get-tuple-element.81.refs_3_.refs_1_, bf16[160,1024]{1,0:T(8,128)(2,1)S(1)} %collective-permute-done.28.refs_2_, f32[8,128]{1,0:T(8,128)S(1)} %copy-done.6), custom_call_target="tpu_custom_call" | custom-call | tf_op jit(solution)/shard_map/pallas_call | solution.py:60
  (102 shorter events, 32.2 us)
Async XLA Ops:
  0.6 12.0 %copy-start = (bf16[1024,1024]{1,0:T(8,128)(2,1)S(1)}, bf16[1024,1024]{1,0:T(8,128)(2,1)}, u32[]{:S(2)}) copy-start(bf16[1024,1024]{1,0:T(8,128)(2,1)} %param.13) | copy-start | bytes 6291460
  0.6 9.0 %collective-permute-start.4 = (s32[8,128]{1,0:T(8,128)}, s32[8,128]{1,0:T(8,128)S(1)}, u32[]{:S(2)}, u32[]{:S(2)}) collective-permute-start(s32[8,128]{1,0:T(8,128)} %bitcast.36), channel_id=1, source_target_pairs={{0,4},{4,0},{8,12},{12,8},{16,20},{20,16},{24,28},{28,24},{1,5},{5... | collective-permute-start | bytes 12296 | tf_op jit(solution)/shard_map/ppermute | solution.py:38
  1.2 10.8 %collective-permute-start.3 = (bf16[128,2048]{1,0:T(8,128)(2,1)}, bf16[128,2048]{1,0:T(8,128)(2,1)S(1)}, u32[]{:S(2)}, u32[]{:S(2)}) collective-permute-start(bf16[128,2048]{1,0:T(8,128)(2,1)} %refs_1_.5), channel_id=1, source_target_pairs={{0,4},{4,0},{8,12},{12,8},{16,20},{20,16},{24,28},{28,24},{1,5},{5... | collective-permute-start | bytes 1572872 | tf_op jit(solution)/shard_map/ppermute | solution.py:38
  2.4 7.3 %copy-start.5 = (s32[128,8]{0,1:T(8,128)S(1)}, s32[128,8]{0,1:T(8,128)}, u32[]{:S(2)}) copy-start(s32[128,8]{0,1:T(8,128)} %param.9) | copy-start | bytes 12292
  4.1 8.0 %copy-start.3 = (bf16[128,2048]{1,0:T(8,128)(2,1)S(1)}, bf16[128,2048]{1,0:T(8,128)(2,1)}, u32[]{:S(2)}) copy-start(bf16[128,2048]{1,0:T(8,128)(2,1)} %refs_1_.5) | copy-start | bytes 1572868
  4.1 15.9 %collective-permute-start = (bf16[64,1024]{1,0:T(8,128)(2,1)}, bf16[64,1024]{1,0:T(8,128)(2,1)S(1)}, u32[]{:S(2)}, u32[]{:S(2)}) collective-permute-start(bf16[64,1024]{1,0:T(8,128)(2,1)} %get-tuple-element.52), channel_id=1, source_target_pairs={{0,1},{1,0},{2,3},{3,2},{4,5},{5,4},{6,7},{7,6},{8,9},{9,8},{10,11... | collective-permute-start | bytes 393224 | tf_op jit(solution)/shard_map/ppermute | solution.py:38
  7.1 13.1 %collective-permute-start.1 = (bf16[64,1024]{1,0:T(8,128)(2,1)}, bf16[64,1024]{1,0:T(8,128)(2,1)S(1)}, u32[]{:S(2)}, u32[]{:S(2)}) collective-permute-start(bf16[64,1024]{1,0:T(8,128)(2,1)} %get-tuple-element.53), channel_id=1, source_target_pairs={{0,2},{1,3},{2,0},{3,1},{4,6},{5,7},{6,4},{7,5},{8,10},{9,11},{10,... | collective-permute-start | bytes 393224 | tf_op jit(solution)/shard_map/ppermute | solution.py:38
  9.7 10.5 %collective-permute-start.2 = (bf16[64,1024]{1,0:T(8,128)(2,1)}, bf16[64,1024]{1,0:T(8,128)(2,1)}, u32[]{:S(2)}, u32[]{:S(2)}) collective-permute-start(bf16[64,1024]{1,0:T(8,128)(2,1)} %get-tuple-element.54), channel_id=1, source_target_pairs={{0,3},{1,2},{2,1},{3,0},{4,7},{5,6},{6,5},{7,4},{8,11},{9,10},{10,... | collective-permute-start | bytes 393224 | tf_op jit(solution)/shard_map/ppermute | solution.py:38
  22.1 2.4 %collective-permute-start.5 = (bf16[256,1024]{1,0:T(8,128)(2,1)S(1)}, bf16[256,1024]{1,0:T(8,128)(2,1)S(1)}, u32[]{:S(2)}, u32[]{:S(2)}) collective-permute-start(bf16[256,1024]{1,0:T(8,128)(2,1)S(1)} %get-tuple-element.57.refs_1_), channel_id=1, source_target_pairs={{0,4},{4,0},{8,12},{12,8},{16,20},{20,16},{24,28},{28,24},{1,5},{5... | collective-permute-start | bytes 1572872 | tf_op jit(solution)/shard_map/ppermute | solution.py:38
  24.0 12.3 %collective-permute-start.8 = (bf16[128,1024]{1,0:T(8,128)(2,1)S(1)}, bf16[128,1024]{1,0:T(8,128)(2,1)S(1)}, u32[]{:S(2)}, u32[]{:S(2)}) collective-permute-start(bf16[128,1024]{1,0:T(8,128)(2,1)S(1)} %get-tuple-element.114), channel_id=1, source_target_pairs={{0,4},{4,0},{8,12},{12,8},{16,20},{20,16},{24,28},{28,24},{1,5},{5... | collective-permute-start | bytes 786440 | tf_op jit(solution)/shard_map/ppermute | solution.py:38
  27.8 6.8 %collective-permute-start.6 = (bf16[512,1024]{1,0:T(8,128)(2,1)S(1)}, bf16[512,1024]{1,0:T(8,128)(2,1)S(1)}, u32[]{:S(2)}, u32[]{:S(2)}) collective-permute-start(bf16[512,1024]{1,0:T(8,128)(2,1)S(1)} %get-tuple-element.118), channel_id=1, source_target_pairs={{0,4},{4,0},{8,12},{12,8},{16,20},{20,16},{24,28},{28,24},{1,5},{5... | collective-permute-start | bytes 3145736 | tf_op jit(solution)/shard_map/ppermute | solution.py:38
  28.6 28.3 %collective-permute-start.7 = (bf16[512,1024]{1,0:T(8,128)(2,1)S(1)}, bf16[512,1024]{1,0:T(8,128)(2,1)S(1)}, u32[]{:S(2)}, u32[]{:S(2)}) collective-permute-start(bf16[512,1024]{1,0:T(8,128)(2,1)S(1)} %convolution_convert_fusion.2), channel_id=1, source_target_pairs={{0,1},{1,0},{2,3},{3,2},{4,5},{5,4},{6,7},{7,6},{8,9},{9,8},{10,11... | collective-permute-start | bytes 3145736 | tf_op jit(solution)/shard_map/ppermute | solution.py:38
  31.5 20.2 %collective-permute-start.11 = (bf16[512,1024]{1,0:T(8,128)(2,1)S(1)}, bf16[512,1024]{1,0:T(8,128)(2,1)S(1)}, u32[]{:S(2)}, u32[]{:S(2)}) collective-permute-start(bf16[512,1024]{1,0:T(8,128)(2,1)S(1)} %convolution_convert_fusion), channel_id=1, source_target_pairs={{0,8},{4,20},{8,0},{12,28},{16,24},{20,4},{24,16},{28,12},{1,9},{5... | collective-permute-start | bytes 3145736 | tf_op jit(solution)/shard_map/ppermute | solution.py:38
  36.9 12.6 %collective-permute-start.9 = (bf16[128,1152]{1,0:T(8,128)(2,1)S(1)}, bf16[128,1152]{1,0:T(8,128)(2,1)S(1)}, u32[]{:S(2)}, u32[]{:S(2)}) collective-permute-start(bf16[128,1152]{1,0:T(8,128)(2,1)S(1)} %get-tuple-element.62), channel_id=1, source_target_pairs={{0,8},{4,20},{8,0},{12,28},{16,24},{20,4},{24,16},{28,12},{1,9},{5... | collective-permute-start | bytes 884744 | tf_op jit(solution)/shard_map/ppermute | solution.py:38
  39.1 20.2 %collective-permute-start.15 = (bf16[256,1024]{1,0:T(8,128)(2,1)S(1)}, bf16[256,1024]{1,0:T(8,128)(2,1)S(1)}, u32[]{:S(2)}, u32[]{:S(2)}) collective-permute-start(bf16[256,1024]{1,0:T(8,128)(2,1)S(1)} %get-tuple-element.71), channel_id=1, source_target_pairs={{0,8},{4,20},{8,0},{12,28},{16,24},{20,4},{24,16},{28,12},{1,9},{5... | collective-permute-start | bytes 1572872 | tf_op jit(solution)/shard_map/ppermute | solution.py:38
  50.2 5.8 %collective-permute-start.10 = (bf16[64,1152]{1,0:T(8,128)(2,1)S(1)}, bf16[64,1152]{1,0:T(8,128)(2,1)S(1)}, u32[]{:S(2)}, u32[]{:S(2)}) collective-permute-start(bf16[64,1152]{1,0:T(8,128)(2,1)S(1)} %get-tuple-element.66), channel_id=1, source_target_pairs={{0,16},{4,12},{8,24},{12,4},{16,0},{20,28},{24,8},{28,20},{1,17},{... | collective-permute-start | bytes 442376 | tf_op jit(solution)/shard_map/ppermute | solution.py:38
  52.5 12.3 %collective-permute-start.13 = (bf16[256,1024]{1,0:T(8,128)(2,1)S(1)}, bf16[256,1024]{1,0:T(8,128)(2,1)S(1)}, u32[]{:S(2)}, u32[]{:S(2)}) collective-permute-start(bf16[256,1024]{1,0:T(8,128)(2,1)S(1)} %get-tuple-element.70), channel_id=1, source_target_pairs={{0,16},{4,12},{8,24},{12,4},{16,0},{20,28},{24,8},{28,20},{1,17},{... | collective-permute-start | bytes 1572872 | tf_op jit(solution)/shard_map/ppermute | solution.py:38
  56.6 5.6 %collective-permute-start.14 = (bf16[64,1152]{1,0:T(8,128)(2,1)S(1)}, bf16[64,1152]{1,0:T(8,128)(2,1)S(1)}, u32[]{:S(2)}, u32[]{:S(2)}) collective-permute-start(bf16[64,1152]{1,0:T(8,128)(2,1)S(1)} %shard_map.155.refs_3_.refs_1_), channel_id=1, source_target_pairs={{0,1},{1,0},{2,3},{3,2},{4,5},{5,4},{6,7},{7,6},{8,9},{9,8},{10,11... | collective-permute-start | bytes 442376 | tf_op jit(solution)/shard_map/ppermute | solution.py:38
  57.8 10.2 %collective-permute-start.12 = (bf16[256,1024]{1,0:T(8,128)(2,1)S(1)}, bf16[256,1024]{1,0:T(8,128)(2,1)S(1)}, u32[]{:S(2)}, u32[]{:S(2)}) collective-permute-start(bf16[256,1024]{1,0:T(8,128)(2,1)S(1)} %get-tuple-element.69), channel_id=1, source_target_pairs={{0,8},{4,20},{8,0},{12,28},{16,24},{20,4},{24,16},{28,12},{1,9},{5... | collective-permute-start | bytes 1572872 | tf_op jit(solution)/shard_map/ppermute | solution.py:38
  60.0 12.5 %collective-permute-start.17 = (bf16[128,1024]{1,0:T(8,128)(2,1)S(1)}, bf16[128,1024]{1,0:T(8,128)(2,1)S(1)}, u32[]{:S(2)}, u32[]{:S(2)}) collective-permute-start(bf16[128,1024]{1,0:T(8,128)(2,1)S(1)} %get-tuple-element.76), channel_id=1, source_target_pairs={{0,1},{1,0},{2,3},{3,2},{4,5},{5,4},{6,7},{7,6},{8,9},{9,8},{10,11... | collective-permute-start | bytes 786440 | tf_op jit(solution)/shard_map/ppermute | solution.py:38
  62.7 11.9 %collective-permute-start.16 = (bf16[64,1152]{1,0:T(8,128)(2,1)S(1)}, bf16[64,1152]{1,0:T(8,128)(2,1)S(1)}, u32[]{:S(2)}, u32[]{:S(2)}) collective-permute-start(bf16[64,1152]{1,0:T(8,128)(2,1)S(1)} %shard_map.158.refs_3_.refs_1_), channel_id=1, source_target_pairs={{0,2},{1,3},{2,0},{3,1},{4,6},{5,7},{6,4},{7,5},{8,10},{9,11},{10,... | collective-permute-start | bytes 442376 | tf_op jit(solution)/shard_map/ppermute | solution.py:38
  65.5 10.8 %collective-permute-start.19 = (bf16[128,1024]{1,0:T(8,128)(2,1)S(1)}, bf16[128,1024]{1,0:T(8,128)(2,1)S(1)}, u32[]{:S(2)}, u32[]{:S(2)}) collective-permute-start(bf16[128,1024]{1,0:T(8,128)(2,1)S(1)} %get-tuple-element.78), channel_id=1, source_target_pairs={{0,1},{1,0},{2,3},{3,2},{4,5},{5,4},{6,7},{7,6},{8,9},{9,8},{10,11... | collective-permute-start | bytes 786440 | tf_op jit(solution)/shard_map/ppermute | solution.py:38
  69.5 8.7 %collective-permute-start.20 = (bf16[128,1024]{1,0:T(8,128)(2,1)S(1)}, bf16[128,1024]{1,0:T(8,128)(2,1)S(1)}, u32[]{:S(2)}, u32[]{:S(2)}) collective-permute-start(bf16[128,1024]{1,0:T(8,128)(2,1)S(1)} %get-tuple-element.79), channel_id=1, source_target_pairs={{0,16},{4,12},{8,24},{12,4},{16,0},{20,28},{24,8},{28,20},{1,17},{... | collective-permute-start | bytes 786440 | tf_op jit(solution)/shard_map/ppermute | solution.py:38
  73.1 5.0 %collective-permute-start.21 = (bf16[64,1024]{1,0:T(8,128)(2,1)S(1)}, bf16[64,1024]{1,0:T(8,128)(2,1)S(1)}, u32[]{:S(2)}, u32[]{:S(2)}) collective-permute-start(bf16[64,1024]{1,0:T(8,128)(2,1)S(1)} %get-tuple-element.80), channel_id=1, source_target_pairs={{0,16},{4,12},{8,24},{12,4},{16,0},{20,28},{24,8},{28,20},{1,17},{... | collective-permute-start | bytes 393224 | tf_op jit(solution)/shard_map/ppermute | solution.py:38
  75.2 5.2 %collective-permute-start.18 = (bf16[64,1152]{1,0:T(8,128)(2,1)S(1)}, bf16[64,1152]{1,0:T(8,128)(2,1)S(1)}, u32[]{:S(2)}, u32[]{:S(2)}) collective-permute-start(bf16[64,1152]{1,0:T(8,128)(2,1)S(1)} %shard_map.162.refs_7_.refs_1_), channel_id=1, source_target_pairs={{0,16},{4,12},{8,24},{12,4},{16,0},{20,28},{24,8},{28,20},{1,17},{... | collective-permute-start | bytes 442376 | tf_op jit(solution)/shard_map/ppermute | solution.py:38
  78.8 15.3 %collective-permute-start.28 = (bf16[160,1024]{1,0:T(8,128)(2,1)S(1)}, bf16[160,1024]{1,0:T(8,128)(2,1)S(1)}, u32[]{:S(2)}, u32[]{:S(2)}) collective-permute-start(bf16[160,1024]{1,0:T(8,128)(2,1)S(1)} %get-tuple-element.91), channel_id=1, source_target_pairs={{0,2},{1,3},{2,0},{3,1},{4,6},{5,7},{6,4},{7,5},{8,10},{9,11},{10,... | collective-permute-start | bytes 983048 | tf_op jit(solution)/shard_map/ppermute | solution.py:38
  81.0 4.7 %collective-permute-start.22 = (bf16[128,384]{1,0:T(8,128)(2,1)S(1)}, bf16[128,384]{1,0:T(8,128)(2,1)S(1)}, u32[]{:S(2)}, u32[]{:S(2)}) collective-permute-start(bf16[128,384]{1,0:T(8,128)(2,1)S(1)} %get-tuple-element.82.refs_1_.refs_7_), channel_id=1, source_target_pairs={{0,8},{4,20},{8,0},{12,28},{16,24},{20,4},{24,16},{28,12},{1,9},{5... | collective-permute-start | bytes 294920 | tf_op jit(solution)/shard_map/ppermute | solution.py:38
  82.5 4.6 %collective-permute-start.23 = (bf16[128,384]{1,0:T(8,128)(2,1)S(1)}, bf16[128,384]{1,0:T(8,128)(2,1)S(1)}, u32[]{:S(2)}, u32[]{:S(2)}) collective-permute-start(bf16[128,384]{1,0:T(8,128)(2,1)S(1)} %get-tuple-element.83.refs_2_), channel_id=1, source_target_pairs={{0,8},{4,20},{8,0},{12,28},{16,24},{20,4},{24,16},{28,12},{1,9},{5... | collective-permute-start | bytes 294920 | tf_op jit(solution)/shard_map/ppermute | solution.py:38
  83.1 5.0 %collective-permute-start.24 = (bf16[128,384]{1,0:T(8,128)(2,1)S(1)}, bf16[128,384]{1,0:T(8,128)(2,1)S(1)}, u32[]{:S(2)}, u32[]{:S(2)}) collective-permute-start(bf16[128,384]{1,0:T(8,128)(2,1)S(1)} %get-tuple-element.84.refs_3_), channel_id=1, source_target_pairs={{0,8},{4,20},{8,0},{12,28},{16,24},{20,4},{24,16},{28,12},{1,9},{5... | collective-permute-start | bytes 294920 | tf_op jit(solution)/shard_map/ppermute | solution.py:38
  88.8 1.5 %collective-permute-start.25 = (bf16[256,384]{1,0:T(8,128)(2,1)S(1)}, bf16[256,384]{1,0:T(8,128)(2,1)S(1)}, u32[]{:S(2)}, u32[]{:S(2)}) collective-permute-start(bf16[256,384]{1,0:T(8,128)(2,1)S(1)} %get-tuple-element.85.refs_1_.refs_7_), channel_id=1, source_target_pairs={{0,4},{4,0},{8,12},{12,8},{16,20},{20,16},{24,28},{28,24},{1,5},{5... | collective-permute-start | bytes 589832 | tf_op jit(solution)/shard_map/ppermute | solution.py:38
  88.8 1.7 %collective-permute-start.26 = (bf16[256,384]{1,0:T(8,128)(2,1)S(1)}, bf16[256,384]{1,0:T(8,128)(2,1)S(1)}, u32[]{:S(2)}, u32[]{:S(2)}) collective-permute-start(bf16[256,384]{1,0:T(8,128)(2,1)S(1)} %get-tuple-element.86.refs_2_), channel_id=1, source_target_pairs={{0,4},{4,0},{8,12},{12,8},{16,20},{20,16},{24,28},{28,24},{1,5},{5... | collective-permute-start | bytes 589832 | tf_op jit(solution)/shard_map/ppermute | solution.py:38
  89.3 1.5 %collective-permute-start.27 = (bf16[256,384]{1,0:T(8,128)(2,1)S(1)}, bf16[256,384]{1,0:T(8,128)(2,1)S(1)}, u32[]{:S(2)}, u32[]{:S(2)}) collective-permute-start(bf16[256,384]{1,0:T(8,128)(2,1)S(1)} %get-tuple-element.87.refs_3_), channel_id=1, source_target_pairs={{0,4},{4,0},{8,12},{12,8},{16,20},{20,16},{24,28},{28,24},{1,5},{5... | collective-permute-start | bytes 589832 | tf_op jit(solution)/shard_map/ppermute | solution.py:38
  (7 other events, 12.9 us)

commit v7 on v6

--- a/solution.py
+++ b/solution.py
@@ -511,6 +511,7 @@
     half = h_rows.shape[1] // 2
     down_kept = inner(h_rows[:, :half], out_rows).astype(kind)
     down_sent = inner(h_rows[:, half:], out_rows).astype(kind)
+    da_rows, _ = lax.optimization_barrier((da_rows, down_sent))
     up_kept = inner(da_rows[:, :half], r_rows).astype(kind)
     up_sent = inner(da_rows[:, half:], r_rows).astype(kind)
     down = Chain(down_kept, down_sent, seq_steps + tp_steps)

time: 96.4 us -> 94.7 us (0.982)
  waiting for transfers between devices: 24.1 us -> 21.7 us
    ppermute x29, waiting for transfers between devices: 24.1 us -> 21.7 us  [swap(): return lax.ppermute(value, axis, pairs)]
where the time goes in v7:
time: 94.7 us; the launch traced here: 94.5 us
  starting transfers between devices  31.7 us (33%)
  Pallas kernels  22.4 us (24%)
  waiting for transfers between devices  21.7 us (23%)
  matrix products  12.6 us (13%)
  local copies, waits for them, and re-layouts  3.19 us (3%)
  other arithmetic  1.67 us (2%)
  between operations  1.14 us (1%)
    ppermute x29, starting transfers between devices, swap(): return lax.ppermute(value, axis, pairs)  31.7 us
    pallas_call x24, Pallas kernels, run(): pl.pallas_call(kernel, out_shape=tuple(outs), grid_spec=pltpu.PrefetchSca...  22.4 us
    ppermute x29, waiting for transfers between devices, swap(): return lax.ppermute(value, axis, pairs)  21.7 us
    dot_general x8, matrix products, inner(): lax.dot_general(left, right, (((0,), (0,)), ((), ())), preferred_element_...  4.63 us
    dot_general x3, matrix products, outer(): lax.dot_general(left, right, (((1,), (1,)), ((), ())), preferred_element_...  3.32 us
    dot_general x2, matrix products, times(): return jnp.dot(left, right, preferred_element_type=F32)  3.21 us
    unnamed x26, local copies, waits for them, and re-layouts  2.63 us
  transfers between devices with their start and end apart: 29, of which 15 were waited for; matrix products, arithmetic and copies ran while one was open for 16% of the time, Pallas kernels for 20%

profile of v7, /device:TPU:0, one launch (start us, length us, event | category | flops | bytes accessed | tf_op | source)
XLA Modules:
  0.0 94.5 jit_solution(15753106614687447287)
XLA Ops:
  2.4 1.7 %shard_map.144 = (bf16[64,1024]{1,0:T(8,128)(2,1)S(1)}, bf16[64,1024]{1,0:T(8,128)(2,1)}, bf16[64,1024]{1,0:T(8,128)(2,1)}, bf16[64,1024]{1,0:T(8,128)(2,1)}) custom-call(s32[13]{0:T(128)S(1)} %stack.55.refs_0_, bf16[256,1024]{1,0:T(8,128)(2,1)S(1)} %copy-done.7), custom_call_target="tpu_custom_call" | custom-call | flops 6000000000 | tf_op jit(solution)/shard_map/pallas_call | solution.py:60
  4.1 3.0 %collective-permute-start = (bf16[64,1024]{1,0:T(8,128)(2,1)}, bf16[64,1024]{1,0:T(8,128)(2,1)S(1)}, u32[]{:S(2)}, u32[]{:S(2)}) collective-permute-start(bf16[64,1024]{1,0:T(8,128)(2,1)} %get-tuple-element.53), channel_id=1, source_target_pairs={{0,1},{1,0},{2,3},{3,2},{4,5},{5,4},{6,7},{7,6},{8,9},{9,8},{10,11... | collective-permute-start | bytes 393224 | tf_op jit(solution)/shard_map/ppermute | solution.py:38
  7.1 2.6 %collective-permute-start.1 = (bf16[64,1024]{1,0:T(8,128)(2,1)}, bf16[64,1024]{1,0:T(8,128)(2,1)S(1)}, u32[]{:S(2)}, u32[]{:S(2)}) collective-permute-start(bf16[64,1024]{1,0:T(8,128)(2,1)} %get-tuple-element.54), channel_id=1, source_target_pairs={{0,2},{1,3},{2,0},{3,1},{4,6},{5,7},{6,4},{7,5},{8,10},{9,11},{10,... | collective-permute-start | bytes 393224 | tf_op jit(solution)/shard_map/ppermute | solution.py:38
  10.5 1.5 %fusion.39 = bf16[512,1024]{1,0:T(8,128)(2,1)S(1)} fusion(bf16[512,256]{1,0:T(8,128)(2,1)S(1)} %get-tuple-element.56.refs_3_, bf16[256,1024]{1,0:T(8,128)(2,1)} %param.14), kind=kOutput, calls=%fused_computation.71 | convolution fusion | flops 268435456 | bytes 1835008 | tf_op jit(solution)/shard_map/dot_general | solution.py:384
  12.7 1.4 %multiply_reduce_fusion.2 = (f32[512]{0:T(512)S(1)}, f32[512,1024]{1,0:T(8,128)S(1)}) fusion(bf16[512,1024]{1,0:T(8,128)(2,1)S(1)} %fusion.39, bf16[512,1024]{1,0:T(8,128)(2,1)S(1)} %shard_map.146, bf16[1024,1024]{1,0:T(8,128)(2,1)S(1)} %copy-done), kind=kOutput, calls=%fused_computation.9 | convolution fusion | flops 1075838464 | bytes 6293504 | tf_op jit(solution)/shard_map/dot_general | solution.py:32
  14.9 2.6 %shard_map.147 = bf16[1024,1024]{1,0:T(8,128)(2,1)S(1)} custom-call(s32[13]{0:T(128)S(1)} %stack.55.refs_0_, bf16[1024,2048]{1,0:T(8,128)(2,1)S(1)} %copy-done.1, bf16[512,1024]{1,0:T(8,128)(2,1)S(1)} %multiply_convert_fusion.3.refs_2_), custom_call_target="tpu_custom_call" | custom-call | tf_op jit(solution)/shard_map/pallas_call | solution.py:60
  17.5 1.8 %multiply_convert_fusion.1 = (bf16[512,1024]{1,0:T(8,128)(2,1)S(1)}, bf16[512,1024]{1,0:T(8,128)(2,1)S(1)}) fusion(bf16[512,1024]{1,0:T(8,128)(2,1)S(1)} %multiply_convert_fusion.3.refs_2_, bf16[1024,1024]{1,0:T(8,128)(2,1)S(1)} %shard_map.147), kind=kOutput, calls=%fused_computation.5 | convolution fusion | flops 1078984704 | bytes 5242880 | tf_op jit(solution)/shard_map/dot_general | solution.py:32
  20.2 2.0 %shard_map.148 = (bf16[256,1024]{1,0:T(8,128)(2,1)S(1)}, bf16[256,256]{1,0:T(8,128)(2,1)S(1)}) custom-call(s32[13]{0:T(128)S(1)} %stack.55.refs_0_, s32[8,128]{1,0:T(8,128)S(1)} %bitcast.38, bf16[64,1024]{1,0:T(8,128)(2,1)S(1)} %get-tuple-element.52.refs_3_.refs_2_, bf16[64,1024]{1,0:T(8,128)(2,1)S(1)} %collective-permute-done.refs_3_, ...), custom_call_target="tpu_custom_call" | custom-call | tf_op jit(solution)/shard_map/pallas_call | solution.py:60
  22.6 1.1 %shard_map.150 = bf16[1024,1024]{1,0:T(8,128)(2,1)S(1)} custom-call(s32[13]{0:T(128)S(1)} %stack.55.refs_0_, bf16[2048,1024]{1,0:T(8,128)(2,1)S(1)} %copy-done.2, bf16[512,1024]{1,0:T(8,128)(2,1)S(1)} %get-tuple-element.57.refs_2_), custom_call_target="tpu_custom_call" | custom-call | tf_op jit(solution)/shard_map/pallas_call | solution.py:60
  25.2 1.3 %multiply_convert_fusion = bf16[512,1024]{1,0:T(8,128)(2,1)S(1)} fusion(bf16[512,1024]{1,0:T(8,128)(2,1)S(1)} %get-tuple-element.60, bf16[512,1024]{1,0:T(8,128)(2,1)S(1)} %shard_map.149, bf16[1024,1024]{1,0:T(8,128)(2,1)S(1)} %shard_map.150), kind=kOutput, calls=%fused_computation.4 | convolution fusion | flops 1075314688 | bytes 5242880 | tf_op jit(solution)/shard_map/dot_general | solution.py:26
  26.5 1.3 %fusion.38 = (bf16[512,1024]{1,0:T(8,128)(2,1)S(1)}, f32[512,1024]{1,0:T(8,128)S(1)}) fusion(bf16[512,1024]{1,0:T(8,128)(2,1)S(1)} %multiply_convert_fusion, bf16[1024,1024]{1,0:T(8,128)(2,1)S(1)} %shard_map.147), kind=kOutput, calls=%fused_computation.70 | convolution fusion | flops 1074266112 | bytes 6291456 | tf_op jit(solution)/shard_map/dot_general | solution.py:26
  28.6 1.8 %collective-permute-start.11 = (bf16[512,1024]{1,0:T(8,128)(2,1)S(1)}, bf16[512,1024]{1,0:T(8,128)(2,1)S(1)}, u32[]{:S(2)}, u32[]{:S(2)}) collective-permute-start(bf16[512,1024]{1,0:T(8,128)(2,1)S(1)} %convolution_convert_fusion.3), channel_id=1, source_target_pairs={{0,8},{4,20},{8,0},{12,28},{16,24},{20,4},{24,16},{28,12},{1,9},{5... | collective-permute-start | bytes 3145736 | tf_op jit(solution)/shard_map/ppermute | solution.py:38
  31.2 1.9 %collective-permute-start.7 = (bf16[512,1024]{1,0:T(8,128)(2,1)S(1)}, bf16[512,1024]{1,0:T(8,128)(2,1)S(1)}, u32[]{:S(2)}, u32[]{:S(2)}) collective-permute-start(bf16[512,1024]{1,0:T(8,128)(2,1)S(1)} %convolution_convert_fusion.1), channel_id=1, source_target_pairs={{0,1},{1,0},{2,3},{3,2},{4,5},{5,4},{6,7},{7,6},{8,9},{9,8},{10,11... | collective-permute-start | bytes 3145736 | tf_op jit(solution)/shard_map/ppermute | solution.py:38
  39.1 1.6 %collective-permute-start.15 = (bf16[256,1024]{1,0:T(8,128)(2,1)S(1)}, bf16[256,1024]{1,0:T(8,128)(2,1)S(1)}, u32[]{:S(2)}, u32[]{:S(2)}) collective-permute-start(bf16[256,1024]{1,0:T(8,128)(2,1)S(1)} %get-tuple-element.73), channel_id=1, source_target_pairs={{0,8},{4,20},{8,0},{12,28},{16,24},{20,4},{24,16},{28,12},{1,9},{5... | collective-permute-start | bytes 1572872 | tf_op jit(solution)/shard_map/ppermute | solution.py:38
  40.6 6.0 %collective-permute-done.9.refs_2_ = bf16[128,1152]{1,0:T(8,128)(2,1)S(1)} collective-permute-done((bf16[128,1152]{1,0:T(8,128)(2,1)S(1)}, bf16[128,1152]{1,0:T(8,128)(2,1)S(1)}, u32[]{:S(2)}, u32[]{:S(2)}) %collective-permute-start.9) | collective-permute-done | bytes 294944 | tf_op jit(solution)/shard_map/ppermute | solution.py:38
  47.3 1.8 %collective-permute-start.10 = (bf16[64,1152]{1,0:T(8,128)(2,1)S(1)}, bf16[64,1152]{1,0:T(8,128)(2,1)S(1)}, u32[]{:S(2)}, u32[]{:S(2)}) collective-permute-start(bf16[64,1152]{1,0:T(8,128)(2,1)S(1)} %get-tuple-element.68), channel_id=1, source_target_pairs={{0,16},{4,12},{8,24},{12,4},{16,0},{20,28},{24,8},{28,20},{1,17},{... | collective-permute-start | bytes 442376 | tf_op jit(solution)/shard_map/ppermute | solution.py:38
  50.2 3.1 %collective-permute-done.10.refs_2_ = bf16[64,1152]{1,0:T(8,128)(2,1)S(1)} collective-permute-done((bf16[64,1152]{1,0:T(8,128)(2,1)S(1)}, bf16[64,1152]{1,0:T(8,128)(2,1)S(1)}, u32[]{:S(2)}, u32[]{:S(2)}) %collective-permute-start.10) | collective-permute-done | bytes 147488 | tf_op jit(solution)/shard_map/ppermute | solution.py:38
  53.9 2.1 %collective-permute-start.14 = (bf16[64,1152]{1,0:T(8,128)(2,1)S(1)}, bf16[64,1152]{1,0:T(8,128)(2,1)S(1)}, u32[]{:S(2)}, u32[]{:S(2)}) collective-permute-start(bf16[64,1152]{1,0:T(8,128)(2,1)S(1)} %shard_map.155.refs_3_.refs_1_), channel_id=1, source_target_pairs={{0,1},{1,0},{2,3},{3,2},{4,5},{5,4},{6,7},{7,6},{8,9},{9,8},{10,11... | collective-permute-start | bytes 442376 | tf_op jit(solution)/shard_map/ppermute | solution.py:38
  59.1 1.9 %collective-permute-start.17 = (bf16[128,1024]{1,0:T(8,128)(2,1)S(1)}, bf16[128,1024]{1,0:T(8,128)(2,1)S(1)}, u32[]{:S(2)}, u32[]{:S(2)}) collective-permute-start(bf16[128,1024]{1,0:T(8,128)(2,1)S(1)} %get-tuple-element.78), channel_id=1, source_target_pairs={{0,1},{1,0},{2,3},{3,2},{4,5},{5,4},{6,7},{7,6},{8,9},{9,8},{10,11... | collective-permute-start | bytes 786440 | tf_op jit(solution)/shard_map/ppermute | solution.py:38
  61.6 2.4 %collective-permute-start.16 = (bf16[64,1152]{1,0:T(8,128)(2,1)S(1)}, bf16[64,1152]{1,0:T(8,128)(2,1)S(1)}, u32[]{:S(2)}, u32[]{:S(2)}) collective-permute-start(bf16[64,1152]{1,0:T(8,128)(2,1)S(1)} %shard_map.158.refs_3_.refs_1_), channel_id=1, source_target_pairs={{0,2},{1,3},{2,0},{3,1},{4,6},{5,7},{6,4},{7,5},{8,10},{9,11},{10,... | collective-permute-start | bytes 442376 | tf_op jit(solution)/shard_map/ppermute | solution.py:38
  65.5 1.3 %collective-permute-done.12.refs_2_ = bf16[256,1024]{1,0:T(8,128)(2,1)S(1)} collective-permute-done((bf16[256,1024]{1,0:T(8,128)(2,1)S(1)}, bf16[256,1024]{1,0:T(8,128)(2,1)S(1)}, u32[]{:S(2)}, u32[]{:S(2)}) %collective-permute-start.12) | collective-permute-done | bytes 524320 | tf_op jit(solution)/shard_map/ppermute | solution.py:38
  69.2 2.3 %collective-permute-done.17.refs_2_ = bf16[128,1024]{1,0:T(8,128)(2,1)S(1)} collective-permute-done((bf16[128,1024]{1,0:T(8,128)(2,1)S(1)}, bf16[128,1024]{1,0:T(8,128)(2,1)S(1)}, u32[]{:S(2)}, u32[]{:S(2)}) %collective-permute-start.17) | collective-permute-done | bytes 262176 | tf_op jit(solution)/shard_map/ppermute | solution.py:38
  72.2 1.6 %collective-permute-start.21 = (bf16[64,1024]{1,0:T(8,128)(2,1)S(1)}, bf16[64,1024]{1,0:T(8,128)(2,1)S(1)}, u32[]{:S(2)}, u32[]{:S(2)}) collective-permute-start(bf16[64,1024]{1,0:T(8,128)(2,1)S(1)} %get-tuple-element.82), channel_id=1, source_target_pairs={{0,16},{4,12},{8,24},{12,4},{16,0},{20,28},{24,8},{28,20},{1,17},{... | collective-permute-start | bytes 393224 | tf_op jit(solution)/shard_map/ppermute | solution.py:38
  75.2 2.1 %collective-permute-done.21.refs_6_ = bf16[64,1024]{1,0:T(8,128)(2,1)S(1)} collective-permute-done((bf16[64,1024]{1,0:T(8,128)(2,1)S(1)}, bf16[64,1024]{1,0:T(8,128)(2,1)S(1)}, u32[]{:S(2)}, u32[]{:S(2)}) %collective-permute-start.21) | collective-permute-done | bytes 131104 | tf_op jit(solution)/shard_map/ppermute | solution.py:38
  78.0 1.7 %collective-permute-start.28 = (bf16[160,1024]{1,0:T(8,128)(2,1)S(1)}, bf16[160,1024]{1,0:T(8,128)(2,1)S(1)}, u32[]{:S(2)}, u32[]{:S(2)}) collective-permute-start(bf16[160,1024]{1,0:T(8,128)(2,1)S(1)} %get-tuple-element.93), channel_id=1, source_target_pairs={{0,2},{1,3},{2,0},{3,1},{4,6},{5,7},{6,4},{7,5},{8,10},{9,11},{10,... | collective-permute-start | bytes 983048 | tf_op jit(solution)/shard_map/ppermute | solution.py:38
  80.2 1.2 %collective-permute-start.22 = (bf16[128,384]{1,0:T(8,128)(2,1)S(1)}, bf16[128,384]{1,0:T(8,128)(2,1)S(1)}, u32[]{:S(2)}, u32[]{:S(2)}) collective-permute-start(bf16[128,384]{1,0:T(8,128)(2,1)S(1)} %get-tuple-element.84.refs_1_.refs_7_), channel_id=1, source_target_pairs={{0,8},{4,20},{8,0},{12,28},{16,24},{20,4},{24,16},{28,12},{1,9},{5... | collective-permute-start | bytes 294920 | tf_op jit(solution)/shard_map/ppermute | solution.py:38
  82.3 1.1 %collective-permute-start.24 = (bf16[128,384]{1,0:T(8,128)(2,1)S(1)}, bf16[128,384]{1,0:T(8,128)(2,1)S(1)}, u32[]{:S(2)}, u32[]{:S(2)}) collective-permute-start(bf16[128,384]{1,0:T(8,128)(2,1)S(1)} %get-tuple-element.86.refs_3_), channel_id=1, source_target_pairs={{0,8},{4,20},{8,0},{12,28},{16,24},{20,4},{24,16},{28,12},{1,9},{5... | collective-permute-start | bytes 294920 | tf_op jit(solution)/shard_map/ppermute | solution.py:38
  83.4 1.5 %collective-permute-done.22.refs_4_ = bf16[128,384]{1,0:T(8,128)(2,1)S(1)} collective-permute-done((bf16[128,384]{1,0:T(8,128)(2,1)S(1)}, bf16[128,384]{1,0:T(8,128)(2,1)S(1)}, u32[]{:S(2)}, u32[]{:S(2)}) %collective-permute-start.22) | collective-permute-done | bytes 98336 | tf_op jit(solution)/shard_map/ppermute | solution.py:38
  84.9 1.1 %collective-permute-done.23.refs_5_ = bf16[128,384]{1,0:T(8,128)(2,1)S(1)} collective-permute-done((bf16[128,384]{1,0:T(8,128)(2,1)S(1)}, bf16[128,384]{1,0:T(8,128)(2,1)S(1)}, u32[]{:S(2)}, u32[]{:S(2)}) %collective-permute-start.23) | collective-permute-done | bytes 98336 | tf_op jit(solution)/shard_map/ppermute | solution.py:38
  86.0 1.1 %collective-permute-done.24.refs_6_ = bf16[128,384]{1,0:T(8,128)(2,1)S(1)} collective-permute-done((bf16[128,384]{1,0:T(8,128)(2,1)S(1)}, bf16[128,384]{1,0:T(8,128)(2,1)S(1)}, u32[]{:S(2)}, u32[]{:S(2)}) %collective-permute-start.24) | collective-permute-done | bytes 98336 | tf_op jit(solution)/shard_map/ppermute | solution.py:38
  89.8 2.0 %shard_map.166 = (f32[256,1024]{1,0:T(8,128)}, f32[256,1024]{1,0:T(8,128)}, f32[8,128]{1,0:T(8,128)}) custom-call(s32[13]{0:T(128)S(1)} %stack.55.refs_0_, bf16[256,384]{1,0:T(8,128)(2,1)S(1)} %get-tuple-element.87.refs_1_.refs_7_, bf16[256,384]{1,0:T(8,128)(2,1)S(1)} %get-tuple-element.88.refs_2_, bf16[256,384]{1,0:T(8,128)(2,1)S(1)} %get-tuple-element.89.refs_3_, ...), custom_call_target="tpu_custom_call" | custom-call | tf_op jit(solution)/shard_map/pallas_call | solution.py:60
  93.1 1.4 %shard_map.167 = (f32[64,1024]{1,0:T(8,128)}, f32[64,1024]{1,0:T(8,128)}, f32[32,1024]{1,0:T(8,128)}) custom-call(s32[13]{0:T(128)S(1)} %stack.55.refs_0_, bf16[160,1024]{1,0:T(8,128)(2,1)S(1)} %get-tuple-element.83.refs_3_.refs_1_, bf16[160,1024]{1,0:T(8,128)(2,1)S(1)} %collective-permute-done.28.refs_2_, f32[8,128]{1,0:T(8,128)S(1)} %copy-done.6), custom_call_target="tpu_custom_call" | custom-call | tf_op jit(solution)/shard_map/pallas_call | solution.py:60
  (102 shorter events, 32.2 us)
Async XLA Ops:
  0.6 12.0 %copy-start = (bf16[1024,1024]{1,0:T(8,128)(2,1)S(1)}, bf16[1024,1024]{1,0:T(8,128)(2,1)}, u32[]{:S(2)}) copy-start(bf16[1024,1024]{1,0:T(8,128)(2,1)} %param.13) | copy-start | bytes 6291460
  0.6 9.0 %collective-permute-start.4 = (s32[8,128]{1,0:T(8,128)}, s32[8,128]{1,0:T(8,128)S(1)}, u32[]{:S(2)}, u32[]{:S(2)}) collective-permute-start(s32[8,128]{1,0:T(8,128)} %bitcast.36), channel_id=1, source_target_pairs={{0,4},{4,0},{8,12},{12,8},{16,20},{20,16},{24,28},{28,24},{1,5},{5... | collective-permute-start | bytes 12296 | tf_op jit(solution)/shard_map/ppermute | solution.py:38
  1.2 10.8 %collective-permute-start.3 = (bf16[128,2048]{1,0:T(8,128)(2,1)}, bf16[128,2048]{1,0:T(8,128)(2,1)S(1)}, u32[]{:S(2)}, u32[]{:S(2)}) collective-permute-start(bf16[128,2048]{1,0:T(8,128)(2,1)} %refs_1_.5), channel_id=1, source_target_pairs={{0,4},{4,0},{8,12},{12,8},{16,20},{20,16},{24,28},{28,24},{1,5},{5... | collective-permute-start | bytes 1572872 | tf_op jit(solution)/shard_map/ppermute | solution.py:38
  2.4 7.3 %copy-start.5 = (s32[128,8]{0,1:T(8,128)S(1)}, s32[128,8]{0,1:T(8,128)}, u32[]{:S(2)}) copy-start(s32[128,8]{0,1:T(8,128)} %param.9) | copy-start | bytes 12292
  4.1 8.0 %copy-start.3 = (bf16[128,2048]{1,0:T(8,128)(2,1)S(1)}, bf16[128,2048]{1,0:T(8,128)(2,1)}, u32[]{:S(2)}) copy-start(bf16[128,2048]{1,0:T(8,128)(2,1)} %refs_1_.5) | copy-start | bytes 1572868
  4.1 15.9 %collective-permute-start = (bf16[64,1024]{1,0:T(8,128)(2,1)}, bf16[64,1024]{1,0:T(8,128)(2,1)S(1)}, u32[]{:S(2)}, u32[]{:S(2)}) collective-permute-start(bf16[64,1024]{1,0:T(8,128)(2,1)} %get-tuple-element.53), channel_id=1, source_target_pairs={{0,1},{1,0},{2,3},{3,2},{4,5},{5,4},{6,7},{7,6},{8,9},{9,8},{10,11... | collective-permute-start | bytes 393224 | tf_op jit(solution)/shard_map/ppermute | solution.py:38
  7.1 13.1 %collective-permute-start.1 = (bf16[64,1024]{1,0:T(8,128)(2,1)}, bf16[64,1024]{1,0:T(8,128)(2,1)S(1)}, u32[]{:S(2)}, u32[]{:S(2)}) collective-permute-start(bf16[64,1024]{1,0:T(8,128)(2,1)} %get-tuple-element.54), channel_id=1, source_target_pairs={{0,2},{1,3},{2,0},{3,1},{4,6},{5,7},{6,4},{7,5},{8,10},{9,11},{10,... | collective-permute-start | bytes 393224 | tf_op jit(solution)/shard_map/ppermute | solution.py:38
  9.7 10.5 %collective-permute-start.2 = (bf16[64,1024]{1,0:T(8,128)(2,1)}, bf16[64,1024]{1,0:T(8,128)(2,1)}, u32[]{:S(2)}, u32[]{:S(2)}) collective-permute-start(bf16[64,1024]{1,0:T(8,128)(2,1)} %get-tuple-element.55), channel_id=1, source_target_pairs={{0,3},{1,2},{2,1},{3,0},{4,7},{5,6},{6,5},{7,4},{8,11},{9,10},{10,... | collective-permute-start | bytes 393224 | tf_op jit(solution)/shard_map/ppermute | solution.py:38
  22.2 2.4 %collective-permute-start.5 = (bf16[256,1024]{1,0:T(8,128)(2,1)S(1)}, bf16[256,1024]{1,0:T(8,128)(2,1)S(1)}, u32[]{:S(2)}, u32[]{:S(2)}) collective-permute-start(bf16[256,1024]{1,0:T(8,128)(2,1)S(1)} %get-tuple-element.58.refs_1_), channel_id=1, source_target_pairs={{0,4},{4,0},{8,12},{12,8},{16,20},{20,16},{24,28},{28,24},{1,5},{5... | collective-permute-start | bytes 1572872 | tf_op jit(solution)/shard_map/ppermute | solution.py:38
  24.0 12.3 %collective-permute-start.8 = (bf16[128,1024]{1,0:T(8,128)(2,1)S(1)}, bf16[128,1024]{1,0:T(8,128)(2,1)S(1)}, u32[]{:S(2)}, u32[]{:S(2)}) collective-permute-start(bf16[128,1024]{1,0:T(8,128)(2,1)S(1)} %get-tuple-element.116), channel_id=1, source_target_pairs={{0,4},{4,0},{8,12},{12,8},{16,20},{20,16},{24,28},{28,24},{1,5},{5... | collective-permute-start | bytes 786440 | tf_op jit(solution)/shard_map/ppermute | solution.py:38
  27.8 6.8 %collective-permute-start.6 = (bf16[512,1024]{1,0:T(8,128)(2,1)S(1)}, bf16[512,1024]{1,0:T(8,128)(2,1)S(1)}, u32[]{:S(2)}, u32[]{:S(2)}) collective-permute-start(bf16[512,1024]{1,0:T(8,128)(2,1)S(1)} %get-tuple-element.120), channel_id=1, source_target_pairs={{0,4},{4,0},{8,12},{12,8},{16,20},{20,16},{24,28},{28,24},{1,5},{5... | collective-permute-start | bytes 3145736 | tf_op jit(solution)/shard_map/ppermute | solution.py:38
  28.6 20.4 %collective-permute-start.11 = (bf16[512,1024]{1,0:T(8,128)(2,1)S(1)}, bf16[512,1024]{1,0:T(8,128)(2,1)S(1)}, u32[]{:S(2)}, u32[]{:S(2)}) collective-permute-start(bf16[512,1024]{1,0:T(8,128)(2,1)S(1)} %convolution_convert_fusion.3), channel_id=1, source_target_pairs={{0,8},{4,20},{8,0},{12,28},{16,24},{20,4},{24,16},{28,12},{1,9},{5... | collective-permute-start | bytes 3145736 | tf_op jit(solution)/shard_map/ppermute | solution.py:38
  31.2 25.6 %collective-permute-start.7 = (bf16[512,1024]{1,0:T(8,128)(2,1)S(1)}, bf16[512,1024]{1,0:T(8,128)(2,1)S(1)}, u32[]{:S(2)}, u32[]{:S(2)}) collective-permute-start(bf16[512,1024]{1,0:T(8,128)(2,1)S(1)} %convolution_convert_fusion.1), channel_id=1, source_target_pairs={{0,1},{1,0},{2,3},{3,2},{4,5},{5,4},{6,7},{7,6},{8,9},{9,8},{10,11... | collective-permute-start | bytes 3145736 | tf_op jit(solution)/shard_map/ppermute | solution.py:38
  37.0 9.7 %collective-permute-start.9 = (bf16[128,1152]{1,0:T(8,128)(2,1)S(1)}, bf16[128,1152]{1,0:T(8,128)(2,1)S(1)}, u32[]{:S(2)}, u32[]{:S(2)}) collective-permute-start(bf16[128,1152]{1,0:T(8,128)(2,1)S(1)} %get-tuple-element.64), channel_id=1, source_target_pairs={{0,8},{4,20},{8,0},{12,28},{16,24},{20,4},{24,16},{28,12},{1,9},{5... | collective-permute-start | bytes 884744 | tf_op jit(solution)/shard_map/ppermute | solution.py:38
  39.1 19.4 %collective-permute-start.15 = (bf16[256,1024]{1,0:T(8,128)(2,1)S(1)}, bf16[256,1024]{1,0:T(8,128)(2,1)S(1)}, u32[]{:S(2)}, u32[]{:S(2)}) collective-permute-start(bf16[256,1024]{1,0:T(8,128)(2,1)S(1)} %get-tuple-element.73), channel_id=1, source_target_pairs={{0,8},{4,20},{8,0},{12,28},{16,24},{20,4},{24,16},{28,12},{1,9},{5... | collective-permute-start | bytes 1572872 | tf_op jit(solution)/shard_map/ppermute | solution.py:38
  47.3 6.1 %collective-permute-start.10 = (bf16[64,1152]{1,0:T(8,128)(2,1)S(1)}, bf16[64,1152]{1,0:T(8,128)(2,1)S(1)}, u32[]{:S(2)}, u32[]{:S(2)}) collective-permute-start(bf16[64,1152]{1,0:T(8,128)(2,1)S(1)} %get-tuple-element.68), channel_id=1, source_target_pairs={{0,16},{4,12},{8,24},{12,4},{16,0},{20,28},{24,8},{28,20},{1,17},{... | collective-permute-start | bytes 442376 | tf_op jit(solution)/shard_map/ppermute | solution.py:38
  49.8 14.2 %collective-permute-start.13 = (bf16[256,1024]{1,0:T(8,128)(2,1)S(1)}, bf16[256,1024]{1,0:T(8,128)(2,1)S(1)}, u32[]{:S(2)}, u32[]{:S(2)}) collective-permute-start(bf16[256,1024]{1,0:T(8,128)(2,1)S(1)} %get-tuple-element.72), channel_id=1, source_target_pairs={{0,16},{4,12},{8,24},{12,4},{16,0},{20,28},{24,8},{28,20},{1,17},{... | collective-permute-start | bytes 1572872 | tf_op jit(solution)/shard_map/ppermute | solution.py:38
  53.9 7.1 %collective-permute-start.14 = (bf16[64,1152]{1,0:T(8,128)(2,1)S(1)}, bf16[64,1152]{1,0:T(8,128)(2,1)S(1)}, u32[]{:S(2)}, u32[]{:S(2)}) collective-permute-start(bf16[64,1152]{1,0:T(8,128)(2,1)S(1)} %shard_map.155.refs_3_.refs_1_), channel_id=1, source_target_pairs={{0,1},{1,0},{2,3},{3,2},{4,5},{5,4},{6,7},{7,6},{8,9},{9,8},{10,11... | collective-permute-start | bytes 442376 | tf_op jit(solution)/shard_map/ppermute | solution.py:38
  57.6 9.2 %collective-permute-start.12 = (bf16[256,1024]{1,0:T(8,128)(2,1)S(1)}, bf16[256,1024]{1,0:T(8,128)(2,1)S(1)}, u32[]{:S(2)}, u32[]{:S(2)}) collective-permute-start(bf16[256,1024]{1,0:T(8,128)(2,1)S(1)} %get-tuple-element.71), channel_id=1, source_target_pairs={{0,8},{4,20},{8,0},{12,28},{16,24},{20,4},{24,16},{28,12},{1,9},{5... | collective-permute-start | bytes 1572872 | tf_op jit(solution)/shard_map/ppermute | solution.py:38
  59.1 12.5 %collective-permute-start.17 = (bf16[128,1024]{1,0:T(8,128)(2,1)S(1)}, bf16[128,1024]{1,0:T(8,128)(2,1)S(1)}, u32[]{:S(2)}, u32[]{:S(2)}) collective-permute-start(bf16[128,1024]{1,0:T(8,128)(2,1)S(1)} %get-tuple-element.78), channel_id=1, source_target_pairs={{0,1},{1,0},{2,3},{3,2},{4,5},{5,4},{6,7},{7,6},{8,9},{9,8},{10,11... | collective-permute-start | bytes 786440 | tf_op jit(solution)/shard_map/ppermute | solution.py:38
  61.6 12.2 %collective-permute-start.16 = (bf16[64,1152]{1,0:T(8,128)(2,1)S(1)}, bf16[64,1152]{1,0:T(8,128)(2,1)S(1)}, u32[]{:S(2)}, u32[]{:S(2)}) collective-permute-start(bf16[64,1152]{1,0:T(8,128)(2,1)S(1)} %shard_map.158.refs_3_.refs_1_), channel_id=1, source_target_pairs={{0,2},{1,3},{2,0},{3,1},{4,6},{5,7},{6,4},{7,5},{8,10},{9,11},{10,... | collective-permute-start | bytes 442376 | tf_op jit(solution)/shard_map/ppermute | solution.py:38
  64.7 10.5 %collective-permute-start.19 = (bf16[128,1024]{1,0:T(8,128)(2,1)S(1)}, bf16[128,1024]{1,0:T(8,128)(2,1)S(1)}, u32[]{:S(2)}, u32[]{:S(2)}) collective-permute-start(bf16[128,1024]{1,0:T(8,128)(2,1)S(1)} %get-tuple-element.80), channel_id=1, source_target_pairs={{0,1},{1,0},{2,3},{3,2},{4,5},{5,4},{6,7},{7,6},{8,9},{9,8},{10,11... | collective-permute-start | bytes 786440 | tf_op jit(solution)/shard_map/ppermute | solution.py:38
  68.3 9.0 %collective-permute-start.20 = (bf16[128,1024]{1,0:T(8,128)(2,1)S(1)}, bf16[128,1024]{1,0:T(8,128)(2,1)S(1)}, u32[]{:S(2)}, u32[]{:S(2)}) collective-permute-start(bf16[128,1024]{1,0:T(8,128)(2,1)S(1)} %get-tuple-element.81), channel_id=1, source_target_pairs={{0,16},{4,12},{8,24},{12,4},{16,0},{20,28},{24,8},{28,20},{1,17},{... | collective-permute-start | bytes 786440 | tf_op jit(solution)/shard_map/ppermute | solution.py:38
  72.2 5.0 %collective-permute-start.21 = (bf16[64,1024]{1,0:T(8,128)(2,1)S(1)}, bf16[64,1024]{1,0:T(8,128)(2,1)S(1)}, u32[]{:S(2)}, u32[]{:S(2)}) collective-permute-start(bf16[64,1024]{1,0:T(8,128)(2,1)S(1)} %get-tuple-element.82), channel_id=1, source_target_pairs={{0,16},{4,12},{8,24},{12,4},{16,0},{20,28},{24,8},{28,20},{1,17},{... | collective-permute-start | bytes 393224 | tf_op jit(solution)/shard_map/ppermute | solution.py:38
  74.4 5.3 %collective-permute-start.18 = (bf16[64,1152]{1,0:T(8,128)(2,1)S(1)}, bf16[64,1152]{1,0:T(8,128)(2,1)S(1)}, u32[]{:S(2)}, u32[]{:S(2)}) collective-permute-start(bf16[64,1152]{1,0:T(8,128)(2,1)S(1)} %shard_map.162.refs_7_.refs_1_), channel_id=1, source_target_pairs={{0,16},{4,12},{8,24},{12,4},{16,0},{20,28},{24,8},{28,20},{1,17},{... | collective-permute-start | bytes 442376 | tf_op jit(solution)/shard_map/ppermute | solution.py:38
  78.0 14.4 %collective-permute-start.28 = (bf16[160,1024]{1,0:T(8,128)(2,1)S(1)}, bf16[160,1024]{1,0:T(8,128)(2,1)S(1)}, u32[]{:S(2)}, u32[]{:S(2)}) collective-permute-start(bf16[160,1024]{1,0:T(8,128)(2,1)S(1)} %get-tuple-element.93), channel_id=1, source_target_pairs={{0,2},{1,3},{2,0},{3,1},{4,6},{5,7},{6,4},{7,5},{8,10},{9,11},{10,... | collective-permute-start | bytes 983048 | tf_op jit(solution)/shard_map/ppermute | solution.py:38
  80.2 4.7 %collective-permute-start.22 = (bf16[128,384]{1,0:T(8,128)(2,1)S(1)}, bf16[128,384]{1,0:T(8,128)(2,1)S(1)}, u32[]{:S(2)}, u32[]{:S(2)}) collective-permute-start(bf16[128,384]{1,0:T(8,128)(2,1)S(1)} %get-tuple-element.84.refs_1_.refs_7_), channel_id=1, source_target_pairs={{0,8},{4,20},{8,0},{12,28},{16,24},{20,4},{24,16},{28,12},{1,9},{5... | collective-permute-start | bytes 294920 | tf_op jit(solution)/shard_map/ppermute | solution.py:38
  81.4 4.6 %collective-permute-start.23 = (bf16[128,384]{1,0:T(8,128)(2,1)S(1)}, bf16[128,384]{1,0:T(8,128)(2,1)S(1)}, u32[]{:S(2)}, u32[]{:S(2)}) collective-permute-start(bf16[128,384]{1,0:T(8,128)(2,1)S(1)} %get-tuple-element.85.refs_2_), channel_id=1, source_target_pairs={{0,8},{4,20},{8,0},{12,28},{16,24},{20,4},{24,16},{28,12},{1,9},{5... | collective-permute-start | bytes 294920 | tf_op jit(solution)/shard_map/ppermute | solution.py:38
  82.3 4.8 %collective-permute-start.24 = (bf16[128,384]{1,0:T(8,128)(2,1)S(1)}, bf16[128,384]{1,0:T(8,128)(2,1)S(1)}, u32[]{:S(2)}, u32[]{:S(2)}) collective-permute-start(bf16[128,384]{1,0:T(8,128)(2,1)S(1)} %get-tuple-element.86.refs_3_), channel_id=1, source_target_pairs={{0,8},{4,20},{8,0},{12,28},{16,24},{20,4},{24,16},{28,12},{1,9},{5... | collective-permute-start | bytes 294920 | tf_op jit(solution)/shard_map/ppermute | solution.py:38
  87.7 1.5 %collective-permute-start.25 = (bf16[256,384]{1,0:T(8,128)(2,1)S(1)}, bf16[256,384]{1,0:T(8,128)(2,1)S(1)}, u32[]{:S(2)}, u32[]{:S(2)}) collective-permute-start(bf16[256,384]{1,0:T(8,128)(2,1)S(1)} %get-tuple-element.87.refs_1_.refs_7_), channel_id=1, source_target_pairs={{0,4},{4,0},{8,12},{12,8},{16,20},{20,16},{24,28},{28,24},{1,5},{5... | collective-permute-start | bytes 589832 | tf_op jit(solution)/shard_map/ppermute | solution.py:38
  87.8 1.7 %collective-permute-start.26 = (bf16[256,384]{1,0:T(8,128)(2,1)S(1)}, bf16[256,384]{1,0:T(8,128)(2,1)S(1)}, u32[]{:S(2)}, u32[]{:S(2)}) collective-permute-start(bf16[256,384]{1,0:T(8,128)(2,1)S(1)} %get-tuple-element.88.refs_2_), channel_id=1, source_target_pairs={{0,4},{4,0},{8,12},{12,8},{16,20},{20,16},{24,28},{28,24},{1,5},{5... | collective-permute-start | bytes 589832 | tf_op jit(solution)/shard_map/ppermute | solution.py:38
  88.3 1.5 %collective-permute-start.27 = (bf16[256,384]{1,0:T(8,128)(2,1)S(1)}, bf16[256,384]{1,0:T(8,128)(2,1)S(1)}, u32[]{:S(2)}, u32[]{:S(2)}) collective-permute-start(bf16[256,384]{1,0:T(8,128)(2,1)S(1)} %get-tuple-element.89.refs_3_), channel_id=1, source_target_pairs={{0,4},{4,0},{8,12},{12,8},{16,20},{20,16},{24,28},{28,24},{1,5},{5... | collective-permute-start | bytes 589832 | tf_op jit(solution)/shard_map/ppermute | solution.py:38
  (7 other events, 13.9 us)

commit v8 on v7

--- a/solution.py
+++ b/solution.py
@@ -363,7 +363,6 @@
         [],
         flops=STEP,
     )
-    blocks = [swap(b, "tp", (m,)) if m else b for m, b in enumerate(blocks)]
     far = pl.BlockSpec(memory_space=pltpu.HBM)
     prev_hot, prev_here = call(
         functools.partial(hots_body, own, tp_count, share_count, height, core_at),
@@ -371,6 +370,11 @@
         [ids_own, ids_other],
         [blocks[0]],
     )
+
+    near_rows, _ = lax.optimization_barrier((blocks[1], prev_hot))
+    blocks = [blocks[0], swap(near_rows, "tp", (1,))] + [
+        swap(blocks[m], "tp", (m,)) for m in range(2, tp_count)
+    ]
 
     def by_slot(value):
         return [value[:, j * slot : (j + 1) * slot] for j in range(own)]

time: 94.7 us -> 94 us (level)
  local copies, waits for them, and re-layouts: 3.19 us -> 4.58 us
  Pallas kernels: 22.4 us -> 21.3 us
  waiting for transfers between devices: 21.7 us -> 20.6 us
    unnamed x26 -> x28, local copies, waits for them, and re-layouts: 2.63 us -> 4.02 us
    pallas_call x24, Pallas kernels: 22.4 us -> 21.3 us  [run(): pl.pallas_call(kernel, out_shape=tuple(outs), grid_spec=pltpu.PrefetchSca...]
    ppermute x29, waiting for transfers between devices: 21.7 us -> 20.6 us  [swap(): return lax.ppermute(value, axis, pairs)]
  transfers between devices with their start and end apart: 29 -> 29, of which waited for: 15 -> 13; matrix products, arithmetic and copies ran while one was open for 16% -> 16% of each run, Pallas kernels for 20% -> 20%
where the time goes in v8:
time: 94 us; the launch traced here: 93.8 us
  starting transfers between devices  31.9 us (34%)
  Pallas kernels  21.3 us (23%)
  waiting for transfers between devices  20.6 us (22%)
  matrix products  12.6 us (13%)
  local copies, waits for them, and re-layouts  4.58 us (5%)
  other arithmetic  1.67 us (2%)
  between operations  1.16 us (1%)
    ppermute x29, starting transfers between devices, swap(): return lax.ppermute(value, axis, pairs)  31.9 us
    pallas_call x24, Pallas kernels, run(): pl.pallas_call(kernel, out_shape=tuple(outs), grid_spec=pltpu.PrefetchSca...  21.3 us
    ppermute x29, waiting for transfers between devices, swap(): return lax.ppermute(value, axis, pairs)  20.6 us
    dot_general x8, matrix products, inner(): lax.dot_general(left, right, (((0,), (0,)), ((), ())), preferred_element_...  4.63 us
    unnamed x28, local copies, waits for them, and re-layouts  4.02 us
    dot_general x3, matrix products, outer(): lax.dot_general(left, right, (((1,), (1,)), ((), ())), preferred_element_...  3.31 us
    dot_general x2, matrix products, times(): return jnp.dot(left, right, preferred_element_type=F32)  3.21 us
  transfers between devices with their start and end apart: 29, of which 13 were waited for; matrix products, arithmetic and copies ran while one was open for 16% of the time, Pallas kernels for 20%

profile of v8, /device:TPU:0, one launch (start us, length us, event | category | flops | bytes accessed | tf_op | source)
XLA Modules:
  0.0 93.8 jit_solution(9072888800712627690)
XLA Ops:
  2.4 1.7 %shard_map.144 = (bf16[64,1024]{1,0:T(8,128)(2,1)S(1)}, bf16[64,1024]{1,0:T(8,128)(2,1)S(1)}, bf16[64,1024]{1,0:T(8,128)(2,1)}, bf16[64,1024]{1,0:T(8,128)(2,1)}) custom-call(s32[13]{0:T(128)S(1)} %stack.55.refs_0_, bf16[256,1024]{1,0:T(8,128)(2,1)S(1)} %copy-done.7), custom_call_target="tpu_custom_call" | custom-call | flops 6000000000 | tf_op jit(solution)/shard_map/pallas_call | solution.py:60
  4.7 4.0 %collective-permute-start.2 = (bf16[64,1024]{1,0:T(8,128)(2,1)}, bf16[64,1024]{1,0:T(8,128)(2,1)S(1)}, u32[]{:S(2)}, u32[]{:S(2)}) collective-permute-start(bf16[64,1024]{1,0:T(8,128)(2,1)} %get-tuple-element.57), channel_id=1, source_target_pairs={{0,2},{1,3},{2,0},{3,1},{4,6},{5,7},{6,4},{7,5},{8,10},{9,11},{10,... | collective-permute-start | bytes 393224 | tf_op jit(solution)/shard_map/ppermute | solution.py:38
  8.7 1.3 %collective-permute-start.3 = (bf16[64,1024]{1,0:T(8,128)(2,1)}, bf16[64,1024]{1,0:T(8,128)(2,1)S(1)}, u32[]{:S(2)}, u32[]{:S(2)}) collective-permute-start(bf16[64,1024]{1,0:T(8,128)(2,1)} %get-tuple-element.58), channel_id=1, source_target_pairs={{0,3},{1,2},{2,1},{3,0},{4,7},{5,6},{6,5},{7,4},{8,11},{9,10},{10,... | collective-permute-start | bytes 393224 | tf_op jit(solution)/shard_map/ppermute | solution.py:38
  11.2 1.5 %fusion.39 = bf16[512,1024]{1,0:T(8,128)(2,1)S(1)} fusion(bf16[512,256]{1,0:T(8,128)(2,1)S(1)} %get-tuple-element.55.refs_3_, bf16[256,1024]{1,0:T(8,128)(2,1)} %param.14), kind=kOutput, calls=%fused_computation.71 | convolution fusion | flops 268435456 | bytes 1835008 | tf_op jit(solution)/shard_map/dot_general | solution.py:388
  13.4 1.4 %multiply_reduce_fusion.2 = (f32[512]{0:T(512)S(1)}, f32[512,1024]{1,0:T(8,128)S(1)}) fusion(bf16[512,1024]{1,0:T(8,128)(2,1)S(1)} %fusion.39, bf16[512,1024]{1,0:T(8,128)(2,1)S(1)} %shard_map.146, bf16[1024,1024]{1,0:T(8,128)(2,1)S(1)} %copy-done), kind=kOutput, calls=%fused_computation.9 | convolution fusion | flops 1075838464 | bytes 6293504 | tf_op jit(solution)/shard_map/dot_general | solution.py:32
  15.6 2.6 %shard_map.147 = bf16[1024,1024]{1,0:T(8,128)(2,1)S(1)} custom-call(s32[13]{0:T(128)S(1)} %stack.55.refs_0_, bf16[1024,2048]{1,0:T(8,128)(2,1)S(1)} %copy-done.1, bf16[512,1024]{1,0:T(8,128)(2,1)S(1)} %multiply_convert_fusion.3.refs_2_), custom_call_target="tpu_custom_call" | custom-call | tf_op jit(solution)/shard_map/pallas_call | solution.py:60
  18.2 1.8 %multiply_convert_fusion.1 = (bf16[512,1024]{1,0:T(8,128)(2,1)S(1)}, bf16[512,1024]{1,0:T(8,128)(2,1)S(1)}) fusion(bf16[512,1024]{1,0:T(8,128)(2,1)S(1)} %multiply_convert_fusion.3.refs_2_, bf16[1024,1024]{1,0:T(8,128)(2,1)S(1)} %shard_map.147), kind=kOutput, calls=%fused_computation.5 | convolution fusion | flops 1078984704 | bytes 5242880 | tf_op jit(solution)/shard_map/dot_general | solution.py:32
  22.7 1.1 %shard_map.150 = bf16[1024,1024]{1,0:T(8,128)(2,1)S(1)} custom-call(s32[13]{0:T(128)S(1)} %stack.55.refs_0_, bf16[2048,1024]{1,0:T(8,128)(2,1)S(1)} %copy-done.2, bf16[512,1024]{1,0:T(8,128)(2,1)S(1)} %get-tuple-element.59.refs_2_), custom_call_target="tpu_custom_call" | custom-call | tf_op jit(solution)/shard_map/pallas_call | solution.py:60
  24.8 1.3 %multiply_convert_fusion = bf16[512,1024]{1,0:T(8,128)(2,1)S(1)} fusion(bf16[512,1024]{1,0:T(8,128)(2,1)S(1)} %get-tuple-element.62, bf16[512,1024]{1,0:T(8,128)(2,1)S(1)} %shard_map.149, bf16[1024,1024]{1,0:T(8,128)(2,1)S(1)} %shard_map.150), kind=kOutput, calls=%fused_computation.4 | convolution fusion | flops 1075314688 | bytes 5242880 | tf_op jit(solution)/shard_map/dot_general | solution.py:26
  26.1 1.3 %fusion.38 = (bf16[512,1024]{1,0:T(8,128)(2,1)S(1)}, f32[512,1024]{1,0:T(8,128)S(1)}) fusion(bf16[512,1024]{1,0:T(8,128)(2,1)S(1)} %multiply_convert_fusion, bf16[1024,1024]{1,0:T(8,128)(2,1)S(1)} %shard_map.147), kind=kOutput, calls=%fused_computation.70 | convolution fusion | flops 1074266112 | bytes 6291456 | tf_op jit(solution)/shard_map/dot_general | solution.py:26
  28.7 1.6 %collective-permute-start.11 = (bf16[512,1024]{1,0:T(8,128)(2,1)S(1)}, bf16[512,1024]{1,0:T(8,128)(2,1)S(1)}, u32[]{:S(2)}, u32[]{:S(2)}) collective-permute-start(bf16[512,1024]{1,0:T(8,128)(2,1)S(1)} %convolution_convert_fusion.3), channel_id=1, source_target_pairs={{0,8},{4,20},{8,0},{12,28},{16,24},{20,4},{24,16},{28,12},{1,9},{5... | collective-permute-start | bytes 3145736 | tf_op jit(solution)/shard_map/ppermute | solution.py:38
  31.0 1.9 %collective-permute-start.7 = (bf16[512,1024]{1,0:T(8,128)(2,1)S(1)}, bf16[512,1024]{1,0:T(8,128)(2,1)S(1)}, u32[]{:S(2)}, u32[]{:S(2)}) collective-permute-start(bf16[512,1024]{1,0:T(8,128)(2,1)S(1)} %convolution_convert_fusion.1), channel_id=1, source_target_pairs={{0,1},{1,0},{2,3},{3,2},{4,5},{5,4},{6,7},{7,6},{8,9},{9,8},{10,11... | collective-permute-start | bytes 3145736 | tf_op jit(solution)/shard_map/ppermute | solution.py:38
  38.9 1.6 %collective-permute-start.15 = (bf16[256,1024]{1,0:T(8,128)(2,1)S(1)}, bf16[256,1024]{1,0:T(8,128)(2,1)S(1)}, u32[]{:S(2)}, u32[]{:S(2)}) collective-permute-start(bf16[256,1024]{1,0:T(8,128)(2,1)S(1)} %get-tuple-element.75), channel_id=1, source_target_pairs={{0,8},{4,20},{8,0},{12,28},{16,24},{20,4},{24,16},{28,12},{1,9},{5... | collective-permute-start | bytes 1572872 | tf_op jit(solution)/shard_map/ppermute | solution.py:38
  40.4 6.3 %collective-permute-done.9.refs_2_ = bf16[128,1152]{1,0:T(8,128)(2,1)S(1)} collective-permute-done((bf16[128,1152]{1,0:T(8,128)(2,1)S(1)}, bf16[128,1152]{1,0:T(8,128)(2,1)S(1)}, u32[]{:S(2)}, u32[]{:S(2)}) %collective-permute-start.9) | collective-permute-done | bytes 294944 | tf_op jit(solution)/shard_map/ppermute | solution.py:38
  47.3 1.6 %collective-permute-start.10 = (bf16[64,1152]{1,0:T(8,128)(2,1)S(1)}, bf16[64,1152]{1,0:T(8,128)(2,1)S(1)}, u32[]{:S(2)}, u32[]{:S(2)}) collective-permute-start(bf16[64,1152]{1,0:T(8,128)(2,1)S(1)} %get-tuple-element.70), channel_id=1, source_target_pairs={{0,16},{4,12},{8,24},{12,4},{16,0},{20,28},{24,8},{28,20},{1,17},{... | collective-permute-start | bytes 442376 | tf_op jit(solution)/shard_map/ppermute | solution.py:38
  50.3 2.7 %collective-permute-done.10.refs_2_ = bf16[64,1152]{1,0:T(8,128)(2,1)S(1)} collective-permute-done((bf16[64,1152]{1,0:T(8,128)(2,1)S(1)}, bf16[64,1152]{1,0:T(8,128)(2,1)S(1)}, u32[]{:S(2)}, u32[]{:S(2)}) %collective-permute-start.10) | collective-permute-done | bytes 147488 | tf_op jit(solution)/shard_map/ppermute | solution.py:38
  53.5 1.9 %collective-permute-start.14 = (bf16[64,1152]{1,0:T(8,128)(2,1)S(1)}, bf16[64,1152]{1,0:T(8,128)(2,1)S(1)}, u32[]{:S(2)}, u32[]{:S(2)}) collective-permute-start(bf16[64,1152]{1,0:T(8,128)(2,1)S(1)} %shard_map.155.refs_3_.refs_1_), channel_id=1, source_target_pairs={{0,1},{1,0},{2,3},{3,2},{4,5},{5,4},{6,7},{7,6},{8,9},{9,8},{10,11... | collective-permute-start | bytes 442376 | tf_op jit(solution)/shard_map/ppermute | solution.py:38
  56.9 1.6 %collective-permute-start.12 = (bf16[256,1024]{1,0:T(8,128)(2,1)S(1)}, bf16[256,1024]{1,0:T(8,128)(2,1)S(1)}, u32[]{:S(2)}, u32[]{:S(2)}) collective-permute-start(bf16[256,1024]{1,0:T(8,128)(2,1)S(1)} %get-tuple-element.73), channel_id=1, source_target_pairs={{0,8},{4,20},{8,0},{12,28},{16,24},{20,4},{24,16},{28,12},{1,9},{5... | collective-permute-start | bytes 1572872 | tf_op jit(solution)/shard_map/ppermute | solution.py:38
  59.1 1.8 %collective-permute-start.17 = (bf16[128,1024]{1,0:T(8,128)(2,1)S(1)}, bf16[128,1024]{1,0:T(8,128)(2,1)S(1)}, u32[]{:S(2)}, u32[]{:S(2)}) collective-permute-start(bf16[128,1024]{1,0:T(8,128)(2,1)S(1)} %get-tuple-element.80), channel_id=1, source_target_pairs={{0,1},{1,0},{2,3},{3,2},{4,5},{5,4},{6,7},{7,6},{8,9},{9,8},{10,11... | collective-permute-start | bytes 786440 | tf_op jit(solution)/shard_map/ppermute | solution.py:38
  61.5 1.8 %collective-permute-start.16 = (bf16[64,1152]{1,0:T(8,128)(2,1)S(1)}, bf16[64,1152]{1,0:T(8,128)(2,1)S(1)}, u32[]{:S(2)}, u32[]{:S(2)}) collective-permute-start(bf16[64,1152]{1,0:T(8,128)(2,1)S(1)} %shard_map.158.refs_3_.refs_1_), channel_id=1, source_target_pairs={{0,2},{1,3},{2,0},{3,1},{4,6},{5,7},{6,4},{7,5},{8,10},{9,11},{10,... | collective-permute-start | bytes 442376 | tf_op jit(solution)/shard_map/ppermute | solution.py:38
  64.0 1.4 %collective-permute-start.19 = (bf16[128,1024]{1,0:T(8,128)(2,1)S(1)}, bf16[128,1024]{1,0:T(8,128)(2,1)S(1)}, u32[]{:S(2)}, u32[]{:S(2)}) collective-permute-start(bf16[128,1024]{1,0:T(8,128)(2,1)S(1)} %get-tuple-element.82), channel_id=1, source_target_pairs={{0,1},{1,0},{2,3},{3,2},{4,5},{5,4},{6,7},{7,6},{8,9},{9,8},{10,11... | collective-permute-start | bytes 786440 | tf_op jit(solution)/shard_map/ppermute | solution.py:38
  68.6 2.6 %collective-permute-done.17.refs_2_ = bf16[128,1024]{1,0:T(8,128)(2,1)S(1)} collective-permute-done((bf16[128,1024]{1,0:T(8,128)(2,1)S(1)}, bf16[128,1024]{1,0:T(8,128)(2,1)S(1)}, u32[]{:S(2)}, u32[]{:S(2)}) %collective-permute-start.17) | collective-permute-done | bytes 262176 | tf_op jit(solution)/shard_map/ppermute | solution.py:38
  71.7 1.1 %collective-permute-start.21 = (bf16[64,1024]{1,0:T(8,128)(2,1)S(1)}, bf16[64,1024]{1,0:T(8,128)(2,1)S(1)}, u32[]{:S(2)}, u32[]{:S(2)}) collective-permute-start(bf16[64,1024]{1,0:T(8,128)(2,1)S(1)} %get-tuple-element.84), channel_id=1, source_target_pairs={{0,16},{4,12},{8,24},{12,4},{16,0},{20,28},{24,8},{28,20},{1,17},{... | collective-permute-start | bytes 393224 | tf_op jit(solution)/shard_map/ppermute | solution.py:38
  74.5 2.3 %collective-permute-done.21.refs_6_ = bf16[64,1024]{1,0:T(8,128)(2,1)S(1)} collective-permute-done((bf16[64,1024]{1,0:T(8,128)(2,1)S(1)}, bf16[64,1024]{1,0:T(8,128)(2,1)S(1)}, u32[]{:S(2)}, u32[]{:S(2)}) %collective-permute-start.21) | collective-permute-done | bytes 131104 | tf_op jit(solution)/shard_map/ppermute | solution.py:38
  77.5 1.5 %collective-permute-start.28 = (bf16[160,1024]{1,0:T(8,128)(2,1)S(1)}, bf16[160,1024]{1,0:T(8,128)(2,1)S(1)}, u32[]{:S(2)}, u32[]{:S(2)}) collective-permute-start(bf16[160,1024]{1,0:T(8,128)(2,1)S(1)} %get-tuple-element.95), channel_id=1, source_target_pairs={{0,2},{1,3},{2,0},{3,1},{4,6},{5,7},{6,4},{7,5},{8,10},{9,11},{10,... | collective-permute-start | bytes 983048 | tf_op jit(solution)/shard_map/ppermute | solution.py:38
  79.6 1.6 %collective-permute-start.22 = (bf16[128,384]{1,0:T(8,128)(2,1)S(1)}, bf16[128,384]{1,0:T(8,128)(2,1)S(1)}, u32[]{:S(2)}, u32[]{:S(2)}) collective-permute-start(bf16[128,384]{1,0:T(8,128)(2,1)S(1)} %get-tuple-element.86.refs_1_.refs_7_), channel_id=1, source_target_pairs={{0,8},{4,20},{8,0},{12,28},{16,24},{20,4},{24,16},{28,12},{1,9},{5... | collective-permute-start | bytes 294920 | tf_op jit(solution)/shard_map/ppermute | solution.py:38
  81.6 1.5 %collective-permute-start.24 = (bf16[128,384]{1,0:T(8,128)(2,1)S(1)}, bf16[128,384]{1,0:T(8,128)(2,1)S(1)}, u32[]{:S(2)}, u32[]{:S(2)}) collective-permute-start(bf16[128,384]{1,0:T(8,128)(2,1)S(1)} %get-tuple-element.88.refs_3_), channel_id=1, source_target_pairs={{0,8},{4,20},{8,0},{12,28},{16,24},{20,4},{24,16},{28,12},{1,9},{5... | collective-permute-start | bytes 294920 | tf_op jit(solution)/shard_map/ppermute | solution.py:38
  83.1 1.1 %collective-permute-done.22.refs_4_ = bf16[128,384]{1,0:T(8,128)(2,1)S(1)} collective-permute-done((bf16[128,384]{1,0:T(8,128)(2,1)S(1)}, bf16[128,384]{1,0:T(8,128)(2,1)S(1)}, u32[]{:S(2)}, u32[]{:S(2)}) %collective-permute-start.22) | collective-permute-done | bytes 98336 | tf_op jit(solution)/shard_map/ppermute | solution.py:38
  84.2 1.5 %collective-permute-done.23.refs_5_ = bf16[128,384]{1,0:T(8,128)(2,1)S(1)} collective-permute-done((bf16[128,384]{1,0:T(8,128)(2,1)S(1)}, bf16[128,384]{1,0:T(8,128)(2,1)S(1)}, u32[]{:S(2)}, u32[]{:S(2)}) %collective-permute-start.23) | collective-permute-done | bytes 98336 | tf_op jit(solution)/shard_map/ppermute | solution.py:38
  85.7 1.1 %collective-permute-done.24.refs_6_ = bf16[128,384]{1,0:T(8,128)(2,1)S(1)} collective-permute-done((bf16[128,384]{1,0:T(8,128)(2,1)S(1)}, bf16[128,384]{1,0:T(8,128)(2,1)S(1)}, u32[]{:S(2)}, u32[]{:S(2)}) %collective-permute-start.24) | collective-permute-done | bytes 98336 | tf_op jit(solution)/shard_map/ppermute | solution.py:38
  89.4 2.0 %shard_map.166 = (f32[256,1024]{1,0:T(8,128)}, f32[256,1024]{1,0:T(8,128)}, f32[8,128]{1,0:T(8,128)}) custom-call(s32[13]{0:T(128)S(1)} %stack.55.refs_0_, bf16[256,384]{1,0:T(8,128)(2,1)S(1)} %get-tuple-element.89.refs_1_.refs_7_, bf16[256,384]{1,0:T(8,128)(2,1)S(1)} %get-tuple-element.90.refs_2_, bf16[256,384]{1,0:T(8,128)(2,1)S(1)} %get-tuple-element.91.refs_3_, ...), custom_call_target="tpu_custom_call" | custom-call | tf_op jit(solution)/shard_map/pallas_call | solution.py:60
  92.4 1.4 %shard_map.167 = (f32[64,1024]{1,0:T(8,128)}, f32[64,1024]{1,0:T(8,128)}, f32[32,1024]{1,0:T(8,128)}) custom-call(s32[13]{0:T(128)S(1)} %stack.55.refs_0_, bf16[160,1024]{1,0:T(8,128)(2,1)S(1)} %get-tuple-element.85.refs_3_.refs_1_, bf16[160,1024]{1,0:T(8,128)(2,1)S(1)} %collective-permute-done.28.refs_2_, f32[8,128]{1,0:T(8,128)S(1)} %copy-done.6), custom_call_target="tpu_custom_call" | custom-call | tf_op jit(solution)/shard_map/pallas_call | solution.py:60
  (104 shorter events, 33.2 us)
Async XLA Ops:
  0.6 12.7 %copy-start = (bf16[1024,1024]{1,0:T(8,128)(2,1)S(1)}, bf16[1024,1024]{1,0:T(8,128)(2,1)}, u32[]{:S(2)}) copy-start(bf16[1024,1024]{1,0:T(8,128)(2,1)} %param.13) | copy-start | bytes 6291460
  0.6 9.4 %collective-permute-start = (s32[8,128]{1,0:T(8,128)}, s32[8,128]{1,0:T(8,128)S(1)}, u32[]{:S(2)}, u32[]{:S(2)}) collective-permute-start(s32[8,128]{1,0:T(8,128)} %bitcast.36), channel_id=1, source_target_pairs={{0,4},{4,0},{8,12},{12,8},{16,20},{20,16},{24,28},{28,24},{1,5},{5... | collective-permute-start | bytes 12296 | tf_op jit(solution)/shard_map/ppermute | solution.py:38
  1.2 11.6 %collective-permute-start.4 = (bf16[128,2048]{1,0:T(8,128)(2,1)}, bf16[128,2048]{1,0:T(8,128)(2,1)S(1)}, u32[]{:S(2)}, u32[]{:S(2)}) collective-permute-start(bf16[128,2048]{1,0:T(8,128)(2,1)} %refs_1_.5), channel_id=1, source_target_pairs={{0,4},{4,0},{8,12},{12,8},{16,20},{20,16},{24,28},{28,24},{1,5},{5... | collective-permute-start | bytes 1572872 | tf_op jit(solution)/shard_map/ppermute | solution.py:38
  2.4 7.7 %copy-start.5 = (s32[128,8]{0,1:T(8,128)S(1)}, s32[128,8]{0,1:T(8,128)}, u32[]{:S(2)}) copy-start(s32[128,8]{0,1:T(8,128)} %param.9) | copy-start | bytes 12292
  4.7 8.0 %copy-start.3 = (bf16[128,2048]{1,0:T(8,128)(2,1)S(1)}, bf16[128,2048]{1,0:T(8,128)(2,1)}, u32[]{:S(2)}) copy-start(bf16[128,2048]{1,0:T(8,128)(2,1)} %refs_1_.5) | copy-start | bytes 1572868
  4.7 16.0 %collective-permute-start.2 = (bf16[64,1024]{1,0:T(8,128)(2,1)}, bf16[64,1024]{1,0:T(8,128)(2,1)S(1)}, u32[]{:S(2)}, u32[]{:S(2)}) collective-permute-start(bf16[64,1024]{1,0:T(8,128)(2,1)} %get-tuple-element.57), channel_id=1, source_target_pairs={{0,2},{1,3},{2,0},{3,1},{4,6},{5,7},{6,4},{7,5},{8,10},{9,11},{10,... | collective-permute-start | bytes 393224 | tf_op jit(solution)/shard_map/ppermute | solution.py:38
  8.7 12.0 %collective-permute-start.3 = (bf16[64,1024]{1,0:T(8,128)(2,1)}, bf16[64,1024]{1,0:T(8,128)(2,1)S(1)}, u32[]{:S(2)}, u32[]{:S(2)}) collective-permute-start(bf16[64,1024]{1,0:T(8,128)(2,1)} %get-tuple-element.58), channel_id=1, source_target_pairs={{0,3},{1,2},{2,1},{3,0},{4,7},{5,6},{6,5},{7,4},{8,11},{9,10},{10,... | collective-permute-start | bytes 393224 | tf_op jit(solution)/shard_map/ppermute | solution.py:38
  10.9 9.8 %collective-permute-start.1 = (bf16[64,1024]{1,0:T(8,128)(2,1)}, bf16[64,1024]{1,0:T(8,128)(2,1)S(1)}, u32[]{:S(2)}, u32[]{:S(2)}) collective-permute-start(bf16[64,1024]{1,0:T(8,128)(2,1)} %copy-done.8), channel_id=1, source_target_pairs={{0,1},{1,0},{2,3},{3,2},{4,5},{5,4},{6,7},{7,6},{8,9},{9,8},{10,11... | collective-permute-start | bytes 393224 | tf_op jit(solution)/shard_map/ppermute | solution.py:38
  21.5 2.7 %collective-permute-start.5 = (bf16[256,1024]{1,0:T(8,128)(2,1)S(1)}, bf16[256,1024]{1,0:T(8,128)(2,1)S(1)}, u32[]{:S(2)}, u32[]{:S(2)}) collective-permute-start(bf16[256,1024]{1,0:T(8,128)(2,1)S(1)} %get-tuple-element.60.refs_1_), channel_id=1, source_target_pairs={{0,4},{4,0},{8,12},{12,8},{16,20},{20,16},{24,28},{28,24},{1,5},{5... | collective-permute-start | bytes 1572872 | tf_op jit(solution)/shard_map/ppermute | solution.py:38
  24.1 12.0 %collective-permute-start.8 = (bf16[128,1024]{1,0:T(8,128)(2,1)S(1)}, bf16[128,1024]{1,0:T(8,128)(2,1)S(1)}, u32[]{:S(2)}, u32[]{:S(2)}) collective-permute-start(bf16[128,1024]{1,0:T(8,128)(2,1)S(1)} %get-tuple-element.118), channel_id=1, source_target_pairs={{0,4},{4,0},{8,12},{12,8},{16,20},{20,16},{24,28},{28,24},{1,5},{5... | collective-permute-start | bytes 786440 | tf_op jit(solution)/shard_map/ppermute | solution.py:38
  27.4 7.0 %collective-permute-start.6 = (bf16[512,1024]{1,0:T(8,128)(2,1)S(1)}, bf16[512,1024]{1,0:T(8,128)(2,1)S(1)}, u32[]{:S(2)}, u32[]{:S(2)}) collective-permute-start(bf16[512,1024]{1,0:T(8,128)(2,1)S(1)} %get-tuple-element.122), channel_id=1, source_target_pairs={{0,4},{4,0},{8,12},{12,8},{16,20},{20,16},{24,28},{28,24},{1,5},{5... | collective-permute-start | bytes 3145736 | tf_op jit(solution)/shard_map/ppermute | solution.py:38
  28.7 20.2 %collective-permute-start.11 = (bf16[512,1024]{1,0:T(8,128)(2,1)S(1)}, bf16[512,1024]{1,0:T(8,128)(2,1)S(1)}, u32[]{:S(2)}, u32[]{:S(2)}) collective-permute-start(bf16[512,1024]{1,0:T(8,128)(2,1)S(1)} %convolution_convert_fusion.3), channel_id=1, source_target_pairs={{0,8},{4,20},{8,0},{12,28},{16,24},{20,4},{24,16},{28,12},{1,9},{5... | collective-permute-start | bytes 3145736 | tf_op jit(solution)/shard_map/ppermute | solution.py:38
  31.0 25.1 %collective-permute-start.7 = (bf16[512,1024]{1,0:T(8,128)(2,1)S(1)}, bf16[512,1024]{1,0:T(8,128)(2,1)S(1)}, u32[]{:S(2)}, u32[]{:S(2)}) collective-permute-start(bf16[512,1024]{1,0:T(8,128)(2,1)S(1)} %convolution_convert_fusion.1), channel_id=1, source_target_pairs={{0,1},{1,0},{2,3},{3,2},{4,5},{5,4},{6,7},{7,6},{8,9},{9,8},{10,11... | collective-permute-start | bytes 3145736 | tf_op jit(solution)/shard_map/ppermute | solution.py:38
  36.7 10.0 %collective-permute-start.9 = (bf16[128,1152]{1,0:T(8,128)(2,1)S(1)}, bf16[128,1152]{1,0:T(8,128)(2,1)S(1)}, u32[]{:S(2)}, u32[]{:S(2)}) collective-permute-start(bf16[128,1152]{1,0:T(8,128)(2,1)S(1)} %get-tuple-element.66), channel_id=1, source_target_pairs={{0,8},{4,20},{8,0},{12,28},{16,24},{20,4},{24,16},{28,12},{1,9},{5... | collective-permute-start | bytes 884744 | tf_op jit(solution)/shard_map/ppermute | solution.py:38
  38.9 19.6 %collective-permute-start.15 = (bf16[256,1024]{1,0:T(8,128)(2,1)S(1)}, bf16[256,1024]{1,0:T(8,128)(2,1)S(1)}, u32[]{:S(2)}, u32[]{:S(2)}) collective-permute-start(bf16[256,1024]{1,0:T(8,128)(2,1)S(1)} %get-tuple-element.75), channel_id=1, source_target_pairs={{0,8},{4,20},{8,0},{12,28},{16,24},{20,4},{24,16},{28,12},{1,9},{5... | collective-permute-start | bytes 1572872 | tf_op jit(solution)/shard_map/ppermute | solution.py:38
  47.3 5.6 %collective-permute-start.10 = (bf16[64,1152]{1,0:T(8,128)(2,1)S(1)}, bf16[64,1152]{1,0:T(8,128)(2,1)S(1)}, u32[]{:S(2)}, u32[]{:S(2)}) collective-permute-start(bf16[64,1152]{1,0:T(8,128)(2,1)S(1)} %get-tuple-element.70), channel_id=1, source_target_pairs={{0,16},{4,12},{8,24},{12,4},{16,0},{20,28},{24,8},{28,20},{1,17},{... | collective-permute-start | bytes 442376 | tf_op jit(solution)/shard_map/ppermute | solution.py:38
  49.7 13.6 %collective-permute-start.13 = (bf16[256,1024]{1,0:T(8,128)(2,1)S(1)}, bf16[256,1024]{1,0:T(8,128)(2,1)S(1)}, u32[]{:S(2)}, u32[]{:S(2)}) collective-permute-start(bf16[256,1024]{1,0:T(8,128)(2,1)S(1)} %get-tuple-element.74), channel_id=1, source_target_pairs={{0,16},{4,12},{8,24},{12,4},{16,0},{20,28},{24,8},{28,20},{1,17},{... | collective-permute-start | bytes 1572872 | tf_op jit(solution)/shard_map/ppermute | solution.py:38
  53.5 7.4 %collective-permute-start.14 = (bf16[64,1152]{1,0:T(8,128)(2,1)S(1)}, bf16[64,1152]{1,0:T(8,128)(2,1)S(1)}, u32[]{:S(2)}, u32[]{:S(2)}) collective-permute-start(bf16[64,1152]{1,0:T(8,128)(2,1)S(1)} %shard_map.155.refs_3_.refs_1_), channel_id=1, source_target_pairs={{0,1},{1,0},{2,3},{3,2},{4,5},{5,4},{6,7},{7,6},{8,9},{9,8},{10,11... | collective-permute-start | bytes 442376 | tf_op jit(solution)/shard_map/ppermute | solution.py:38
  56.9 9.2 %collective-permute-start.12 = (bf16[256,1024]{1,0:T(8,128)(2,1)S(1)}, bf16[256,1024]{1,0:T(8,128)(2,1)S(1)}, u32[]{:S(2)}, u32[]{:S(2)}) collective-permute-start(bf16[256,1024]{1,0:T(8,128)(2,1)S(1)} %get-tuple-element.73), channel_id=1, source_target_pairs={{0,8},{4,20},{8,0},{12,28},{16,24},{20,4},{24,16},{28,12},{1,9},{5... | collective-permute-start | bytes 1572872 | tf_op jit(solution)/shard_map/ppermute | solution.py:38
  59.1 12.0 %collective-permute-start.17 = (bf16[128,1024]{1,0:T(8,128)(2,1)S(1)}, bf16[128,1024]{1,0:T(8,128)(2,1)S(1)}, u32[]{:S(2)}, u32[]{:S(2)}) collective-permute-start(bf16[128,1024]{1,0:T(8,128)(2,1)S(1)} %get-tuple-element.80), channel_id=1, source_target_pairs={{0,1},{1,0},{2,3},{3,2},{4,5},{5,4},{6,7},{7,6},{8,9},{9,8},{10,11... | collective-permute-start | bytes 786440 | tf_op jit(solution)/shard_map/ppermute | solution.py:38
  61.5 11.3 %collective-permute-start.16 = (bf16[64,1152]{1,0:T(8,128)(2,1)S(1)}, bf16[64,1152]{1,0:T(8,128)(2,1)S(1)}, u32[]{:S(2)}, u32[]{:S(2)}) collective-permute-start(bf16[64,1152]{1,0:T(8,128)(2,1)S(1)} %shard_map.158.refs_3_.refs_1_), channel_id=1, source_target_pairs={{0,2},{1,3},{2,0},{3,1},{4,6},{5,7},{6,4},{7,5},{8,10},{9,11},{10,... | collective-permute-start | bytes 442376 | tf_op jit(solution)/shard_map/ppermute | solution.py:38
  64.0 10.5 %collective-permute-start.19 = (bf16[128,1024]{1,0:T(8,128)(2,1)S(1)}, bf16[128,1024]{1,0:T(8,128)(2,1)S(1)}, u32[]{:S(2)}, u32[]{:S(2)}) collective-permute-start(bf16[128,1024]{1,0:T(8,128)(2,1)S(1)} %get-tuple-element.82), channel_id=1, source_target_pairs={{0,1},{1,0},{2,3},{3,2},{4,5},{5,4},{6,7},{7,6},{8,9},{9,8},{10,11... | collective-permute-start | bytes 786440 | tf_op jit(solution)/shard_map/ppermute | solution.py:38
  67.6 9.2 %collective-permute-start.20 = (bf16[128,1024]{1,0:T(8,128)(2,1)S(1)}, bf16[128,1024]{1,0:T(8,128)(2,1)S(1)}, u32[]{:S(2)}, u32[]{:S(2)}) collective-permute-start(bf16[128,1024]{1,0:T(8,128)(2,1)S(1)} %get-tuple-element.83), channel_id=1, source_target_pairs={{0,16},{4,12},{8,24},{12,4},{16,0},{20,28},{24,8},{28,20},{1,17},{... | collective-permute-start | bytes 786440 | tf_op jit(solution)/shard_map/ppermute | solution.py:38
  71.7 5.0 %collective-permute-start.21 = (bf16[64,1024]{1,0:T(8,128)(2,1)S(1)}, bf16[64,1024]{1,0:T(8,128)(2,1)S(1)}, u32[]{:S(2)}, u32[]{:S(2)}) collective-permute-start(bf16[64,1024]{1,0:T(8,128)(2,1)S(1)} %get-tuple-element.84), channel_id=1, source_target_pairs={{0,16},{4,12},{8,24},{12,4},{16,0},{20,28},{24,8},{28,20},{1,17},{... | collective-permute-start | bytes 393224 | tf_op jit(solution)/shard_map/ppermute | solution.py:38
  73.4 5.5 %collective-permute-start.18 = (bf16[64,1152]{1,0:T(8,128)(2,1)S(1)}, bf16[64,1152]{1,0:T(8,128)(2,1)S(1)}, u32[]{:S(2)}, u32[]{:S(2)}) collective-permute-start(bf16[64,1152]{1,0:T(8,128)(2,1)S(1)} %shard_map.162.refs_7_.refs_1_), channel_id=1, source_target_pairs={{0,16},{4,12},{8,24},{12,4},{16,0},{20,28},{24,8},{28,20},{1,17},{... | collective-permute-start | bytes 442376 | tf_op jit(solution)/shard_map/ppermute | solution.py:38
  77.5 14.2 %collective-permute-start.28 = (bf16[160,1024]{1,0:T(8,128)(2,1)S(1)}, bf16[160,1024]{1,0:T(8,128)(2,1)S(1)}, u32[]{:S(2)}, u32[]{:S(2)}) collective-permute-start(bf16[160,1024]{1,0:T(8,128)(2,1)S(1)} %get-tuple-element.95), channel_id=1, source_target_pairs={{0,2},{1,3},{2,0},{3,1},{4,6},{5,7},{6,4},{7,5},{8,10},{9,11},{10,... | collective-permute-start | bytes 983048 | tf_op jit(solution)/shard_map/ppermute | solution.py:38
  79.6 4.7 %collective-permute-start.22 = (bf16[128,384]{1,0:T(8,128)(2,1)S(1)}, bf16[128,384]{1,0:T(8,128)(2,1)S(1)}, u32[]{:S(2)}, u32[]{:S(2)}) collective-permute-start(bf16[128,384]{1,0:T(8,128)(2,1)S(1)} %get-tuple-element.86.refs_1_.refs_7_), channel_id=1, source_target_pairs={{0,8},{4,20},{8,0},{12,28},{16,24},{20,4},{24,16},{28,12},{1,9},{5... | collective-permute-start | bytes 294920 | tf_op jit(solution)/shard_map/ppermute | solution.py:38
  81.1 4.6 %collective-permute-start.23 = (bf16[128,384]{1,0:T(8,128)(2,1)S(1)}, bf16[128,384]{1,0:T(8,128)(2,1)S(1)}, u32[]{:S(2)}, u32[]{:S(2)}) collective-permute-start(bf16[128,384]{1,0:T(8,128)(2,1)S(1)} %get-tuple-element.87.refs_2_), channel_id=1, source_target_pairs={{0,8},{4,20},{8,0},{12,28},{16,24},{20,4},{24,16},{28,12},{1,9},{5... | collective-permute-start | bytes 294920 | tf_op jit(solution)/shard_map/ppermute | solution.py:38
  81.6 5.1 %collective-permute-start.24 = (bf16[128,384]{1,0:T(8,128)(2,1)S(1)}, bf16[128,384]{1,0:T(8,128)(2,1)S(1)}, u32[]{:S(2)}, u32[]{:S(2)}) collective-permute-start(bf16[128,384]{1,0:T(8,128)(2,1)S(1)} %get-tuple-element.88.refs_3_), channel_id=1, source_target_pairs={{0,8},{4,20},{8,0},{12,28},{16,24},{20,4},{24,16},{28,12},{1,9},{5... | collective-permute-start | bytes 294920 | tf_op jit(solution)/shard_map/ppermute | solution.py:38
  87.4 1.5 %collective-permute-start.25 = (bf16[256,384]{1,0:T(8,128)(2,1)S(1)}, bf16[256,384]{1,0:T(8,128)(2,1)S(1)}, u32[]{:S(2)}, u32[]{:S(2)}) collective-permute-start(bf16[256,384]{1,0:T(8,128)(2,1)S(1)} %get-tuple-element.89.refs_1_.refs_7_), channel_id=1, source_target_pairs={{0,4},{4,0},{8,12},{12,8},{16,20},{20,16},{24,28},{28,24},{1,5},{5... | collective-permute-start | bytes 589832 | tf_op jit(solution)/shard_map/ppermute | solution.py:38
  87.5 1.7 %collective-permute-start.26 = (bf16[256,384]{1,0:T(8,128)(2,1)S(1)}, bf16[256,384]{1,0:T(8,128)(2,1)S(1)}, u32[]{:S(2)}, u32[]{:S(2)}) collective-permute-start(bf16[256,384]{1,0:T(8,128)(2,1)S(1)} %get-tuple-element.90.refs_2_), channel_id=1, source_target_pairs={{0,4},{4,0},{8,12},{12,8},{16,20},{20,16},{24,28},{28,24},{1,5},{5... | collective-permute-start | bytes 589832 | tf_op jit(solution)/shard_map/ppermute | solution.py:38
  88.0 1.5 %collective-permute-start.27 = (bf16[256,384]{1,0:T(8,128)(2,1)S(1)}, bf16[256,384]{1,0:T(8,128)(2,1)S(1)}, u32[]{:S(2)}, u32[]{:S(2)}) collective-permute-start(bf16[256,384]{1,0:T(8,128)(2,1)S(1)} %get-tuple-element.91.refs_3_), channel_id=1, source_target_pairs={{0,4},{4,0},{8,12},{12,8},{16,20},{20,16},{24,28},{28,24},{1,5},{5... | collective-permute-start | bytes 589832 | tf_op jit(solution)/shard_map/ppermute | solution.py:38
  (8 other events, 12.7 us)
